TPU v7x, 32 devices: a whole 2x2x4 slice. The times are simulated.
32 devices in a mesh: dp: 16 (over z, y, core), stream: 2 (over x).
Axes of the slice: x: 2, y: 2, z: 4, core: 2. Of those that a mesh axis runs over, the one named last changes fastest.
Arguments:
- patches: bfloat16 [32768, 768], P(('dp', 'stream')), may hold values from -6 to 6
- embedding: float32 [128, 768], P(('dp', 'stream')), may hold values from -6 to 6
- long_image: int32 [32], P(('dp', 'stream')), may hold values 0 or 1
- routes: int32 [32768, 2], P(('dp', 'stream')), may hold values from 0 to 7, all different within a row; in each aligned block of 1024 rows (0 to 1023, 1024 to 2047, ...) at most 288 rows name the same one
- cotangent: bfloat16 [32768, 768], P(('dp', 'stream')), may hold values from -6 to 6
- ada_weight: bfloat16 [768, 4608], replicated, may hold values from -0.4375 to 0.4375
- qkv_weight: bfloat16 [768, 2304], replicated, may hold values from -0.21875 to 0.21875
- out_weight: bfloat16 [768, 768], replicated, may hold values from -0.875 to 0.875
- shared_up: bfloat16 [768, 3072], replicated, may hold values from -0.21875 to 0.21875
- shared_down: bfloat16 [3072, 768], replicated, may hold values from -0.109375 to 0.109375
- router_weight: bfloat16 [768, 8], replicated, may hold values from -0.15625 to 0.15625
- expert_up: bfloat16 [8, 768, 3072], P('stream'), may hold values from -0.21875 to 0.21875
- expert_down: bfloat16 [8, 3072, 768], P('stream'), may hold values from -0.109375 to 0.109375
Outputs:
- mixed: bfloat16 [32768, 768], P(('dp', 'stream'))
- grad_patches: float32 [32768, 768], P(('dp', 'stream'))
- grad_embedding: float32 [128, 768], P(('dp', 'stream'))
- grad_ada: float32 [768, 4608], P('dp')
- grad_qkv: float32 [768, 2304], P('dp')
- grad_out_weight: float32 [768, 768], P('dp')
- grad_shared_up: float32 [768, 3072], P('dp')
- grad_shared_down: float32 [3072, 768], P('dp')
- grad_router: float32 [768, 8], P('dp')
- grad_expert_up: float32 [8, 768, 3072], P('stream', 'dp')
- grad_expert_down: float32 [8, 3072, 768], P('stream', 'dp')
Inputs may be any that keep to these rules, and one draw needn't show every extreme that they name: `routes`: in the rows of one device (aligned blocks of 1024 rows) each expert is named by at most 288 rows; a row names two different experts. `long_image`: 1: the device's patches are one image; 0: they are images of 256 patches.
All inputs are finite; a program needn't handle non-finite values.
Results may differ from a plain program's by a relative error of at most 0.022.
The roundings to bfloat16 on the way count: a program that leaves them out, or rounds other values in their place, can miss the bound.
Values may be sent and summed in bfloat16 or wider, within the bound.
No kernel may reach another device: no remote copies, remote signals or barrier semaphores. Data moves between devices by JAX's collectives and lax.ppermute only.
A program may use at most 384 MiB of HBM per device.

v0:
```python
import math

import jax
import jax.numpy as jnp
from jax import lax
from jax.sharding import PartitionSpec as P

HEADS = 12
HEAD_DIM = 64
EXPERTS = 8
CAP = 288


HIGH = lax.Precision.HIGHEST
EPSILON = 1e-06


def gelu_tanh(values):
    return jax.nn.gelu(values, approximate=True)


def normalize(values):
    centered = values - jnp.mean(values, -1, keepdims=True)
    spread = lax.rsqrt(jnp.mean(centered * centered, -1, keepdims=True) + EPSILON)
    return (centered * spread, spread)


def normalize_back(grad_normed, normed, spread):
    return spread * (
        grad_normed
        - jnp.mean(grad_normed, -1, keepdims=True)
        - normed * jnp.mean(grad_normed * normed, -1, keepdims=True)
    )


def split_packed(packed, seg_len):
    row_count = packed.shape[0]
    model_width = packed.shape[1] // 3
    groups = row_count // seg_len
    block_rows = min(512, seg_len)
    part_count = seg_len // block_rows
    queries = (
        packed[:, :model_width]
        .reshape(groups, part_count, block_rows, HEADS, HEAD_DIM)
        .swapaxes(0, 1)
    )
    key_heads = packed[:, model_width : 2 * model_width].reshape(groups, seg_len, HEADS, HEAD_DIM)
    values = packed[:, 2 * model_width :].reshape(groups, seg_len, HEADS, HEAD_DIM)
    return (queries, key_heads, values, groups, block_rows, part_count)


def attend(packed, seg_len):
    row_count = packed.shape[0]
    model_width = packed.shape[1] // 3
    factor = 1.0 / math.sqrt(HEAD_DIM)
    queries, key_heads, values, groups, block_rows, part_count = split_packed(packed, seg_len)

    def one_block(query_block):
        scores = (
            jnp.einsum(
                "gqhd,gkhd->ghqk", query_block, key_heads, preferred_element_type=jnp.float32
            )
            * factor
        )
        row_max = jnp.max(scores, -1, keepdims=True)
        shifted = jnp.exp(scores - row_max)
        row_sum = jnp.sum(shifted, -1, keepdims=True)
        weights = (shifted / row_sum).astype(jnp.bfloat16)
        mixture = jnp.einsum("ghqk,gkhd->gqhd", weights, values, preferred_element_type=jnp.float32)
        return (mixture, row_max[..., 0] + jnp.log(row_sum[..., 0]))

    mixture, logsum = lax.map(one_block, queries)
    return (mixture.swapaxes(0, 1).reshape(row_count, model_width), logsum.reshape(-1))


def attend_back(packed, logsum, grad_mixture, seg_len):
    row_count = packed.shape[0]
    model_width = packed.shape[1] // 3
    factor = 1.0 / math.sqrt(HEAD_DIM)
    queries, key_heads, values, groups, block_rows, part_count = split_packed(packed, seg_len)
    grad_blocks = grad_mixture.reshape(groups, part_count, block_rows, HEADS, HEAD_DIM).swapaxes(
        0, 1
    )
    logsum_blocks = logsum.reshape(part_count, groups, HEADS, block_rows)

    def one_block(carried, inputs):
        grad_keys, grad_values = carried
        query_block, grad_block, logsum_block = inputs
        scores = (
            jnp.einsum(
                "gqhd,gkhd->ghqk", query_block, key_heads, preferred_element_type=jnp.float32
            )
            * factor
        )
        prob_full = jnp.exp(scores - logsum_block[..., None])
        grad_values = grad_values + jnp.einsum(
            "ghqk,gqhd->gkhd",
            prob_full.astype(jnp.bfloat16),
            grad_block,
            preferred_element_type=jnp.float32,
        )
        grad_probs = jnp.einsum(
            "gqhd,gkhd->ghqk", grad_block, values, preferred_element_type=jnp.float32
        )
        row_inner = jnp.sum(grad_probs * prob_full, -1, keepdims=True)
        grad_scores = (prob_full * (grad_probs - row_inner)).astype(jnp.bfloat16)
        grad_query = (
            jnp.einsum(
                "ghqk,gkhd->gqhd", grad_scores, key_heads, preferred_element_type=jnp.float32
            )
            * factor
        )
        grad_keys = (
            grad_keys
            + jnp.einsum(
                "ghqk,gqhd->gkhd", grad_scores, query_block, preferred_element_type=jnp.float32
            )
            * factor
        )
        return ((grad_keys, grad_values), grad_query)

    zeros_kv = jnp.zeros((groups, seg_len, HEADS, HEAD_DIM), jnp.float32)
    (grad_keys, grad_values), grad_query = lax.scan(
        one_block, (zeros_kv, zeros_kv), (queries, grad_blocks, logsum_blocks)
    )
    return jnp.concatenate(
        [
            grad_query.swapaxes(0, 1).reshape(row_count, model_width),
            grad_keys.reshape(row_count, model_width),
            grad_values.reshape(row_count, model_width),
        ],
        1,
    )


def local(
    patches,
    embedding,
    long_image,
    routes,
    cotangent,
    ada_weight,
    qkv_weight,
    out_weight,
    shared_up,
    shared_down,
    router_weight,
    expert_up,
    expert_down,
):
    row_count, model_width = patches.shape
    block_count = embedding.shape[0]
    short_len = row_count // block_count
    lane_count = lax.axis_size("stream")
    local_experts = expert_up.shape[0]
    is_long = long_image[0] > 0

    def blocks(values):
        return values.reshape(block_count, short_len, model_width)

    def flatten(values):
        return values.reshape(row_count, model_width)

    used = jnp.where(is_long, jnp.broadcast_to(embedding[0:1], embedding.shape), embedding)
    activated, silu_back = jax.vjp(jax.nn.silu, used)
    ada_full = ada_weight.astype(jnp.float32)
    modulation = jnp.dot(activated, ada_full, precision=HIGH)
    pieces = [
        modulation[:, column * model_width : (column + 1) * model_width][:, None, :]
        for column in range(6)
    ]
    shift_one, scale_one, gate_one, shift_two, scale_two, gate_two = pieces
    inputs_full = blocks(patches.astype(jnp.float32))
    normed_one, spread_one = normalize(inputs_full)
    hidden_one = flatten(normed_one * (1.0 + scale_one) + shift_one).astype(jnp.bfloat16)
    packed = jnp.dot(hidden_one, qkv_weight, preferred_element_type=jnp.float32).astype(
        jnp.bfloat16
    )
    attended, logsum = lax.cond(
        is_long,
        lambda packed_in: attend(packed_in, row_count),
        lambda packed_in: attend(packed_in, short_len),
        packed,
    )
    attended_low = attended.astype(jnp.bfloat16)
    branch_one = blocks(jnp.dot(attended_low, out_weight, preferred_element_type=jnp.float32))
    middle = inputs_full + gate_one * branch_one
    normed_two, spread_two = normalize(middle)
    hidden_two = flatten(normed_two * (1.0 + scale_two) + shift_two).astype(jnp.bfloat16)
    shared_pre = jnp.dot(hidden_two, shared_up, preferred_element_type=jnp.float32)
    shared_act, shared_back = jax.vjp(gelu_tanh, shared_pre)
    shared_low = shared_act.astype(jnp.bfloat16)
    shared_out = jnp.dot(shared_low, shared_down, preferred_element_type=jnp.float32)
    logits = jnp.dot(hidden_two, router_weight, preferred_element_type=jnp.float32)
    chosen_hot = (routes[:, :, None] == jnp.arange(EXPERTS)[None, None, :]).astype(jnp.float32)
    gates = jax.nn.softmax(jnp.sum(chosen_hot * logits[:, None, :], -1), -1)
    flat_routes = routes.reshape(-1)
    route_hits = (flat_routes[:, None] == jnp.arange(EXPERTS)[None, :]).astype(jnp.int32)
    earlier = jnp.cumsum(route_hits, 0) - route_hits
    target = flat_routes * CAP + jnp.sum(earlier * route_hits, 1)

    def spread_rows(rows_low):
        buffer = jnp.zeros((EXPERTS * CAP, model_width), jnp.bfloat16).at[target].set(rows_low)
        return buffer.reshape(lane_count, local_experts, CAP, model_width)

    def collect(arrived):
        return (
            arrived.reshape(EXPERTS * CAP, model_width)[target]
            .astype(jnp.float32)
            .reshape(row_count, 2, model_width)
        )

    def by_expert(arrived):
        return arrived.swapaxes(0, 1).reshape(local_experts, lane_count * CAP, model_width)

    def by_source(results):
        return results.reshape(local_experts, lane_count, CAP, model_width).swapaxes(0, 1)

    expert_in = by_expert(
        lax.all_to_all(
            spread_rows(jnp.repeat(hidden_two, 2, axis=0)),
            "stream",
            split_axis=0,
            concat_axis=0,
            tiled=True,
        )
    )
    expert_pre = jnp.einsum(
        "jrd,jdf->jrf", expert_in, expert_up, preferred_element_type=jnp.float32
    )
    expert_act, expert_back = jax.vjp(gelu_tanh, expert_pre)
    expert_low = expert_act.astype(jnp.bfloat16)
    expert_out = jnp.einsum(
        "jrf,jfd->jrd", expert_low, expert_down, preferred_element_type=jnp.float32
    ).astype(jnp.bfloat16)
    picked = collect(
        lax.all_to_all(by_source(expert_out), "stream", split_axis=0, concat_axis=0, tiled=True)
    )
    routed = jnp.sum(gates[:, :, None] * picked, 1)
    branch_two = blocks(shared_out + routed)
    mixed = flatten(middle + gate_two * branch_two).astype(jnp.bfloat16)
    grad_top = blocks(cotangent.astype(jnp.float32))
    grad_gate_two = jnp.sum(grad_top * branch_two, 1)
    grad_branch = flatten(grad_top * gate_two)
    grad_pick = (
        (gates[:, :, None] * grad_branch[:, None, :])
        .astype(jnp.bfloat16)
        .reshape(2 * row_count, model_width)
    )
    grad_arrived = by_expert(
        lax.all_to_all(spread_rows(grad_pick), "stream", split_axis=0, concat_axis=0, tiled=True)
    )
    grad_expert_down = jnp.einsum(
        "jrf,jrd->jfd", expert_low, grad_arrived, preferred_element_type=jnp.float32
    )
    grad_expert_act = jnp.einsum(
        "jrd,jfd->jrf", grad_arrived, expert_down, preferred_element_type=jnp.float32
    )
    grad_expert_pre = expert_back(grad_expert_act)[0].astype(jnp.bfloat16)
    grad_expert_up = jnp.einsum(
        "jrd,jrf->jdf", expert_in, grad_expert_pre, preferred_element_type=jnp.float32
    )
    grad_expert_in = jnp.einsum(
        "jrf,jdf->jrd", grad_expert_pre, expert_up, preferred_element_type=jnp.float32
    ).astype(jnp.bfloat16)
    grad_routed = jnp.sum(
        collect(
            lax.all_to_all(
                by_source(grad_expert_in), "stream", split_axis=0, concat_axis=0, tiled=True
            )
        ),
        1,
    )
    grad_shared_low = grad_branch.astype(jnp.bfloat16)
    grad_shared_down = jnp.einsum(
        "rf,rd->fd", shared_low, grad_shared_low, preferred_element_type=jnp.float32
    )
    grad_shared_act = jnp.einsum(
        "rd,fd->rf", grad_shared_low, shared_down, preferred_element_type=jnp.float32
    )
    grad_shared_pre = shared_back(grad_shared_act)[0].astype(jnp.bfloat16)
    grad_shared_up = jnp.einsum(
        "rd,rf->df", hidden_two, grad_shared_pre, preferred_element_type=jnp.float32
    )
    grad_gates = jnp.sum(picked * grad_branch[:, None, :], -1)
    grad_chosen = gates * (grad_gates - jnp.sum(gates * grad_gates, -1, keepdims=True))
    grad_logits = jnp.sum(chosen_hot * grad_chosen[:, :, None], 1)
    hidden_two_full = hidden_two.astype(jnp.float32)
    router_full = router_weight.astype(jnp.float32)
    grad_router = jnp.dot(hidden_two_full.T, grad_logits, precision=HIGH)
    grad_hidden = jnp.dot(grad_logits, router_full.T, precision=HIGH) + grad_routed
    grad_hidden = blocks(
        grad_hidden
        + jnp.einsum("rf,df->rd", grad_shared_pre, shared_up, preferred_element_type=jnp.float32)
    )
    grad_shift_two = jnp.sum(grad_hidden, 1)
    grad_scale_two = jnp.sum(grad_hidden * normed_two, 1)
    grad_middle = grad_top + normalize_back(grad_hidden * (1.0 + scale_two), normed_two, spread_two)
    grad_gate_one = jnp.sum(grad_middle * branch_one, 1)
    grad_branch_one = flatten(grad_middle * gate_one).astype(jnp.bfloat16)
    grad_out_weight = jnp.einsum(
        "rd,re->de", attended_low, grad_branch_one, preferred_element_type=jnp.float32
    )
    grad_attended = jnp.einsum(
        "re,de->rd", grad_branch_one, out_weight, preferred_element_type=jnp.float32
    ).astype(jnp.bfloat16)
    grad_packed = lax.cond(
        is_long,
        lambda packed_in, logsum_in, grad_in: attend_back(packed_in, logsum_in, grad_in, row_count),
        lambda packed_in, logsum_in, grad_in: attend_back(packed_in, logsum_in, grad_in, short_len),
        packed,
        logsum,
        grad_attended,
    ).astype(jnp.bfloat16)
    grad_qkv = jnp.einsum("rd,re->de", hidden_one, grad_packed, preferred_element_type=jnp.float32)
    grad_hidden_one = blocks(
        jnp.einsum("re,de->rd", grad_packed, qkv_weight, preferred_element_type=jnp.float32)
    )
    grad_shift_one = jnp.sum(grad_hidden_one, 1)
    grad_scale_one = jnp.sum(grad_hidden_one * normed_one, 1)
    grad_inputs = grad_middle + normalize_back(
        grad_hidden_one * (1.0 + scale_one), normed_one, spread_one
    )
    grad_modulation = jnp.concatenate(
        [
            grad_shift_one,
            grad_scale_one,
            grad_gate_one,
            grad_shift_two,
            grad_scale_two,
            grad_gate_two,
        ],
        1,
    )
    grad_ada = jnp.dot(activated.T, grad_modulation, precision=HIGH)
    grad_used = silu_back(jnp.dot(grad_modulation, ada_full.T, precision=HIGH))[0]
    grad_embedding = jnp.where(
        is_long, jnp.zeros_like(grad_used).at[0].set(jnp.sum(grad_used, 0)), grad_used
    )
    shares = (
        lax.psum_scatter(
            grad_ada.astype(jnp.bfloat16), "dp", scatter_dimension=0, tiled=True
        ).astype(jnp.float32),
        lax.psum_scatter(
            grad_qkv.astype(jnp.bfloat16), "dp", scatter_dimension=0, tiled=True
        ).astype(jnp.float32),
        lax.psum_scatter(
            grad_out_weight.astype(jnp.bfloat16), "dp", scatter_dimension=0, tiled=True
        ).astype(jnp.float32),
        lax.psum_scatter(
            grad_shared_up.astype(jnp.bfloat16), "dp", scatter_dimension=0, tiled=True
        ).astype(jnp.float32),
        lax.psum_scatter(
            grad_shared_down.astype(jnp.bfloat16), "dp", scatter_dimension=0, tiled=True
        ).astype(jnp.float32),
        lax.psum_scatter(
            grad_router.astype(jnp.bfloat16), "dp", scatter_dimension=0, tiled=True
        ).astype(jnp.float32),
    )
    expert_summed = (
        lax.psum_scatter(
            grad_expert_up.astype(jnp.bfloat16), "dp", scatter_dimension=1, tiled=True
        ).astype(jnp.float32),
        lax.psum_scatter(
            grad_expert_down.astype(jnp.bfloat16), "dp", scatter_dimension=1, tiled=True
        ).astype(jnp.float32),
    )
    summed = (
        lax.psum(shares[0].astype(jnp.bfloat16), "stream").astype(jnp.float32),
        lax.psum(shares[1].astype(jnp.bfloat16), "stream").astype(jnp.float32),
        lax.psum(shares[2].astype(jnp.bfloat16), "stream").astype(jnp.float32),
        lax.psum(shares[3].astype(jnp.bfloat16), "stream").astype(jnp.float32),
        lax.psum(shares[4].astype(jnp.bfloat16), "stream").astype(jnp.float32),
        lax.psum(shares[5].astype(jnp.bfloat16), "stream").astype(jnp.float32),
    )
    return (
        mixed,
        flatten(grad_inputs),
        grad_embedding,
        summed[0],
        summed[1],
        summed[2],
        summed[3],
        summed[4],
        summed[5],
        expert_summed[0],
        expert_summed[1],
    )


def solution(mesh):
    return jax.shard_map(
        local,
        mesh=mesh,
        in_specs=(
            P(("dp", "stream"), None),
            P(("dp", "stream"), None),
            P(("dp", "stream")),
            P(("dp", "stream"), None),
            P(("dp", "stream"), None),
            P(),
            P(),
            P(),
            P(),
            P(),
            P(),
            P("stream", None, None),
            P("stream", None, None),
        ),
        out_specs=(
            P(("dp", "stream"), None),
            P(("dp", "stream"), None),
            P(("dp", "stream"), None),
            P("dp", None),
            P("dp", None),
            P("dp", None),
            P("dp", None),
            P("dp", None),
            P("dp", None),
            P("stream", "dp", None),
            P("stream", "dp", None),
        ),
        check_vma=False,
    )
```

profile of v0, /device:TPU:0, one launch (start us, length us, event | category | flops | bytes accessed | tf_op | source)
XLA Modules:
  0.0 1550.1 jit_solution(14358259760670645465)
XLA Ops:
  74.3 38.1 %conditional.12 = (f32[12288]{0:T(1024)}, bf16[1024,768]{0,1:T(8,128)(2,1)S(1)}) conditional(s32[]{:T(128)} %convert_element_type.191, bf16[1024,2304]{0,1:T(8,128)(2,1)} %copy.181, bf16[1024,2304]{0,1:T(8,128)(2,1)} %copy.181), branch_computations={%region_2.5_spmd, %region_5.10_spmd} | conditional | flops 1667229696 | bytes 122626360
  129.0 13.0 scatter_custom_fusion.1
  159.8 12.5 scatter_custom_fusion
  205.9 22.6 %fusion.124 = f32[4,576,3072]{2,1,0:T(8,128)} fusion(bf16[4,576,768]{2,1,0:T(8,128)(2,1)} %bitcast.343, bf16[4,3072,768]{2,1,0:T(8,128)(2,1)} %param.35), kind=kOutput, calls=%fused_computation.221 | convolution fusion | flops 10871635968 | bytes 50724864 | tf_op jit(solution)/shard_map/jrd,jfd->jrf/dot_general | solution.py:256
  228.4 38.7 %fusion.74 = (bf16[4,576,3072]{2,1,0:T(8,128)(2,1)}, f32[4,576,3072]{2,1,0:T(8,128)}) fusion(f32[4,576,3072]{2,1,0:T(8,128)} %fusion.124, bf16[4,576,768]{2,1,0:T(8,128)(2,1)} %bitcast.345, bf16[4,768,3072]{2,1,0:T(8,128)(2,1)} %param.34), kind=kOutput, calls=%fused_computation.91 | convolution fusion | flops 11013193728 | bytes 93192192 | tf_op jit(solution)/shard_map/jrd,jdf->jrf/dot_general | solution.py:228
  267.2 19.7 %convolution_convert_fusion.7 = bf16[4,576,768]{2,1,0:T(8,128)(2,1)} fusion(bf16[4,576,3072]{2,1,0:T(8,128)(2,1)} %get-tuple-element.392, bf16[4,768,3072]{2,1,0:T(8,128)(2,1)} %param.34), kind=kOutput, calls=%fused_computation.154 | convolution fusion | flops 10873405440 | bytes 36569088 | tf_op jit(solution)/shard_map/jrf,jdf->jrd/dot_general | solution.py:263
  296.2 23.1 %convolution_convert_fusion.8 = bf16[4,576,768]{2,1,0:T(8,128)(2,1)} fusion(bf16[4,3072,768]{2,1,0:T(8,128)(2,1)} %param.35, f32[4,576,3072]{2,1,0:T(8,128)} %get-tuple-element.393), kind=kOutput, calls=%fused_computation.155 | convolution fusion | flops 10937106432 | bytes 50724864 | tf_op jit(solution)/shard_map/jrf,jfd->jrd/dot_general | solution.py:233
  328.7 16.2 %fusion.81 = bf16[1024,3072]{1,0:T(8,128)(2,1)S(1)} fusion(f32[1024,3072]{1,0:T(8,128)} %fusion.122, bf16[3072,768]{1,0:T(8,128)(2,1)} %param.32, f32[1024,768]{1,0:T(8,128)} %get-tuple-element.397), kind=kOutput, calls=%fused_computation.101 | convolution fusion | flops 4895539200 | bytes 26738688 | tf_op jit(solution)/shard_map/rd,fd->rf/dot_general | solution.py:278
  356.5 12.5 gather_fusion.1
  376.8 13.0 gather_fusion
  397.6 17.2 %multiply_reduce_fusion.4 = (f32[1024,2]{1,0:T(8,128)}, f32[1024,768]{1,0:T(8,128)}) fusion(f32[1024,2,768]{2,1,0:T(2,128)} %reshape.632, f32[1024,768]{1,0:T(8,128)} %get-tuple-element.397, f32[1024,2]{1,0:T(8,128)} %copy.183), kind=kLoop, calls=%fused_computation.107 | loop fusion | flops 5502976 | bytes 12599296 | tf_op jit(solution)/shard_map/reduce_sum | solution.py:285
  437.1 16.5 %fusion.83 = (bf16[1024,768]{1,0:T(8,128)(2,1)}, f32[1024,768]{1,0:T(8,128)}, bf16[1024,768]{1,0:T(8,128)(2,1)}, f32[1024,768]{1,0:T(8,128)}) fusion(f32[4,768]{1,0:T(4,128)S(1)} %copy-done.40, f32[1024]{0:T(1024)S(1)} %broadcast_multiply_fusion.3, f32[1024,768]{1,0:T(8,128)S(1)} %copy-done.2, f32[1024]{0:T(1024)S(1)} %copy-done.43, ...), kind=kOutput, calls=%fused_computation.124 | convolution fusion | flops 4871946240 | bytes 37801984 | tf_op jit(solution)/shard_map/dot_general | solution.py:193
  457.5 12.7 convolution_convert_fusion.4
  483.8 100.6 %conditional.13 = (bf16[1024,2304]{0,1:T(8,128)(2,1)}) conditional(s32[]{:T(128)} %convert_element_type.191, (bf16[1024,2304]{1,0:T(8,128)(2,1)}, f32[12288]{0:T(1024)}, bf16[1024,768]{1,0:T(8,128)(2,1)}) %tuple.60, (bf16[1024,2304]{1,0:T(8,128)(2,1)}, bf16[1024,768]{1,0:T(8,128)(2,1)}, f32[12288]{0:T(1024)}) %tuple.61), branch_computations={%region_27.29_spmd, %region_29.33_spmd} | conditional | flops 4120897536 | bytes 273277248
  613.3 13.2 convolution_convert_fusion.2
  630.9 70.8 %reduce-scatter.19.cloned.1.call-done = bf16[192,768]{1,0:T(8,128)(2,1)} async-done(((bf16[3072,768]{1,0:T(8,128)(2,1)}), bf16[192,768]{1,0:T(8,128)(2,1)}) %reduce-scatter.19.cloned.1.call-update) | async-done | bytes 294928 | tf_op jit(solution)/shard_map/reduce_scatter | solution.py:353
  701.7 79.0 %reduce-scatter.17.cloned.1.call-done = bf16[48,3072]{1,0:T(8,128)(2,1)} async-done(((bf16[768,3072]{1,0:T(8,128)(2,1)}), bf16[48,3072]{1,0:T(8,128)(2,1)}) %reduce-scatter.17.cloned.1.call-update) | async-done | bytes 294928 | tf_op jit(solution)/shard_map/reduce_scatter | solution.py:350
  780.8 163.5 %reduce-scatter.13.cloned.1.call-done = bf16[48,2304]{1,0:T(8,128)(2,1)} async-done(((bf16[768,2304]{1,0:T(8,128)(2,1)}), bf16[48,2304]{1,0:T(8,128)(2,1)}) %reduce-scatter.13.cloned.1.call-update) | async-done | bytes 221200 | tf_op jit(solution)/shard_map/reduce_scatter | solution.py:344
  944.3 92.8 %reduce-scatter.11.cloned.1.call-done = bf16[48,4608]{1,0:T(8,128)(2,1)} async-done(((bf16[768,4608]{1,0:T(8,128)(2,1)}), bf16[48,4608]{1,0:T(8,128)(2,1)}) %reduce-scatter.11.cloned.1.call-update) | async-done | bytes 442384 | tf_op jit(solution)/shard_map/reduce_scatter | solution.py:341
  1037.4 23.4 %convolution_convert_fusion.1 = bf16[4,768,3072]{2,1,0:T(8,128)(2,1)} fusion(bf16[4,576,768]{2,1,0:T(8,128)(2,1)} %bitcast.346, bf16[4,576,3072]{2,1,0:T(8,128)(2,1)} %get-tuple-element.392), kind=kOutput, calls=%fused_computation.104 | convolution fusion | flops 10881073152 | bytes 36569088 | tf_op jit(solution)/shard_map/jrd,jrf->jdf/dot_general | solution.py:260
  1060.8 26.7 %convolution_convert_fusion = bf16[4,3072,768]{2,1,0:T(8,128)(2,1)} fusion(bf16[4,576,768]{2,1,0:T(8,128)(2,1)} %bitcast.344, f32[4,576,3072]{2,1,0:T(8,128)} %get-tuple-element.393), kind=kOutput, calls=%fused_computation.103 | convolution fusion | flops 10944774144 | bytes 50724864 | tf_op jit(solution)/shard_map/jrf,jrd->jfd/dot_general | solution.py:253
  1107.3 36.1 %all-reduce.4.cloned.1.call-done = (bf16[48,4608]{1,0:T(8,128)(2,1)}, bf16[48,2304]{1,0:T(8,128)(2,1)}, bf16[48,768]{1,0:T(8,128)(2,1)}, bf16[48,3072]{1,0:T(8,128)(2,1)}, bf16[192,768]{1,0:T(8,128)(2,1)}) async-done(((bf16[48,4608]{1,0:T(8,128)(2,1)}, bf16[48,2304]{1,0:T(8,128)(2,1)}, bf16[48,768]{1,0:T(8,128)(2,1)}, bf16[48,3072]{1,0:T(8,128)(2,1)}, bf16[192,768]{1,0:T(8,128)(2,1)}), ...) | async-done | bytes 1327120 | tf_op jit(solution)/shard_map/psum | solution.py:369
  1152.2 190.1 %reduce-scatter.21.cloned.1.call-done = bf16[4,48,3072]{2,1,0:T(8,128)(2,1)} async-done(((bf16[4,768,3072]{2,1,0:T(8,128)(2,1)}), bf16[4,48,3072]{2,1,0:T(8,128)(2,1)}) %reduce-scatter.21.cloned.1.call-update) | async-done | bytes 1179664 | tf_op jit(solution)/shard_map/reduce_scatter | solution.py:361
  1345.3 195.3 %reduce-scatter.23.cloned.1.call-done = bf16[4,192,768]{2,1,0:T(8,128)(2,1)} async-done(((bf16[4,3072,768]{2,1,0:T(8,128)(2,1)}), bf16[4,192,768]{2,1,0:T(8,128)(2,1)}) %reduce-scatter.23.cloned.1.call-update) | async-done | bytes 1179664 | tf_op jit(solution)/shard_map/reduce_scatter | solution.py:364
  (295 shorter events, 403.6 us)
Async XLA Ops:
  7.2 39.8 %copy-start = (bf16[768,2304]{1,0:T(8,128)(2,1)S(1)}, bf16[768,2304]{1,0:T(8,128)(2,1)}, u32[]{:S(2)}) copy-start(bf16[768,2304]{1,0:T(8,128)(2,1)} %param.29) | copy-start | bytes 10616836
  17.3 24.0 %copy-start.53 = (f32[1024]{0:T(1024)}, f32[1024]{0:T(1024)S(1)}, u32[]{:S(2)}) copy-start(f32[1024]{0:T(1024)S(1)} %broadcast_multiply_fusion.6) | copy-start | bytes 12292
  26.4 19.4 %copy-start.49 = (f32[4,768]{1,0:T(4,128)}, f32[4,768]{1,0:T(4,128)S(1)}, u32[]{:S(2)}) copy-start(f32[4,768]{1,0:T(4,128)S(1)} %get-tuple-element.389) | copy-start | bytes 36868
  74.3 39.2 %copy-start.39 = (f32[4,768]{1,0:T(4,128)S(1)}, f32[4,768]{1,0:T(4,128)}, u32[]{:S(2)}) copy-start(f32[4,768]{1,0:T(4,128)} %get-tuple-element.390) | copy-start | bytes 36868
  121.9 20.1 %copy-start.35 = (f32[1024,2]{0,1:T(2,128)}, f32[1024,2]{0,1:T(2,128)S(1)}, u32[]{:S(2)}) copy-start(f32[1024,2]{0,1:T(2,128)S(1)} %select_reduce_fusion.1) | copy-start | bytes 24580
  122.0 20.0 %copy-start.55 = (f32[1024]{0:T(1024)}, f32[1024]{0:T(1024)S(1)}, u32[]{:S(2)}) copy-start(f32[1024]{0:T(1024)S(1)} %reduce_max.28) | copy-start | bytes 12292
  142.0 30.3 %all-to-all-start.2 = ((bf16[2,4,288,768]{3,2,1,0:T(8,128)(2,1)}), bf16[2,4,288,768]{3,2,1,0:T(8,128)(2,1)}, u32[]{:S(2)}, u32[]{:S(2)}) async-start(bf16[2,4,288,768]{3,2,1,0:T(8,128)(2,1)} %bitcast.331), calls=%async_computation.2 | async-start | bytes 7077888 | tf_op jit(solution)/shard_map/all_to_all | solution.py:251
  172.3 29.5 %all-to-all-start = ((bf16[2,4,288,768]{3,2,1,0:T(8,128)(2,1)}), bf16[2,4,288,768]{3,2,1,0:T(8,128)(2,1)}, u32[]{:S(2)}, u32[]{:S(2)}) async-start(bf16[2,4,288,768]{3,2,1,0:T(8,128)(2,1)} %bitcast.330), calls=%async_computation | async-start | bytes 7077888 | tf_op jit(solution)/shard_map/all_to_all | solution.py:220
  290.8 32.4 %all-to-all-start.3 = ((bf16[2,4,288,768]{3,2,1,0:T(8,128)(2,1)}), bf16[2,4,288,768]{3,2,1,0:T(8,128)(2,1)}, u32[]{:S(2)}, u32[]{:S(2)}) async-start(bf16[2,4,288,768]{3,2,1,0:T(8,128)(2,1)} %bitcast.329), calls=%async_computation.3 | async-start | bytes 7077888 | tf_op jit(solution)/shard_map/all_to_all | solution.py:268
  323.3 53.5 %all-to-all-start.1 = ((bf16[2,4,288,768]{3,2,1,0:T(8,128)(2,1)}), bf16[2,4,288,768]{3,2,1,0:T(8,128)(2,1)}, u32[]{:S(2)}, u32[]{:S(2)}) async-start(bf16[2,4,288,768]{3,2,1,0:T(8,128)(2,1)} %bitcast.328), calls=%async_computation.1 | async-start | bytes 7077888 | tf_op jit(solution)/shard_map/all_to_all | solution.py:237
  328.7 302.2 %reduce-scatter.15.cloned.1.call-start = ((), (), s32[]{:S(2)}) async-start(), calls=%async_computation.14 | async-start | bytes 1253376 | tf_op jit(solution)/shard_map/reduce_scatter | solution.py:347
  397.6 19.1 %copy-start.36 = (f32[1024,2]{0,1:T(2,128)S(1)}, f32[1024,2]{0,1:T(2,128)}, u32[]{:S(2)}) copy-start(f32[1024,2]{0,1:T(2,128)} %copy-done.35) | copy-start | bytes 24580
  397.6 20.6 %copy-start.46 = (s32[1024,2]{0,1:T(2,128)S(1)}, s32[1024,2]{0,1:T(2,128)}, u32[]{:S(2)}) copy-start(s32[1024,2]{0,1:T(2,128)} %param.26) | copy-start | bytes 24580
  436.9 16.6 %copy-start.6 = (f32[1024,768]{1,0:T(8,128)}, f32[1024,768]{1,0:T(8,128)S(1)}, u32[]{:S(2)}) copy-start(f32[1024,768]{1,0:T(8,128)S(1)} %get-tuple-element.394) | copy-start | bytes 9437188
  437.0 16.6 %copy-start.64 = (f32[1024]{0:T(1024)}, f32[1024]{0:T(1024)S(1)}, u32[]{:S(2)}) copy-start(f32[1024]{0:T(1024)S(1)} %broadcast_multiply_fusion.4) | copy-start | bytes 12292
  437.0 16.6 %copy-start.65 = (f32[1024]{0:T(1024)}, f32[1024]{0:T(1024)S(1)}, u32[]{:S(2)}) copy-start(f32[1024]{0:T(1024)S(1)} %broadcast_multiply_fusion.3) | copy-start | bytes 12292
  457.5 244.3 %reduce-scatter.19.cloned.1.call-start = ((), (), s32[]{:S(2)}) async-start(), calls=%async_computation.16 | async-start | bytes 5013504 | tf_op jit(solution)/shard_map/reduce_scatter | solution.py:353
  470.2 310.6 %reduce-scatter.17.cloned.1.call-start = ((), (), s32[]{:S(2)}) async-start(), calls=%async_computation.15 | async-start | bytes 5013504 | tf_op jit(solution)/shard_map/reduce_scatter | solution.py:350
  479.4 464.9 %reduce-scatter.13.cloned.1.call-start = ((), (), s32[]{:S(2)}) async-start(), calls=%async_computation.13 | async-start | bytes 3760128 | tf_op jit(solution)/shard_map/reduce_scatter | solution.py:344
  592.9 444.2 %reduce-scatter.11.cloned.1.call-start = ((), (), s32[]{:S(2)}) async-start(), calls=%async_computation.12 | async-start | bytes 7520256 | tf_op jit(solution)/shard_map/reduce_scatter | solution.py:341
  626.5 474.4 %reduce-scatter.25.cloned.1.call-start = ((), (), s32[]{:S(2)}) async-start(), calls=%async_computation.19 | async-start | bytes 208896
  630.8 512.5 %all-reduce.4.cloned.1.call-start = ((), (), s32[]{:S(2)}) async-start(), calls=%async_computation.20 | async-start | bytes 2654208 | tf_op jit(solution)/shard_map/psum | solution.py:369
  1037.2 305.2 %reduce-scatter.21.cloned.1.call-start = ((), (), s32[]{:S(2)}) async-start(), calls=%async_computation.17 | async-start | bytes 20054016 | tf_op jit(solution)/shard_map/reduce_scatter | solution.py:361
  1060.8 479.7 %reduce-scatter.23.cloned.1.call-start = ((), (), s32[]{:S(2)}) async-start(), calls=%async_computation.18 | async-start | bytes 20054016 | tf_op jit(solution)/shard_map/reduce_scatter | solution.py:364
  (60 other events, 423.1 us)
Sparse Core Ops, SparseCore 0:
  457.6 165.6 reduce-scatter.14
  627.2 74.5 reduce-scatter.18
  706.1 74.6 reduce-scatter.16
  784.5 159.7 reduce-scatter.12
  948.2 88.9 reduce-scatter.10
  1041.5 53.1 reduce-scatter.24
  1097.3 45.9 all-reduce.3
  1147.4 194.8 reduce-scatter.20
  1346.5 194.0 reduce-scatter.22
where the time goes:
time: 1570 us; the launch traced here: 1550 us
  waiting for transfers between devices  838 us (53%)
  matrix products  345 us (22%)
  local copies, waits for them, and re-layouts  194 us (12%)
  other arithmetic  108 us (7%)
  starting transfers between devices  23.1 us (1%)
  loops' own time  22.3 us (1%)
    reduce_scatter x1, waiting for transfers between devices, local(): lax.psum_scatter(grad_expert_down.astype(jnp.bfloat16), 'dp', scatter_dim...  195 us
    reduce_scatter x1, waiting for transfers between devices, local(): lax.psum_scatter(grad_expert_up.astype(jnp.bfloat16), 'dp', scatter_dimen...  190 us
    reduce_scatter x1, waiting for transfers between devices, local(): lax.psum_scatter(grad_qkv.astype(jnp.bfloat16), 'dp', scatter_dimension=0...  164 us
    reduce_scatter x1, waiting for transfers between devices, local(): lax.psum_scatter(grad_ada.astype(jnp.bfloat16), 'dp', scatter_dimension=0...  92.8 us
    reduce_scatter x1, waiting for transfers between devices, local(): lax.psum_scatter(grad_shared_up.astype(jnp.bfloat16), 'dp', scatter_dimen...  79 us
    reduce_scatter x1, waiting for transfers between devices, local(): lax.psum_scatter(grad_shared_down.astype(jnp.bfloat16), 'dp', scatter_dim...  70.8 us
    dot_general x1, matrix products, local(): jnp.einsum('jrd,jdf->jrf', expert_in, expert_up, preferred_element_type=j...  38.7 us
    psum x1, waiting for transfers between devices, local(): lax.psum(shares[0].astype(jnp.bfloat16), 'stream').astype(jnp.float32)  36.1 us
  transfers between devices with their start and end apart: 13, of which 8 were waited for; matrix products, arithmetic and copies ran while one was open for 22% of the time, Pallas kernels for 0%

commit v1 on v0

--- a/solution.py
+++ b/solution.py
@@ -1,8 +1,11 @@
+import functools
 import math
 
 import jax
 import jax.numpy as jnp
 from jax import lax
+from jax.experimental import pallas as pl
+from jax.experimental.pallas import tpu as pltpu
 from jax.sharding import PartitionSpec as P
 
 HEADS = 12
@@ -13,6 +16,9 @@
 
 HIGH = lax.Precision.HIGHEST
 EPSILON = 1e-06
+F32 = jnp.float32
+BF16 = jnp.bfloat16
+MIB = 1 << 20
 
 
 def gelu_tanh(values):
@@ -133,7 +139,7 @@
     )
 
 
-def local(
+def local_general(
     patches,
     embedding,
     long_image,
@@ -386,6 +392,971 @@
         expert_summed[0],
         expert_summed[1],
     )
+
+
+def nn(left, right):
+    return jnp.dot(left, right, preferred_element_type=F32)
+
+
+def nt(left, right):
+    return lax.dot_general(left, right, (((1,), (1,)), ((), ())), preferred_element_type=F32)
+
+
+def tn(left, right):
+    return lax.dot_general(left, right, (((0,), (0,)), ((), ())), preferred_element_type=F32)
+
+
+def three_parts(values):
+    first = values.astype(BF16)
+    rest = values - first.astype(F32)
+    second = rest.astype(BF16)
+    third = (rest - second.astype(F32)).astype(BF16)
+    return first, second, third
+
+
+def sigmoid(values):
+    return 1.0 / (1.0 + jnp.exp(-values))
+
+
+def gelu_and_slope(values):
+    inner = math.sqrt(2.0 / math.pi)
+    square = values * values
+    bend = jnp.tanh(values * (inner + (inner * 0.044715) * square))
+    half = 0.5 + 0.5 * bend
+    slope = half + values * (0.5 - 0.5 * bend * bend) * (inner + (3.0 * inner * 0.044715) * square)
+    return values * half, slope
+
+
+def params(limit=56):
+    return pltpu.CompilerParams(vmem_limit_bytes=limit * MIB)
+
+
+def cost(flops, moved):
+    return pl.CostEstimate(flops=int(flops), bytes_accessed=int(moved), transcendentals=0)
+
+
+def full(shape):
+    return pl.BlockSpec(shape, lambda *_: (0,) * len(shape))
+
+
+def modulate_kernel(long_ref, emb_ref, ada_ref, mod_ref, act_ref):
+    emb = emb_ref[...]
+    used = jnp.where(long_ref[0] > 0, jnp.broadcast_to(emb[0:1], emb.shape), emb)
+    act = used * sigmoid(used)
+    act_ref[...] = act
+    weight = ada_ref[...]
+    total = 0.0
+    for part in three_parts(act):
+        total = total + nn(part, weight)
+    mod_ref[0] = total
+
+
+def modulate(long_image, emb_pad, ada_weight):
+    rows, width = emb_pad.shape
+    pieces = ada_weight.shape[1] // width
+    return pl.pallas_call(
+        modulate_kernel,
+        grid_spec=pltpu.PrefetchScalarGridSpec(
+            num_scalar_prefetch=1,
+            grid=(pieces,),
+            in_specs=[
+                pl.BlockSpec((rows, width), lambda i, *_: (0, 0)),
+                pl.BlockSpec((width, width), lambda i, *_: (0, i)),
+            ],
+            out_specs=[
+                pl.BlockSpec((1, rows, width), lambda i, *_: (i, 0, 0)),
+                pl.BlockSpec((rows, width), lambda i, *_: (0, 0)),
+            ],
+        ),
+        out_shape=[
+            jax.ShapeDtypeStruct((pieces, rows, width), F32),
+            jax.ShapeDtypeStruct((rows, width), F32),
+        ],
+        compiler_params=params(),
+        cost_estimate=cost(0, ada_weight.size * 2),
+        name="modulate",
+    )(long_image, emb_pad, ada_weight)
+
+
+def norm_parts(values):
+    centered = values - jnp.mean(values, -1, keepdims=True)
+    spread = lax.rsqrt(jnp.mean(centered * centered, -1, keepdims=True) + EPSILON)
+    return centered * spread, spread
+
+
+def norm_back(grad, normed, spread):
+    return spread * (
+        grad
+        - jnp.mean(grad, -1, keepdims=True)
+        - normed * jnp.mean(grad * normed, -1, keepdims=True)
+    )
+
+
+def qkv_kernel(x_ref, mod_ref, w_ref, packed_ref):
+    block = pl.program_id(0)
+    normed, _ = norm_parts(x_ref[...].astype(F32))
+    shift, scale = mod_ref[0, pl.ds(block, 1), :], mod_ref[1, pl.ds(block, 1), :]
+    hidden = (normed * (1.0 + scale) + shift).astype(BF16)
+    packed_ref[...] = nn(hidden, w_ref[...]).astype(BF16)
+
+
+def qkv_forward(patches, mod, weight, blocks):
+    rows, width = patches.shape
+    short = rows // blocks
+    wide = weight.shape[1]
+    return pl.pallas_call(
+        qkv_kernel,
+        grid=(blocks,),
+        in_specs=[pl.BlockSpec((short, width), lambda i: (i, 0)), full(mod.shape), full(weight.shape)],
+        out_specs=pl.BlockSpec((short, wide), lambda i: (i, 0)),
+        out_shape=jax.ShapeDtypeStruct((rows, wide), BF16),
+        compiler_params=params(),
+        cost_estimate=cost(2 * rows * width * wide, rows * wide * 2),
+        name="qkv",
+    )(patches, mod, weight)
+
+
+def attend_kernel(short, long_ref, q_ref, k_ref, v_ref, o_ref, lse_ref):
+    rows, lanes = q_ref.shape
+    first = lax.broadcasted_iota(jnp.int32, (1, lanes), 1) < HEAD_DIM
+    factor = 1.0 / math.sqrt(HEAD_DIM)
+
+    def part(query_at, key_at, key_count):
+        queries = q_ref[query_at : query_at + short, :]
+        keys = k_ref[key_at : key_at + key_count, :]
+        values = v_ref[key_at : key_at + key_count, :]
+        zero = jnp.zeros_like(queries)
+        outs, sums = [], []
+        for mine in (first, jnp.logical_not(first)):
+            scores = nt(jnp.where(mine, queries, zero), keys) * factor
+            top = jnp.max(scores, -1, keepdims=True)
+            shifted = jnp.exp(scores - top)
+            total = jnp.sum(shifted, -1, keepdims=True)
+            outs.append(nn(shifted.astype(BF16), values) * (1.0 / total))
+            sums.append(top + jnp.log(total))
+        o_ref[query_at : query_at + short, :] = jnp.where(first, outs[0], outs[1]).astype(BF16)
+        lse_ref[query_at : query_at + short, :] = jnp.where(first, sums[0], sums[1])
+
+    @pl.when(long_ref[0] > 0)
+    def _():
+        for at in range(0, rows, short):
+            part(at, 0, rows)
+
+    @pl.when(long_ref[0] <= 0)
+    def _():
+        for at in range(0, rows, short):
+            part(at, at, short)
+
+
+def attend_forward(long_image, packed, short):
+    rows = packed.shape[0]
+    width = packed.shape[1] // 3
+    lanes = 2 * HEAD_DIM
+    pairs = width // lanes
+    spec = [
+        pl.BlockSpec((rows, lanes), functools.partial(lambda shift, i, *_: (0, i + shift), shift))
+        for shift in (0, pairs, 2 * pairs)
+    ]
+    return pl.pallas_call(
+        functools.partial(attend_kernel, short),
+        grid_spec=pltpu.PrefetchScalarGridSpec(
+            num_scalar_prefetch=1, grid=(pairs,), in_specs=spec, out_specs=[spec[0], spec[0]]
+        ),
+        out_shape=[
+            jax.ShapeDtypeStruct((rows, width), BF16),
+            jax.ShapeDtypeStruct((rows, width), F32),
+        ],
+        compiler_params=params(),
+        cost_estimate=cost(16 * rows * rows * width, rows * width * 12),
+        name="attend",
+    )(long_image, packed, packed, packed)
+
+
+def attend_back_kernel(
+    short, long_ref, q_ref, k_ref, v_ref, o_ref, lse_ref, do_ref, dq_ref, dk_ref, dv_ref,
+    dk_acc, dv_acc,
+):
+    rows, lanes = q_ref.shape
+    first = lax.broadcasted_iota(jnp.int32, (1, lanes), 1) < HEAD_DIM
+    factor = 1.0 / math.sqrt(HEAD_DIM)
+    product = do_ref[...].astype(F32) * o_ref[...].astype(F32)
+    lse_t = jnp.transpose(lse_ref[...])
+    product_t = jnp.transpose(product)
+    lse_rows = [lse_t[0:1], lse_t[HEAD_DIM : HEAD_DIM + 1]]
+    delta_rows = [
+        jnp.sum(product_t[:HEAD_DIM], 0, keepdims=True),
+        jnp.sum(product_t[HEAD_DIM:], 0, keepdims=True),
+    ]
+
+    def part(query_at, key_at, key_count, fresh):
+        chunk = slice(query_at, query_at + short)
+        span = slice(key_at, key_at + key_count)
+        queries, grads = q_ref[chunk, :], do_ref[chunk, :]
+        keys, values = k_ref[span, :], v_ref[span, :]
+        zero, zero_keys = jnp.zeros_like(queries), jnp.zeros_like(keys)
+        dq = dk = dv = 0.0
+        for head, mine in enumerate((first, jnp.logical_not(first))):
+            query_own = jnp.where(mine, queries, zero)
+            grad_own = jnp.where(mine, grads, zero)
+            key_own = jnp.where(mine, keys, zero_keys)
+            scores = nt(keys, query_own) * factor
+            probs = jnp.exp(scores - lse_rows[head][:, chunk])
+            grad_probs = nt(values, grad_own)
+            grad_scores = (probs * (grad_probs - delta_rows[head][:, chunk])).astype(BF16)
+            dv = dv + nn(probs.astype(BF16), grad_own)
+            dk = dk + nn(grad_scores, query_own)
+            dq = dq + tn(grad_scores, key_own)
+        dq_ref[chunk, :] = (dq * factor).astype(BF16)
+        if fresh:
+            dk_acc[span, :] = dk
+            dv_acc[span, :] = dv
+        else:
+            dk_acc[span, :] += dk
+            dv_acc[span, :] += dv
+
+    @pl.when(long_ref[0] > 0)
+    def _():
+        for at in range(0, rows, short):
+            part(at, 0, rows, at == 0)
+
+    @pl.when(long_ref[0] <= 0)
+    def _():
+        for at in range(0, rows, short):
+            part(at, at, short, True)
+
+    dk_ref[...] = (dk_acc[...] * factor).astype(BF16)
+    dv_ref[...] = dv_acc[...].astype(BF16)
+
+
+def attend_backward(long_image, packed, attended, logsum, grad, short):
+    rows, width = attended.shape
+    lanes = 2 * HEAD_DIM
+    pairs = width // lanes
+    spec = [
+        pl.BlockSpec((rows, lanes), functools.partial(lambda shift, i, *_: (0, i + shift), shift))
+        for shift in (0, pairs, 2 * pairs)
+    ]
+    return pl.pallas_call(
+        functools.partial(attend_back_kernel, short),
+        grid_spec=pltpu.PrefetchScalarGridSpec(
+            num_scalar_prefetch=1,
+            grid=(pairs,),
+            in_specs=spec + [spec[0]] * 3,
+            out_specs=[spec[0]] * 3,
+            scratch_shapes=[pltpu.VMEM((rows, lanes), F32)] * 2,
+        ),
+        out_shape=[jax.ShapeDtypeStruct((rows, width), BF16)] * 3,
+        compiler_params=params(),
+        cost_estimate=cost(40 * rows * rows * width, rows * width * 20),
+        name="attend_back",
+    )(long_image, packed, packed, packed, attended, logsum, grad)
+
+
+def middle_kernel(att_ref, x_ref, mod_ref, w_ref, branch_ref, hidden_ref):
+    block = pl.program_id(0)
+    branch = nn(att_ref[...], w_ref[...])
+    branch_ref[...] = branch
+    middle = x_ref[...].astype(F32) + mod_ref[2, pl.ds(block, 1), :] * branch
+    normed, _ = norm_parts(middle)
+    shift, scale = mod_ref[3, pl.ds(block, 1), :], mod_ref[4, pl.ds(block, 1), :]
+    hidden_ref[...] = (normed * (1.0 + scale) + shift).astype(BF16)
+
+
+def middle_forward(attended, patches, mod, out_weight, blocks):
+    rows, width = patches.shape
+    tile = pl.BlockSpec((rows // blocks, width), lambda i: (i, 0))
+    return pl.pallas_call(
+        middle_kernel,
+        grid=(blocks,),
+        in_specs=[tile, tile, full(mod.shape), full(out_weight.shape)],
+        out_specs=[tile, tile],
+        out_shape=[
+            jax.ShapeDtypeStruct((rows, width), F32),
+            jax.ShapeDtypeStruct((rows, width), BF16),
+        ],
+        compiler_params=params(),
+        cost_estimate=cost(2 * rows * width * width, rows * width * 10),
+        name="middle",
+    )(attended, patches, mod, out_weight)
+
+
+def rank_kernel(base_ref, routes_ref, row_ref, col_ref):
+    rows = routes_ref.shape[2]
+    ids = base_ref[0] + lax.broadcasted_iota(jnp.int32, (8, rows), 0)
+    hits = jnp.logical_or(routes_ref[0, 0:1, :] == ids, routes_ref[0, 1:2, :] == ids)
+    before = lax.broadcasted_iota(jnp.int32, (rows, rows), 0)
+    after = lax.broadcasted_iota(jnp.int32, (rows, rows), 1)
+    upper = (before < after).astype(F32).astype(BF16)
+    earlier = nn(hits.astype(F32).astype(BF16), upper)
+    rank = jnp.where(hits, earlier, -1.0)
+    row_ref[0] = rank.astype(jnp.int32)
+    tall = jnp.concatenate([rank, jnp.full((120, rows), -1.0, F32)], 0)
+    col_ref[0] = jnp.transpose(tall).astype(jnp.int32)
+
+
+def ranks(base, routes_all):
+    count, _, rows = routes_all.shape
+    return pl.pallas_call(
+        rank_kernel,
+        grid_spec=pltpu.PrefetchScalarGridSpec(
+            num_scalar_prefetch=1,
+            grid=(count,),
+            in_specs=[pl.BlockSpec((1, 2, rows), lambda i, *_: (i, 0, 0))],
+            out_specs=[
+                pl.BlockSpec((1, 8, rows), lambda i, *_: (i, 0, 0)),
+                pl.BlockSpec((1, rows, 128), lambda i, *_: (i, 0, 0)),
+            ],
+        ),
+        out_shape=[
+            jax.ShapeDtypeStruct((count, 8, rows), jnp.int32),
+            jax.ShapeDtypeStruct((count, rows, 128), jnp.int32),
+        ],
+        compiler_params=params(),
+        cost_estimate=cost(0, 4 << 20),
+        name="ranks",
+    )(base, routes_all)
+
+
+def gate_rows(hidden, routes, router_t, ids):
+    logits = nt(router_t, hidden)
+    every = lax.broadcasted_iota(jnp.int32, logits.shape, 0)
+    first, second = routes[0:1, :], routes[1:2, :]
+    zero = jnp.zeros_like(logits)
+    logit_one = jnp.sum(jnp.where(every == first, logits, zero), 0, keepdims=True)
+    logit_two = jnp.sum(jnp.where(every == second, logits, zero), 0, keepdims=True)
+    gate_one = sigmoid(logit_one - logit_two)
+    gate_two = sigmoid(logit_two - logit_one)
+    return jnp.where(ids == first, gate_one, 0.0) + jnp.where(ids == second, gate_two, 0.0)
+
+
+def ffn_phase_one(x, g, up_ref, down_ref, act_ref, pre_ref, step=256):
+    wide = act_ref.shape[1]
+    for at in range(0, wide, step):
+        cols = slice(at, at + step)
+        act, slope = gelu_and_slope(nn(x, up_ref[0, :, cols]))
+        back = nt(g, down_ref[0, cols, :])
+        act_ref[:, cols] = act.astype(BF16)
+        pre_ref[:, cols] = (back * slope).astype(BF16)
+
+
+def expert_kernel(
+    slot, has_prior, scal_ref, h0_ref, h1_ref, g0_ref, g1_ref, rank_ref, routes_ref, router_ref,
+    up_ref, down_ref, *rest,
+):
+    if has_prior:
+        prior_up_ref, prior_down_ref = rest[:2]
+        rest = rest[2:]
+    (dup_ref, ddown_ref, out_ref, gx_ref, gg_ref,
+     x_s, xt_s, g_s, gt_s, b_s, gate_s, act_s, pre_s, out_acc, gx_acc) = rest
+    tile = pl.program_id(0)
+    last = pl.num_programs(0) - 1
+    rows = h0_ref.shape[0]
+    own = lax.broadcasted_iota(jnp.int32, (CAP, rows), 0)
+
+    def hot(source):
+        return (own == rank_ref[source, slot : slot + 1, :]).astype(F32)
+
+    @pl.when(tile == 0)
+    def _():
+        for source, (h_ref, b_ref) in enumerate(((h0_ref, g0_ref), (h1_ref, g1_ref))):
+            span = slice(source * CAP, (source + 1) * CAP)
+            pick = hot(source)
+            pick_low = pick.astype(BF16)
+            gate = gate_rows(h_ref[...], routes_ref[source], router_ref[...], scal_ref[1])
+            gate_col = jnp.sum(pick * gate[0:1], -1, keepdims=True)
+            branch = nn(pick_low, b_ref[...])
+            x_s[span, :] = nn(pick_low, h_ref[...]).astype(BF16)
+            b_s[span, :] = branch.astype(BF16)
+            g_s[span, :] = (branch * gate_col).astype(BF16)
+            gate_s[span, :] = jnp.broadcast_to(gate_col, (CAP, 128))
+        xt_s[...] = jnp.transpose(x_s[...])
+        gt_s[...] = jnp.transpose(g_s[...])
+        out_acc[...] = jnp.zeros_like(out_acc)
+        gx_acc[...] = jnp.zeros_like(gx_acc)
+
+    ffn_phase_one(x_s[...], g_s[...], up_ref, down_ref, act_s, pre_s)
+    act, pre = act_s[...], pre_s[...]
+    out_acc[...] += nn(act, down_ref[0])
+    gx_acc[...] += nt(pre, up_ref[0])
+    dup = nn(xt_s[...], pre)
+    ddown = nn(gt_s[...], act)
+    if has_prior:
+        dup = dup + prior_up_ref[...].astype(F32)
+        split = ddown_ref.shape[2]
+        for piece in range(ddown_ref.shape[0]):
+            ddown_ref[piece] = (
+                ddown[:, piece * split : (piece + 1) * split] + prior_down_ref[piece].astype(F32)
+            ).astype(BF16)
+    else:
+        split = ddown_ref.shape[2]
+        for piece in range(ddown_ref.shape[0]):
+            ddown_ref[piece] = ddown[:, piece * split : (piece + 1) * split].astype(BF16)
+    dup_ref[...] = dup.astype(BF16)
+
+    @pl.when(tile == last)
+    def _():
+        for source in range(2):
+            span = slice(source * CAP, (source + 1) * CAP)
+            out = out_acc[span, :]
+            out_ref[source] = (out * gate_s[span, 0:1]).astype(BF16)
+            gx_ref[source] = gx_acc[span, :].astype(BF16)
+            inner = jnp.sum(out * b_s[span, :].astype(F32), -1, keepdims=True)
+            gg_ref[source] = jnp.sum(hot(source) * inner, 0, keepdims=True)
+
+
+def expert_call(slot, scal, hiddens, branches, rank_rows, routes, router_t, up, down, prior, zy):
+    rows, width = hiddens[0].shape
+    wide = up.shape[2]
+    tile = width
+    tiles = wide // tile
+    split = wide // zy
+    per = tile // split
+    count = 2 * CAP
+    weights = [
+        pl.BlockSpec((1, width, tile), lambda f, s: (s[0], 0, f)),
+        pl.BlockSpec((1, tile, width), lambda f, s: (s[0], f, 0)),
+    ]
+    grads = [
+        pl.BlockSpec((width, tile), lambda f, s: (0, f)),
+        pl.BlockSpec((per, width, split), lambda f, s: (f, 0, 0)),
+    ]
+    whole = lambda a: pl.BlockSpec(a.shape, lambda f, s: (0,) * a.ndim)
+    shared = [*hiddens, *branches, rank_rows, routes, router_t]
+    out_shape = [
+        jax.ShapeDtypeStruct((width, wide), BF16),
+        jax.ShapeDtypeStruct((zy, width, split), BF16),
+        jax.ShapeDtypeStruct((2, CAP, width), BF16),
+        jax.ShapeDtypeStruct((2, CAP, width), BF16),
+        jax.ShapeDtypeStruct((2, 1, rows), F32),
+    ]
+    return pl.pallas_call(
+        functools.partial(expert_kernel, slot, prior is not None),
+        grid_spec=pltpu.PrefetchScalarGridSpec(
+            num_scalar_prefetch=1,
+            grid=(tiles,),
+            in_specs=[whole(a) for a in shared] + weights + (grads if prior is not None else []),
+            out_specs=grads + [whole(a) for a in out_shape[2:]],
+            scratch_shapes=[
+                pltpu.VMEM((count, width), BF16),
+                pltpu.VMEM((width, count), BF16),
+                pltpu.VMEM((count, width), BF16),
+                pltpu.VMEM((width, count), BF16),
+                pltpu.VMEM((count, width), BF16),
+                pltpu.VMEM((count, 128), F32),
+                pltpu.VMEM((count, tile), BF16),
+                pltpu.VMEM((count, tile), BF16),
+                pltpu.VMEM((count, width), F32),
+                pltpu.VMEM((count, width), F32),
+            ],
+        ),
+        out_shape=out_shape,
+        compiler_params=params(),
+        cost_estimate=cost(12 * count * width * wide, width * wide * 8),
+        name="expert",
+    )(scal, *shared, up, down, *(prior if prior is not None else ()))
+
+
+def shared_kernel(
+    h_ref, b_ref, up_ref, down_ref, dup_ref, ddown_ref, out_ref, gx_ref,
+    xt_s, gt_s, act_s, pre_s,
+):
+    @pl.when(pl.program_id(0) == 0)
+    def _():
+        xt_s[...] = jnp.transpose(h_ref[...])
+        gt_s[...] = jnp.transpose(b_ref[...])
+        out_ref[...] = jnp.zeros_like(out_ref)
+        gx_ref[...] = jnp.zeros_like(gx_ref)
+
+    ffn_phase_one(h_ref[...], b_ref[...], up_ref, down_ref, act_s, pre_s)
+    act, pre = act_s[...], pre_s[...]
+    out_ref[...] += nn(act, down_ref[0])
+    gx_ref[...] += nt(pre, up_ref[0])
+    dup_ref[0] = nn(xt_s[...], pre).astype(BF16)
+    ddown_ref[0] = nn(gt_s[...], act).astype(BF16)
+
+
+def shared_call(hidden, branch, up, down):
+    rows, width = hidden.shape
+    wide = up.shape[1]
+    tile = width
+    tiles = wide // tile
+    whole = lambda a: pl.BlockSpec(a.shape, lambda f: (0,) * a.ndim)
+    return pl.pallas_call(
+        shared_kernel,
+        grid=(tiles,),
+        in_specs=[
+            whole(hidden),
+            whole(branch),
+            pl.BlockSpec((1, width, tile), lambda f: (0, 0, f)),
+            pl.BlockSpec((1, tile, width), lambda f: (0, f, 0)),
+        ],
+        out_specs=[
+            pl.BlockSpec((1, width, tile), lambda f: (f, 0, 0)),
+            pl.BlockSpec((1, width, tile), lambda f: (f, 0, 0)),
+            whole(hidden),
+            whole(hidden),
+        ],
+        out_shape=[
+            jax.ShapeDtypeStruct((tiles, width, tile), BF16),
+            jax.ShapeDtypeStruct((tiles, width, tile), BF16),
+            jax.ShapeDtypeStruct((rows, width), F32),
+            jax.ShapeDtypeStruct((rows, width), F32),
+        ],
+        scratch_shapes=[
+            pltpu.VMEM((width, rows), BF16),
+            pltpu.VMEM((width, rows), BF16),
+            pltpu.VMEM((rows, tile), BF16),
+            pltpu.VMEM((rows, tile), BF16),
+        ],
+        compiler_params=params(),
+        cost_estimate=cost(12 * rows * width * wide, width * wide * 8),
+        name="shared",
+    )(hidden, branch, up[None], down[None])
+
+
+def combine_kernel(slots, col_ref, *rest):
+    rows_refs, (out_ref, gx_ref) = rest[: 2 * slots], rest[2 * slots :]
+    rows = col_ref.shape[1]
+    own = lax.broadcasted_iota(jnp.int32, (rows, CAP), 1)
+    out = gx = 0.0
+    for slot in range(slots):
+        pick = (col_ref[0, :, slot : slot + 1] == own).astype(F32).astype(BF16)
+        out = out + nn(pick, rows_refs[2 * slot][0])
+        gx = gx + nn(pick, rows_refs[2 * slot + 1][0])
+    out_ref[0] = out.astype(BF16)
+    gx_ref[0] = gx.astype(BF16)
+
+
+def combine(rank_cols, pairs):
+    count, rows, _ = rank_cols.shape
+    width = pairs[0][0].shape[2]
+    part = pl.BlockSpec((1, CAP, width), lambda i: (i, 0, 0))
+    whole = pl.BlockSpec((1, rows, width), lambda i: (i, 0, 0))
+    return pl.pallas_call(
+        functools.partial(combine_kernel, len(pairs)),
+        grid=(count,),
+        in_specs=[pl.BlockSpec((1, rows, 128), lambda i: (i, 0, 0))] + [part] * (2 * len(pairs)),
+        out_specs=[whole, whole],
+        out_shape=[jax.ShapeDtypeStruct((count, rows, width), BF16)] * 2,
+        compiler_params=params(),
+        cost_estimate=cost(8 * count * rows * CAP * width, count * rows * width * 8),
+        name="combine",
+    )(rank_cols, *[a for pair in pairs for a in pair])
+
+
+def middle_back_kernel(
+    gs_ref, ga_ref, gb_ref, gc_ref, gg_ref, ids_ref, routes_ref, router_ref, router_rel_ref,
+    hidden_ref, cot_ref, branch_ref, x_ref, mod_ref, w_ref, att_ref,
+    gm_ref, gatt_ref, mods_ref, drouter_ref, dout_ref,
+):
+    block = pl.program_id(0)
+    hidden = hidden_ref[...]
+    gates = gate_rows(hidden, routes_ref[...], router_ref[...], ids_ref[:, 0:1])
+    grad_gates = gg_ref[...]
+    inner = jnp.sum(gates * grad_gates, 0, keepdims=True)
+    grad_logits = gates * (grad_gates - inner)
+    grad = gs_ref[...] + ga_ref[...].astype(F32) + gb_ref[...].astype(F32) + gc_ref[...].astype(F32)
+    drouter = 0.0
+    for piece in three_parts(grad_logits):
+        grad = grad + tn(piece, router_rel_ref[...])
+        drouter = drouter + nn(piece, hidden)
+    branch = branch_ref[...]
+    gate_one = mod_ref[2, pl.ds(block, 1), :]
+    middle = x_ref[...].astype(F32) + gate_one * branch
+    normed, spread = norm_parts(middle)
+    scale = mod_ref[4, pl.ds(block, 1), :]
+    mods_ref[1, pl.ds(block, 1), :] = jnp.sum(grad, 0, keepdims=True)
+    mods_ref[2, pl.ds(block, 1), :] = jnp.sum(grad * normed, 0, keepdims=True)
+    grad_middle = cot_ref[...].astype(F32) + norm_back(grad * (1.0 + scale), normed, spread)
+    mods_ref[0, pl.ds(block, 1), :] = jnp.sum(grad_middle * branch, 0, keepdims=True)
+    gm_ref[...] = grad_middle
+    grad_branch = (grad_middle * gate_one).astype(BF16)
+    gatt_ref[...] = nt(grad_branch, w_ref[...]).astype(BF16)
+    dout = tn(att_ref[...], grad_branch)
+
+    @pl.when(block == 0)
+    def _():
+        drouter_ref[...] = drouter
+        dout_ref[...] = dout
+
+    @pl.when(block > 0)
+    def _():
+        drouter_ref[...] += drouter
+        dout_ref[...] += dout
+
+
+def middle_backward(parts, gg, ids, routes_t, router_t, router_rel, hidden, cot, branch, patches, mod,
+                    out_weight, attended, blocks):
+    rows, width = patches.shape
+    short = rows // blocks
+    tile = pl.BlockSpec((short, width), lambda i: (i, 0))
+    cols = lambda a: pl.BlockSpec((a.shape[0], short), lambda i: (0, i))
+    specs = (
+        [tile] * 4 + [cols(gg), full(ids.shape), cols(routes_t), full(router_t.shape)]
+        + [full(router_rel.shape)] + [tile] * 4 + [full(mod.shape), full(out_weight.shape), tile]
+    )
+    out_shape = [
+        jax.ShapeDtypeStruct((rows, width), F32),
+        jax.ShapeDtypeStruct((rows, width), BF16),
+        jax.ShapeDtypeStruct((3, 8, width), F32),
+        jax.ShapeDtypeStruct((router_rel.shape[0], width), F32),
+        jax.ShapeDtypeStruct((width, width), F32),
+    ]
+    return pl.pallas_call(
+        middle_back_kernel,
+        grid=(blocks,),
+        in_specs=specs,
+        out_specs=[tile, tile] + [full(a.shape) for a in out_shape[2:]],
+        out_shape=out_shape,
+        compiler_params=params(),
+        cost_estimate=cost(4 * rows * width * width, rows * width * 30),
+        name="middle_back",
+    )(*parts, gg, ids, routes_t, router_t, router_rel, hidden, cot, branch, patches, mod, out_weight,
+      attended)
+
+
+def mixed_kernel(so_ref, ra_ref, rb_ref, rc_ref, cot_ref, branch_ref, x_ref, mod_ref, mixed_ref, gate_ref):
+    block = pl.program_id(0)
+    second = so_ref[...] + ra_ref[...].astype(F32) + rb_ref[...].astype(F32) + rc_ref[...].astype(F32)
+    middle = x_ref[...].astype(F32) + mod_ref[2, pl.ds(block, 1), :] * branch_ref[...]
+    mixed_ref[...] = (middle + mod_ref[5, pl.ds(block, 1), :] * second).astype(BF16)
+    gate_ref[pl.ds(block, 1), :] = jnp.sum(cot_ref[...].astype(F32) * second, 0, keepdims=True)
+
+
+def mixed_forward(parts, cot, branch, patches, mod, blocks):
+    rows, width = patches.shape
+    tile = pl.BlockSpec((rows // blocks, width), lambda i: (i, 0))
+    return pl.pallas_call(
+        mixed_kernel,
+        grid=(blocks,),
+        in_specs=[tile] * 7 + [full(mod.shape)],
+        out_specs=[tile, full((8, width))],
+        out_shape=[
+            jax.ShapeDtypeStruct((rows, width), BF16),
+            jax.ShapeDtypeStruct((8, width), F32),
+        ],
+        compiler_params=params(),
+        cost_estimate=cost(0, rows * width * 22),
+        name="mixed",
+    )(*parts, cot, branch, patches, mod)
+
+
+def qkv_weight_kernel(x_ref, mod_ref, dq_ref, dk_ref, dv_ref, dw_ref, hidden_t):
+    blocks = mod_ref.shape[1]
+    short = x_ref.shape[0] // 4
+
+    @pl.when(pl.program_id(0) == 0)
+    def _():
+        for block in range(x_ref.shape[0] // short):
+            span = slice(block * short, (block + 1) * short)
+            normed, _ = norm_parts(x_ref[span, :].astype(F32))
+            hidden = normed * (1.0 + mod_ref[1, block : block + 1, :]) + mod_ref[0, block : block + 1, :]
+            hidden_t[:, span] = jnp.transpose(hidden.astype(BF16))
+
+    for index, ref in enumerate((dq_ref, dk_ref, dv_ref)):
+
+        @pl.when(pl.program_id(0) == index)
+        def _():
+            dw_ref[...] = nn(hidden_t[...], ref[...]).astype(BF16)
+
+
+def qkv_weight_grad(patches, mod, grads):
+    rows, width = patches.shape
+    return pl.pallas_call(
+        qkv_weight_kernel,
+        grid=(3,),
+        in_specs=[full(patches.shape), full(mod.shape)] + [full(patches.shape)] * 3,
+        out_specs=pl.BlockSpec((width, width), lambda i: (0, i)),
+        out_shape=jax.ShapeDtypeStruct((width, 3 * width), BF16),
+        scratch_shapes=[pltpu.VMEM((width, rows), BF16)],
+        compiler_params=params(),
+        cost_estimate=cost(6 * rows * width * width, rows * width * 14),
+        name="qkv_weight",
+    )(patches, mod, *grads)
+
+
+def inputs_back_kernel(dq_ref, dk_ref, dv_ref, w_ref, x_ref, gm_ref, mod_ref, gp_ref, mods_ref):
+    block = pl.program_id(0)
+    width = x_ref.shape[1]
+    grad = nt(dq_ref[...], w_ref[:, :width])
+    grad = grad + nt(dk_ref[...], w_ref[:, width : 2 * width])
+    grad = grad + nt(dv_ref[...], w_ref[:, 2 * width :])
+    normed, spread = norm_parts(x_ref[...].astype(F32))
+    mods_ref[0, pl.ds(block, 1), :] = jnp.sum(grad, 0, keepdims=True)
+    mods_ref[1, pl.ds(block, 1), :] = jnp.sum(grad * normed, 0, keepdims=True)
+    scale = mod_ref[1, pl.ds(block, 1), :]
+    gp_ref[...] = gm_ref[...] + norm_back(grad * (1.0 + scale), normed, spread)
+
+
+def inputs_backward(grads, weight, patches, grad_middle, mod, blocks):
+    rows, width = patches.shape
+    tile = pl.BlockSpec((rows // blocks, width), lambda i: (i, 0))
+    return pl.pallas_call(
+        inputs_back_kernel,
+        grid=(blocks,),
+        in_specs=[tile] * 3 + [full(weight.shape), tile, tile, full(mod.shape)],
+        out_specs=[tile, full((2, 8, width))],
+        out_shape=[
+            jax.ShapeDtypeStruct((rows, width), F32),
+            jax.ShapeDtypeStruct((2, 8, width), F32),
+        ],
+        compiler_params=params(),
+        cost_estimate=cost(6 * rows * width * width, rows * width * 20),
+        name="inputs_back",
+    )(*grads, weight, patches, grad_middle, mod)
+
+
+def used_kernel(block_count, long_ref, gm_ref, ada_ref, emb_ref, out_ref):
+    piece = pl.program_id(0)
+
+    @pl.when(piece == 0)
+    def _():
+        out_ref[...] = jnp.zeros_like(out_ref)
+
+    for part in three_parts(gm_ref[0]):
+        out_ref[...] += nt(part, ada_ref[...])
+
+    @pl.when(piece == pl.num_programs(0) - 1)
+    def _():
+        emb = emb_ref[...]
+        is_long = long_ref[0] > 0
+        used = jnp.where(is_long, jnp.broadcast_to(emb[0:1], emb.shape), emb)
+        gate = sigmoid(used)
+        grad = out_ref[...] * (gate * (1.0 + used * (1.0 - gate)))
+        row = lax.broadcasted_iota(jnp.int32, grad.shape, 0)
+        grad = jnp.where(row < block_count, grad, 0.0)
+        total = jnp.sum(grad, 0, keepdims=True)
+        out_ref[...] = jnp.where(is_long, jnp.where(row == 0, total, 0.0), grad)
+
+
+def used_backward(long_image, grad_mod, ada_weight, emb_pad, block_count):
+    rows, width = emb_pad.shape
+    pieces = grad_mod.shape[0]
+    return pl.pallas_call(
+        functools.partial(used_kernel, block_count),
+        grid_spec=pltpu.PrefetchScalarGridSpec(
+            num_scalar_prefetch=1,
+            grid=(pieces,),
+            in_specs=[
+                pl.BlockSpec((1, rows, width), lambda i, *_: (i, 0, 0)),
+                pl.BlockSpec((width, width), lambda i, *_: (0, i)),
+                pl.BlockSpec((rows, width), lambda i, *_: (0, 0)),
+            ],
+            out_specs=pl.BlockSpec((rows, width), lambda i, *_: (0, 0)),
+        ),
+        out_shape=jax.ShapeDtypeStruct((rows, width), F32),
+        compiler_params=params(),
+        cost_estimate=cost(0, ada_weight.size * 2),
+        name="used_back",
+    )(long_image, grad_mod, ada_weight, emb_pad)
+
+
+def swap(values, axis, bit):
+    size = lax.axis_size(axis)
+    return lax.ppermute(values, axis, [(i, i ^ bit) for i in range(size)])
+
+
+def half_sum(values, at, own, axis, bit):
+    keep = lax.dynamic_index_in_dim(values, own, at, keepdims=False)
+    send = lax.dynamic_index_in_dim(values, 1 - own, at, keepdims=False)
+    arrived = swap(send.astype(BF16), axis, bit)
+    return keep.astype(F32) + arrived.astype(F32)
+
+
+def paired(values, at, own, axis, bit):
+    arrived = swap(values, axis, bit)
+    ahead = jnp.where(own == 0, values, arrived)
+    behind = jnp.where(own == 0, arrived, values)
+    return jnp.stack([ahead, behind], at)
+
+
+def gather_group(values):
+    dp = lax.axis_index("dp")
+    stream = lax.axis_index("stream")
+    held = paired(values, 0, stream, "stream", 1)
+    bit = 1
+    while bit < lax.axis_size("dp"):
+        held = paired(held, 0, (dp // bit) % 2, "dp", bit)
+        held = held.reshape((-1,) + values.shape)
+        bit *= 2
+    return held
+
+
+def reduce_zy(values, at):
+    size = lax.axis_size("dp")
+    dp = lax.axis_index("dp")
+    order = [2] + [bit for bit in (1 << k for k in range(2, size.bit_length() - 1))]
+    groups = values.shape[at]
+    lead, tail = values.shape[:at], values.shape[at + 1 :]
+    bits = groups.bit_length() - 1
+    held = values.reshape(lead + (2,) * bits + tail)
+    left = list(range(bits))
+    for bit in order:
+        place = bit.bit_length() - 2
+        position = at + [len(left) - 1 - i for i, b in enumerate(sorted(left))][sorted(left).index(place)]
+        held = half_sum(held, position, (dp // bit) % 2, "dp", bit)
+        left.remove(place)
+    return held
+
+
+def reduce_copied(values):
+    size = lax.axis_size("dp")
+    rows, columns = values.shape
+    dp, stream = lax.axis_index("dp"), lax.axis_index("stream")
+    held = values.reshape(size // 2, 2, rows // size, 2, columns // 2)
+    held = half_sum(held, 1, dp % 2, "dp", 1)
+    held = half_sum(held, 2, stream, "stream", 1)
+    held = reduce_zy(held, 0)
+    both = paired(held.astype(BF16), 1, stream, "stream", 1)
+    return both.reshape(rows // size, columns).astype(F32)
+
+
+def local_pair(
+    patches, embedding, long_image, routes, cotangent, ada_weight, qkv_weight, out_weight, shared_up,
+    shared_down, router_weight, expert_up, expert_down,
+):
+    rows, width = patches.shape
+    blocks = embedding.shape[0]
+    short = rows // blocks
+    dp_size = lax.axis_size("dp")
+    zy = dp_size // 2
+    dp, stream = lax.axis_index("dp"), lax.axis_index("stream")
+    core = dp % 2
+    local_experts = expert_up.shape[0]
+    here = local_experts // 2
+    group = stream * 2 + core
+
+    emb_pad = jnp.pad(embedding, ((0, 8 - blocks), (0, 0)))
+    mod, act = modulate(long_image, emb_pad, ada_weight)
+    cot_full = cotangent.astype(F32).reshape(blocks, short, width)
+    branch_grad = (cot_full * mod[5, :blocks][:, None, :]).astype(BF16).reshape(rows, width)
+    routes_t = routes.T
+    routes_x = swap(routes_t, "stream", 1)
+    routes_near = jnp.stack([routes_t, swap(routes_t, "dp", 1)])
+    routes_far = jnp.stack([routes_x, swap(routes_x, "dp", 1)])
+    base = (stream * local_experts + core * here).astype(jnp.int32)
+    rank_near, cols_near = ranks(base[None], routes_near)
+    rank_far, cols_far = ranks(base[None], routes_far)
+    router_t = jnp.pad(router_weight.T, ((0, 16 - router_weight.shape[1]), (0, 0)))
+    branch_x = swap(branch_grad, "stream", 1)
+    branches_near = (branch_grad, swap(branch_grad, "dp", 1))
+    branches_far = (branch_x, swap(branch_x, "dp", 1))
+
+    packed = qkv_forward(patches, mod, qkv_weight, blocks)
+    attended, logsum = attend_forward(long_image, packed, short)
+    branch_one, hidden = middle_forward(attended, patches, mod, out_weight, blocks)
+
+    hidden_x = swap(hidden, "stream", 1)
+    hiddens_near = (hidden, swap(hidden, "dp", 1))
+    hiddens_far = (hidden_x, swap(hidden_x, "dp", 1))
+
+    def expert(slot, far, prior):
+        scal = jnp.stack([core * here + slot, base + slot]).astype(jnp.int32)
+        return expert_call(
+            slot, scal, hiddens_far if far else hiddens_near, branches_far if far else branches_near,
+            rank_far if far else rank_near, routes_far if far else routes_near, router_t,
+            expert_up, expert_down, prior, zy,
+        )
+
+    near = [expert(slot, False, None) for slot in range(here)]
+    far = [expert(slot, True, near[slot][:2]) for slot in range(here)]
+    out_far, gx_far = combine(cols_far, [(r[2], r[3]) for r in far])
+    gg_far = jnp.stack([r[4][:, 0] for r in far], 1)
+    gx_back = swap(gx_far[0] + swap(gx_far[1], "dp", 1), "stream", 1)
+    out_back = swap(out_far[0] + swap(out_far[1], "dp", 1), "stream", 1)
+    gg_back = swap(jnp.concatenate([gg_far[0], swap(gg_far[1], "dp", 1)], 0), "stream", 1)
+    out_near, gx_near = combine(cols_near, [(r[2], r[3]) for r in near])
+    gg_near = jnp.stack([r[4][:, 0] for r in near], 1)
+    gx_core = swap(gx_near[1], "dp", 1)
+    out_core = swap(out_near[1], "dp", 1)
+    gg_core = swap(gg_near[1], "dp", 1)
+    gg = jnp.concatenate([gg_near[0], gg_core, gg_back], 0)
+    relative = jnp.arange(EXPERTS, dtype=jnp.int32)
+    ids = ((relative // here) ^ group) * here + relative % here
+    router_rel = router_weight.T[ids]
+
+    dup, ddown, shared_out, shared_gx = shared_call(hidden, branch_grad, shared_up, shared_down)
+
+    pad8 = lambda a: jnp.pad(a, ((0, 16 - EXPERTS),) + ((0, 0),) * (a.ndim - 1))
+    ids16 = jnp.broadcast_to(jnp.pad(ids, (0, 16 - EXPERTS), constant_values=-1)[:, None], (16, 128))
+    grad_middle, grad_attended, mods_two, drouter, dout = middle_backward(
+        (shared_gx, gx_near[0], gx_core, gx_back), pad8(gg), ids16, routes_t, router_t, pad8(router_rel),
+        hidden, cotangent, branch_one, patches, mod, out_weight, attended, blocks,
+    )
+    mixed, gate_two = mixed_forward(
+        (shared_out, out_near[0], out_core, out_back), cotangent, branch_one, patches, mod, blocks
+    )
+    grads = attend_backward(long_image, packed, attended, logsum, grad_attended, short)
+    dqkv = qkv_weight_grad(patches, mod, grads)
+    grad_patches, mods_one = inputs_backward(grads, qkv_weight, patches, grad_middle, mod, blocks)
+    grad_mod = jnp.concatenate([mods_one, mods_two, gate_two[None]], 0)
+    grad_embedding = used_backward(long_image, grad_mod, ada_weight, emb_pad, blocks)[:blocks]
+
+    early = jnp.concatenate([act[:blocks], *[a[:blocks] for a in (*mods_two, gate_two)]], 1)
+    early = gather_group(early.astype(BF16))
+    late = gather_group(jnp.concatenate([mods_one[0, :blocks], mods_one[1, :blocks]], 1).astype(BF16))
+    early = early.reshape(-1, early.shape[-1])
+    late = late.reshape(-1, late.shape[-1])
+    acts = lax.dynamic_slice_in_dim(early, dp * (width // dp_size), width // dp_size, 1)
+    factors = jnp.concatenate([late, early[:, width:]], 1)
+    grad_ada = lax.dot_general(acts, factors, (((0,), (0,)), ((), ())), preferred_element_type=F32)
+
+    own = jnp.zeros((EXPERTS, EXPERTS), F32).at[ids, jnp.arange(EXPERTS)].set(1.0)
+    drouter_abs = jnp.dot(own, drouter[:EXPERTS], precision=HIGH)
+    drouter_sum = lax.psum(drouter_abs, ("dp", "stream"))
+    grad_router = lax.dynamic_slice_in_dim(drouter_sum, dp * (width // dp_size), width // dp_size, 1).T
+
+    part = width // zy
+    wide = expert_up.shape[2]
+    ups, downs = [], []
+    for slot in range(here):
+        up_sum = reduce_zy(far[slot][0].reshape(zy, part, wide), 0)
+        down_sum = reduce_zy(far[slot][1], 0)
+        ups.append(up_sum)
+        downs.append(down_sum.T)
+
+    def to_cores(held):
+        halves = jnp.stack(held)
+        halves = halves.reshape(here, 2, halves.shape[1] // 2, halves.shape[2])
+        keep = lax.dynamic_index_in_dim(halves, core, 1, False)
+        send = lax.dynamic_index_in_dim(halves, 1 - core, 1, False)
+        arrived = swap(send.astype(BF16), "dp", 1).astype(F32)
+        return jnp.concatenate(
+            [jnp.where(core == 0, keep, arrived), jnp.where(core == 0, arrived, keep)], 0
+        )
+
+    grad_expert_up = to_cores(ups)
+    grad_expert_down = to_cores(downs)
+
+    def reduce_tiles(tiles, scatter):
+        held = tiles.reshape((2, 2) + tiles.shape[1:])
+        held = half_sum(held, 0, core, "dp", 1)
+        held = half_sum(held, 0, stream, "stream", 1)
+        return reduce_zy(held, scatter)
+
+    up_tiles = dup.reshape(4, zy, part, -1)
+    up_own = reduce_tiles(up_tiles, 0).astype(BF16).reshape(2, part // 2, -1)
+    keep = lax.dynamic_index_in_dim(up_own, core, 0, False)
+    send = lax.dynamic_index_in_dim(up_own, 1 - core, 0, False)
+    arrived = swap(send, "dp", 1)
+    both = jnp.stack([jnp.where(core == 0, keep, arrived), jnp.where(core == 0, arrived, keep)], 1)
+    both = paired(both, 2, stream, "stream", 1)
+    grad_shared_up = both.reshape(part // 2, -1).astype(F32)
+
+    down_full = jnp.swapaxes(ddown, 1, 2).reshape(shared_down.shape)
+    grad_shared_down = reduce_copied(down_full)
+    grad_qkv = reduce_copied(dqkv)
+    grad_out_weight = reduce_copied(dout.astype(BF16))
+    return (
+        mixed, grad_patches, grad_embedding, grad_ada, grad_qkv, grad_out_weight, grad_shared_up,
+        grad_shared_down, grad_router, grad_expert_up, grad_expert_down,
+    )
+
+
+def local(*arrays):
+    if lax.axis_size("stream") == 2 and arrays[11].shape[0] % 2 == 0:
+        return local_pair(*arrays)
+    return local_general(*arrays)
 
 
 def solution(mesh):

time: 1570 us -> 888 us (0.57)
  waiting for transfers between devices: 838 us -> 286 us
  matrix products: 345 us -> 2.33 us
  Pallas kernels: 0 us -> 286 us
  local copies, waits for them, and re-layouts: 194 us -> 93.6 us
  starting transfers between devices: 23.1 us -> 106 us
  other arithmetic: 108 us -> 62.5 us
  blocking collectives: 4.98 us -> 40.8 us
  loops' own time: 22.3 us -> 0 us
    reduce_scatter x7 -> x0, waiting for transfers between devices: 792 us -> none  [the longest x1 195 us: local(): lax.psum_scatter(grad_expert_down.astype(jnp.bfloat16), 'dp', scatter_dim...]
    dot_general x31 -> x2, matrix products: 345 us -> 2.33 us  [the longest x1 2.17 us: local_pair(): lax.dot_general(acts, factors, (((0,), (0,)), ((), ())), preferred_elemen...]
    pallas_call x0 -> x19, Pallas kernels: none -> 286 us  [the longest x4 127 us: expert_call(): pl.pallas_call(functools.partial(expert_kernel, slot, prior is not None),...]
    ppermute x0 -> x67, waiting for transfers between devices: none -> 286 us  [swap(): return lax.ppermute(values, axis, [(i, i ^ bit) for i in range(size)])]
    ppermute x0 -> x67, starting transfers between devices: none -> 106 us  [swap(): return lax.ppermute(values, axis, [(i, i ^ bit) for i in range(size)])]
    reduce_sum x12 -> x0, other arithmetic: 42 us -> none  [the longest x1 17.2 us: local(): grad_gates = jnp.sum(picked * grad_branch[:, None, :], -1)]
    psum x1 -> x0, waiting for transfers between devices: 36.1 us -> none  [local(): lax.psum(shares[0].astype(jnp.bfloat16), 'stream').astype(jnp.float32)]
    psum x1, blocking collectives: 4.98 us -> 40.8 us  [local_pair(): drouter_sum = lax.psum(drouter_abs, ('dp', 'stream'))]
  transfers between devices with their start and end apart: 13 -> 67, of which waited for: 8 -> 29; matrix products, arithmetic and copies ran while one was open for 22% -> 18% of each run, Pallas kernels for 0% -> 33%
where the time goes in v1:
time: 888 us; the launch traced here: 880 us
  Pallas kernels  286 us (32%)
  waiting for transfers between devices  286 us (32%)
  starting transfers between devices  106 us (12%)
  local copies, waits for them, and re-layouts  93.6 us (11%)
  other arithmetic  62.5 us (7%)
  blocking collectives  40.8 us (5%)
    ppermute x67, waiting for transfers between devices, swap(): return lax.ppermute(values, axis, [(i, i ^ bit) for i in range(size)])  286 us
    pallas_call x4, Pallas kernels, expert_call(): pl.pallas_call(functools.partial(expert_kernel, slot, prior is not None),...  127 us
    ppermute x67, starting transfers between devices, swap(): return lax.ppermute(values, axis, [(i, i ^ bit) for i in range(size)])  106 us
    psum x1, blocking collectives, local_pair(): drouter_sum = lax.psum(drouter_abs, ('dp', 'stream'))  40.8 us
    add x26, other arithmetic, half_sum(): return keep.astype(F32) + arrived.astype(F32)  37.3 us
    pallas_call x1, Pallas kernels, shared_call(): pl.pallas_call(shared_kernel, grid=(tiles,), in_specs=[whole(hidden), who...  36.3 us
    pallas_call x2, Pallas kernels, combine(): pl.pallas_call(functools.partial(combine_kernel, len(pairs)), grid=(count...  19.8 us
  transfers between devices with their start and end apart: 67, of which 29 were waited for; matrix products, arithmetic and copies ran while one was open for 18% of the time, Pallas kernels for 33%

profile of v1, /device:TPU:0, one launch (start us, length us, event | category | flops | bytes accessed | tf_op | source)
XLA Modules:
  0.0 879.5 jit_solution(9568315384253498535)
XLA Ops:
  21.2 9.9 %attend.1 = (bf16[1024,768]{1,0:T(8,128)(2,1)}, f32[1024,768]{1,0:T(8,128)}) custom-call(s32[1]{0:T(128)S(6)} %copy.98.long_ref, bf16[1024,2304]{1,0:T(8,128)(2,1)} %qkv.1.q_ref.k_ref.v_ref, bf16[1024,2304]{1,0:T(8,128)(2,1)} %qkv.1.q_ref.k_ref.v_ref, bf16[1024,2304]{1,0:T(8,128)(2,1)} %qkv.1.q_ref.k_ref.v_ref), custom_call_target="tpu_custom_call" | custom-call | flops 12884901888 | bytes 9437184 | tf_op jit(solution)/shard_map/attend/pallas_call | solution.py:560
  39.8 36.3 %shared.1 = (bf16[4,768,768]{2,1,0:T(8,128)(2,1)}, bf16[4,768,768]{2,1,0:T(8,128)(2,1)}, f32[1024,768]{1,0:T(8,128)}, f32[1024,768]{1,0:T(8,128)}) custom-call(bf16[1024,768]{1,0:T(8,128)(2,1)} %get-tuple-element.63.h_ref.h0_ref.hidden_ref, bf16[1024,768]{1,0:T(8,128)(2,1)} %fusion.b_ref.g0_ref, bf16[1,768,3072]{2,1,0:T(8,128)(2,1)} %bitcast.420, ...), custom_call_target="tpu_custom_call" | custom-call | flops 28991029248 | bytes 18874368 | tf_op jit(solution)/shard_map/shared/pallas_call | solution.py:884
  82.8 10.1 %reshape_reshape.21 = bf16[8,2,192,2,384]{4,3,2,1,0:T(2,128)(2,1)} reshape(bf16[4,768,768]{2,1,0:T(8,128)(2,1)} %copy.59) | data formatting | bytes 9437184 | tf_op jit(solution)/shard_map/reshape;reshape | solution.py:1206
  111.6 31.2 %expert.4 = (bf16[768,3072]{1,0:T(8,128)(2,1)}, bf16[8,768,384]{2,1,0:T(8,128)(2,1)}, bf16[2,288,768]{2,1,0:T(8,128)(2,1)}, bf16[2,288,768]{2,1,0:T(8,128)(2,1)}, f32[2,1,1024]{2,1,0:T(1,128)}) custom-call(s32[2]{0:T(128)} %get-tuple-element.159.scal_ref, bf16[1024,768]{1,0:T(8,128)(2,1)} %get-tuple-element.63.h_ref.h0_ref.hidden_ref, ...), custom_call_target="tpu_custom_call" | custom-call | flops 16307453952 | bytes 18874368 | tf_op jit(solution)/shard_map/expert/pallas_call | solution.py:832
  142.9 31.3 %expert.5 = (bf16[768,3072]{1,0:T(8,128)(2,1)}, bf16[8,768,384]{2,1,0:T(8,128)(2,1)}, bf16[2,288,768]{2,1,0:T(8,128)(2,1)}, bf16[2,288,768]{2,1,0:T(8,128)(2,1)}, f32[2,1,1024]{2,1,0:T(1,128)}) custom-call(s32[2]{0:T(128)} %get-tuple-element.160.scal_ref, bf16[1024,768]{1,0:T(8,128)(2,1)} %get-tuple-element.63.h_ref.h0_ref.hidden_ref, ...), custom_call_target="tpu_custom_call" | custom-call | flops 16307453952 | bytes 18874368 | tf_op jit(solution)/shard_map/expert/pallas_call | solution.py:832
  176.3 9.9 %combine.2 = (bf16[2,1024,768]{2,1,0:T(8,128)(2,1)}, bf16[2,1024,768]{2,1,0:T(8,128)(2,1)}) custom-call(s32[2,1024,128]{2,1,0:T(8,128)} %get-tuple-element.65.col_ref, bf16[2,288,768]{2,1,0:T(8,128)(2,1)} %get-tuple-element.67.rest_0_, bf16[2,288,768]{2,1,0:T(8,128)(2,1)} %get-tuple-element.68.rest_1_, bf16[2,288,768]{2,1,0:T(8,128)(2,1)} %get-tuple-element.69.rest_2_, ...), custom_call_target="tpu_custom_call" | custom-call | flops 3623878656 | bytes 12582912 | tf_op jit(solution)/shard_map/combine/pallas_call | solution.py:935
  207.1 32.0 %expert.6 = (bf16[768,3072]{1,0:T(8,128)(2,1)}, bf16[8,768,384]{2,1,0:T(8,128)(2,1)}, bf16[2,288,768]{2,1,0:T(8,128)(2,1)}, bf16[2,288,768]{2,1,0:T(8,128)(2,1)}, f32[2,1,1024]{2,1,0:T(1,128)}) custom-call(s32[2]{0:T(128)} %get-tuple-element.159.scal_ref, bf16[1024,768]{1,0:T(8,128)(2,1)} %collective-permute-done.6.h0_ref, ...), custom_call_target="tpu_custom_call" | custom-call | flops 16307453952 | bytes 18874368 | tf_op jit(solution)/shard_map/expert/pallas_call | solution.py:832
  242.6 17.5 %collective-permute-start.60 = (bf16[2,2,768,384]{3,2,1,0:T(8,128)(2,1)}, bf16[2,2,768,384]{3,2,1,0:T(8,128)(2,1)}, u32[]{:S(2)}, u32[]{:S(2)}) collective-permute-start(bf16[2,2,768,384]{3,2,1,0:T(8,128)(2,1)} %dynamic-slice_bitcast_fusion.1), channel_id=1, source_target_pairs={{0,4},{2,6},{4,0},{6,2},{8,12},{10,14},{12,8},{14,10},{16,20},{18,... | collective-permute-start | bytes 7077896 | tf_op jit(solution)/shard_map/ppermute | solution.py:1156
  261.6 32.3 %expert.7 = (bf16[768,3072]{1,0:T(8,128)(2,1)}, bf16[8,768,384]{2,1,0:T(8,128)(2,1)}, bf16[2,288,768]{2,1,0:T(8,128)(2,1)}, bf16[2,288,768]{2,1,0:T(8,128)(2,1)}, f32[2,1,1024]{2,1,0:T(1,128)}) custom-call(s32[2]{0:T(128)} %get-tuple-element.160.scal_ref, bf16[1024,768]{1,0:T(8,128)(2,1)} %collective-permute-done.6.h0_ref, ...), custom_call_target="tpu_custom_call" | custom-call | flops 16307453952 | bytes 18874368 | tf_op jit(solution)/shard_map/expert/pallas_call | solution.py:832
  297.3 9.9 %combine.3 = (bf16[2,1024,768]{2,1,0:T(8,128)(2,1)}, bf16[2,1024,768]{2,1,0:T(8,128)(2,1)}) custom-call(s32[2,1024,128]{2,1,0:T(8,128)} %get-tuple-element.72.col_ref, bf16[2,288,768]{2,1,0:T(8,128)(2,1)} %get-tuple-element.76.rest_0_, bf16[2,288,768]{2,1,0:T(8,128)(2,1)} %get-tuple-element.77.rest_1_, bf16[2,288,768]{2,1,0:T(8,128)(2,1)} %get-tuple-element.80.rest_2_, ...), custom_call_target="tpu_custom_call" | custom-call | flops 3623878656 | bytes 12582912 | tf_op jit(solution)/shard_map/combine/pallas_call | solution.py:935
  320.1 9.3 %collective-permute-done.42 = bf16[2,2,96,768]{3,2,1,0:T(8,128)(2,1)S(1)} collective-permute-done((bf16[2,2,96,768]{3,2,1,0:T(8,128)(2,1)S(1)}, bf16[2,2,96,768]{3,2,1,0:T(8,128)(2,1)S(1)}, u32[]{:S(2)}, u32[]{:S(2)}) %collective-permute-start.42) | collective-permute-done | bytes 589856 | tf_op jit(solution)/shard_map/ppermute | solution.py:1156
  329.6 12.5 %collective-permute-done.49 = bf16[2,2,192,384]{3,2,1,0:T(8,128)(2,1)S(1)} collective-permute-done((bf16[2,2,192,384]{3,2,1,0:T(8,128)(2,1)S(1)}, bf16[2,2,192,384]{3,2,1,0:T(8,128)(2,1)S(1)}, u32[]{:S(2)}, u32[]{:S(2)}) %collective-permute-start.49) | collective-permute-done | bytes 589856 | tf_op jit(solution)/shard_map/ppermute | solution.py:1156
  403.7 39.6 %collective-permute-done.53 = bf16[2,2,96,3072]{3,2,1,0:T(8,128)(2,1)} collective-permute-done((bf16[2,2,96,3072]{3,2,1,0:T(8,128)(2,1)S(1)}, bf16[2,2,96,3072]{3,2,1,0:T(8,128)(2,1)}, u32[]{:S(2)}, u32[]{:S(2)}) %collective-permute-start.53) | collective-permute-done | bytes 2359328 | tf_op jit(solution)/shard_map/ppermute | solution.py:1156
  447.5 45.7 %collective-permute-done.56 = bf16[2,2,96,3072]{3,2,1,0:T(8,128)(2,1)} collective-permute-done((bf16[2,2,96,3072]{3,2,1,0:T(8,128)(2,1)}, bf16[2,2,96,3072]{3,2,1,0:T(8,128)(2,1)}, u32[]{:S(2)}, u32[]{:S(2)}) %collective-permute-start.56) | collective-permute-done | bytes 2359328 | tf_op jit(solution)/shard_map/ppermute | solution.py:1156
  502.7 14.7 %middle_back.1 = (f32[1024,768]{1,0:T(8,128)}, bf16[1024,768]{1,0:T(8,128)(2,1)}, f32[3,8,768]{2,1,0:T(8,128)}, f32[16,768]{1,0:T(8,128)}, f32[768,768]{1,0:T(8,128)}) custom-call(f32[1024,768]{1,0:T(8,128)} %get-tuple-element.86.gs_ref, bf16[1024,768]{1,0:T(8,128)(2,1)} %get-tuple-element.114.ga_ref, bf16[1024,768]{1,0:T(8,128)(2,1)} %collective-permute-done.12.gb_ref, ...), custom_call_target="tpu_custom_call" | custom-call | flops 2415919104 | bytes 23592960 | tf_op jit(solution)/shard_map/middle_back/pallas_call | solution.py:1005
  521.4 16.2 %attend_back.1 = (bf16[1024,768]{1,0:T(8,128)(2,1)}, bf16[1024,768]{1,0:T(8,128)(2,1)}, bf16[1024,768]{1,0:T(8,128)(2,1)}) custom-call(s32[1]{0:T(128)S(6)} %copy.98.long_ref, bf16[1024,2304]{1,0:T(8,128)(2,1)} %qkv.1.q_ref.k_ref.v_ref, bf16[1024,2304]{1,0:T(8,128)(2,1)} %qkv.1.q_ref.k_ref.v_ref, bf16[1024,2304]{1,0:T(8,128)(2,1)} %qkv.1.q_ref.k_ref.v_ref, ...), custom_call_target="tpu_custom_call" | custom-call | flops 32212254720 | bytes 15728640 | tf_op jit(solution)/shard_map/attend_back/pallas_call | solution.py:639
  537.7 9.1 %qkv_weight.1 = bf16[768,2304]{1,0:T(8,128)(2,1)} custom-call(bf16[1024,768]{1,0:T(8,128)(2,1)} %x_ref.11, f32[6,8,768]{2,1,0:T(8,128)} %get-tuple-element.61.mod_ref, bf16[1024,768]{1,0:T(8,128)(2,1)} %get-tuple-element.94.dq_ref, bf16[1024,768]{1,0:T(8,128)(2,1)} %get-tuple-element.95.dk_ref, bf16[1024,768]{1,0:T(8,128)(2,1)} %get-tuple-element.96.dv_ref), custom_call_target="tpu_custom_call" | custom-call | flops 3623878656 | bytes 11010048 | tf_op jit(solution)/shard_map/qkv_weight/pallas_call | solution.py:1065
  553.5 10.1 %inputs_back.1 = (f32[1024,768]{1,0:T(8,128)}, f32[2,8,768]{2,1,0:T(8,128)}) custom-call(bf16[1024,768]{1,0:T(8,128)(2,1)} %get-tuple-element.94.dq_ref, bf16[1024,768]{1,0:T(8,128)(2,1)} %get-tuple-element.95.dk_ref, bf16[1024,768]{1,0:T(8,128)(2,1)} %get-tuple-element.96.dv_ref, bf16[768,2304]{1,0:T(8,128)(2,1)} %w_ref.7, bf16[1024,768]{1,0:T(8,128)(2,1)} %x_ref.11, ...), custom_call_target="tpu_custom_call" | custom-call | flops 3623878656 | bytes 15728640 | tf_op jit(solution)/shard_map/inputs_back/pallas_call | solution.py:1094
  570.7 23.5 %collective-permute-start.23 = (bf16[4,1536]{1,0:T(4,128)(2,1)}, bf16[4,1536]{1,0:T(4,128)(2,1)S(1)}, u32[]{:S(2)}, u32[]{:S(2)}) collective-permute-start(bf16[4,1536]{1,0:T(4,128)(2,1)} %pad_maximum_fusion.15), channel_id=1, source_target_pairs={{0,1},{1,0},{2,3},{3,2},{4,5},{5,4},{6,7},{7,6},{8,9},{9,8},{10,11... | collective-permute-start | bytes 36872 | tf_op jit(solution)/shard_map/ppermute | solution.py:1156
  604.3 40.8 %psum.7 = f32[8,768]{1,0:T(8,128)S(1)} all-reduce(f32[8,768]{1,0:T(8,128)S(1)} %fusion.47), channel_id=1, replica_groups=mesh['dp'=16,'stream'=2] {'dp','stream'}, use_global_device_ids=true, to_apply=%region_1.2 | all-reduce | flops 6144 | bytes 49152 | tf_op jit(solution)/shard_map/psum | solution.py:1306
  718.4 67.6 %collective-permute-done.22 = bf16[16,4,3840]{2,1,0:T(4,128)(2,1)S(1)} collective-permute-done((bf16[16,4,3840]{2,1,0:T(4,128)(2,1)S(1)}, bf16[16,4,3840]{2,1,0:T(4,128)(2,1)S(1)}, u32[]{:S(2)}, u32[]{:S(2)}) %collective-permute-start.22) | collective-permute-done | bytes 491552 | tf_op jit(solution)/shard_map/ppermute | solution.py:1156
  801.9 9.5 %collective-permute-done.55 = bf16[96,3072]{1,0:T(8,128)(2,1)} collective-permute-done((bf16[96,3072]{1,0:T(8,128)(2,1)}, bf16[96,3072]{1,0:T(8,128)(2,1)}, u32[]{:S(2)}, u32[]{:S(2)}) %collective-permute-start.55) | collective-permute-done | bytes 589856 | tf_op jit(solution)/shard_map/ppermute | solution.py:1156
  813.9 9.6 %collective-permute-done.58 = bf16[96,3072]{1,0:T(8,128)(2,1)} collective-permute-done((bf16[96,3072]{1,0:T(8,128)(2,1)}, bf16[96,3072]{1,0:T(8,128)(2,1)}, u32[]{:S(2)}, u32[]{:S(2)}) %collective-permute-start.58) | collective-permute-done | bytes 589856 | tf_op jit(solution)/shard_map/ppermute | solution.py:1156
  831.8 17.5 %collective-permute-done.39 = bf16[48,384]{1,0:T(8,128)(2,1)S(1)} collective-permute-done((bf16[48,384]{1,0:T(8,128)(2,1)S(1)}, bf16[48,384]{1,0:T(8,128)(2,1)S(1)}, u32[]{:S(2)}, u32[]{:S(2)}) %collective-permute-start.39) | collective-permute-done | bytes 36896 | tf_op jit(solution)/shard_map/ppermute | solution.py:1156
  (406 shorter events, 330.4 us)
Async XLA Ops:
  0.6 102.2 %collective-permute-start = (s32[2,1024]{1,0:T(2,128)}, s32[2,1024]{1,0:T(2,128)S(1)}, u32[]{:S(2)}, u32[]{:S(2)}) collective-permute-start(s32[2,1024]{1,0:T(2,128)} %bitcast.413), channel_id=1, source_target_pairs={{0,2},{2,0},{4,6},{6,4},{8,10},{10,8},{12,14},{14,12},{16,18},{18,... | collective-permute-start | bytes 24584 | tf_op jit(solution)/shard_map/ppermute | solution.py:1156
  1.2 103.5 %collective-permute-start.4 = (s32[2,1024]{1,0:T(2,128)}, s32[2,1024]{1,0:T(2,128)S(1)}, u32[]{:S(2)}, u32[]{:S(2)}) collective-permute-start(s32[2,1024]{1,0:T(2,128)} %bitcast.414), channel_id=1, source_target_pairs={{0,1},{1,0},{2,3},{3,2},{4,5},{5,4},{6,7},{7,6},{8,9},{9,8},{10,11... | collective-permute-start | bytes 24584 | tf_op jit(solution)/shard_map/ppermute | solution.py:1156
  37.3 138.5 %collective-permute-start.6 = (bf16[1024,768]{1,0:T(8,128)(2,1)}, bf16[1024,768]{1,0:T(8,128)(2,1)}, u32[]{:S(2)}, u32[]{:S(2)}) collective-permute-start(bf16[1024,768]{1,0:T(8,128)(2,1)} %get-tuple-element.63.h_ref.h0_ref.hidden_ref), channel_id=1, source_target_pairs={{0,1},{1,0},{2,3},{3,2},{4,5},{5,4},{6,7},{7,6},{8,9},{9,8},{10,11... | collective-permute-start | bytes 4718600 | tf_op jit(solution)/shard_map/ppermute | solution.py:1156
  108.1 84.0 %collective-permute-start.47 = (bf16[8,192,2,384]{3,2,1,0:T(2,128)(2,1)}, bf16[8,192,2,384]{3,2,1,0:T(2,128)(2,1)}, u32[]{:S(2)}, u32[]{:S(2)}) collective-permute-start(bf16[8,192,2,384]{3,2,1,0:T(2,128)(2,1)} %dynamic-slice_bitcast_fusion.4), channel_id=1, source_target_pairs={{0,2},{2,0},{4,6},{6,4},{8,10},{10,8},{12,14},{14,12},{16,18},{18,... | collective-permute-start | bytes 7077896 | tf_op jit(solution)/shard_map/ppermute | solution.py:1156
  111.5 88.0 %collective-permute-start.40 = (bf16[2,8,96,768]{3,2,1,0:T(8,128)(2,1)S(1)}, bf16[2,8,96,768]{3,2,1,0:T(8,128)(2,1)}, u32[]{:S(2)}, u32[]{:S(2)}) collective-permute-start(bf16[2,8,96,768]{3,2,1,0:T(8,128)(2,1)S(1)} %dynamic-slice_bitcast_fusion.5), channel_id=1, source_target_pairs={{0,2},{2,0},{4,6},{6,4},{8,10},{10,8},{12,14},{14,12},{16,18},{18,... | collective-permute-start | bytes 7077896 | tf_op jit(solution)/shard_map/ppermute | solution.py:1156
  175.5 143.2 %collective-permute-start.15 = (f32[2,1024]{1,0:T(2,128)}, f32[2,1024]{1,0:T(2,128)}, u32[]{:S(2)}, u32[]{:S(2)}) collective-permute-start(f32[2,1024]{1,0:T(2,128)} %get-tuple-element.156), channel_id=1, source_target_pairs={{0,2},{2,0},{4,6},{6,4},{8,10},{10,8},{12,14},{14,12},{16,18},{18,... | collective-permute-start | bytes 24584 | tf_op jit(solution)/shard_map/ppermute | solution.py:1156
  199.1 114.2 %collective-permute-start.48 = (bf16[8,192,384]{2,1,0:T(8,128)(2,1)S(1)}, bf16[8,192,384]{2,1,0:T(8,128)(2,1)}, u32[]{:S(2)}, u32[]{:S(2)}) collective-permute-start(bf16[8,192,384]{2,1,0:T(8,128)(2,1)S(1)} %bitcast.399), channel_id=1, source_target_pairs={{0,1},{1,0},{2,3},{3,2},{4,5},{5,4},{6,7},{7,6},{8,9},{9,8},{10,11... | collective-permute-start | bytes 3538952 | tf_op jit(solution)/shard_map/ppermute | solution.py:1156
  202.9 108.8 %collective-permute-start.41 = (bf16[8,96,768]{2,1,0:T(8,128)(2,1)}, bf16[8,96,768]{2,1,0:T(8,128)(2,1)}, u32[]{:S(2)}, u32[]{:S(2)}) collective-permute-start(bf16[8,96,768]{2,1,0:T(8,128)(2,1)} %fusion.1), channel_id=1, source_target_pairs={{0,1},{1,0},{2,3},{3,2},{4,5},{5,4},{6,7},{7,6},{8,9},{9,8},{10,11... | collective-permute-start | bytes 3538952 | tf_op jit(solution)/shard_map/ppermute | solution.py:1156
  242.6 151.4 %collective-permute-start.60 = (bf16[2,2,768,384]{3,2,1,0:T(8,128)(2,1)}, bf16[2,2,768,384]{3,2,1,0:T(8,128)(2,1)}, u32[]{:S(2)}, u32[]{:S(2)}) collective-permute-start(bf16[2,2,768,384]{3,2,1,0:T(8,128)(2,1)} %dynamic-slice_bitcast_fusion.1), channel_id=1, source_target_pairs={{0,4},{2,6},{4,0},{6,2},{8,12},{10,14},{12,8},{14,10},{16,20},{18,... | collective-permute-start | bytes 7077896 | tf_op jit(solution)/shard_map/ppermute | solution.py:1156
  384.6 114.3 %collective-permute-start.12 = (bf16[1024,768]{1,0:T(8,128)(2,1)}, bf16[1024,768]{1,0:T(8,128)(2,1)}, u32[]{:S(2)}, u32[]{:S(2)}) collective-permute-start(bf16[1024,768]{1,0:T(8,128)(2,1)} %get-tuple-element.113), channel_id=1, source_target_pairs={{0,2},{2,0},{4,6},{6,4},{8,10},{10,8},{12,14},{14,12},{16,18},{18,... | collective-permute-start | bytes 4718600 | tf_op jit(solution)/shard_map/ppermute | solution.py:1156
  392.2 101.0 %collective-permute-start.56 = (bf16[2,2,96,3072]{3,2,1,0:T(8,128)(2,1)}, bf16[2,2,96,3072]{3,2,1,0:T(8,128)(2,1)}, u32[]{:S(2)}, u32[]{:S(2)}) collective-permute-start(bf16[2,2,96,3072]{3,2,1,0:T(8,128)(2,1)} %dynamic-slice_bitcast_fusion.2), channel_id=1, source_target_pairs={{0,4},{2,6},{4,0},{6,2},{8,12},{10,14},{12,8},{14,10},{16,20},{18,... | collective-permute-start | bytes 7077896 | tf_op jit(solution)/shard_map/ppermute | solution.py:1156
  394.0 175.3 %collective-permute-start.3 = (bf16[1024,768]{1,0:T(8,128)(2,1)}, bf16[1024,768]{1,0:T(8,128)(2,1)}, u32[]{:S(2)}, u32[]{:S(2)}) collective-permute-start(bf16[1024,768]{1,0:T(8,128)(2,1)} %get-tuple-element.115), channel_id=1, source_target_pairs={{0,2},{2,0},{4,6},{6,4},{8,10},{10,8},{12,14},{14,12},{16,18},{18,... | collective-permute-start | bytes 4718600 | tf_op jit(solution)/shard_map/ppermute | solution.py:1156
  398.2 102.0 %collective-permute-start.14 = (bf16[1024,768]{1,0:T(8,128)(2,1)S(1)}, bf16[1024,768]{1,0:T(8,128)(2,1)S(1)}, u32[]{:S(2)}, u32[]{:S(2)}) collective-permute-start(bf16[1024,768]{1,0:T(8,128)(2,1)S(1)} %copy-done.24), channel_id=1, source_target_pairs={{0,1},{1,0},{2,3},{3,2},{4,5},{5,4},{6,7},{7,6},{8,9},{9,8},{10,11... | collective-permute-start | bytes 4718600 | tf_op jit(solution)/shard_map/ppermute | solution.py:1156
  443.3 127.4 %collective-permute-start.11 = (bf16[1024,768]{1,0:T(8,128)(2,1)}, bf16[1024,768]{1,0:T(8,128)(2,1)}, u32[]{:S(2)}, u32[]{:S(2)}) collective-permute-start(bf16[1024,768]{1,0:T(8,128)(2,1)} %bitcast_add_fusion.8), channel_id=1, source_target_pairs={{0,1},{1,0},{2,3},{3,2},{4,5},{5,4},{6,7},{7,6},{8,9},{9,8},{10,11... | collective-permute-start | bytes 4718600 | tf_op jit(solution)/shard_map/ppermute | solution.py:1156
  493.2 196.7 %collective-permute-start.61 = (bf16[2,768,384]{2,1,0:T(8,128)(2,1)}, bf16[2,768,384]{2,1,0:T(8,128)(2,1)}, u32[]{:S(2)}, u32[]{:S(2)}) collective-permute-start(bf16[2,768,384]{2,1,0:T(8,128)(2,1)} %fusion.4), channel_id=1, source_target_pairs={{0,8},{2,10},{4,12},{6,14},{8,0},{10,2},{12,4},{14,6},{16,24},{18,... | collective-permute-start | bytes 3538952 | tf_op jit(solution)/shard_map/ppermute | solution.py:1156
  498.8 195.1 %collective-permute-start.64 = (bf16[2,768,384]{2,1,0:T(8,128)(2,1)}, bf16[2,768,384]{2,1,0:T(8,128)(2,1)}, u32[]{:S(2)}, u32[]{:S(2)}) collective-permute-start(bf16[2,768,384]{2,1,0:T(8,128)(2,1)} %fusion.5), channel_id=1, source_target_pairs={{0,8},{2,10},{4,12},{6,14},{8,0},{10,2},{12,4},{14,6},{16,24},{18,... | collective-permute-start | bytes 3538952 | tf_op jit(solution)/shard_map/ppermute | solution.py:1156
  501.4 195.8 %collective-permute-start.54 = (bf16[2,96,3072]{2,1,0:T(8,128)(2,1)}, bf16[2,96,3072]{2,1,0:T(8,128)(2,1)}, u32[]{:S(2)}, u32[]{:S(2)}) collective-permute-start(bf16[2,96,3072]{2,1,0:T(8,128)(2,1)} %fusion.2), channel_id=1, source_target_pairs={{0,8},{2,10},{4,12},{6,14},{8,0},{10,2},{12,4},{14,6},{16,24},{18,... | collective-permute-start | bytes 3538952 | tf_op jit(solution)/shard_map/ppermute | solution.py:1156
  569.4 132.1 %collective-permute-start.57 = (bf16[2,96,3072]{2,1,0:T(8,128)(2,1)}, bf16[2,96,3072]{2,1,0:T(8,128)(2,1)}, u32[]{:S(2)}, u32[]{:S(2)}) collective-permute-start(bf16[2,96,3072]{2,1,0:T(8,128)(2,1)} %fusion.3), channel_id=1, source_target_pairs={{0,8},{2,10},{4,12},{6,14},{8,0},{10,2},{12,4},{14,6},{16,24},{18,... | collective-permute-start | bytes 3538952 | tf_op jit(solution)/shard_map/ppermute | solution.py:1156
  570.7 87.6 %collective-permute-start.23 = (bf16[4,1536]{1,0:T(4,128)(2,1)}, bf16[4,1536]{1,0:T(4,128)(2,1)S(1)}, u32[]{:S(2)}, u32[]{:S(2)}) collective-permute-start(bf16[4,1536]{1,0:T(4,128)(2,1)} %pad_maximum_fusion.15), channel_id=1, source_target_pairs={{0,1},{1,0},{2,3},{3,2},{4,5},{5,4},{6,7},{7,6},{8,9},{9,8},{10,11... | collective-permute-start | bytes 36872 | tf_op jit(solution)/shard_map/ppermute | solution.py:1156
  689.9 135.4 %collective-permute-start.28 = (bf16[8,48,2,1152]{3,1,0,2:T(8,128)(2,1)}, bf16[8,48,2,1152]{3,1,0,2:T(8,128)(2,1)}, u32[]{:S(2)}, u32[]{:S(2)}) collective-permute-start(bf16[8,48,2,1152]{3,1,0,2:T(8,128)(2,1)} %bitcast.352), channel_id=1, source_target_pairs={{0,2},{2,0},{4,6},{6,4},{8,10},{10,8},{12,14},{14,12},{16,18},{18,... | collective-permute-start | bytes 5308424 | tf_op jit(solution)/shard_map/ppermute | solution.py:1156
  697.2 97.0 %collective-permute-start.62 = (bf16[768,384]{1,0:T(8,128)(2,1)}, bf16[768,384]{1,0:T(8,128)(2,1)}, u32[]{:S(2)}, u32[]{:S(2)}) collective-permute-start(bf16[768,384]{1,0:T(8,128)(2,1)} %fusion.25), channel_id=1, source_target_pairs={{0,16},{2,18},{4,20},{6,22},{8,24},{10,26},{12,28},{14,30},{16,0},... | collective-permute-start | bytes 1769480 | tf_op jit(solution)/shard_map/ppermute | solution.py:1156
  701.5 98.3 %collective-permute-start.65 = (bf16[768,384]{1,0:T(8,128)(2,1)}, bf16[768,384]{1,0:T(8,128)(2,1)}, u32[]{:S(2)}, u32[]{:S(2)}) collective-permute-start(bf16[768,384]{1,0:T(8,128)(2,1)} %fusion.26), channel_id=1, source_target_pairs={{0,16},{2,18},{4,20},{6,22},{8,24},{10,26},{12,28},{14,30},{16,0},... | collective-permute-start | bytes 1769480 | tf_op jit(solution)/shard_map/ppermute | solution.py:1156
  705.4 80.7 %collective-permute-start.22 = (bf16[16,4,3840]{2,1,0:T(4,128)(2,1)S(1)}, bf16[16,4,3840]{2,1,0:T(4,128)(2,1)S(1)}, u32[]{:S(2)}, u32[]{:S(2)}) collective-permute-start(bf16[16,4,3840]{2,1,0:T(4,128)(2,1)S(1)} %bitcast.396), channel_id=1, source_target_pairs={{0,16},{2,18},{4,20},{6,22},{8,24},{10,26},{12,28},{14,30},{16,0},... | collective-permute-start | bytes 1474568 | tf_op jit(solution)/shard_map/ppermute | solution.py:1156
  716.6 94.8 %collective-permute-start.55 = (bf16[96,3072]{1,0:T(8,128)(2,1)}, bf16[96,3072]{1,0:T(8,128)(2,1)}, u32[]{:S(2)}, u32[]{:S(2)}) collective-permute-start(bf16[96,3072]{1,0:T(8,128)(2,1)} %fusion.23), channel_id=1, source_target_pairs={{0,16},{2,18},{4,20},{6,22},{8,24},{10,26},{12,28},{14,30},{16,0},... | collective-permute-start | bytes 1769480 | tf_op jit(solution)/shard_map/ppermute | solution.py:1156
  (96 other events, 2036.3 us)

commit v2 on v0

--- a/solution.py
+++ b/solution.py
@@ -1,8 +1,11 @@
+import functools
 import math
 
 import jax
 import jax.numpy as jnp
 from jax import lax
+from jax.experimental import pallas as pl
+from jax.experimental.pallas import tpu as pltpu
 from jax.sharding import PartitionSpec as P
 
 HEADS = 12
@@ -13,6 +16,9 @@
 
 HIGH = lax.Precision.HIGHEST
 EPSILON = 1e-06
+F32 = jnp.float32
+BF16 = jnp.bfloat16
+MIB = 1 << 20
 
 
 def gelu_tanh(values):
@@ -133,7 +139,7 @@
     )
 
 
-def local(
+def local_general(
     patches,
     embedding,
     long_image,
@@ -386,6 +392,1183 @@
         expert_summed[0],
         expert_summed[1],
     )
+
+
+def nn(left, right):
+    return jnp.dot(left, right, preferred_element_type=F32)
+
+
+def nt(left, right):
+    return lax.dot_general(left, right, (((1,), (1,)), ((), ())), preferred_element_type=F32)
+
+
+def tn(left, right):
+    return lax.dot_general(left, right, (((0,), (0,)), ((), ())), preferred_element_type=F32)
+
+
+def three_parts(values):
+    first = values.astype(BF16)
+    rest = values - first.astype(F32)
+    second = rest.astype(BF16)
+    third = (rest - second.astype(F32)).astype(BF16)
+    return first, second, third
+
+
+def sigmoid(values):
+    return 1.0 / (1.0 + jnp.exp(-values))
+
+
+def gelu_and_slope(values):
+    inner = math.sqrt(2.0 / math.pi)
+    square = values * values
+    bend = jnp.tanh(values * (inner + (inner * 0.044715) * square))
+    half = 0.5 + 0.5 * bend
+    slope = half + values * (0.5 - 0.5 * bend * bend) * (inner + (3.0 * inner * 0.044715) * square)
+    return values * half, slope
+
+
+def run(kernel, args, grid, in_specs, out_specs, out_shape, name, scalars=(), scratch=(), after=(), limit=56):
+    count = len(scalars) + len(args)
+
+    def body(*refs):
+        kernel(*refs[:count], *refs[count + len(after) :])
+
+    return pl.pallas_call(
+        body,
+        grid_spec=pltpu.PrefetchScalarGridSpec(
+            num_scalar_prefetch=len(scalars),
+            grid=grid,
+            in_specs=list(in_specs) + [pl.BlockSpec(memory_space=pl.ANY)] * len(after),
+            out_specs=out_specs,
+            scratch_shapes=list(scratch),
+        ),
+        out_shape=out_shape,
+        compiler_params=pltpu.CompilerParams(vmem_limit_bytes=limit * MIB),
+        cost_estimate=pl.CostEstimate(flops=1000, bytes_accessed=1000, transcendentals=0),
+        name=name,
+    )(*scalars, *args, *after)
+
+
+def full(shape):
+    return pl.BlockSpec(shape, lambda *_: (0,) * len(shape))
+
+
+def like(array):
+    return full(array.shape)
+
+
+def rows_spec(rows, width):
+    return pl.BlockSpec((rows, width), lambda i, *_: (i, 0))
+
+
+def shape(dims, dtype):
+    return jax.ShapeDtypeStruct(tuple(dims), dtype)
+
+
+LONG, CORE, STREAM, ROW_Y, ROW_Z, FIRST_HERE, FIRST_ALL = range(7)
+
+
+def flipped(value, bits):
+    total = 0
+    for bit in range(bits):
+        total = total + (((value >> bit) & 1) << (bits - 1 - bit))
+    return total
+
+
+def modulate_kernel(blocks, pos_ref, emb_ref, ada_ref, cot_ref, mod_ref, act_ref, branch_ref):
+    emb = emb_ref[...]
+    used = jnp.where(pos_ref[LONG] > 0, jnp.broadcast_to(emb[0:1], emb.shape), emb)
+    act = used * sigmoid(used)
+    act_ref[...] = act
+    weight = ada_ref[...]
+    total = 0.0
+    for part in three_parts(act):
+        total = total + nn(part, weight)
+    mod_ref[0] = total
+
+    @pl.when(pl.program_id(0) == pl.num_programs(0) - 1)
+    def _():
+        short = cot_ref.shape[0] // blocks
+        for block in range(blocks):
+            span = slice(block * short, (block + 1) * short)
+            branch_ref[span, :] = (cot_ref[span, :].astype(F32) * total[block : block + 1]).astype(BF16)
+
+
+def modulate(pos, emb_pad, ada_weight, cot, blocks):
+    rows, width = emb_pad.shape
+    pieces = ada_weight.shape[1] // width
+    return run(
+        functools.partial(modulate_kernel, blocks), (emb_pad, ada_weight, cot), (pieces,),
+        [like(emb_pad), pl.BlockSpec((width, width), lambda i, *_: (0, i)), like(cot)],
+        [pl.BlockSpec((1, rows, width), lambda i, *_: (i, 0, 0)), like(emb_pad), like(cot)],
+        [shape((pieces, rows, width), F32), shape((rows, width), F32), shape(cot.shape, BF16)],
+        "modulate", scalars=(pos,),
+    )
+
+
+def norm_parts(values):
+    centered = values - jnp.mean(values, -1, keepdims=True)
+    spread = lax.rsqrt(jnp.mean(centered * centered, -1, keepdims=True) + EPSILON)
+    return centered * spread, spread
+
+
+def norm_back(grad, normed, spread):
+    return spread * (
+        grad
+        - jnp.mean(grad, -1, keepdims=True)
+        - normed * jnp.mean(grad * normed, -1, keepdims=True)
+    )
+
+
+def qkv_kernel(x_ref, mod_ref, w_ref, packed_ref):
+    block = pl.program_id(0)
+    normed, _ = norm_parts(x_ref[...].astype(F32))
+    shift, scale = mod_ref[0, pl.ds(block, 1), :], mod_ref[1, pl.ds(block, 1), :]
+    hidden = (normed * (1.0 + scale) + shift).astype(BF16)
+    packed_ref[...] = nn(hidden, w_ref[...]).astype(BF16)
+
+
+def qkv_forward(patches, mod, weight, blocks, after):
+    rows, width = patches.shape
+    short = rows // blocks
+    wide = weight.shape[1]
+    return run(
+        qkv_kernel, (patches, mod, weight), (blocks,),
+        [rows_spec(short, width), like(mod), like(weight)], rows_spec(short, wide),
+        shape((rows, wide), BF16), "qkv", after=after,
+    )
+
+
+def attend_kernel(short, pos_ref, q_ref, k_ref, v_ref, o_ref, lse_ref):
+    rows, lanes = q_ref.shape
+    first = lax.broadcasted_iota(jnp.int32, (1, lanes), 1) < HEAD_DIM
+    factor = 1.0 / math.sqrt(HEAD_DIM)
+
+    def part(query_at, key_at, key_count):
+        queries = q_ref[query_at : query_at + short, :]
+        keys = k_ref[key_at : key_at + key_count, :]
+        values = v_ref[key_at : key_at + key_count, :]
+        zero = jnp.zeros_like(queries)
+        outs, sums = [], []
+        for mine in (first, jnp.logical_not(first)):
+            scores = nt(jnp.where(mine, queries, zero), keys) * factor
+            top = jnp.max(scores, -1, keepdims=True)
+            shifted = jnp.exp(scores - top)
+            total = jnp.sum(shifted, -1, keepdims=True)
+            outs.append(nn(shifted.astype(BF16), values) * (1.0 / total))
+            sums.append(top + jnp.log(total))
+        o_ref[query_at : query_at + short, :] = jnp.where(first, outs[0], outs[1]).astype(BF16)
+        lse_ref[query_at : query_at + short, :] = jnp.where(first, sums[0], sums[1])
+
+    @pl.when(pos_ref[LONG] > 0)
+    def _():
+        for at in range(0, rows, short):
+            part(at, 0, rows)
+
+    @pl.when(pos_ref[LONG] <= 0)
+    def _():
+        for at in range(0, rows, short):
+            part(at, at, short)
+
+
+def pair_specs(rows, width):
+    lanes = 2 * HEAD_DIM
+    pairs = width // lanes
+    return [
+        pl.BlockSpec((rows, lanes), functools.partial(lambda shift, i, *_: (0, i + shift), shift))
+        for shift in (0, pairs, 2 * pairs)
+    ]
+
+
+def attend_forward(pos, packed, short):
+    rows = packed.shape[0]
+    width = packed.shape[1] // 3
+    spec = pair_specs(rows, width)
+    return run(
+        functools.partial(attend_kernel, short), (packed, packed, packed), (width // (2 * HEAD_DIM),),
+        spec, [spec[0], spec[0]], [shape((rows, width), BF16), shape((rows, width), F32)],
+        "attend", scalars=(pos,),
+    )
+
+
+def attend_back_kernel(
+    short, pos_ref, q_ref, k_ref, v_ref, o_ref, lse_ref, do_ref, dq_ref, dk_ref, dv_ref,
+    dk_acc, dv_acc,
+):
+    rows, lanes = q_ref.shape
+    first = lax.broadcasted_iota(jnp.int32, (1, lanes), 1) < HEAD_DIM
+    factor = 1.0 / math.sqrt(HEAD_DIM)
+    product = do_ref[...].astype(F32) * o_ref[...].astype(F32)
+    lse_t = jnp.transpose(lse_ref[...])
+    product_t = jnp.transpose(product)
+    lse_rows = [lse_t[0:1], lse_t[HEAD_DIM : HEAD_DIM + 1]]
+    delta_rows = [
+        jnp.sum(product_t[:HEAD_DIM], 0, keepdims=True),
+        jnp.sum(product_t[HEAD_DIM:], 0, keepdims=True),
+    ]
+
+    def part(query_at, key_at, key_count, fresh):
+        chunk = slice(query_at, query_at + short)
+        span = slice(key_at, key_at + key_count)
+        queries, grads = q_ref[chunk, :], do_ref[chunk, :]
+        keys, values = k_ref[span, :], v_ref[span, :]
+        zero, zero_keys = jnp.zeros_like(queries), jnp.zeros_like(keys)
+        dq = dk = dv = 0.0
+        for head, mine in enumerate((first, jnp.logical_not(first))):
+            query_own = jnp.where(mine, queries, zero)
+            grad_own = jnp.where(mine, grads, zero)
+            key_own = jnp.where(mine, keys, zero_keys)
+            scores = nt(keys, query_own) * factor
+            probs = jnp.exp(scores - lse_rows[head][:, chunk])
+            grad_probs = nt(values, grad_own)
+            grad_scores = (probs * (grad_probs - delta_rows[head][:, chunk])).astype(BF16)
+            dv = dv + nn(probs.astype(BF16), grad_own)
+            dk = dk + nn(grad_scores, query_own)
+            dq = dq + tn(grad_scores, key_own)
+        dq_ref[chunk, :] = (dq * factor).astype(BF16)
+        if fresh:
+            dk_acc[span, :] = dk
+            dv_acc[span, :] = dv
+        else:
+            dk_acc[span, :] += dk
+            dv_acc[span, :] += dv
+
+    @pl.when(pos_ref[LONG] > 0)
+    def _():
+        for at in range(0, rows, short):
+            part(at, 0, rows, at == 0)
+
+    @pl.when(pos_ref[LONG] <= 0)
+    def _():
+        for at in range(0, rows, short):
+            part(at, at, short, True)
+
+    dk_ref[...] = (dk_acc[...] * factor).astype(BF16)
+    dv_ref[...] = dv_acc[...].astype(BF16)
+
+
+def attend_backward(pos, packed, attended, logsum, grad, short, after):
+    rows, width = attended.shape
+    lanes = 2 * HEAD_DIM
+    spec = pair_specs(rows, width)
+    return run(
+        functools.partial(attend_back_kernel, short),
+        (packed, packed, packed, attended, logsum, grad), (width // lanes,),
+        spec + [spec[0]] * 3, [spec[0]] * 3, [shape((rows, width), BF16)] * 3,
+        "attend_back", scalars=(pos,), scratch=[pltpu.VMEM((rows, lanes), F32)] * 2, after=after,
+    )
+
+
+def middle_kernel(att_ref, x_ref, mod_ref, w_ref, branch_ref, hidden_ref):
+    block = pl.program_id(0)
+    branch = nn(att_ref[...], w_ref[...])
+    branch_ref[...] = branch
+    middle = x_ref[...].astype(F32) + mod_ref[2, pl.ds(block, 1), :] * branch
+    normed, _ = norm_parts(middle)
+    shift, scale = mod_ref[3, pl.ds(block, 1), :], mod_ref[4, pl.ds(block, 1), :]
+    hidden_ref[...] = (normed * (1.0 + scale) + shift).astype(BF16)
+
+
+def middle_forward(attended, patches, mod, out_weight, blocks, after):
+    rows, width = patches.shape
+    tile = rows_spec(rows // blocks, width)
+    return run(
+        middle_kernel, (attended, patches, mod, out_weight), (blocks,),
+        [tile, tile, like(mod), like(out_weight)], [tile, tile],
+        [shape((rows, width), F32), shape((rows, width), BF16)], "middle", after=after,
+    )
+
+
+def rank_kernel(pos_ref, *refs):
+    count = (len(refs) - 2) // 1
+    routes, (row_ref, col_ref) = refs[:count], refs[count:]
+    rows = routes[0].shape[1]
+    before = lax.broadcasted_iota(jnp.int32, (rows, rows), 0)
+    after = lax.broadcasted_iota(jnp.int32, (rows, rows), 1)
+    upper = (before < after).astype(F32).astype(BF16)
+    ids = pos_ref[FIRST_ALL] + lax.broadcasted_iota(jnp.int32, (8, rows), 0)
+    for source, ref in enumerate(routes):
+        hits = jnp.logical_or(ref[0:1, :] == ids, ref[1:2, :] == ids)
+        earlier = nn(hits.astype(F32).astype(BF16), upper)
+        rank = jnp.where(hits, earlier, -1.0)
+        row_ref[source] = rank.astype(jnp.int32)
+        tall = jnp.concatenate([rank, jnp.full((120, rows), -1.0, F32)], 0)
+        col_ref[source] = jnp.transpose(tall).astype(jnp.int32)
+
+
+def ranks(pos, routes, after):
+    count, rows = len(routes), routes[0].shape[1]
+    out = [shape((count, 8, rows), jnp.int32), shape((count, rows, 128), jnp.int32)]
+    return run(
+        rank_kernel, routes, (1,), [like(a) for a in routes], [like(a) for a in out], out, "ranks",
+        scalars=(pos,), after=after,
+    )
+
+
+def touch(array, after):
+    count = len(after)
+
+    def body(*refs):
+        del refs
+
+    return pl.pallas_call(
+        body,
+        in_specs=[pl.BlockSpec(memory_space=pl.ANY)] * (1 + count),
+        out_specs=pl.BlockSpec(memory_space=pl.ANY),
+        out_shape=shape(array.shape, array.dtype),
+        input_output_aliases={0: 0},
+        name="touch",
+    )(array, *after)
+
+
+def gate_rows(hidden, routes, router_t, ids):
+    logits = nt(router_t, hidden)
+    every = lax.broadcasted_iota(jnp.int32, logits.shape, 0)
+    first, second = routes[0:1, :], routes[1:2, :]
+    zero = jnp.zeros_like(logits)
+    logit_one = jnp.sum(jnp.where(every == first, logits, zero), 0, keepdims=True)
+    logit_two = jnp.sum(jnp.where(every == second, logits, zero), 0, keepdims=True)
+    gate_one = sigmoid(logit_one - logit_two)
+    gate_two = sigmoid(logit_two - logit_one)
+    return jnp.where(ids == first, gate_one, 0.0) + jnp.where(ids == second, gate_two, 0.0)
+
+
+def ffn_phase_one(x, g, up_ref, down_ref, act_ref, pre_ref, step=256):
+    wide = act_ref.shape[1]
+    for at in range(0, wide, step):
+        cols = slice(at, at + step)
+        act, slope = gelu_and_slope(nn(x, up_ref[0, :, cols]))
+        back = nt(g, down_ref[0, cols, :])
+        act_ref[:, cols] = act.astype(BF16)
+        pre_ref[:, cols] = (back * slope).astype(BF16)
+
+
+def relative_rows(pos_ref, target, values, nz):
+    bits = nz.bit_length() - 1
+    part = values.shape[0] // (2 * nz)
+    for block in range(2 * nz):
+        place = (block % 2) ^ pos_ref[ROW_Y]
+        place = place * nz + flipped((block // 2) ^ pos_ref[ROW_Z], bits)
+        at = pl.multiple_of(place * part, part)
+        target[pl.ds(at, part), :] = values[block * part : (block + 1) * part]
+
+
+def sides(pos_ref, values):
+    half = values.shape[1] // 2
+    low, high = values[:, :half], values[:, half:]
+    own_low = pos_ref[ROW_Y] == 0
+    return jnp.where(own_low, low, high), jnp.where(own_low, high, low)
+
+
+def expert_kernel(
+    slot, sends, has_prior, pos_ref, h0_ref, h1_ref, g0_ref, g1_ref, rank_ref, routes0_ref, routes1_ref,
+    router_ref, up_ref, down_ref, *rest,
+):
+    count = 1 + sends
+    priors, rest = (rest[:count], rest[count:]) if has_prior else ((), rest)
+    targets, rest = rest[:count], rest[count:]
+    keep_ref = targets[0]
+    (out_ref, gx_ref, gg_ref,
+     x_s, xt_s, g_s, gt_s, b_s, gate_s, act_s, pre_s, out_acc, gx_acc) = rest
+    tile = pl.program_id(0)
+    last = pl.num_programs(0) - 1
+    rows = h0_ref.shape[0]
+    nz = keep_ref.shape[2] // keep_ref.shape[3] * 2
+    part = h0_ref.shape[1] // (2 * nz)
+    own = lax.broadcasted_iota(jnp.int32, (CAP, rows), 0)
+
+    def hot(source):
+        return (own == rank_ref[source, slot : slot + 1, :]).astype(F32)
+
+    @pl.when(tile == 0)
+    def _():
+        sources = ((h0_ref, g0_ref, routes0_ref), (h1_ref, g1_ref, routes1_ref))
+        for source, (h_ref, b_ref, routes_ref) in enumerate(sources):
+            span = slice(source * CAP, (source + 1) * CAP)
+            pick = hot(source)
+            pick_low = pick.astype(BF16)
+            expert = pos_ref[FIRST_ALL] + slot
+            gate = gate_rows(h_ref[...], routes_ref[...], router_ref[...], expert)
+            gate_col = jnp.sum(pick * gate[0:1], -1, keepdims=True)
+            branch = nn(pick_low, b_ref[...])
+            x_s[span, :] = nn(pick_low, h_ref[...]).astype(BF16)
+            b_s[span, :] = branch.astype(BF16)
+            g_s[span, :] = (branch * gate_col).astype(BF16)
+            gate_s[span, :] = jnp.broadcast_to(gate_col, (CAP, 128))
+        relative_rows(pos_ref, xt_s, jnp.transpose(x_s[...]), nz)
+        gt_s[...] = jnp.transpose(g_s[...])
+        out_acc[...] = jnp.zeros_like(out_acc)
+        gx_acc[...] = jnp.zeros_like(gx_acc)
+
+    ffn_phase_one(x_s[...], g_s[...], up_ref, down_ref, act_s, pre_s)
+    act, pre = act_s[...], pre_s[...]
+    out_acc[...] += nn(act, down_ref[0])
+    gx_acc[...] += nt(pre, up_ref[0])
+
+    def place(side, kind):
+        return (0, kind) if side == 0 else (1, kind) if sends == 1 else (1 + kind, 0)
+
+    dup = nn(xt_s[...], pre)
+    half = dup.shape[1] // 2
+    for side in range(2):
+        at, entry = place(side, 0)
+        for z in range(nz):
+            for lanes in range(2):
+                row, into = (side * nz + z) * part, (z * 2 + lanes) * part
+                piece = dup[row : row + part, lanes * half : (lanes + 1) * half]
+                if has_prior:
+                    piece = piece + priors[at][0, entry, into : into + part, :].astype(F32)
+                targets[at][0, entry, into : into + part, :] = piece.astype(BF16)
+    for side, piece in enumerate(sides(pos_ref, nn(gt_s[...], act))):
+        at, entry = place(side, 1)
+        if has_prior:
+            piece = piece + priors[at][0, entry].astype(F32)
+        targets[at][0, entry] = piece.astype(BF16)
+
+    @pl.when(tile == last)
+    def _():
+        for source in range(2):
+            span = slice(source * CAP, (source + 1) * CAP)
+            out = out_acc[span, :]
+            out_ref[source] = (out * gate_s[span, 0:1]).astype(BF16)
+            gx_ref[source] = gx_acc[span, :].astype(BF16)
+            inner = jnp.sum(out * b_s[span, :].astype(F32), -1, keepdims=True)
+            gg_ref[source] = jnp.sum(hot(source) * inner, 0, keepdims=True)
+
+
+def expert_call(
+    slot, sends, pos, hiddens, branches, rank_rows, routes, router_t, up, down, prior, nz, after
+):
+    rows, width = hiddens[0].shape
+    wide = up.shape[2]
+    tile = wide // nz
+    bits = nz.bit_length() - 1
+    count = 2 * CAP
+    weights = [
+        pl.BlockSpec((1, width, tile), lambda f, s: (s[FIRST_HERE] + slot, 0, f)),
+        pl.BlockSpec((1, tile, width), lambda f, s: (s[FIRST_HERE] + slot, f, 0)),
+    ]
+    kinds = [2, 2] if sends == 1 else [2, 1, 1]
+    grads = [
+        pl.BlockSpec((1, kind, width, tile // 2), lambda f, s: (flipped(f ^ s[ROW_Z], bits), 0, 0, 0))
+        for kind in kinds
+    ]
+    once = [*hiddens, *branches, rank_rows, *routes, router_t]
+    out_shape = (
+        [shape((nz, kind, width, tile // 2), BF16) for kind in kinds]
+        + [shape((2, CAP, width), BF16)] * 2
+        + [shape((2, 1, rows), F32)]
+    )
+    prior = () if prior is None else tuple(prior)
+    return run(
+        functools.partial(expert_kernel, slot, sends, bool(prior)), (*once, up, down, *prior), (nz,),
+        [like(a) for a in once] + weights + (grads if prior else []),
+        grads + [like(a) for a in out_shape[len(grads) :]], out_shape, "expert", scalars=(pos,), after=after,
+        scratch=[
+            pltpu.VMEM((count, width), BF16),
+            pltpu.VMEM((width, count), BF16),
+            pltpu.VMEM((count, width), BF16),
+            pltpu.VMEM((width, count), BF16),
+            pltpu.VMEM((count, width), BF16),
+            pltpu.VMEM((count, 128), F32),
+            pltpu.VMEM((count, tile), BF16),
+            pltpu.VMEM((count, tile), BF16),
+            pltpu.VMEM((count, width), F32),
+            pltpu.VMEM((count, width), F32),
+        ],
+    )
+
+
+def shared_kernel(
+    pos_ref, h_ref, b_ref, up_ref, down_ref, ku_ref, su_ref, kd_ref, sd_ref, out_ref, gx_ref,
+    xt_s, gt_s, act_s, pre_s,
+):
+    step = pl.program_id(0)
+    nz, block = 4, kd_ref.shape[3]
+
+    @pl.when(step == 0)
+    def _():
+        relative_rows(pos_ref, xt_s, jnp.transpose(h_ref[...]), nz)
+        turned = jnp.transpose(b_ref[...])
+        for slice_at in range(4):
+            place = ((slice_at % 2) ^ pos_ref[CORE]) * 2 + ((slice_at // 2) ^ pos_ref[STREAM])
+            at = pl.multiple_of(place * block, block)
+            gt_s[pl.ds(at, block), :] = turned[slice_at * block : (slice_at + 1) * block]
+        out_ref[...] = jnp.zeros_like(out_ref)
+        gx_ref[...] = jnp.zeros_like(gx_ref)
+
+    ffn_phase_one(h_ref[...], b_ref[...], up_ref, down_ref, act_s, pre_s)
+    act, pre = act_s[...], pre_s[...]
+    out_ref[...] += nn(act, down_ref[0])
+    gx_ref[...] += nt(pre, up_ref[0])
+    dup = nn(xt_s[...], pre).astype(BF16)
+
+    @pl.when(step < 2)
+    def _():
+        ku_ref[0] = dup
+
+    @pl.when(step >= 2)
+    def _():
+        su_ref[0] = dup
+
+    for y, piece in enumerate(sides(pos_ref, nn(gt_s[...], act))):
+        for place, ref in ((0, kd_ref), (1, kd_ref), (2, sd_ref), (3, sd_ref)):
+            ref[place % 2, y, 0] = piece[place * block : (place + 1) * block].astype(BF16)
+
+
+def shared_call(pos, hidden, branch, up, down, after):
+    rows, width = hidden.shape
+    wide = up.shape[1]
+    nz = 4
+    tile = wide // nz
+    block = width // 4
+
+    def unit(f, s):
+        return (f % 2 ^ s[STREAM]) * 2 + (f // 2 ^ s[CORE])
+
+    keep = pl.BlockSpec((1, width, tile), lambda f, s: (jnp.minimum(f, 1), 0, 0))
+    send = pl.BlockSpec((1, width, tile), lambda f, s: (jnp.maximum(f - 2, 0), 0, 0))
+    downs = pl.BlockSpec(
+        (2, 2, 1, block, tile // 2), lambda f, s: (0, 0, flipped(unit(f, s) ^ s[ROW_Z], 2), 0, 0)
+    )
+    return run(
+        shared_kernel, (hidden, branch, up[None], down[None]), (nz,),
+        [
+            like(hidden),
+            like(branch),
+            pl.BlockSpec((1, width, tile), lambda f, s: (0, 0, unit(f, s))),
+            pl.BlockSpec((1, tile, width), lambda f, s: (0, unit(f, s), 0)),
+        ],
+        [keep, send, downs, downs, like(hidden), like(hidden)],
+        [shape((2, width, tile), BF16)] * 2
+        + [shape((2, 2, nz, block, tile // 2), BF16)] * 2
+        + [shape((rows, width), F32)] * 2,
+        "shared", scalars=(pos,), after=after,
+        scratch=[
+            pltpu.VMEM((width, rows), BF16),
+            pltpu.VMEM((width, rows), BF16),
+            pltpu.VMEM((rows, tile), BF16),
+            pltpu.VMEM((rows, tile), BF16),
+        ],
+    )
+
+
+def combine_kernel(slots, col_ref, *refs):
+    rows_refs, refs = refs[: 2 * slots], refs[2 * slots :]
+    targets, stacks = refs[:4], refs[4:]
+
+    @pl.when(pl.program_id(0) == 0)
+    def _():
+        for slot in range(slots):
+            for kind in range(2):
+                for source in range(2):
+                    stacks[kind][source, slot * CAP : (slot + 1) * CAP, :] = rows_refs[2 * slot + kind][source]
+
+    block = col_ref.shape[1]
+    own = lax.broadcasted_iota(jnp.int32, (block, slots * CAP), 1)
+    for source in range(2):
+        hits = None
+        for slot in range(slots):
+            rank = col_ref[source, :, slot : slot + 1]
+            place = jnp.where(rank < 0, -1, rank + slot * CAP)
+            hit = place == own
+            hits = hit if hits is None else jnp.logical_or(hits, hit)
+        pick = hits.astype(F32).astype(BF16)
+        for kind in range(2):
+            targets[2 * kind + source][...] = nn(pick, stacks[kind][source]).astype(BF16)
+
+
+def combine(rank_cols, pairs, after):
+    count, rows, _ = rank_cols.shape
+    width = pairs[0][0].shape[2]
+    block = rows // 4
+    flat = [a for pair in pairs for a in pair]
+    return run(
+        functools.partial(combine_kernel, len(pairs)), (rank_cols, *flat), (rows // block,),
+        [pl.BlockSpec((count, block, 128), lambda i: (0, i, 0))] + [like(a) for a in flat],
+        [rows_spec(block, width)] * 4, [shape((rows, width), BF16)] * 4, "combine",
+        scratch=[pltpu.VMEM((2, len(pairs) * CAP, width), BF16)] * 2, after=after,
+    )
+
+
+def add_kernel(*refs):
+    count = len(refs) // 3
+    for left, right, out in zip(refs[:count], refs[count : 2 * count], refs[2 * count :]):
+        out[...] = (left[...].astype(F32) + right[...].astype(F32)).astype(out.dtype)
+
+
+def add_rows(lefts, rights, after=()):
+    rows, width = lefts[0].shape
+    count = len(lefts)
+    tile = rows_spec(rows // 4, width)
+    return run(
+        add_kernel, (*lefts, *rights), (4,), [tile] * (2 * count), [tile] * count,
+        [shape((rows, width), BF16)] * count, "add_rows", after=after,
+    )
+
+
+def total_of(keep, arrived):
+    return keep.astype(F32) + arrived.astype(F32)
+
+
+def halve_kinds_kernel(kinds, *refs):
+    keep_ref, send_ref = refs[-2:]
+    refs = iter(refs[:-2])
+    for at, kind in enumerate(kinds):
+        if kind == 0:
+            total = total_of(next(refs)[0, 0], next(refs)[0, 0])
+            half = total.shape[0] // 2
+            keep_ref[at, 0], send_ref[at, 0] = total[:half], total[half:].astype(BF16)
+        else:
+            keep_ref[at, 0] = total_of(next(refs)[0, 0], next(refs)[0, 0])
+            send_ref[at, 0] = total_of(next(refs)[0, 0], next(refs)[0, 0]).astype(BF16)
+
+
+def halve_y(keep, arrived, kinds, after):
+    nz, _, rows, cols = keep.shape
+    split = lambda a: a.reshape(nz, -1, rows // 2, cols)
+    args, specs = [], []
+    for at, kind in enumerate(kinds):
+        for add in (0, nz // 2) if kind else (0,):
+            for array, entry in ((keep, kind), (arrived, at)):
+                if kind == 0:
+                    args.append(array)
+                    index = functools.partial(lambda entry, t: (t, entry, 0, 0), entry)
+                    specs.append(pl.BlockSpec((1, 1, rows, cols), index))
+                else:
+                    args.append(split(array))
+                    index = functools.partial(
+                        lambda entry, add, t: (t // 2 + add, 2 * entry + t % 2, 0, 0), entry, add
+                    )
+                    specs.append(pl.BlockSpec((1, 1, rows // 2, cols), index))
+    out = pl.BlockSpec((len(kinds), 1, rows // 2, cols), lambda t: (0, t, 0, 0))
+    dims = (len(kinds), nz, rows // 2, cols)
+    return run(
+        functools.partial(halve_kinds_kernel, kinds), args, (nz,), specs, [out, out],
+        [shape(dims, F32), shape(dims, BF16)], "halve_y", after=after,
+    )
+
+
+def halve_z(keep, arrived, kinds, after):
+    _, nz, rows, cols = keep.shape
+    split = lambda a: a.reshape(len(kinds), 2 * nz, rows // 2, cols)
+    args, specs = [], []
+    for at, kind in enumerate(kinds):
+        for add in (0, nz) if kind else (0,):
+            for array, flip in ((keep, 0), (arrived, nz // 2)):
+                if kind == 0:
+                    args.append(array)
+                    index = functools.partial(lambda at, flip, t: (at, t ^ flip, 0, 0), at, flip)
+                    specs.append(pl.BlockSpec((1, 1, rows, cols), index))
+                else:
+                    args.append(split(array))
+                    index = functools.partial(lambda at, add, t: (at, t + add, 0, 0), at, add)
+                    specs.append(pl.BlockSpec((1, 1, rows // 2, cols), index))
+    out = pl.BlockSpec((len(kinds), 1, rows // 2, cols), lambda t: (0, t, 0, 0))
+    dims = (len(kinds), nz, rows // 2, cols)
+    return run(
+        functools.partial(halve_kinds_kernel, kinds), args, (nz,), specs, [out, out],
+        [shape(dims, F32), shape(dims, BF16)], "halve_z", after=after,
+    )
+
+
+def core_halves(pos_ref, values):
+    half = values.shape[0] // 2
+    low, high = values[:half], values[half:]
+    own_low = pos_ref[CORE] == 0
+    return jnp.where(own_low, low, high), jnp.where(own_low, high, low).astype(BF16)
+
+
+def finish_kinds_kernel(kinds, pos_ref, *refs):
+    inputs, outs = refs[: 2 * len(kinds)], refs[2 * len(kinds) :]
+    for at, kind in enumerate(kinds):
+        keep_ref, arrived_ref = inputs[2 * at : 2 * at + 2]
+        mine, sent = outs[2 * at : 2 * at + 2]
+        if kind == 0:
+            up = total_of(keep_ref[0, 0], arrived_ref[0, 0])
+            half = up.shape[0] // 2
+            mine[...], sent[...] = core_halves(pos_ref, jnp.concatenate([up[:half], up[half:]], 1))
+        else:
+
+            @pl.when(pl.program_id(0) == 0)
+            def _():
+                down = total_of(keep_ref[0], arrived_ref[0])
+                down = down.reshape(down.shape[0] * down.shape[1], down.shape[2])
+                mine[...], sent[...] = core_halves(pos_ref, jnp.transpose(down))
+
+
+def finish_kinds(pos, keep, arrived, kinds, after):
+    _, nz, rows, cols = keep.shape
+    bits = nz.bit_length() - 1
+    args, specs, out_specs, outs = [], [], [], []
+    for at, kind in enumerate(kinds):
+        args += [keep, arrived]
+        if kind == 0:
+            for flip in (0, 1):
+                index = functools.partial(lambda at, flip, t, s: (at, t ^ flip, 0, 0), at, flip)
+                specs.append(pl.BlockSpec((1, 1, rows, cols), index))
+            dims = (rows // 4, 2 * cols * nz)
+            out = pl.BlockSpec((rows // 4, 2 * cols), lambda t, s: (0, flipped(t, bits) ^ s[ROW_Z]))
+        else:
+            index = functools.partial(lambda at, t, s: (at, 0, 0, 0), at)
+            specs += [pl.BlockSpec((1, nz, rows, cols), index)] * 2
+            dims = (cols // 2, nz * rows)
+            out = full(dims)
+        out_specs += [out, out]
+        outs += [shape(dims, F32), shape(dims, BF16)]
+    return run(
+        functools.partial(finish_kinds_kernel, kinds), args, (nz,), specs, out_specs, outs, "finish_kinds",
+        scalars=(pos,), after=after,
+    )
+
+
+def halve_slices_kernel(ku_ref, au_ref, kd_ref, ad_ref, keep_ref, send_ref):
+    for at, ref in enumerate((keep_ref, send_ref)):
+        up = total_of(ku_ref[at], au_ref[at])
+        half = up.shape[1] // 2
+        for side in range(2):
+            ref[0, side * up.shape[0] : (side + 1) * up.shape[0], :] = up[:, side * half : (side + 1) * half].astype(ref.dtype)
+        ref[1] = total_of(kd_ref[at], ad_ref[at]).astype(ref.dtype)
+
+
+def halve_slices(up_keep, up_arrived, down_keep, down_arrived, after):
+    _, rows, cols = up_keep.shape
+    steps = 8
+    ups = pl.BlockSpec((2, rows // steps, cols), lambda i: (0, i, 0))
+    downs = pl.BlockSpec((2, 2 * rows // steps, cols // 2), lambda i: (0, i, 0))
+    dims = (2, 2 * rows, cols // 2)
+    return run(
+        halve_slices_kernel, (up_keep, up_arrived, down_keep, down_arrived), (steps,), [ups, ups, downs, downs],
+        [downs, downs], [shape(dims, F32), shape(dims, BF16)], "halve_slices", after=after,
+    )
+
+
+def halve_kernel(keep_ref, arrived_ref, keep_out, send_out):
+    keep_out[...] = total_of(keep_ref[:, 0], arrived_ref[:, 0])
+    send_out[...] = total_of(keep_ref[:, 1], arrived_ref[:, 1]).astype(BF16)
+
+
+def halve(keep, arrived, after, steps=2):
+    kinds, rows, cols = keep.shape
+    split = lambda a: a.reshape(kinds, 2, rows // 2, cols)
+    into = pl.BlockSpec((kinds, 2, rows // 2 // steps, cols), lambda i: (0, 0, i, 0))
+    out = pl.BlockSpec((kinds, rows // 2 // steps, cols), lambda i: (0, i, 0))
+    dims = (kinds, rows // 2, cols)
+    return run(
+        halve_kernel, (split(keep), split(arrived)), (steps,), [into, into], [out, out],
+        [shape(dims, F32), shape(dims, BF16)], "halve", after=after,
+    )
+
+
+def halve_parts_kernel(keep_ref, first_ref, second_ref, keep_out, send_out):
+    keep_out[0] = total_of(keep_ref[0], first_ref[...])
+    send_out[0] = total_of(keep_ref[1], second_ref[...]).astype(BF16)
+
+
+def halve_parts(keep, arrived, after, steps=2):
+    _, rows, cols = keep.shape
+    into = pl.BlockSpec((2, rows // steps, cols), lambda i: (0, i, 0))
+    out = pl.BlockSpec((1, rows // steps, cols), lambda i: (0, i, 0))
+    return run(
+        halve_parts_kernel, (keep, *arrived), (steps,), [into] + [rows_spec(rows // steps, cols)] * 2,
+        [out, out], [shape((1, rows, cols), F32), shape((1, rows, cols), BF16)], "halve_parts", after=after,
+    )
+
+
+def finish_slices_kernel(merged, pos_ref, keep_ref, arrived_ref, *outs):
+    total = total_of(keep_ref[...], arrived_ref[...])
+    up = total[0]
+    if merged:
+        half = up.shape[0] // 2
+        up = jnp.concatenate([up[:half], up[half:]], 1)
+        outs[2][...], outs[3][...] = core_halves(pos_ref, jnp.transpose(total[1]))
+    outs[0][...], outs[1][...] = core_halves(pos_ref, up)
+
+
+def finish_slices(pos, keep, arrived, merged, after):
+    _, rows, cols = keep.shape
+    dims = [(rows // 4, 2 * cols), (cols // 2, rows)] if merged else [(rows // 2, cols)]
+    outs = [shape(d, t) for d in dims for t in (F32, BF16)]
+    return run(
+        functools.partial(finish_slices_kernel, merged), (keep, arrived), (1,), [like(keep), like(arrived)],
+        [like(a) for a in outs], outs, "finish_slices", scalars=(pos,), after=after,
+    )
+
+
+def middle_back_kernel(
+    gs_ref, ga_ref, gb_ref, gc_ref, gg_ref, routes_ref, router_ref,
+    hidden_ref, cot_ref, branch_ref, x_ref, mod_ref, w_ref,
+    gm_ref, gatt_ref, back_ref, mods_ref, drouter_ref,
+):
+    block = pl.program_id(0)
+    hidden = hidden_ref[...]
+    grad_gates = gg_ref[...]
+    ids = lax.broadcasted_iota(jnp.int32, grad_gates.shape, 0)
+    gates = gate_rows(hidden, routes_ref[...], router_ref[...], ids)
+    inner = jnp.sum(gates * grad_gates, 0, keepdims=True)
+    grad_logits = gates * (grad_gates - inner)
+    grad = gs_ref[...] + ga_ref[...].astype(F32) + gb_ref[...].astype(F32) + gc_ref[...].astype(F32)
+    drouter = 0.0
+    for piece in three_parts(grad_logits):
+        grad = grad + tn(piece, router_ref[...])
+        drouter = drouter + nn(piece, hidden)
+    branch = branch_ref[...]
+    gate_one = mod_ref[2, pl.ds(block, 1), :]
+    middle = x_ref[...].astype(F32) + gate_one * branch
+    normed, spread = norm_parts(middle)
+    scale = mod_ref[4, pl.ds(block, 1), :]
+    mods_ref[1, pl.ds(block, 1), :] = jnp.sum(grad, 0, keepdims=True)
+    mods_ref[2, pl.ds(block, 1), :] = jnp.sum(grad * normed, 0, keepdims=True)
+    grad_middle = cot_ref[...].astype(F32) + norm_back(grad * (1.0 + scale), normed, spread)
+    mods_ref[0, pl.ds(block, 1), :] = jnp.sum(grad_middle * branch, 0, keepdims=True)
+    gm_ref[...] = grad_middle
+    grad_branch = (grad_middle * gate_one).astype(BF16)
+    back_ref[...] = grad_branch
+    gatt_ref[...] = nt(grad_branch, w_ref[...]).astype(BF16)
+
+    @pl.when(block == 0)
+    def _():
+        drouter_ref[...] = drouter
+
+    @pl.when(block > 0)
+    def _():
+        drouter_ref[...] += drouter
+
+
+def middle_backward(parts, gg, routes_t, router_t, hidden, cot, branch, patches, mod, out_weight, blocks, after):
+    rows, width = patches.shape
+    short = rows // blocks
+    tile = rows_spec(short, width)
+    cols = lambda a: pl.BlockSpec((a.shape[0], short), lambda i: (0, i))
+    out_shape = [
+        shape((rows, width), F32),
+        shape((rows, width), BF16),
+        shape((rows, width), BF16),
+        shape((3, 8, width), F32),
+        shape((router_t.shape[0], width), F32),
+    ]
+    return run(
+        middle_back_kernel,
+        (*parts, gg, routes_t, router_t, hidden, cot, branch, patches, mod, out_weight), (blocks,),
+        [tile] * 4 + [cols(gg), cols(routes_t), like(router_t)] + [tile] * 4 + [like(mod), like(out_weight)],
+        [tile] * 3 + [like(a) for a in out_shape[3:]], out_shape, "middle_back", after=after,
+    )
+
+
+def mixed_kernel(so_ref, ra_ref, rb_ref, rc_ref, cot_ref, branch_ref, x_ref, mod_ref, mixed_ref, gate_ref):
+    block = pl.program_id(0)
+    second = so_ref[...] + ra_ref[...].astype(F32) + rb_ref[...].astype(F32) + rc_ref[...].astype(F32)
+    middle = x_ref[...].astype(F32) + mod_ref[2, pl.ds(block, 1), :] * branch_ref[...]
+    mixed_ref[...] = (middle + mod_ref[5, pl.ds(block, 1), :] * second).astype(BF16)
+    gate_ref[pl.ds(block, 1), :] = jnp.sum(cot_ref[...].astype(F32) * second, 0, keepdims=True)
+
+
+def mixed_forward(parts, cot, branch, patches, mod, blocks, after):
+    rows, width = patches.shape
+    tile = rows_spec(rows // blocks, width)
+    return run(
+        mixed_kernel, (*parts, cot, branch, patches, mod), (blocks,), [tile] * 7 + [like(mod)],
+        [tile, full((8, width))], [shape((rows, width), BF16), shape((8, width), F32)], "mixed", after=after,
+    )
+
+
+def weight_kernel(
+    pos_ref, x_ref, mod_ref, dq_ref, dk_ref, dv_ref, att_ref, back_ref, keep_ref, first_ref, second_ref, turned
+):
+    rows = x_ref.shape[0]
+    short = rows // 4
+    step = pl.program_id(0)
+    matrix = ((step % 2) ^ pos_ref[STREAM]) * 2 + ((step // 2) ^ pos_ref[CORE])
+    nz = 4
+
+    @pl.when(step == 0)
+    def _():
+        for block in range(4):
+            span = slice(block * short, (block + 1) * short)
+            normed, _ = norm_parts(x_ref[span, :].astype(F32))
+            hidden = normed * (1.0 + mod_ref[1, block : block + 1, :]) + mod_ref[0, block : block + 1, :]
+            relative_rows(pos_ref, turned.at[0, :, span], jnp.transpose(hidden.astype(BF16)), nz)
+        relative_rows(pos_ref, turned.at[1], jnp.transpose(att_ref[...]), nz)
+
+    for index, (left, ref) in enumerate(((0, dq_ref), (0, dk_ref), (0, dv_ref), (1, back_ref))):
+
+        @pl.when(matrix == index)
+        def _():
+            total = nn(turned[left], ref[...]).astype(BF16)
+
+            @pl.when(step < 2)
+            def _():
+                keep_ref[0] = total
+
+            @pl.when(step == 2)
+            def _():
+                first_ref[...] = total
+
+            @pl.when(step == 3)
+            def _():
+                second_ref[...] = total
+
+
+def weight_grads(pos, patches, mod, grads, attended, back, after):
+    rows, width = patches.shape
+    args = (patches, mod, *grads, attended, back)
+    keep = pl.BlockSpec((1, width, width), lambda f, s: (jnp.minimum(f, 1), 0, 0))
+    send = full((width, width))
+    outs = run(
+        weight_kernel, args, (4,), [like(a) for a in args], [keep, send, send],
+        [shape((2, width, width), BF16)] + [shape((width, width), BF16)] * 2, "weight_grads", scalars=(pos,),
+        scratch=[pltpu.VMEM((2, width, rows), BF16)], after=after,
+    )
+    return outs[0], outs[1:]
+
+
+def inputs_back_kernel(dq_ref, dk_ref, dv_ref, w_ref, x_ref, gm_ref, mod_ref, gp_ref, mods_ref):
+    block = pl.program_id(0)
+    width = x_ref.shape[1]
+    grad = nt(dq_ref[...], w_ref[:, :width])
+    grad = grad + nt(dk_ref[...], w_ref[:, width : 2 * width])
+    grad = grad + nt(dv_ref[...], w_ref[:, 2 * width :])
+    normed, spread = norm_parts(x_ref[...].astype(F32))
+    mods_ref[0, pl.ds(block, 1), :] = jnp.sum(grad, 0, keepdims=True)
+    mods_ref[1, pl.ds(block, 1), :] = jnp.sum(grad * normed, 0, keepdims=True)
+    scale = mod_ref[1, pl.ds(block, 1), :]
+    gp_ref[...] = gm_ref[...] + norm_back(grad * (1.0 + scale), normed, spread)
+
+
+def inputs_backward(grads, weight, patches, grad_middle, mod, blocks, after):
+    rows, width = patches.shape
+    tile = rows_spec(rows // blocks, width)
+    return run(
+        inputs_back_kernel, (*grads, weight, patches, grad_middle, mod), (blocks,),
+        [tile] * 3 + [like(weight), tile, tile, like(mod)], [tile, full((2, 8, width))],
+        [shape((rows, width), F32), shape((2, 8, width), F32)], "inputs_back", after=after,
+    )
+
+
+def used_kernel(block_count, pos_ref, gm_ref, ada_ref, emb_ref, out_ref):
+    piece = pl.program_id(0)
+
+    @pl.when(piece == 0)
+    def _():
+        out_ref[...] = jnp.zeros_like(out_ref)
+
+    for part in three_parts(gm_ref[0]):
+        out_ref[...] += nt(part, ada_ref[...])
+
+    @pl.when(piece == pl.num_programs(0) - 1)
+    def _():
+        emb = emb_ref[...]
+        is_long = pos_ref[LONG] > 0
+        used = jnp.where(is_long, jnp.broadcast_to(emb[0:1], emb.shape), emb)
+        gate = sigmoid(used)
+        grad = out_ref[...] * (gate * (1.0 + used * (1.0 - gate)))
+        row = lax.broadcasted_iota(jnp.int32, grad.shape, 0)
+        grad = jnp.where(row < block_count, grad, 0.0)
+        total = jnp.sum(grad, 0, keepdims=True)
+        out_ref[...] = jnp.where(is_long, jnp.where(row == 0, total, 0.0), grad)
+
+
+def used_backward(pos, grad_mod, ada_weight, emb_pad, block_count, after):
+    rows, width = emb_pad.shape
+    pieces = grad_mod.shape[0]
+    return run(
+        functools.partial(used_kernel, block_count), (grad_mod, ada_weight, emb_pad), (pieces,),
+        [
+            pl.BlockSpec((1, rows, width), lambda i, *_: (i, 0, 0)),
+            pl.BlockSpec((width, width), lambda i, *_: (0, i)),
+            like(emb_pad),
+        ],
+        like(emb_pad), shape((rows, width), F32), "used_back", scalars=(pos,), after=after,
+    )
+
+
+def swap(values, axis, bit):
+    size = lax.axis_size(axis)
+    return lax.ppermute(values, axis, [(i, i ^ bit) for i in range(size)])
+
+
+def swap_all(arrays, axis, bit):
+    return [swap(a, axis, bit) for a in arrays]
+
+
+def in_order(own, mine, arrived, axis):
+    return jnp.concatenate(
+        [jnp.where(own == 0, mine, arrived), jnp.where(own == 0, arrived, mine)], axis
+    )
+
+
+def local_pair(
+    patches, embedding, long_image, routes, cotangent, ada_weight, qkv_weight, out_weight, shared_up,
+    shared_down, router_weight, expert_up, expert_down,
+):
+    rows, width = patches.shape
+    blocks = embedding.shape[0]
+    short = rows // blocks
+    dp_size = lax.axis_size("dp")
+    nz = dp_size // 4
+    dp, stream = lax.axis_index("dp"), lax.axis_index("stream")
+    core, row_y, row_z = dp % 2, (dp // 2) % 2, dp // 4
+    local_experts = expert_up.shape[0]
+    here = local_experts // 2
+    first_here = core * here
+    first_all = stream * local_experts + first_here
+    places = [long_image[0], core, stream, row_y, row_z, first_here, first_all, 0]
+    pos = jnp.stack([jnp.asarray(a, jnp.int32) for a in places])
+
+    routes_t = routes.T
+    routes_x = swap(routes_t, "stream", 1)
+    routes_near = (routes_t, swap(routes_t, "dp", 1))
+    routes_far = (routes_x, swap(routes_x, "dp", 1))
+    emb_pad = jnp.pad(embedding, ((0, 8 - blocks), (0, 0)))
+    router_t = jnp.pad(router_weight.T, ((0, 16 - router_weight.shape[1]), (0, 0)))
+    mod, act, branch_grad = modulate(pos, emb_pad, ada_weight, cotangent, blocks)
+    rank_near, cols_near = ranks(pos, routes_near, (mod,))
+    rank_far, cols_far = ranks(pos, routes_far, (rank_near,))
+    branch_grad = touch(branch_grad, (rank_far,))
+    branch_x = swap(branch_grad, "stream", 1)
+    branches_near = (branch_grad, swap(branch_grad, "dp", 1))
+    branches_far = (branch_x, swap(branch_x, "dp", 1))
+
+    packed = qkv_forward(patches, mod, qkv_weight, blocks, (branch_grad,))
+    attended, logsum = attend_forward(pos, packed, short)
+    branch_one, hidden = middle_forward(
+        attended, patches, mod, out_weight, blocks, (branch_x, branches_near[1])
+    )
+    hidden_x = swap(hidden, "stream", 1)
+    hiddens_near = (hidden, swap(hidden, "dp", 1))
+
+    def expert(slot, is_far, sends, prior, after):
+        group = (
+            (hiddens_far, branches_far, rank_far, routes_far)
+            if is_far
+            else (hiddens_near, branches_near, rank_near, routes_near)
+        )
+        out = expert_call(slot, sends, pos, *group, router_t, expert_up, expert_down, prior, nz, after)
+        return out[: 1 + sends], out[1 + sends :]
+
+    first, first_near = expert(0, False, 1, None, (branches_far[1],))
+    hidden_x = touch(hidden_x, (first_near[2],))
+    hiddens_far = (hidden_x, swap(hidden_x, "dp", 1))
+    first, first_far = expert(0, True, 1, first, ())
+    first_arrived = swap(first[1], "dp", 2)
+    second, second_near = expert(1, False, 2, None, (first_far[2],))
+    second, second_far = expert(1, True, 2, second, ())
+    up_half_arrived = swap(second[1], "dp", 2)
+    out_x, out_xc, gx_x, gx_xc = combine(cols_far, [r[:2] for r in (first_far, second_far)], ())
+    gx_xc, out_xc = swap(gx_xc, "dp", 1), swap(out_xc, "dp", 1)
+    out_near, out_core, gx_near, gx_core = combine(
+        cols_near, [r[:2] for r in (first_near, second_near)], (gx_x,)
+    )
+    gx_core = swap(gx_core, "dp", 1)
+    out_core = swap(out_core, "dp", 1)
+    (gx_sum,) = add_rows([gx_x], [gx_xc], (out_near,))
+    gx_back = swap(gx_sum, "stream", 1)
+    (out_sum,) = add_rows([out_x], [out_xc], (gx_sum,))
+    out_back = swap(out_sum, "stream", 1)
+    near, far = (first_near, second_near), (first_far, second_far)
+    gg_near = [jnp.concatenate([r[2][source] for r in near], 0) for source in range(2)]
+    gg_far = [jnp.concatenate([r[2][source] for r in far], 0) for source in range(2)]
+    gg_back = swap(jnp.concatenate([gg_far[0], swap(gg_far[1], "dp", 1)], 0), "stream", 1)
+    gg_rel = jnp.concatenate([gg_near[0], swap(gg_near[1], "dp", 1), gg_back], 0)
+    order = jnp.arange(4, dtype=jnp.int32) ^ (stream * 2 + core)
+    gg = gg_rel.reshape(4, here, rows)[order].reshape(EXPERTS, rows)
+    gg = jnp.pad(gg, ((0, 16 - EXPERTS), (0, 0)))
+
+    up_keep, up_send, down_keep, down_send, shared_out, shared_gx = shared_call(
+        pos, hidden, branch_grad, shared_up, shared_down, (out_sum, gx_core, out_core, gg)
+    )
+    up_arrived, down_arrived = swap(up_send, "dp", 1), swap(down_send, "dp", 1)
+
+    grad_middle, grad_attended, back, mods_two, drouter = middle_backward(
+        (shared_gx, gx_near, gx_core, gx_back), gg, routes_t, router_t, hidden, cotangent, branch_one,
+        patches, mod, out_weight, blocks, (),
+    )
+    both, up, down = (0, 1), (0,), (1,)
+    flat = lambda a: a.reshape(a.shape[0], -1, a.shape[-1])
+    ea_keep, ea_send = halve_y(first[0], first_arrived, both, (grad_attended,))
+    ea_arrived = swap(ea_send, "dp", 4)
+    down_half = touch(second[2], (up_half_arrived, ea_send))
+    down_half_arrived = swap(down_half, "dp", 2)
+    sh_keep, sh_send = halve_slices(up_keep, up_arrived, flat(down_keep), flat(down_arrived), (down_half,))
+    sh_arrived = swap(sh_send, "stream", 1)
+    bu_keep, bu_send = halve_y(second[0], up_half_arrived, up, (sh_send,))
+    bu_arrived = swap(bu_send, "dp", 4)
+    grads = attend_backward(pos, packed, attended, logsum, grad_attended, short, (bu_send,))
+    mixed, gate_two = mixed_forward(
+        (shared_out, out_near, out_core, out_back), cotangent, branch_one, patches, mod, blocks, (grads[0],)
+    )
+    qk_keep, qk_send = weight_grads(pos, patches, mod, grads, attended, back, (gate_two,))
+    qk_arrived = [swap(a, "dp", 1) for a in qk_send]
+    ea_keep, ea_send = halve_z(ea_keep, ea_arrived, both, (qk_send[0],))
+    ea_arrived = swap(ea_send, "dp", 8)
+    bu_keep, bu_send = halve_z(bu_keep, bu_arrived, up, (ea_send,))
+    bu_arrived = swap(bu_send, "dp", 8)
+    bd_keep, bd_send = halve_y(second[0], down_half_arrived, down, (bu_send,))
+    bd_arrived = swap(bd_send, "dp", 4)
+    sh_keep, sh_send = halve(sh_keep, sh_arrived, (bd_send,))
+    sh_arrived = swap(sh_send, "dp", 2)
+    qk_keep, qk_send = halve_parts(qk_keep, qk_arrived, (sh_send,))
+    qk_arrived = swap(qk_send, "stream", 1)
+    grad_patches, mods_one = inputs_backward(grads, qkv_weight, patches, grad_middle, mod, blocks, (qk_send,))
+    factors = [act, *mods_one, *mods_two, gate_two]
+    factors = jnp.concatenate([a[:blocks] for a in factors] + [drouter[:EXPERTS].reshape(blocks, -1)], 1)
+    factors = lax.all_gather(factors.astype(BF16), ("dp", "stream"), axis=0, tiled=True)
+    grad_mod = jnp.concatenate([mods_one, mods_two, gate_two[None]], 0)
+    grad_embedding = used_backward(pos, grad_mod, ada_weight, emb_pad, blocks, (mods_one,))
+
+    bd_keep, bd_send = halve_z(bd_keep, bd_arrived, down, (grad_embedding,))
+    bd_arrived = swap(bd_send, "dp", 8)
+    sh_keep, sh_send = halve(sh_keep, sh_arrived, (bd_send,))
+    sh_arrived = swap(sh_send, "dp", 4)
+    qk_keep, qk_send = halve(qk_keep, qk_arrived, (sh_send,))
+    qk_arrived = swap(qk_send, "dp", 2)
+    ea_done = finish_kinds(pos, ea_keep, ea_arrived, both, (qk_send,))
+    ea_others = [swap(ea_done[1], "dp", 1), swap(ea_done[3], "dp", 1)]
+    sh_keep, sh_send = halve(sh_keep, sh_arrived, (ea_done[1],))
+    sh_arrived = swap(sh_send, "dp", 8)
+    qk_keep, qk_send = halve(qk_keep, qk_arrived, (sh_send,))
+    qk_arrived = swap(qk_send, "dp", 4)
+    bu_done = finish_kinds(pos, bu_keep, bu_arrived, up, (qk_send,))
+    bu_others = swap(bu_done[1], "dp", 1)
+    qk_keep, qk_send = halve(qk_keep, qk_arrived, (bu_done[1],))
+    qk_arrived = swap(qk_send, "dp", 8)
+    sh_done = finish_slices(pos, sh_keep, sh_arrived, True, (qk_send,))
+    bd_done = finish_kinds(pos, bd_keep, bd_arrived, down, (sh_done[1],))
+    bd_others = swap(bd_done[1], "dp", 1)
+    qk_done = finish_slices(pos, qk_keep, qk_arrived, False, (bd_done[1],))
+
+    share = width // dp_size
+    factors = touch(factors, (sh_done[1],))
+    acts = lax.dynamic_slice_in_dim(factors[:, :width], dp * share, share, 1)
+    wide = 7 * width
+    grad_ada = lax.dot_general(acts, factors[:, width:wide], (((0,), (0,)), ((), ())), preferred_element_type=F32)
+    drouter_sum = jnp.sum(factors[:, wide:].astype(F32).reshape(-1, blocks, 2 * width), 0)
+    drouter_sum = drouter_sum.reshape(EXPERTS, width)
+    grad_router = lax.dynamic_slice_in_dim(drouter_sum, dp * share, share, 1).T
+
+    def experts_out(one, two, one_other, two_other):
+        mine, others = jnp.stack([one, two]), jnp.stack([one_other, two_other]).astype(F32)
+        return in_order(core, mine, others, 0)
+
+    def slices_out(keep, send):
+        chip = in_order(core, keep.astype(BF16), swap(send, "dp", 1), 1)
+        return in_order(stream, chip, swap(chip, "stream", 1), 1).astype(F32)
+
+    grad_qkv_out = slices_out(*qk_done)
+    return (
+        mixed, grad_patches, grad_embedding[:blocks], grad_ada, grad_qkv_out[:, : 3 * width],
+        grad_qkv_out[:, 3 * width :], slices_out(*sh_done[:2]), slices_out(*sh_done[2:]), grad_router,
+        experts_out(ea_done[0], bu_done[0], ea_others[0], bu_others),
+        experts_out(ea_done[2], bd_done[0], ea_others[1], bd_others),
+    )
+
+
+def local(*arrays):
+    experts, width, wide = arrays[11].shape
+    pair = lax.axis_size("stream") == 2 and experts == 4 and lax.axis_size("dp") == 16
+    if pair and wide == 4 * width:
+        return local_pair(*arrays)
+    return local_general(*arrays)
 
 
 def solution(mesh):

time: 1570 us -> 620 us (0.39)
  waiting for transfers between devices: 838 us -> 108 us
  Pallas kernels: 0 us -> 386 us
  matrix products: 345 us -> 1.33 us
  local copies, waits for them, and re-layouts: 194 us -> 39.7 us
  other arithmetic: 108 us -> 11.8 us
  starting transfers between devices: 23.1 us -> 47.3 us
  loops' own time: 22.3 us -> 0 us
    reduce_scatter x7 -> x0, waiting for transfers between devices: 792 us -> none  [the longest x1 195 us: local(): lax.psum_scatter(grad_expert_down.astype(jnp.bfloat16), 'dp', scatter_dim...]
    pallas_call x0 -> x44, Pallas kernels: none -> 386 us  [the longest x40 386 us: run(): pl.pallas_call(body, grid_spec=pltpu.PrefetchScalarGridSpec(num_scalar_pr...]
    dot_general x31 -> x1, matrix products: 345 us -> 1.33 us  [local_pair(): lax.dot_general(acts, factors[:, width:wide], (((0,), (0,)), ((), ())), p...]
    ppermute x0 -> x49, waiting for transfers between devices: none -> 97.4 us  [swap(): return lax.ppermute(values, axis, [(i, i ^ bit) for i in range(size)])]
    ppermute x0 -> x49, starting transfers between devices: none -> 47.3 us  [swap(): return lax.ppermute(values, axis, [(i, i ^ bit) for i in range(size)])]
    reduce_sum x12 -> x1, other arithmetic: 42 us -> 0.13 us  [local_pair(): jnp.sum(factors[:, wide:].astype(F32).reshape(-1, blocks, 2 * width), 0)]
    psum x1 -> x0, waiting for transfers between devices: 36.1 us -> none  [local(): lax.psum(shares[0].astype(jnp.bfloat16), 'stream').astype(jnp.float32)]
    reshape x7 -> x5, local copies, waits for them, and re-layouts: 30.9 us -> 1.01 us  [the longest x1 0.72 us: local_pair(): drouter[:EXPERTS].reshape(blocks, -1)]
  transfers between devices with their start and end apart: 13 -> 50, of which waited for: 8 -> 12; matrix products, arithmetic and copies ran while one was open for 22% -> 4% of each run, Pallas kernels for 0% -> 56%
where the time goes in v2:
time: 620 us; the launch traced here: 610 us
  Pallas kernels  386 us (62%)
  waiting for transfers between devices  108 us (17%)
  starting transfers between devices  47.3 us (8%)
  local copies, waits for them, and re-layouts  39.7 us (6%)
  between operations  15.6 us (3%)
  other arithmetic  11.8 us (2%)
    pallas_call x40, Pallas kernels, run(): pl.pallas_call(body, grid_spec=pltpu.PrefetchScalarGridSpec(num_scalar_pr...  386 us
    ppermute x49, waiting for transfers between devices, swap(): return lax.ppermute(values, axis, [(i, i ^ bit) for i in range(size)])  97.4 us
    ppermute x49, starting transfers between devices, swap(): return lax.ppermute(values, axis, [(i, i ^ bit) for i in range(size)])  47.3 us
    unnamed x104, local copies, waits for them, and re-layouts  30 us
  transfers between devices with their start and end apart: 50, of which 12 were waited for; matrix products, arithmetic and copies ran while one was open for 4% of the time, Pallas kernels for 56%

profile of v2, /device:TPU:0, one launch (start us, length us, event | category | flops | bytes accessed | tf_op | source)
XLA Modules:
  0.0 609.8 jit_solution(9227006157169607309)
XLA Ops:
  14.7 9.0 %modulate.1 = (f32[6,8,768]{2,1,0:T(8,128)}, f32[8,768]{1,0:T(8,128)}, bf16[1024,768]{1,0:T(8,128)(2,1)}) custom-call(s32[8]{0:T(128)} %stack.63.refs_0_, f32[8,768]{1,0:T(8,128)} %pad.12.refs_1_.refs_3_, bf16[768,4608]{1,0:T(8,128)(2,1)} %refs_2_.5, bf16[1024,768]{1,0:T(8,128)(2,1)} %refs_4_.2), custom_call_target="tpu_custom_call" | custom-call | flops 1000 | bytes 1000 | tf_op jit(solution)/shard_map/modulate/pallas_call | solution.py:436
  33.2 8.5 %qkv.1.refs_1_.refs_2_.refs_3_ = bf16[1024,2304]{1,0:T(8,128)(2,1)} custom-call(bf16[1024,768]{1,0:T(8,128)(2,1)} %refs_4_.3, f32[6,8,768]{2,1,0:T(8,128)} %get-tuple-element.115.refs_3_.refs_1_.refs_2_.refs_11_.refs_7_.refs_6_, bf16[768,2304]{1,0:T(8,128)(2,1)} %refs_3_.5, bf16[1024,768]{1,0:T(8,128)(2,1)} %touch.4.refs_3_.refs_2_), custom_call_target="tpu_custom_call" | custom-call | flops 1000 | bytes 1000 | tf_op jit(solution)/shard_map/qkv/pallas_call | solution.py:436
  41.6 10.6 %attend.1 = (bf16[1024,768]{1,0:T(8,128)(2,1)}, f32[1024,768]{1,0:T(8,128)}) custom-call(s32[8]{0:T(128)} %stack.63.refs_0_, bf16[1024,2304]{1,0:T(8,128)(2,1)} %qkv.1.refs_1_.refs_2_.refs_3_, bf16[1024,2304]{1,0:T(8,128)(2,1)} %qkv.1.refs_1_.refs_2_.refs_3_, bf16[1024,2304]{1,0:T(8,128)(2,1)} %qkv.1.refs_1_.refs_2_.refs_3_), custom_call_target="tpu_custom_call" | custom-call | flops 1000 | bytes 1000 | tf_op jit(solution)/shard_map/attend/pallas_call | solution.py:436
  52.2 16.0 %collective-permute-done.3.refs_4_.refs_3_ = bf16[1024,768]{1,0:T(8,128)(2,1)S(1)} collective-permute-done((bf16[1024,768]{1,0:T(8,128)(2,1)}, bf16[1024,768]{1,0:T(8,128)(2,1)S(1)}, u32[]{:S(2)}, u32[]{:S(2)}) %collective-permute-start.3) | collective-permute-done | bytes 1572896 | tf_op jit(solution)/shard_map/ppermute | solution.py:1387
  82.9 31.2 %expert.4 = (bf16[4,2,768,384]{3,2,1,0:T(8,128)(2,1)}, bf16[4,2,768,384]{3,2,1,0:T(8,128)(2,1)}, bf16[2,288,768]{2,1,0:T(8,128)(2,1)}, bf16[2,288,768]{2,1,0:T(8,128)(2,1)}, f32[2,1,1024]{2,1,0:T(1,128)}) custom-call(s32[8]{0:T(128)} %stack.63.refs_0_, bf16[1024,768]{1,0:T(8,128)(2,1)} %get-tuple-element.120.refs_1_.refs_7_, bf16[1024,768]{1,0:T(8,128)(2,1)} %copy-done.7, ...), custom_call_target="tpu_custom_call" | custom-call | flops 1000 | bytes 1000 | tf_op jit(solution)/shard_map/expert/pallas_call | solution.py:436
  120.0 32.7 %expert.5 = (bf16[4,2,768,384]{3,2,1,0:T(8,128)(2,1)}, bf16[4,2,768,384]{3,2,1,0:T(8,128)(2,1)}, bf16[2,288,768]{2,1,0:T(8,128)(2,1)}, bf16[2,288,768]{2,1,0:T(8,128)(2,1)}, f32[2,1,1024]{2,1,0:T(1,128)}) custom-call(s32[8]{0:T(128)} %stack.63.refs_0_, bf16[1024,768]{1,0:T(8,128)(2,1)} %touch.5.refs_1_, bf16[1024,768]{1,0:T(8,128)(2,1)} %copy-done.10, ...), custom_call_target="tpu_custom_call" | custom-call | flops 1000 | bytes 1000 | tf_op jit(solution)/shard_map/expert/pallas_call | solution.py:436
  155.6 31.4 %expert.6 = (bf16[4,2,768,384]{3,2,1,0:T(8,128)(2,1)}, bf16[4,1,768,384]{3,2,1,0:T(8,128)(2,1)}, bf16[4,1,768,384]{3,2,1,0:T(8,128)(2,1)}, bf16[2,288,768]{2,1,0...) custom-call(s32[8]{0:T(128)} %stack.63.refs_0_, ...), custom_call_target="tpu_custom_call" | custom-call | flops 1000 | bytes 1000 | tf_op jit(solution)/shard_map/expert/pallas_call | solution.py:436
  187.0 32.7 %expert.7 = (bf16[4,2,768,384]{3,2,1,0:T(8,128)(2,1)}, bf16[4,1,768,384]{3,2,1,0:T(8,128)(2,1)}, bf16[4,1,768,384]{3,2,1,0:T(8,128)(2,1)}, bf16[2,288,768]{2,1,0...) custom-call(s32[8]{0:T(128)} %stack.63.refs_0_, bf16[1024,768]{1,0:T(8,128)(2,1)} %touch.5.refs_1_, ...), custom_call_target="tpu_custom_call" | custom-call | flops 1000 | bytes 1000 | tf_op jit(solution)/shard_map/expert/pallas_call | solution.py:436
  219.7 9.5 %combine.2 = (bf16[1024,768]{1,0:T(8,128)(2,1)}, bf16[1024,768]{1,0:T(8,128)(2,1)}, bf16[1024,768]{1,0:T(8,128)(2,1)}, bf16[1024,768]{1,0:T(8,128)(2,1)}) custom-call(s32[2,1024,128]{2,1,0:T(8,128)} %get-tuple-element.121.refs_0_, bf16[2,288,768]{2,1,0:T(8,128)(2,1)} %get-tuple-element.125.refs_1_, bf16[2,288,768]{2,1,0:T(8,128)(2,1)} %get-tuple-element.126.refs_2_, ...), custom_call_target="tpu_custom_call" | custom-call | flops 1000 | bytes 1000 | tf_op jit(solution)/shard_map/combine/pallas_call | solution.py:436
  230.4 9.4 %combine.3 = (bf16[1024,768]{1,0:T(8,128)(2,1)}, bf16[1024,768]{1,0:T(8,128)(2,1)}, bf16[1024,768]{1,0:T(8,128)(2,1)}, bf16[1024,768]{1,0:T(8,128)(2,1)}) custom-call(s32[2,1024,128]{2,1,0:T(8,128)} %get-tuple-element.137.refs_0_, bf16[2,288,768]{2,1,0:T(8,128)(2,1)} %get-tuple-element.138.refs_1_, bf16[2,288,768]{2,1,0:T(8,128)(2,1)} %get-tuple-element.139.refs_2_, ...), custom_call_target="tpu_custom_call" | custom-call | flops 1000 | bytes 1000 | tf_op jit(solution)/shard_map/combine/pallas_call | solution.py:436
  253.8 42.4 %shared.1 = (bf16[2,768,768]{2,1,0:T(8,128)(2,1)}, bf16[2,768,768]{2,1,0:T(8,128)(2,1)}, bf16[2,2,4,192,384]{4,3,2,1,0:T(8,128)(2,1)}, bf16[2,2,4,192,384]{4,3,2...) custom-call(s32[8]{0:T(128)} %stack.63.refs_0_, bf16[1024,768]{1,0:T(8,128)(2,1)} %get-tuple-element.120.refs_1_.refs_7_, ...), custom_call_target="tpu_custom_call" | custom-call | flops 1000 | bytes 1000 | tf_op jit(solution)/shard_map/shared/pallas_call | solution.py:436
  296.8 12.5 %middle_back.1 = (f32[1024,768]{1,0:T(8,128)}, bf16[1024,768]{1,0:T(8,128)(2,1)}, bf16[1024,768]{1,0:T(8,128)(2,1)}, f32[3,8,768]{2,1,0:T(8,128)}, f32[16,768]{1,0:T(8,128)}) custom-call(f32[1024,768]{1,0:T(8,128)} %get-tuple-element.150.refs_0_, bf16[1024,768]{1,0:T(8,128)(2,1)} %get-tuple-element.151.refs_1_, bf16[1024,768]{1,0:T(8,128)(2,1)} %copy-done.9, ...), custom_call_target="tpu_custom_call" | custom-call | flops 1000 | bytes 1000 | tf_op jit(solution)/shard_map/middle_back/pallas_call | solution.py:436
  309.4 7.0 %halve_y.3 = (f32[2,4,384,384]{3,2,1,0:T(8,128)}, bf16[2,4,384,384]{3,2,1,0:T(8,128)(2,1)}) custom-call(bf16[4,2,768,384]{3,2,1,0:T(8,128)(2,1)} %get-tuple-element.160.refs_0_, bf16[4,2,768,384]{3,2,1,0:T(8,128)(2,1)} %collective-permute-done.21.refs_1_, bf16[4,4,384,384]{3,2,1,0:T(8,128)(2,1)} %bitcast.82, ...), custom_call_target="tpu_custom_call" | custom-call | flops 1000 | bytes 1000 | tf_op jit(solution)/shard_map/halve_y/pallas_call | solution.py:436
  321.1 8.8 %halve_slices.1 = (f32[2,1536,384]{2,1,0:T(8,128)}, bf16[2,1536,384]{2,1,0:T(8,128)(2,1)}) custom-call(bf16[2,768,768]{2,1,0:T(8,128)(2,1)} %get-tuple-element.155.refs_0_, bf16[2,768,768]{2,1,0:T(8,128)(2,1)} %collective-permute-done.19.refs_1_, bf16[2,1536,384]{2,1,0:T(8,128)(2,1)} %bitcast.102, bf16[2,1536,384]{2,1,0:T(8,128)(2,1)} %bitcast.20.refs_3_, ...), custom_call_target="tpu_custom_call" | custom-call | flops 1000 | bytes 1000 | tf_op jit(solution)/shard_map/halve_slices/pallas_call | solution.py:436
  335.8 16.9 %attend_back.1 = (bf16[1024,768]{1,0:T(8,128)(2,1)}, bf16[1024,768]{1,0:T(8,128)(2,1)}, bf16[1024,768]{1,0:T(8,128)(2,1)}) custom-call(s32[8]{0:T(128)} %stack.63.refs_0_, bf16[1024,2304]{1,0:T(8,128)(2,1)} %qkv.1.refs_1_.refs_2_.refs_3_, bf16[1024,2304]{1,0:T(8,128)(2,1)} %qkv.1.refs_1_.refs_2_.refs_3_, bf16[1024,2304]{1,0:T(8,128)(2,1)} %qkv.1.refs_1_.refs_2_.refs_3_, ...), custom_call_target="tpu_custom_call" | custom-call | flops 1000 | bytes 1000 | tf_op jit(solution)/shard_map/attend_back/pallas_call | solution.py:436
  356.0 7.6 %mixed.1 = (bf16[1024,768]{1,0:T(8,128)(2,1)}, f32[8,768]{1,0:T(8,128)}) custom-call(f32[1024,768]{1,0:T(8,128)} %get-tuple-element.147.refs_0_, bf16[1024,768]{1,0:T(8,128)(2,1)} %get-tuple-element.142.refs_2_.refs_1_, bf16[1024,768]{1,0:T(8,128)(2,1)} %copy-done.8, bf16[1024,768]{1,0:T(8,128)(2,1)} %collective-permute-done.16.refs_3_, ...), custom_call_target="tpu_custom_call" | custom-call | flops 1000 | bytes 1000 | tf_op jit(solution)/shard_map/mixed/pallas_call | solution.py:436
  363.6 14.5 %weight_grads.1 = (bf16[2,768,768]{2,1,0:T(8,128)(2,1)}, bf16[768,768]{1,0:T(8,128)(2,1)}, bf16[768,768]{1,0:T(8,128)(2,1)}) custom-call(s32[8]{0:T(128)} %stack.63.refs_0_, bf16[1024,768]{1,0:T(8,128)(2,1)} %refs_4_.3, f32[6,8,768]{2,1,0:T(8,128)} %get-tuple-element.115.refs_3_.refs_1_.refs_2_.refs_11_.refs_7_.refs_6_, ...), custom_call_target="tpu_custom_call" | custom-call | flops 1000 | bytes 1000 | tf_op jit(solution)/shard_map/weight_grads/pallas_call | solution.py:436
  384.9 10.6 %collective-permute-done.26.refs_1_ = bf16[1,4,384,384]{3,2,1,0:T(8,128)(2,1)S(1)} collective-permute-done((bf16[1,4,384,384]{3,2,1,0:T(8,128)(2,1)}, bf16[1,4,384,384]{3,2,1,0:T(8,128)(2,1)S(1)}, u32[]{:S(2)}, u32[]{:S(2)}) %collective-permute-start.26) | collective-permute-done | bytes 1179680 | tf_op jit(solution)/shard_map/ppermute | solution.py:1387
  406.4 10.8 %collective-permute-start.29 = (bf16[1,4,384,384]{3,2,1,0:T(8,128)(2,1)}, bf16[1,4,384,384]{3,2,1,0:T(8,128)(2,1)S(1)}, u32[]{:S(2)}, u32[]{:S(2)}) collective-permute-start(bf16[1,4,384,384]{3,2,1,0:T(8,128)(2,1)} %get-tuple-element.180.refs_2_), channel_id=1, source_target_pairs={{0,8},{2,10},{4,12},{6,14},{8,0},{10,2},{12,4},{14,6},{16,24},{18,... | collective-permute-start | bytes 3538952 | tf_op jit(solution)/shard_map/ppermute | solution.py:1387
  436.1 10.2 %inputs_back.1 = (f32[1024,768]{1,0:T(8,128)}, f32[2,8,768]{2,1,0:T(8,128)}) custom-call(bf16[1024,768]{1,0:T(8,128)(2,1)} %get-tuple-element.165.refs_8_.refs_3_.refs_0_, bf16[1024,768]{1,0:T(8,128)(2,1)} %get-tuple-element.167.refs_4_.refs_1_, bf16[1024,768]{1,0:T(8,128)(2,1)} %get-tuple-element.168.refs_5_.refs_2_, bf16[768,2304]{1,0:T(8,128)(2,1)} %refs_3_.5, ...), custom_call_target="tpu_custom_call" | custom-call | flops 1000 | bytes 1000 | tf_op jit(solution)/shard_map/inputs_back/pallas_call | solution.py:436
  448.1 9.5 %used_back.1.refs_4_ = f32[8,768]{1,0:T(8,128)} custom-call(s32[8]{0:T(128)} %stack.63.refs_0_, f32[6,8,768]{2,1,0:T(8,128)} %pad_maximum_fusion.6.refs_1_, bf16[768,4608]{1,0:T(8,128)(2,1)} %refs_2_.5, f32[8,768]{1,0:T(8,128)} %pad.12.refs_1_.refs_3_, f32[2,8,768]{2,1,0:T(8,128)} %get-tuple-element.184.refs_4_), custom_call_target="tpu_custom_call" | custom-call | flops 1000 | bytes 1000 | tf_op jit(solution)/shard_map/used_back/pallas_call | solution.py:436
  476.4 37.5 %collective-permute-done.31.refs_2_.refs_4_ = bf16[2,4,192,384]{3,2,1,0:T(8,128)(2,1)S(1)} collective-permute-done((bf16[2,4,192,384]{3,2,1,0:T(8,128)(2,1)S(1)}, bf16[2,4,192,384]{3,2,1,0:T(8,128)(2,1)S(1)}, u32[]{:S(2)}, u32[]{:S(2)}) %collective-permute-start.31) | collective-permute-done | bytes 1179680 | tf_op jit(solution)/shard_map/ppermute | solution.py:1387
  536.0 18.3 %collective-permute-done.35 = bf16[1,192,768]{2,1,0:T(8,128)(2,1)S(1)} collective-permute-done((bf16[1,192,768]{2,1,0:T(8,128)(2,1)}, bf16[1,192,768]{2,1,0:T(8,128)(2,1)S(1)}, u32[]{:S(2)}, u32[]{:S(2)}) %collective-permute-start.35) | collective-permute-done | bytes 294944 | tf_op jit(solution)/shard_map/ppermute | solution.py:1387
  583.4 10.9 %all-gather.3.cloned.1.call-done = bf16[32,4,6912]{2,1,0:T(4,128)(2,1)} async-done(((bf16[1,4,6912]{2,1,0:T(4,128)(2,1)}), bf16[32,4,6912]{2,1,0:T(4,128)(2,1)}) %all-gather.3.cloned.1.call-update) | async-done | bytes 1769488 | tf_op jit(solution)/shard_map/all_gather | solution.py:1515
  (273 shorter events, 185.8 us)
Async XLA Ops:
  7.2 587.1 %all-gather.3.cloned.1.call-start = ((), (), s32[]{:S(2)}) async-start(), calls=%async_computation | async-start | bytes 1824768 | tf_op jit(solution)/shard_map/all_gather | solution.py:1515
  30.9 37.3 %collective-permute-start.3 = (bf16[1024,768]{1,0:T(8,128)(2,1)}, bf16[1024,768]{1,0:T(8,128)(2,1)S(1)}, u32[]{:S(2)}, u32[]{:S(2)}) collective-permute-start(bf16[1024,768]{1,0:T(8,128)(2,1)} %touch.4.refs_3_.refs_2_), channel_id=1, source_target_pairs={{0,1},{1,0},{2,3},{3,2},{4,5},{5,4},{6,7},{7,6},{8,9},{9,8},{10,11... | collective-permute-start | bytes 4718600 | tf_op jit(solution)/shard_map/ppermute | solution.py:1387
  32.9 35.3 %collective-permute-start.4 = (bf16[1024,768]{1,0:T(8,128)(2,1)}, bf16[1024,768]{1,0:T(8,128)(2,1)S(1)}, u32[]{:S(2)}, u32[]{:S(2)}) collective-permute-start(bf16[1024,768]{1,0:T(8,128)(2,1)} %touch.4.refs_3_.refs_2_), channel_id=1, source_target_pairs={{0,2},{2,0},{4,6},{6,4},{8,10},{10,8},{12,14},{14,12},{16,18},{18,... | collective-permute-start | bytes 4718600 | tf_op jit(solution)/shard_map/ppermute | solution.py:1387
  76.4 37.7 %collective-permute-start.5 = (bf16[1024,768]{1,0:T(8,128)(2,1)}, bf16[1024,768]{1,0:T(8,128)(2,1)S(1)}, u32[]{:S(2)}, u32[]{:S(2)}) collective-permute-start(bf16[1024,768]{1,0:T(8,128)(2,1)} %get-tuple-element.120.refs_1_.refs_7_), channel_id=1, source_target_pairs={{0,1},{1,0},{2,3},{3,2},{4,5},{5,4},{6,7},{7,6},{8,9},{9,8},{10,11... | collective-permute-start | bytes 4718600 | tf_op jit(solution)/shard_map/ppermute | solution.py:1387
  152.7 156.7 %collective-permute-start.21 = (bf16[4,2,768,384]{3,2,1,0:T(8,128)(2,1)}, bf16[4,2,768,384]{3,2,1,0:T(8,128)(2,1)}, u32[]{:S(2)}, u32[]{:S(2)}) collective-permute-start(bf16[4,2,768,384]{3,2,1,0:T(8,128)(2,1)} %get-tuple-element.161), channel_id=1, source_target_pairs={{0,4},{2,6},{4,0},{6,2},{8,12},{10,14},{12,8},{14,10},{16,20},{18,... | collective-permute-start | bytes 14155784 | tf_op jit(solution)/shard_map/ppermute | solution.py:1387
  245.7 51.1 %collective-permute-start.17 = (bf16[1024,768]{1,0:T(8,128)(2,1)}, bf16[1024,768]{1,0:T(8,128)(2,1)}, u32[]{:S(2)}, u32[]{:S(2)}) collective-permute-start(bf16[1024,768]{1,0:T(8,128)(2,1)} %add_rows.2.refs_2_), channel_id=1, source_target_pairs={{0,1},{1,0},{2,3},{3,2},{4,5},{5,4},{6,7},{7,6},{8,9},{9,8},{10,11... | collective-permute-start | bytes 4718600 | tf_op jit(solution)/shard_map/ppermute | solution.py:1387
  247.9 71.7 %collective-permute-start.18 = (bf16[4,1,768,384]{3,2,1,0:T(8,128)(2,1)}, bf16[4,1,768,384]{3,2,1,0:T(8,128)(2,1)}, u32[]{:S(2)}, u32[]{:S(2)}) collective-permute-start(bf16[4,1,768,384]{3,2,1,0:T(8,128)(2,1)} %get-tuple-element.154), channel_id=1, source_target_pairs={{0,4},{2,6},{4,0},{6,2},{8,12},{10,14},{12,8},{14,10},{16,20},{18,... | collective-permute-start | bytes 7077896 | tf_op jit(solution)/shard_map/ppermute | solution.py:1387
  316.4 61.8 %collective-permute-start.27 = (bf16[2,4,384,384]{3,2,1,0:T(8,128)(2,1)}, bf16[2,4,384,384]{3,2,1,0:T(8,128)(2,1)S(1)}, u32[]{:S(2)}, u32[]{:S(2)}) collective-permute-start(bf16[2,4,384,384]{3,2,1,0:T(8,128)(2,1)} %get-tuple-element.162.refs_2_), channel_id=1, source_target_pairs={{0,8},{2,10},{4,12},{6,14},{8,0},{10,2},{12,4},{14,6},{16,24},{18,... | collective-permute-start | bytes 7077896 | tf_op jit(solution)/shard_map/ppermute | solution.py:1387
  318.4 37.6 %collective-permute-start.16 = (bf16[1024,768]{1,0:T(8,128)(2,1)}, bf16[1024,768]{1,0:T(8,128)(2,1)}, u32[]{:S(2)}, u32[]{:S(2)}) collective-permute-start(bf16[1024,768]{1,0:T(8,128)(2,1)} %add_rows.3.refs_5_), channel_id=1, source_target_pairs={{0,1},{1,0},{2,3},{3,2},{4,5},{5,4},{6,7},{7,6},{8,9},{9,8},{10,11... | collective-permute-start | bytes 4718600 | tf_op jit(solution)/shard_map/ppermute | solution.py:1387
  319.6 80.9 %collective-permute-start.25 = (bf16[4,1,768,384]{3,2,1,0:T(8,128)(2,1)}, bf16[4,1,768,384]{3,2,1,0:T(8,128)(2,1)S(1)}, u32[]{:S(2)}, u32[]{:S(2)}) collective-permute-start(bf16[4,1,768,384]{3,2,1,0:T(8,128)(2,1)} %touch.6.refs_4_), channel_id=1, source_target_pairs={{0,4},{2,6},{4,0},{6,2},{8,12},{10,14},{12,8},{14,10},{16,20},{18,... | collective-permute-start | bytes 7077896 | tf_op jit(solution)/shard_map/ppermute | solution.py:1387
  329.9 87.3 %collective-permute-start.24 = (bf16[2,1536,384]{2,1,0:T(8,128)(2,1)}, bf16[2,1536,384]{2,1,0:T(8,128)(2,1)S(1)}, u32[]{:S(2)}, u32[]{:S(2)}) collective-permute-start(bf16[2,1536,384]{2,1,0:T(8,128)(2,1)} %get-tuple-element.163.refs_2_), channel_id=1, source_target_pairs={{0,1},{1,0},{2,3},{3,2},{4,5},{5,4},{6,7},{7,6},{8,9},{9,8},{10,11... | collective-permute-start | bytes 7077896 | tf_op jit(solution)/shard_map/ppermute | solution.py:1387
  335.4 60.0 %collective-permute-start.26 = (bf16[1,4,384,384]{3,2,1,0:T(8,128)(2,1)}, bf16[1,4,384,384]{3,2,1,0:T(8,128)(2,1)S(1)}, u32[]{:S(2)}, u32[]{:S(2)}) collective-permute-start(bf16[1,4,384,384]{3,2,1,0:T(8,128)(2,1)} %get-tuple-element.164.refs_7_), channel_id=1, source_target_pairs={{0,8},{2,10},{4,12},{6,14},{8,0},{10,2},{12,4},{14,6},{16,24},{18,... | collective-permute-start | bytes 3538952 | tf_op jit(solution)/shard_map/ppermute | solution.py:1387
  378.2 45.4 %collective-permute-start.22 = (bf16[768,768]{1,0:T(8,128)(2,1)}, bf16[768,768]{1,0:T(8,128)(2,1)}, u32[]{:S(2)}, u32[]{:S(2)}) collective-permute-start(bf16[768,768]{1,0:T(8,128)(2,1)} %get-tuple-element.173.refs_6_), channel_id=1, source_target_pairs={{0,2},{2,0},{4,6},{6,4},{8,10},{10,8},{12,14},{14,12},{16,18},{18,... | collective-permute-start | bytes 3538952 | tf_op jit(solution)/shard_map/ppermute | solution.py:1387
  378.2 45.4 %collective-permute-start.23 = (bf16[768,768]{1,0:T(8,128)(2,1)}, bf16[768,768]{1,0:T(8,128)(2,1)}, u32[]{:S(2)}, u32[]{:S(2)}) collective-permute-start(bf16[768,768]{1,0:T(8,128)(2,1)} %get-tuple-element.174), channel_id=1, source_target_pairs={{0,2},{2,0},{4,6},{6,4},{8,10},{10,8},{12,14},{14,12},{16,18},{18,... | collective-permute-start | bytes 3538952 | tf_op jit(solution)/shard_map/ppermute | solution.py:1387
  406.4 52.4 %collective-permute-start.29 = (bf16[1,4,384,384]{3,2,1,0:T(8,128)(2,1)}, bf16[1,4,384,384]{3,2,1,0:T(8,128)(2,1)S(1)}, u32[]{:S(2)}, u32[]{:S(2)}) collective-permute-start(bf16[1,4,384,384]{3,2,1,0:T(8,128)(2,1)} %get-tuple-element.180.refs_2_), channel_id=1, source_target_pairs={{0,8},{2,10},{4,12},{6,14},{8,0},{10,2},{12,4},{14,6},{16,24},{18,... | collective-permute-start | bytes 3538952 | tf_op jit(solution)/shard_map/ppermute | solution.py:1387
  423.1 40.8 %collective-permute-start.28 = (bf16[2,768,384]{2,1,0:T(8,128)(2,1)}, bf16[2,768,384]{2,1,0:T(8,128)(2,1)S(1)}, u32[]{:S(2)}, u32[]{:S(2)}) collective-permute-start(bf16[2,768,384]{2,1,0:T(8,128)(2,1)} %get-tuple-element.181.refs_3_), channel_id=1, source_target_pairs={{0,4},{2,6},{4,0},{6,2},{8,12},{10,14},{12,8},{14,10},{16,20},{18,... | collective-permute-start | bytes 3538952 | tf_op jit(solution)/shard_map/ppermute | solution.py:1387
  427.4 40.5 %collective-permute-start.32 = (bf16[1,768,768]{2,1,0:T(8,128)(2,1)}, bf16[1,768,768]{2,1,0:T(8,128)(2,1)}, u32[]{:S(2)}, u32[]{:S(2)}) collective-permute-start(bf16[1,768,768]{2,1,0:T(8,128)(2,1)} %get-tuple-element.182.refs_7_), channel_id=1, source_target_pairs={{0,1},{1,0},{2,3},{3,2},{4,5},{5,4},{6,7},{7,6},{8,9},{9,8},{10,11... | collective-permute-start | bytes 3538952 | tf_op jit(solution)/shard_map/ppermute | solution.py:1387
  433.4 80.4 %collective-permute-start.31 = (bf16[2,4,192,384]{3,2,1,0:T(8,128)(2,1)S(1)}, bf16[2,4,192,384]{3,2,1,0:T(8,128)(2,1)S(1)}, u32[]{:S(2)}, u32[]{:S(2)}) collective-permute-start(bf16[2,4,192,384]{3,2,1,0:T(8,128)(2,1)S(1)} %copy-done.15), channel_id=1, source_target_pairs={{0,16},{2,18},{4,20},{6,22},{8,24},{10,26},{12,28},{14,30},{16,0},... | collective-permute-start | bytes 3538952 | tf_op jit(solution)/shard_map/ppermute | solution.py:1387
  447.7 81.4 %collective-permute-start.36 = (bf16[1,4,192,384]{3,2,1,0:T(8,128)(2,1)S(1)}, bf16[1,4,192,384]{3,2,1,0:T(8,128)(2,1)S(1)}, u32[]{:S(2)}, u32[]{:S(2)}) collective-permute-start(bf16[1,4,192,384]{3,2,1,0:T(8,128)(2,1)S(1)} %copy-done.19), channel_id=1, source_target_pairs={{0,16},{2,18},{4,20},{6,22},{8,24},{10,26},{12,28},{14,30},{16,0},... | collective-permute-start | bytes 1769480 | tf_op jit(solution)/shard_map/ppermute | solution.py:1387
  467.9 52.7 %collective-permute-start.30 = (bf16[2,384,384]{2,1,0:T(8,128)(2,1)}, bf16[2,384,384]{2,1,0:T(8,128)(2,1)S(1)}, u32[]{:S(2)}, u32[]{:S(2)}) collective-permute-start(bf16[2,384,384]{2,1,0:T(8,128)(2,1)} %get-tuple-element.192.refs_2_), channel_id=1, source_target_pairs={{0,8},{2,10},{4,12},{6,14},{8,0},{10,2},{12,4},{14,6},{16,24},{18,... | collective-permute-start | bytes 1769480 | tf_op jit(solution)/shard_map/ppermute | solution.py:1387
  471.0 52.7 %collective-permute-start.34 = (bf16[1,384,768]{2,1,0:T(8,128)(2,1)}, bf16[1,384,768]{2,1,0:T(8,128)(2,1)S(1)}, u32[]{:S(2)}, u32[]{:S(2)}) collective-permute-start(bf16[1,384,768]{2,1,0:T(8,128)(2,1)} %get-tuple-element.195.refs_5_), channel_id=1, source_target_pairs={{0,4},{2,6},{4,0},{6,2},{8,12},{10,14},{12,8},{14,10},{16,20},{18,... | collective-permute-start | bytes 1769480 | tf_op jit(solution)/shard_map/ppermute | solution.py:1387
  474.0 86.3 %collective-permute-start.38 = (bf16[1,4,192,384]{3,2,1,0:T(8,128)(2,1)S(1)}, bf16[1,4,192,384]{3,2,1,0:T(8,128)(2,1)S(1)}, u32[]{:S(2)}, u32[]{:S(2)}) collective-permute-start(bf16[1,4,192,384]{3,2,1,0:T(8,128)(2,1)S(1)} %copy-done.24), channel_id=1, source_target_pairs={{0,16},{2,18},{4,20},{6,22},{8,24},{10,26},{12,28},{14,30},{16,0},... | collective-permute-start | bytes 1769480 | tf_op jit(solution)/shard_map/ppermute | solution.py:1387
  520.5 44.1 %collective-permute-start.45 = (bf16[48,3072]{1,0:T(8,128)(2,1)}, bf16[48,3072]{1,0:T(8,128)(2,1)S(1)}, u32[]{:S(2)}, u32[]{:S(2)}) collective-permute-start(bf16[48,3072]{1,0:T(8,128)(2,1)} %get-tuple-element.196.refs_2_), channel_id=1, source_target_pairs={{0,2},{2,0},{4,6},{6,4},{8,10},{10,8},{12,14},{14,12},{16,18},{18,... | collective-permute-start | bytes 884744 | tf_op jit(solution)/shard_map/ppermute | solution.py:1387
  523.6 33.3 %collective-permute-start.33 = (bf16[2,192,384]{2,1,0:T(8,128)(2,1)}, bf16[2,192,384]{2,1,0:T(8,128)(2,1)S(1)}, u32[]{:S(2)}, u32[]{:S(2)}) collective-permute-start(bf16[2,192,384]{2,1,0:T(8,128)(2,1)} %get-tuple-element.198.refs_2_), channel_id=1, source_target_pairs={{0,16},{2,18},{4,20},{6,22},{8,24},{10,26},{12,28},{14,30},{16,0},... | collective-permute-start | bytes 884744 | tf_op jit(solution)/shard_map/ppermute | solution.py:1387
  (74 other events, 583.9 us)
Sparse Core Ops, SparseCore 0:
  536.1 58.1 all-gather.2

commit v3 on v2

--- a/solution.py
+++ b/solution.py
@@ -544,31 +544,31 @@
     first = lax.broadcasted_iota(jnp.int32, (1, lanes), 1) < HEAD_DIM
     factor = 1.0 / math.sqrt(HEAD_DIM)
 
-    def part(query_at, key_at, key_count):
-        queries = q_ref[query_at : query_at + short, :]
-        keys = k_ref[key_at : key_at + key_count, :]
-        values = v_ref[key_at : key_at + key_count, :]
+    def part(at, count):
+        span = slice(at, at + count)
+        queries = (q_ref[span, :].astype(F32) * factor).astype(BF16)
+        keys, values = k_ref[span, :], v_ref[span, :]
         zero = jnp.zeros_like(queries)
-        outs, sums = [], []
-        for mine in (first, jnp.logical_not(first)):
-            scores = nt(jnp.where(mine, queries, zero), keys) * factor
-            top = jnp.max(scores, -1, keepdims=True)
-            shifted = jnp.exp(scores - top)
-            total = jnp.sum(shifted, -1, keepdims=True)
-            outs.append(nn(shifted.astype(BF16), values) * (1.0 / total))
-            sums.append(top + jnp.log(total))
-        o_ref[query_at : query_at + short, :] = jnp.where(first, outs[0], outs[1]).astype(BF16)
-        lse_ref[query_at : query_at + short, :] = jnp.where(first, sums[0], sums[1])
+        wide = jnp.concatenate([values, jnp.ones_like(values)], 1)
+        masks = (first, jnp.logical_not(first))
+        scores = [nt(jnp.where(mine, queries, zero), keys) for mine in masks]
+        tops = [jnp.max(a, -1, keepdims=True) for a in scores]
+        shifted = [jnp.exp(a - top).astype(BF16) for a, top in zip(scores, tops)]
+        mixtures = [nn(a, wide) for a in shifted]
+        totals = [a[:, lanes:] for a in mixtures]
+        outs = [a[:, :lanes] / total for a, total in zip(mixtures, totals)]
+        sums = [top + jnp.log(total) for top, total in zip(tops, totals)]
+        o_ref[span, :] = jnp.where(first, outs[0], outs[1]).astype(BF16)
+        lse_ref[span, :] = jnp.where(first, sums[0], sums[1])
 
     @pl.when(pos_ref[LONG] > 0)
     def _():
-        for at in range(0, rows, short):
-            part(at, 0, rows)
+        part(0, rows)
 
     @pl.when(pos_ref[LONG] <= 0)
     def _():
         for at in range(0, rows, short):
-            part(at, at, short)
+            part(at, short)
 
 
 def pair_specs(rows, width):
@@ -610,22 +610,27 @@
     def part(query_at, key_at, key_count, fresh):
         chunk = slice(query_at, query_at + short)
         span = slice(key_at, key_at + key_count)
-        queries, grads = q_ref[chunk, :], do_ref[chunk, :]
+        queries, grads = (q_ref[chunk, :].astype(F32) * factor).astype(BF16), do_ref[chunk, :]
         keys, values = k_ref[span, :], v_ref[span, :]
-        zero, zero_keys = jnp.zeros_like(queries), jnp.zeros_like(keys)
-        dq = dk = dv = 0.0
-        for head, mine in enumerate((first, jnp.logical_not(first))):
-            query_own = jnp.where(mine, queries, zero)
-            grad_own = jnp.where(mine, grads, zero)
-            key_own = jnp.where(mine, keys, zero_keys)
-            scores = nt(keys, query_own) * factor
-            probs = jnp.exp(scores - lse_rows[head][:, chunk])
-            grad_probs = nt(values, grad_own)
-            grad_scores = (probs * (grad_probs - delta_rows[head][:, chunk])).astype(BF16)
-            dv = dv + nn(probs.astype(BF16), grad_own)
-            dk = dk + nn(grad_scores, query_own)
-            dq = dq + tn(grad_scores, key_own)
-        dq_ref[chunk, :] = (dq * factor).astype(BF16)
+        masks = (first, jnp.logical_not(first))
+
+        def apart(array):
+            return [jnp.where(mine, array, jnp.zeros_like(array)) for mine in masks]
+
+        query_own, grad_own, key_own = apart(queries), apart(grads), apart(keys)
+        probs = [
+            jnp.exp(nt(keys, query) - lse[:, chunk]) for query, lse in zip(query_own, lse_rows)
+        ]
+        grad_probs = [nt(values, grad) for grad in grad_own]
+        grad_scores = [
+            (prob * (grad - delta[:, chunk])).astype(BF16)
+            for prob, grad, delta in zip(probs, grad_probs, delta_rows)
+        ]
+        low = [prob.astype(BF16) for prob in probs]
+        dv = nn(jnp.concatenate(low, 1), jnp.concatenate(grad_own, 0))
+        dk = nn(jnp.concatenate(grad_scores, 1), jnp.concatenate(query_own, 0))
+        dq = nn(jnp.transpose(jnp.concatenate(key_own, 0)), jnp.concatenate(grad_scores, 0))
+        dq_ref[chunk, :] = (jnp.transpose(dq) * factor).astype(BF16)
         if fresh:
             dk_acc[span, :] = dk
             dv_acc[span, :] = dv
@@ -643,7 +648,7 @@
         for at in range(0, rows, short):
             part(at, at, short, True)
 
-    dk_ref[...] = (dk_acc[...] * factor).astype(BF16)
+    dk_ref[...] = dk_acc[...].astype(BF16)
     dv_ref[...] = dv_acc[...].astype(BF16)
 
 
@@ -880,8 +885,8 @@
 
 
 def shared_kernel(
-    pos_ref, h_ref, b_ref, up_ref, down_ref, ku_ref, su_ref, kd_ref, sd_ref, out_ref, gx_ref,
-    xt_s, gt_s, act_s, pre_s,
+    pos_ref, h_ref, b_ref, up_ref, down_ref, ku_ref, su0_ref, su1_ref, kd_ref, sd0_ref, sd1_ref,
+    out_ref, gx_ref, xt_s, gt_s, act_s, pre_s,
 ):
     step = pl.program_id(0)
     nz, block = 4, kd_ref.shape[3]
@@ -907,13 +912,18 @@
     def _():
         ku_ref[0] = dup
 
-    @pl.when(step >= 2)
+    @pl.when(step == 2)
     def _():
-        su_ref[0] = dup
+        su0_ref[...] = dup
+
+    @pl.when(step == 3)
+    def _():
+        su1_ref[...] = dup
 
     for y, piece in enumerate(sides(pos_ref, nn(gt_s[...], act))):
-        for place, ref in ((0, kd_ref), (1, kd_ref), (2, sd_ref), (3, sd_ref)):
-            ref[place % 2, y, 0] = piece[place * block : (place + 1) * block].astype(BF16)
+        pieces = [piece[place * block : (place + 1) * block].astype(BF16) for place in range(4)]
+        kd_ref[0, y, 0], kd_ref[1, y, 0] = pieces[0], pieces[1]
+        sd0_ref[y, 0], sd1_ref[y, 0] = pieces[2], pieces[3]
 
 
 def shared_call(pos, hidden, branch, up, down, after):
@@ -927,11 +937,11 @@
         return (f % 2 ^ s[STREAM]) * 2 + (f // 2 ^ s[CORE])
 
     keep = pl.BlockSpec((1, width, tile), lambda f, s: (jnp.minimum(f, 1), 0, 0))
-    send = pl.BlockSpec((1, width, tile), lambda f, s: (jnp.maximum(f - 2, 0), 0, 0))
     downs = pl.BlockSpec(
         (2, 2, 1, block, tile // 2), lambda f, s: (0, 0, flipped(unit(f, s) ^ s[ROW_Z], 2), 0, 0)
     )
-    return run(
+    sent = pl.BlockSpec((2, 1, block, tile // 2), lambda f, s: (0, flipped(unit(f, s) ^ s[ROW_Z], 2), 0, 0))
+    outs = run(
         shared_kernel, (hidden, branch, up[None], down[None]), (nz,),
         [
             like(hidden),
@@ -939,9 +949,9 @@
             pl.BlockSpec((1, width, tile), lambda f, s: (0, 0, unit(f, s))),
             pl.BlockSpec((1, tile, width), lambda f, s: (0, unit(f, s), 0)),
         ],
-        [keep, send, downs, downs, like(hidden), like(hidden)],
-        [shape((2, width, tile), BF16)] * 2
-        + [shape((2, 2, nz, block, tile // 2), BF16)] * 2
+        [keep] + [full((width, tile))] * 2 + [downs, sent, sent, like(hidden), like(hidden)],
+        [shape((2, width, tile), BF16)] + [shape((width, tile), BF16)] * 2
+        + [shape((2, 2, nz, block, tile // 2), BF16)] + [shape((2, nz, block, tile // 2), BF16)] * 2
         + [shape((rows, width), F32)] * 2,
         "shared", scalars=(pos,), after=after,
         scratch=[
@@ -951,18 +961,20 @@
             pltpu.VMEM((rows, tile), BF16),
         ],
     )
-
-
-def combine_kernel(slots, col_ref, *refs):
+    return outs[0], outs[1:3], outs[3], outs[4:6], *outs[6:]
+
+
+def combine_kernel(places, col_ref, *refs):
+    slots = len(places)
     rows_refs, refs = refs[: 2 * slots], refs[2 * slots :]
-    targets, stacks = refs[:4], refs[4:]
+    targets, stacks = refs[:5], refs[5:]
 
     @pl.when(pl.program_id(0) == 0)
     def _():
         for slot in range(slots):
             for kind in range(2):
                 for source in range(2):
-                    stacks[kind][source, slot * CAP : (slot + 1) * CAP, :] = rows_refs[2 * slot + kind][source]
+                    stacks[kind][source, slot * CAP : (slot + 1) * CAP, :] = rows_refs[2 * slot + kind][places[slot] + source]
 
     block = col_ref.shape[1]
     own = lax.broadcasted_iota(jnp.int32, (block, slots * CAP), 1)
@@ -975,35 +987,55 @@
             hits = hit if hits is None else jnp.logical_or(hits, hit)
         pick = hits.astype(F32).astype(BF16)
         for kind in range(2):
-            targets[2 * kind + source][...] = nn(pick, stacks[kind][source]).astype(BF16)
-
-
-def combine(rank_cols, pairs, after):
+            total = nn(pick, stacks[kind][source]).astype(BF16)
+            if 2 * kind + source < 3:
+                targets[2 * kind + source][...] = total
+            else:
+                early = pl.program_id(0) < pl.num_programs(0) // 2
+
+                @pl.when(early)
+                def _():
+                    targets[3][...] = total
+
+                @pl.when(jnp.logical_not(early))
+                def _():
+                    targets[4][...] = total
+
+
+def combine(rank_cols, pairs, places, after):
     count, rows, _ = rank_cols.shape
     width = pairs[0][0].shape[2]
     block = rows // 4
     flat = [a for pair in pairs for a in pair]
-    return run(
-        functools.partial(combine_kernel, len(pairs)), (rank_cols, *flat), (rows // block,),
+    halves = [
+        pl.BlockSpec((block, width), lambda i: (jnp.minimum(i, 1), 0)),
+        pl.BlockSpec((block, width), lambda i: (jnp.maximum(i - 2, 0), 0)),
+    ]
+    *outs, low, high = run(
+        functools.partial(combine_kernel, places), (rank_cols, *flat), (rows // block,),
         [pl.BlockSpec((count, block, 128), lambda i: (0, i, 0))] + [like(a) for a in flat],
-        [rows_spec(block, width)] * 4, [shape((rows, width), BF16)] * 4, "combine",
+        [rows_spec(block, width)] * 3 + halves,
+        [shape((rows, width), BF16)] * 3 + [shape((rows // 2, width), BF16)] * 2, "combine",
         scratch=[pltpu.VMEM((2, len(pairs) * CAP, width), BF16)] * 2, after=after,
     )
-
-
-def add_kernel(*refs):
-    count = len(refs) // 3
-    for left, right, out in zip(refs[:count], refs[count : 2 * count], refs[2 * count :]):
-        out[...] = (left[...].astype(F32) + right[...].astype(F32)).astype(out.dtype)
-
-
-def add_rows(lefts, rights, after=()):
-    rows, width = lefts[0].shape
-    count = len(lefts)
+    return (*outs, (low, high))
+
+
+def add_kernel(left_ref, low_ref, high_ref, second_ref, third_ref, one_ref, two_ref):
+    two_ref[...] = (second_ref[...].astype(F32) + third_ref[...].astype(F32)).astype(BF16)
+    low = pl.program_id(0) < pl.num_programs(0) // 2
+    right = jnp.where(low, low_ref[...], high_ref[...])
+    one_ref[...] = (left_ref[...].astype(F32) + right.astype(F32)).astype(BF16)
+
+
+def add_rows(left, halves, second, third, after):
+    rows, width = left.shape
     tile = rows_spec(rows // 4, width)
-    return run(
-        add_kernel, (*lefts, *rights), (4,), [tile] * (2 * count), [tile] * count,
-        [shape((rows, width), BF16)] * count, "add_rows", after=after,
+    low = pl.BlockSpec((rows // 4, width), lambda i: (jnp.minimum(i, 1), 0))
+    high = pl.BlockSpec((rows // 4, width), lambda i: (jnp.maximum(i - 2, 0), 0))
+    return run(
+        add_kernel, (left, *halves, second, third), (4,), [tile, low, high, tile, tile], [tile] * 2,
+        [shape((rows, width), BF16)] * 2, "add_rows", after=after,
     )
 
 
@@ -1122,23 +1154,28 @@
     )
 
 
-def halve_slices_kernel(ku_ref, au_ref, kd_ref, ad_ref, keep_ref, send_ref):
+def halve_slices_kernel(ku_ref, kd_ref, au0_ref, au1_ref, ad0_ref, ad1_ref, keep_ref, send_ref):
+    ups, downs = (au0_ref, au1_ref), (ad0_ref, ad1_ref)
     for at, ref in enumerate((keep_ref, send_ref)):
-        up = total_of(ku_ref[at], au_ref[at])
-        half = up.shape[1] // 2
+        up = total_of(ku_ref[at], ups[at][...])
+        rows, half = up.shape[0], up.shape[1] // 2
         for side in range(2):
-            ref[0, side * up.shape[0] : (side + 1) * up.shape[0], :] = up[:, side * half : (side + 1) * half].astype(ref.dtype)
-        ref[1] = total_of(kd_ref[at], ad_ref[at]).astype(ref.dtype)
-
-
-def halve_slices(up_keep, up_arrived, down_keep, down_arrived, after):
+            piece = up[:, side * half : (side + 1) * half]
+            ref[0, side * rows : (side + 1) * rows, :] = piece.astype(ref.dtype)
+        ref[1] = total_of(kd_ref[at], downs[at][...]).astype(ref.dtype)
+
+
+def halve_slices(up_keep, down_keep, arrived, after):
     _, rows, cols = up_keep.shape
     steps = 8
+    down_keep = down_keep.reshape(2, 2 * rows, cols // 2)
+    arrived = [a.reshape(-1, a.shape[-1]) for a in arrived]
     ups = pl.BlockSpec((2, rows // steps, cols), lambda i: (0, i, 0))
     downs = pl.BlockSpec((2, 2 * rows // steps, cols // 2), lambda i: (0, i, 0))
     dims = (2, 2 * rows, cols // 2)
     return run(
-        halve_slices_kernel, (up_keep, up_arrived, down_keep, down_arrived), (steps,), [ups, ups, downs, downs],
+        halve_slices_kernel, (up_keep, down_keep, *arrived), (steps,),
+        [ups, downs] + [rows_spec(a.shape[0] // steps, a.shape[1]) for a in arrived],
         [downs, downs], [shape(dims, F32), shape(dims, BF16)], "halve_slices", after=after,
     )
 
@@ -1181,14 +1218,16 @@
     if merged:
         half = up.shape[0] // 2
         up = jnp.concatenate([up[:half], up[half:]], 1)
-        outs[2][...], outs[3][...] = core_halves(pos_ref, jnp.transpose(total[1]))
-    outs[0][...], outs[1][...] = core_halves(pos_ref, up)
+        mine, outs[3][...] = core_halves(pos_ref, jnp.transpose(total[1]))
+        outs[2][...] = mine.astype(BF16)
+    mine, outs[1][...] = core_halves(pos_ref, up)
+    outs[0][...] = mine.astype(BF16)
 
 
 def finish_slices(pos, keep, arrived, merged, after):
     _, rows, cols = keep.shape
     dims = [(rows // 4, 2 * cols), (cols // 2, rows)] if merged else [(rows // 2, cols)]
-    outs = [shape(d, t) for d in dims for t in (F32, BF16)]
+    outs = [shape(d, BF16) for d in dims for _ in range(2)]
     return run(
         functools.partial(finish_slices_kernel, merged), (keep, arrived), (1,), [like(keep), like(arrived)],
         [like(a) for a in outs], outs, "finish_slices", scalars=(pos,), after=after,
@@ -1196,7 +1235,7 @@
 
 
 def middle_back_kernel(
-    gs_ref, ga_ref, gb_ref, gc_ref, gg_ref, routes_ref, router_ref,
+    gs_ref, ga_ref, low_ref, high_ref, gc_ref, gg_ref, routes_ref, router_ref,
     hidden_ref, cot_ref, branch_ref, x_ref, mod_ref, w_ref,
     gm_ref, gatt_ref, back_ref, mods_ref, drouter_ref,
 ):
@@ -1207,7 +1246,8 @@
     gates = gate_rows(hidden, routes_ref[...], router_ref[...], ids)
     inner = jnp.sum(gates * grad_gates, 0, keepdims=True)
     grad_logits = gates * (grad_gates - inner)
-    grad = gs_ref[...] + ga_ref[...].astype(F32) + gb_ref[...].astype(F32) + gc_ref[...].astype(F32)
+    core = jnp.where(block < pl.num_programs(0) // 2, low_ref[...], high_ref[...])
+    grad = gs_ref[...] + ga_ref[...].astype(F32) + core.astype(F32) + gc_ref[...].astype(F32)
     drouter = 0.0
     for piece in three_parts(grad_logits):
         grad = grad + tn(piece, router_ref[...])
@@ -1240,6 +1280,9 @@
     short = rows // blocks
     tile = rows_spec(short, width)
     cols = lambda a: pl.BlockSpec((a.shape[0], short), lambda i: (0, i))
+    half = blocks // 2
+    low = pl.BlockSpec((short, width), lambda i: (jnp.minimum(i, half - 1), 0))
+    high = pl.BlockSpec((short, width), lambda i: (jnp.maximum(i - half, 0), 0))
     out_shape = [
         shape((rows, width), F32),
         shape((rows, width), BF16),
@@ -1250,7 +1293,7 @@
     return run(
         middle_back_kernel,
         (*parts, gg, routes_t, router_t, hidden, cot, branch, patches, mod, out_weight), (blocks,),
-        [tile] * 4 + [cols(gg), cols(routes_t), like(router_t)] + [tile] * 4 + [like(mod), like(out_weight)],
+        [tile, tile, low, high, tile] + [cols(gg), cols(routes_t), like(router_t)] + [tile] * 4 + [like(mod), like(out_weight)],
         [tile] * 3 + [like(a) for a in out_shape[3:]], out_shape, "middle_back", after=after,
     )
 
@@ -1389,6 +1432,15 @@
 
 def swap_all(arrays, axis, bit):
     return [swap(a, axis, bit) for a in arrays]
+
+
+def swap_across(values):
+    stream = lax.axis_size("stream")
+    pairs = [
+        (i, ((i // stream) ^ 1) * stream + ((i % stream) ^ 1))
+        for i in range(lax.axis_size("dp") * stream)
+    ]
+    return lax.ppermute(values, ("dp", "stream"), pairs)
 
 
 def in_order(own, mine, arrived, axis):
@@ -1422,20 +1474,21 @@
     emb_pad = jnp.pad(embedding, ((0, 8 - blocks), (0, 0)))
     router_t = jnp.pad(router_weight.T, ((0, 16 - router_weight.shape[1]), (0, 0)))
     mod, act, branch_grad = modulate(pos, emb_pad, ada_weight, cotangent, blocks)
-    rank_near, cols_near = ranks(pos, routes_near, (mod,))
-    rank_far, cols_far = ranks(pos, routes_far, (rank_near,))
-    branch_grad = touch(branch_grad, (rank_far,))
+    branch_grad = touch(branch_grad, (routes_far[1], routes_near[1]))
     branch_x = swap(branch_grad, "stream", 1)
     branches_near = (branch_grad, swap(branch_grad, "dp", 1))
-    branches_far = (branch_x, swap(branch_x, "dp", 1))
 
     packed = qkv_forward(patches, mod, qkv_weight, blocks, (branch_grad,))
     attended, logsum = attend_forward(pos, packed, short)
     branch_one, hidden = middle_forward(
-        attended, patches, mod, out_weight, blocks, (branch_x, branches_near[1])
+        attended, patches, mod, out_weight, blocks, ()
     )
     hidden_x = swap(hidden, "stream", 1)
     hiddens_near = (hidden, swap(hidden, "dp", 1))
+    rank_near, cols_near = ranks(pos, routes_near, (hidden,))
+    rank_far, cols_far = ranks(pos, routes_far, (rank_near,))
+    branch_x = touch(branch_x, (rank_far,))
+    branches_far = (branch_x, swap(branch_x, "dp", 1))
 
     def expert(slot, is_far, sends, prior, after):
         group = (
@@ -1446,25 +1499,28 @@
         out = expert_call(slot, sends, pos, *group, router_t, expert_up, expert_down, prior, nz, after)
         return out[: 1 + sends], out[1 + sends :]
 
-    first, first_near = expert(0, False, 1, None, (branches_far[1],))
+    first, first_near = expert(0, False, 1, None, (branch_x,))
     hidden_x = touch(hidden_x, (first_near[2],))
     hiddens_far = (hidden_x, swap(hidden_x, "dp", 1))
     first, first_far = expert(0, True, 1, first, ())
     first_arrived = swap(first[1], "dp", 2)
+
     second, second_near = expert(1, False, 2, None, (first_far[2],))
     second, second_far = expert(1, True, 2, second, ())
     up_half_arrived = swap(second[1], "dp", 2)
-    out_x, out_xc, gx_x, gx_xc = combine(cols_far, [r[:2] for r in (first_far, second_far)], ())
-    gx_xc, out_xc = swap(gx_xc, "dp", 1), swap(out_xc, "dp", 1)
+    out_x, out_xc, gx_x, gx_xc = combine(cols_far, [r[:2] for r in (first_far, second_far)], (0, 0), ())
+    gx_xc, out_xc = swap_all(gx_xc, "dp", 1), swap(out_xc, "dp", 1)
     out_near, out_core, gx_near, gx_core = combine(
-        cols_near, [r[:2] for r in (first_near, second_near)], (gx_x,)
-    )
-    gx_core = swap(gx_core, "dp", 1)
+        cols_near, [r[:2] for r in (first_near, second_near)], (0, 0), (gx_x,)
+    )
+    gx_core = swap_all(gx_core, "dp", 1)
     out_core = swap(out_core, "dp", 1)
-    (gx_sum,) = add_rows([gx_x], [gx_xc], (out_near,))
+    gx_sum, out_sum = add_rows(gx_x, gx_xc, out_x, out_xc, (gx_near,))
     gx_back = swap(gx_sum, "stream", 1)
-    (out_sum,) = add_rows([out_x], [out_xc], (gx_sum,))
     out_back = swap(out_sum, "stream", 1)
+    both, up, down = (0, 1), (0,), (1,)
+    ea_keep, ea_send = halve_y(first[0], first_arrived, both, (out_sum,))
+    ea_arrived = swap(ea_send, "dp", 4)
     near, far = (first_near, second_near), (first_far, second_far)
     gg_near = [jnp.concatenate([r[2][source] for r in near], 0) for source in range(2)]
     gg_far = [jnp.concatenate([r[2][source] for r in far], 0) for source in range(2)]
@@ -1474,85 +1530,98 @@
     gg = gg_rel.reshape(4, here, rows)[order].reshape(EXPERTS, rows)
     gg = jnp.pad(gg, ((0, 16 - EXPERTS), (0, 0)))
 
+    out_core = touch(out_core, (ea_send,))
+    down_half = touch(second[2], (out_core,))
+    down_half_arrived = swap(down_half, "dp", 2)
     up_keep, up_send, down_keep, down_send, shared_out, shared_gx = shared_call(
-        pos, hidden, branch_grad, shared_up, shared_down, (out_sum, gx_core, out_core, gg)
-    )
-    up_arrived, down_arrived = swap(up_send, "dp", 1), swap(down_send, "dp", 1)
+        pos, hidden, branch_grad, shared_up, shared_down, (down_half, *gx_core, gg)
+    )
+    sh_arrived = swap_all([*up_send, *down_send], "dp", 1)
 
     grad_middle, grad_attended, back, mods_two, drouter = middle_backward(
-        (shared_gx, gx_near, gx_core, gx_back), gg, routes_t, router_t, hidden, cotangent, branch_one,
+        (shared_gx, gx_near, *gx_core, gx_back), gg, routes_t, router_t, hidden, cotangent, branch_one,
         patches, mod, out_weight, blocks, (),
     )
-    both, up, down = (0, 1), (0,), (1,)
-    flat = lambda a: a.reshape(a.shape[0], -1, a.shape[-1])
-    ea_keep, ea_send = halve_y(first[0], first_arrived, both, (grad_attended,))
-    ea_arrived = swap(ea_send, "dp", 4)
-    down_half = touch(second[2], (up_half_arrived, ea_send))
-    down_half_arrived = swap(down_half, "dp", 2)
-    sh_keep, sh_send = halve_slices(up_keep, up_arrived, flat(down_keep), flat(down_arrived), (down_half,))
+    ea_keep, ea_send = halve_z(ea_keep, ea_arrived, both, (grad_attended,))
+    ea_arrived = swap(ea_send, "dp", 8)
+    bu_keep, bu_send = halve_y(second[0], up_half_arrived, up, (ea_send,))
+    bu_arrived = swap(bu_send, "dp", 4)
+    sh_keep, sh_send = halve_slices(up_keep, down_keep, sh_arrived, (bu_send,))
     sh_arrived = swap(sh_send, "stream", 1)
-    bu_keep, bu_send = halve_y(second[0], up_half_arrived, up, (sh_send,))
-    bu_arrived = swap(bu_send, "dp", 4)
-    grads = attend_backward(pos, packed, attended, logsum, grad_attended, short, (bu_send,))
-    mixed, gate_two = mixed_forward(
-        (shared_out, out_near, out_core, out_back), cotangent, branch_one, patches, mod, blocks, (grads[0],)
-    )
-    qk_keep, qk_send = weight_grads(pos, patches, mod, grads, attended, back, (gate_two,))
-    qk_arrived = [swap(a, "dp", 1) for a in qk_send]
-    ea_keep, ea_send = halve_z(ea_keep, ea_arrived, both, (qk_send[0],))
-    ea_arrived = swap(ea_send, "dp", 8)
-    bu_keep, bu_send = halve_z(bu_keep, bu_arrived, up, (ea_send,))
+    grads = attend_backward(pos, packed, attended, logsum, grad_attended, short, (sh_send,))
+    out_back = touch(out_back, (grads[0],))
+    bd_keep, bd_send = halve_y(second[0], down_half_arrived, down, (out_back,))
+    bd_arrived = swap(bd_send, "dp", 4)
+    bu_keep, bu_send = halve_z(bu_keep, bu_arrived, up, (bd_send,))
     bu_arrived = swap(bu_send, "dp", 8)
-    bd_keep, bd_send = halve_y(second[0], down_half_arrived, down, (bu_send,))
-    bd_arrived = swap(bd_send, "dp", 4)
-    sh_keep, sh_send = halve(sh_keep, sh_arrived, (bd_send,))
+    ea_arrived = touch(ea_arrived, (bu_send,))
+    qk_keep, qk_send = weight_grads(pos, patches, mod, grads, attended, back, (ea_arrived,))
+    qk_arrived = swap_all(qk_send, "dp", 1)
+    sh_keep, sh_send = halve(sh_keep, sh_arrived, (qk_send[0],))
     sh_arrived = swap(sh_send, "dp", 2)
     qk_keep, qk_send = halve_parts(qk_keep, qk_arrived, (sh_send,))
     qk_arrived = swap(qk_send, "stream", 1)
-    grad_patches, mods_one = inputs_backward(grads, qkv_weight, patches, grad_middle, mod, blocks, (qk_send,))
-    factors = [act, *mods_one, *mods_two, gate_two]
-    factors = jnp.concatenate([a[:blocks] for a in factors] + [drouter[:EXPERTS].reshape(blocks, -1)], 1)
-    factors = lax.all_gather(factors.astype(BF16), ("dp", "stream"), axis=0, tiled=True)
+    mixed, gate_two = mixed_forward(
+        (shared_out, out_near, out_core, out_back), cotangent, branch_one, patches, mod, blocks, (qk_send,)
+    )
+    grad_patches, mods_one = inputs_backward(grads, qkv_weight, patches, grad_middle, mod, blocks, (gate_two,))
+    factors = [a[:blocks] for a in (act, *mods_one, *mods_two, gate_two)]
+    factors = jnp.concatenate(factors + [drouter[:EXPERTS].reshape(blocks, -1)], 1).astype(BF16)
+
+    def doubled(axis, bit, after):
+        return jnp.concatenate([factors, touch(swap(factors, axis, bit), (after,))], 0)
+
     grad_mod = jnp.concatenate([mods_one, mods_two, gate_two[None]], 0)
-    grad_embedding = used_backward(pos, grad_mod, ada_weight, emb_pad, blocks, (mods_one,))
-
-    bd_keep, bd_send = halve_z(bd_keep, bd_arrived, down, (grad_embedding,))
+    bu_arrived = touch(bu_arrived, (mods_one,))
+    bd_keep, bd_send = halve_z(bd_keep, bd_arrived, down, (bu_arrived,))
     bd_arrived = swap(bd_send, "dp", 8)
-    sh_keep, sh_send = halve(sh_keep, sh_arrived, (bd_send,))
+    qk_keep, qk_send = halve(qk_keep, qk_arrived, (bd_send,))
+    qk_arrived = swap(qk_send, "dp", 2)
+    factors = doubled("dp", 8, qk_send)
+    sh_keep, sh_send = halve(sh_keep, sh_arrived, (qk_send,))
     sh_arrived = swap(sh_send, "dp", 4)
-    qk_keep, qk_send = halve(qk_keep, qk_arrived, (sh_send,))
-    qk_arrived = swap(qk_send, "dp", 2)
-    ea_done = finish_kinds(pos, ea_keep, ea_arrived, both, (qk_send,))
-    ea_others = [swap(ea_done[1], "dp", 1), swap(ea_done[3], "dp", 1)]
-    sh_keep, sh_send = halve(sh_keep, sh_arrived, (ea_done[1],))
+    grad_embedding = used_backward(pos, grad_mod, ada_weight, emb_pad, blocks, (sh_send,))
+    factors = doubled("dp", 4, grad_embedding)
+    qk_keep, qk_send = halve(qk_keep, qk_arrived, (grad_embedding,))
+    qk_arrived = swap(qk_send, "dp", 4)
+    bd_arrived = touch(bd_arrived, (qk_send,))
+    factors = doubled("dp", 2, bd_arrived)
+    ea_done = finish_kinds(pos, ea_keep, ea_arrived, both, (bd_arrived,))
+    qk_keep, qk_send = halve(qk_keep, qk_arrived, (ea_done[1],))
+    qk_arrived = swap(qk_send, "dp", 8)
+    factors = doubled("stream", 1, qk_send)
+    sh_keep, sh_send = halve(sh_keep, sh_arrived, (qk_send,))
     sh_arrived = swap(sh_send, "dp", 8)
-    qk_keep, qk_send = halve(qk_keep, qk_arrived, (sh_send,))
-    qk_arrived = swap(qk_send, "dp", 4)
-    bu_done = finish_kinds(pos, bu_keep, bu_arrived, up, (qk_send,))
-    bu_others = swap(bu_done[1], "dp", 1)
-    qk_keep, qk_send = halve(qk_keep, qk_arrived, (bu_done[1],))
-    qk_arrived = swap(qk_send, "dp", 8)
-    sh_done = finish_slices(pos, sh_keep, sh_arrived, True, (qk_send,))
-    bd_done = finish_kinds(pos, bd_keep, bd_arrived, down, (sh_done[1],))
-    bd_others = swap(bd_done[1], "dp", 1)
-    qk_done = finish_slices(pos, qk_keep, qk_arrived, False, (bd_done[1],))
+    bu_done = finish_kinds(pos, bu_keep, bu_arrived, up, (sh_send,))
+    bd_done = finish_kinds(pos, bd_keep, bd_arrived, down, (bu_done[1],))
+    factors = doubled("dp", 1, bd_done[1])
+    ea_others = [touch(swap(a, "dp", 1), (bd_done[1],)) for a in (ea_done[1], ea_done[3])]
+    sh_arrived = touch(sh_arrived, (bd_done[1],))
 
     share = width // dp_size
-    factors = touch(factors, (sh_done[1],))
-    acts = lax.dynamic_slice_in_dim(factors[:, :width], dp * share, share, 1)
+
+    def own_share(values):
+        return lax.dynamic_slice_in_dim(values, dp * share, share, 1)
+
     wide = 7 * width
+    acts = own_share(factors[:, :width])
     grad_ada = lax.dot_general(acts, factors[:, width:wide], (((0,), (0,)), ((), ())), preferred_element_type=F32)
     drouter_sum = jnp.sum(factors[:, wide:].astype(F32).reshape(-1, blocks, 2 * width), 0)
-    drouter_sum = drouter_sum.reshape(EXPERTS, width)
-    grad_router = lax.dynamic_slice_in_dim(drouter_sum, dp * share, share, 1).T
+    grad_router = own_share(drouter_sum.reshape(EXPERTS, width)).T
+
+    qk_done = finish_slices(pos, qk_keep, qk_arrived, False, (grad_ada, sh_arrived, *ea_others))
+    bu_others = touch(swap(bu_done[1], "dp", 1), (qk_done[1],))
+    bd_others = touch(swap(bd_done[1], "dp", 1), (qk_done[1],))
+    sh_done = finish_slices(pos, sh_keep, sh_arrived, True, (qk_done[1],))
 
     def experts_out(one, two, one_other, two_other):
         mine, others = jnp.stack([one, two]), jnp.stack([one_other, two_other]).astype(F32)
         return in_order(core, mine, others, 0)
 
-    def slices_out(keep, send):
-        chip = in_order(core, keep.astype(BF16), swap(send, "dp", 1), 1)
-        return in_order(stream, chip, swap(chip, "stream", 1), 1).astype(F32)
+    def slices_out(mine, send):
+        near = in_order(core, mine, swap(send, "dp", 1), 1)
+        far = in_order(core, swap(mine, "stream", 1), swap_across(send), 1)
+        return in_order(stream, near, far, 1).astype(F32)
 
     grad_qkv_out = slices_out(*qk_done)
     return (

time: 620 us -> 573 us (0.924)
  waiting for transfers between devices: 108 us -> 71.5 us
  between operations: 15.6 us -> 2.27 us
  starting transfers between devices: 47.3 us -> 56.2 us
    ppermute x49 -> x58, waiting for transfers between devices: 97.4 us -> 71.5 us  [swap(): return lax.ppermute(values, axis, [(i, i ^ bit) for i in range(size)])]
    all_gather x1 -> x0, waiting for transfers between devices: 10.9 us -> none  [local_pair(): lax.all_gather(factors.astype(BF16), ('dp', 'stream'), axis=0, tiled=True)]
    unnamed x104 -> x133, local copies, waits for them, and re-layouts: 30 us -> 20.3 us
    concatenate x1 -> x3, local copies, waits for them, and re-layouts: 0.61 us -> 9.24 us  [the longest x2 9.22 us: doubled(): jnp.concatenate([factors, touch(swap(factors, axis, bit), (after,))], 0)]
    ppermute x49 -> x58, starting transfers between devices: 47.3 us -> 55.1 us  [swap(): return lax.ppermute(values, axis, [(i, i ^ bit) for i in range(size)])]
    pallas_call x40 -> x39, Pallas kernels: 386 us -> 383 us  [run(): pl.pallas_call(body, grid_spec=pltpu.PrefetchScalarGridSpec(num_scalar_pr...]
  transfers between devices with their start and end apart: 50 -> 61, of which waited for: 12 -> 20; matrix products, arithmetic and copies ran while one was open for 4% -> 5% of each run, Pallas kernels for 56% -> 61%
where the time goes in v3:
time: 573 us; the launch traced here: 564 us
  Pallas kernels  383 us (67%)
  waiting for transfers between devices  71.5 us (12%)
  starting transfers between devices  56.2 us (10%)
  local copies, waits for them, and re-layouts  36.4 us (6%)
  other arithmetic  12.9 us (2%)
    pallas_call x39, Pallas kernels, run(): pl.pallas_call(body, grid_spec=pltpu.PrefetchScalarGridSpec(num_scalar_pr...  383 us
    ppermute x58, waiting for transfers between devices, swap(): return lax.ppermute(values, axis, [(i, i ^ bit) for i in range(size)])  71.5 us
    ppermute x58, starting transfers between devices, swap(): return lax.ppermute(values, axis, [(i, i ^ bit) for i in range(size)])  55.1 us
    unnamed x133, local copies, waits for them, and re-layouts  20.3 us
  transfers between devices with their start and end apart: 61, of which 20 were waited for; matrix products, arithmetic and copies ran while one was open for 5% of the time, Pallas kernels for 61%

profile of v3, /device:TPU:0, one launch (start us, length us, event | category | flops | bytes accessed | tf_op | source)
XLA Modules:
  0.0 564.0 jit_solution(13897793659045099489)
XLA Ops:
  8.1 9.0 %modulate.1 = (f32[6,8,768]{2,1,0:T(8,128)}, f32[8,768]{1,0:T(8,128)}, bf16[1024,768]{1,0:T(8,128)(2,1)}) custom-call(s32[8]{0:T(128)} %stack.63.refs_0_, f32[8,768]{1,0:T(8,128)} %pad.12.refs_1_.refs_3_, bf16[768,4608]{1,0:T(8,128)(2,1)} %refs_2_.5, bf16[1024,768]{1,0:T(8,128)(2,1)} %refs_4_.2), custom_call_target="tpu_custom_call" | custom-call | flops 1000 | bytes 1000 | tf_op jit(solution)/shard_map/modulate/pallas_call | solution.py:436
  17.7 8.6 %qkv.1.refs_1_.refs_2_.refs_3_ = bf16[1024,2304]{1,0:T(8,128)(2,1)} custom-call(bf16[1024,768]{1,0:T(8,128)(2,1)} %refs_4_.3, f32[6,8,768]{2,1,0:T(8,128)} %get-tuple-element.121.refs_1_.refs_2_.refs_12_.refs_7_.refs_6_, bf16[768,2304]{1,0:T(8,128)(2,1)} %refs_3_.5, bf16[1024,768]{1,0:T(8,128)(2,1)} %touch.19.refs_3_.refs_2_), custom_call_target="tpu_custom_call" | custom-call | flops 1000 | bytes 1000 | tf_op jit(solution)/shard_map/qkv/pallas_call | solution.py:436
  28.3 11.1 %attend.1 = (bf16[1024,768]{1,0:T(8,128)(2,1)}, f32[1024,768]{1,0:T(8,128)}) custom-call(s32[8]{0:T(128)} %stack.63.refs_0_, bf16[1024,2304]{1,0:T(8,128)(2,1)} %qkv.1.refs_1_.refs_2_.refs_3_, bf16[1024,2304]{1,0:T(8,128)(2,1)} %qkv.1.refs_1_.refs_2_.refs_3_, bf16[1024,2304]{1,0:T(8,128)(2,1)} %qkv.1.refs_1_.refs_2_.refs_3_), custom_call_target="tpu_custom_call" | custom-call | flops 1000 | bytes 1000 | tf_op jit(solution)/shard_map/attend/pallas_call | solution.py:436
  39.4 5.9 %middle.1 = (f32[1024,768]{1,0:T(8,128)}, bf16[1024,768]{1,0:T(8,128)(2,1)}) custom-call(bf16[1024,768]{1,0:T(8,128)(2,1)} %get-tuple-element.123.refs_0_.refs_4_.refs_6_, bf16[1024,768]{1,0:T(8,128)(2,1)} %refs_4_.3, f32[6,8,768]{2,1,0:T(8,128)} %get-tuple-element.121.refs_1_.refs_2_.refs_12_.refs_7_.refs_6_, bf16[768,768]{1,0:T(8,128)(2,1)} %refs_13_.1), custom_call_target="tpu_custom_call" | custom-call | flops 1000 | bytes 1000 | tf_op jit(solution)/shard_map/middle/pallas_call | solution.py:436
  45.3 8.6 %collective-permute-start.4 = (bf16[1024,768]{1,0:T(8,128)(2,1)}, bf16[1024,768]{1,0:T(8,128)(2,1)}, u32[]{:S(2)}, u32[]{:S(2)}) collective-permute-start(bf16[1024,768]{1,0:T(8,128)(2,1)} %get-tuple-element.124.refs_3_.refs_1_.refs_8_), channel_id=1, source_target_pairs={{0,2},{2,0},{4,6},{6,4},{8,10},{10,8},{12,14},{14,12},{16,18},{18,... | collective-permute-start | bytes 4718600 | tf_op jit(solution)/shard_map/ppermute | solution.py:1430
  64.8 31.2 %expert.4 = (bf16[4,2,768,384]{3,2,1,0:T(8,128)(2,1)}, bf16[4,2,768,384]{3,2,1,0:T(8,128)(2,1)}, bf16[2,288,768]{2,1,0:T(8,128)(2,1)}, bf16[2,288,768]{2,1,0:T(8,128)(2,1)}, f32[2,1,1024]{2,1,0:T(1,128)}) custom-call(s32[8]{0:T(128)} %stack.63.refs_0_, bf16[1024,768]{1,0:T(8,128)(2,1)} %get-tuple-element.124.refs_3_.refs_1_.refs_8_, ...), custom_call_target="tpu_custom_call" | custom-call | flops 1000 | bytes 1000 | tf_op jit(solution)/shard_map/expert/pallas_call | solution.py:436
  104.0 32.8 %expert.5 = (bf16[4,2,768,384]{3,2,1,0:T(8,128)(2,1)}, bf16[4,2,768,384]{3,2,1,0:T(8,128)(2,1)}, bf16[2,288,768]{2,1,0:T(8,128)(2,1)}, bf16[2,288,768]{2,1,0:T(8,128)(2,1)}, f32[2,1,1024]{2,1,0:T(1,128)}) custom-call(s32[8]{0:T(128)} %stack.63.refs_0_, bf16[1024,768]{1,0:T(8,128)(2,1)} %touch.21.refs_1_, bf16[1024,768]{1,0:T(8,128)(2,1)} %copy-done.7, ...), custom_call_target="tpu_custom_call" | custom-call | flops 1000 | bytes 1000 | tf_op jit(solution)/shard_map/expert/pallas_call | solution.py:436
  138.7 31.1 %expert.6 = (bf16[4,2,768,384]{3,2,1,0:T(8,128)(2,1)}, bf16[4,1,768,384]{3,2,1,0:T(8,128)(2,1)}, bf16[4,1,768,384]{3,2,1,0:T(8,128)(2,1)}, bf16[2,288,768]{2,1,0...) custom-call(s32[8]{0:T(128)} %stack.63.refs_0_, ...), custom_call_target="tpu_custom_call" | custom-call | flops 1000 | bytes 1000 | tf_op jit(solution)/shard_map/expert/pallas_call | solution.py:436
  169.8 32.7 %expert.7 = (bf16[4,2,768,384]{3,2,1,0:T(8,128)(2,1)}, bf16[4,1,768,384]{3,2,1,0:T(8,128)(2,1)}, bf16[4,1,768,384]{3,2,1,0:T(8,128)(2,1)}, bf16[2,288,768]{2,1,0...) custom-call(s32[8]{0:T(128)} %stack.63.refs_0_, bf16[1024,768]{1,0:T(8,128)(2,1)} %touch.21.refs_1_, ...), custom_call_target="tpu_custom_call" | custom-call | flops 1000 | bytes 1000 | tf_op jit(solution)/shard_map/expert/pallas_call | solution.py:436
  202.5 10.1 %combine.2 = (bf16[1024,768]{1,0:T(8,128)(2,1)}, bf16[1024,768]{1,0:T(8,128)(2,1)}, bf16[1024,768]{1,0:T(8,128)(2,1)}, bf16[512,768]{1,0:T(8,128)(2,1)}, bf16[512,768]{1,0:T(8,128)(2,1)}) custom-call(s32[2,1024,128]{2,1,0:T(8,128)} %get-tuple-element.140.refs_0_, bf16[2,288,768]{2,1,0:T(8,128)(2,1)} %get-tuple-element.141.refs_1_, ...), custom_call_target="tpu_custom_call" | custom-call | flops 1000 | bytes 1000 | tf_op jit(solution)/shard_map/combine/pallas_call | solution.py:436
  212.7 10.1 %combine.3 = (bf16[1024,768]{1,0:T(8,128)(2,1)}, bf16[1024,768]{1,0:T(8,128)(2,1)}, bf16[1024,768]{1,0:T(8,128)(2,1)}, bf16[512,768]{1,0:T(8,128)(2,1)}, bf16[512,768]{1,0:T(8,128)(2,1)}) custom-call(s32[2,1024,128]{2,1,0:T(8,128)} %get-tuple-element.135.refs_0_, bf16[2,288,768]{2,1,0:T(8,128)(2,1)} %get-tuple-element.136.refs_1_, ...), custom_call_target="tpu_custom_call" | custom-call | flops 1000 | bytes 1000 | tf_op jit(solution)/shard_map/combine/pallas_call | solution.py:436
  232.2 9.6 %collective-permute-done.10.refs_1_ = bf16[4,2,768,384]{3,2,1,0:T(8,128)(2,1)S(1)} collective-permute-done((bf16[4,2,768,384]{3,2,1,0:T(8,128)(2,1)}, bf16[4,2,768,384]{3,2,1,0:T(8,128)(2,1)S(1)}, u32[]{:S(2)}, u32[]{:S(2)}) %collective-permute-start.10) | collective-permute-done | bytes 4718624 | tf_op jit(solution)/shard_map/ppermute | solution.py:1430
  248.9 7.0 %halve_y.3 = (f32[2,4,384,384]{3,2,1,0:T(8,128)}, bf16[2,4,384,384]{3,2,1,0:T(8,128)(2,1)}) custom-call(bf16[4,2,768,384]{3,2,1,0:T(8,128)(2,1)} %get-tuple-element.147.refs_0_, bf16[4,2,768,384]{3,2,1,0:T(8,128)(2,1)} %copy-done, bf16[4,4,384,384]{3,2,1,0:T(8,128)(2,1)} %bitcast.82, bf16[4,4,384,384]{3,2,1,0:T(8,128)(2,1)} %bitcast.84, ...), custom_call_target="tpu_custom_call" | custom-call | flops 1000 | bytes 1000 | tf_op jit(solution)/shard_map/halve_y/pallas_call | solution.py:436
  261.1 42.8 %shared.1 = (bf16[2,768,768]{2,1,0:T(8,128)(2,1)}, bf16[768,768]{1,0:T(8,128)(2,1)}, bf16[768,768]{1,0:T(8,128)(2,1)}, bf16[2,2,4,192,384]{4,3,2,1,0:T(8,128)(2,...) custom-call(s32[8]{0:T(128)} %stack.63.refs_0_, ...), custom_call_target="tpu_custom_call" | custom-call | flops 1000 | bytes 1000 | tf_op jit(solution)/shard_map/shared/pallas_call | solution.py:436
  309.1 12.8 %middle_back.1 = (f32[1024,768]{1,0:T(8,128)}, bf16[1024,768]{1,0:T(8,128)(2,1)}, bf16[1024,768]{1,0:T(8,128)(2,1)}, f32[3,8,768]{2,1,0:T(8,128)}, f32[16,768]{1,0:T(8,128)}) custom-call(f32[1024,768]{1,0:T(8,128)} %get-tuple-element.163.refs_0_, bf16[1024,768]{1,0:T(8,128)(2,1)} %get-tuple-element.153.refs_5_.refs_1_, bf16[512,768]{1,0:T(8,128)(2,1)} %copy-done.16, ...), custom_call_target="tpu_custom_call" | custom-call | flops 1000 | bytes 1000 | tf_op jit(solution)/shard_map/middle_back/pallas_call | solution.py:436
  336.1 9.0 %halve_slices.1 = (f32[2,1536,384]{2,1,0:T(8,128)}, bf16[2,1536,384]{2,1,0:T(8,128)(2,1)}) custom-call(bf16[2,768,768]{2,1,0:T(8,128)(2,1)} %get-tuple-element.167.refs_0_, bf16[2,1536,384]{2,1,0:T(8,128)(2,1)} %bitcast.103, bf16[768,768]{1,0:T(8,128)(2,1)} %copy-done.29, bf16[768,768]{1,0:T(8,128)(2,1)} %copy-done.30, bf16[1536,384]{1,0:T(8,128)(2,1)} %bitcast.22.refs_4_, ...), custom_call_target="tpu_custom_call" | custom-call | flops 1000 | bytes 1000 | tf_op jit(solution)/shard_map/halve_slices/pallas_call | solution.py:436
  345.9 14.7 %attend_back.1 = (bf16[1024,768]{1,0:T(8,128)(2,1)}, bf16[1024,768]{1,0:T(8,128)(2,1)}, bf16[1024,768]{1,0:T(8,128)(2,1)}) custom-call(s32[8]{0:T(128)} %stack.63.refs_0_, bf16[1024,2304]{1,0:T(8,128)(2,1)} %qkv.1.refs_1_.refs_2_.refs_3_, bf16[1024,2304]{1,0:T(8,128)(2,1)} %qkv.1.refs_1_.refs_2_.refs_3_, bf16[1024,2304]{1,0:T(8,128)(2,1)} %qkv.1.refs_1_.refs_2_.refs_3_, ...), custom_call_target="tpu_custom_call" | custom-call | flops 1000 | bytes 1000 | tf_op jit(solution)/shard_map/attend_back/pallas_call | solution.py:436
  365.2 21.4 %collective-permute-done.28.refs_1_ = bf16[1,4,384,384]{3,2,1,0:T(8,128)(2,1)S(1)} collective-permute-done((bf16[1,4,384,384]{3,2,1,0:T(8,128)(2,1)}, bf16[1,4,384,384]{3,2,1,0:T(8,128)(2,1)S(1)}, u32[]{:S(2)}, u32[]{:S(2)}) %collective-permute-start.28) | collective-permute-done | bytes 1179680 | tf_op jit(solution)/shard_map/ppermute | solution.py:1430
  392.7 14.7 %weight_grads.1 = (bf16[2,768,768]{2,1,0:T(8,128)(2,1)}, bf16[768,768]{1,0:T(8,128)(2,1)}, bf16[768,768]{1,0:T(8,128)(2,1)}) custom-call(s32[8]{0:T(128)} %stack.63.refs_0_, bf16[1024,768]{1,0:T(8,128)(2,1)} %refs_4_.3, f32[6,8,768]{2,1,0:T(8,128)} %get-tuple-element.121.refs_1_.refs_2_.refs_12_.refs_7_.refs_6_, ...), custom_call_target="tpu_custom_call" | custom-call | flops 1000 | bytes 1000 | tf_op jit(solution)/shard_map/weight_grads/pallas_call | solution.py:436
  421.9 7.6 %mixed.1 = (bf16[1024,768]{1,0:T(8,128)(2,1)}, f32[8,768]{1,0:T(8,128)}) custom-call(f32[1024,768]{1,0:T(8,128)} %get-tuple-element.160.refs_0_, bf16[1024,768]{1,0:T(8,128)(2,1)} %get-tuple-element.161.refs_1_, bf16[1024,768]{1,0:T(8,128)(2,1)} %touch.22.refs_1_.refs_2_, bf16[1024,768]{1,0:T(8,128)(2,1)} %touch.24.refs_4_.refs_3_, ...), custom_call_target="tpu_custom_call" | custom-call | flops 1000 | bytes 1000 | tf_op jit(solution)/shard_map/mixed/pallas_call | solution.py:436
  429.5 10.1 %inputs_back.1 = (f32[1024,768]{1,0:T(8,128)}, f32[2,8,768]{2,1,0:T(8,128)}) custom-call(bf16[1024,768]{1,0:T(8,128)(2,1)} %get-tuple-element.179.refs_1_.refs_3_.refs_0_, bf16[1024,768]{1,0:T(8,128)(2,1)} %get-tuple-element.180.refs_4_.refs_1_, bf16[1024,768]{1,0:T(8,128)(2,1)} %get-tuple-element.181.refs_5_.refs_2_, bf16[768,2304]{1,0:T(8,128)(2,1)} %refs_3_.5, ...), custom_call_target="tpu_custom_call" | custom-call | flops 1000 | bytes 1000 | tf_op jit(solution)/shard_map/inputs_back/pallas_call | solution.py:436
  442.0 7.5 %collective-permute-done.36.refs_0_ = bf16[1,4,192,384]{3,2,1,0:T(8,128)(2,1)S(1)} collective-permute-done((bf16[1,4,192,384]{3,2,1,0:T(8,128)(2,1)S(1)}, bf16[1,4,192,384]{3,2,1,0:T(8,128)(2,1)S(1)}, u32[]{:S(2)}, u32[]{:S(2)}) %collective-permute-start.36) | collective-permute-done | bytes 589856 | tf_op jit(solution)/shard_map/ppermute | solution.py:1430
  468.2 9.7 %used_back.1.refs_1_.refs_2_ = f32[8,768]{1,0:T(8,128)} custom-call(s32[8]{0:T(128)} %stack.63.refs_0_, f32[6,8,768]{2,1,0:T(8,128)} %pad_maximum_fusion.8.refs_1_, bf16[768,4608]{1,0:T(8,128)(2,1)} %refs_2_.5, f32[8,768]{1,0:T(8,128)} %pad.12.refs_1_.refs_3_, bf16[2,384,384]{2,1,0:T(8,128)(2,1)} %get-tuple-element.203.refs_4_), custom_call_target="tpu_custom_call" | custom-call | flops 1000 | bytes 1000 | tf_op jit(solution)/shard_map/used_back/pallas_call | solution.py:436
  523.3 8.0 %collective-permute-done.47.refs_0_ = bf16[2,192,384]{2,1,0:T(8,128)(2,1)S(1)} collective-permute-done((bf16[2,192,384]{2,1,0:T(8,128)(2,1)}, bf16[2,192,384]{2,1,0:T(8,128)(2,1)S(1)}, u32[]{:S(2)}, u32[]{:S(2)}) %collective-permute-start.47) | collective-permute-done | bytes 294944 | tf_op jit(solution)/shard_map/ppermute | solution.py:1430
  (342 shorter events, 195.9 us)
Async XLA Ops:
  26.3 37.3 %collective-permute-start.6 = (bf16[1024,768]{1,0:T(8,128)(2,1)S(1)}, bf16[1024,768]{1,0:T(8,128)(2,1)S(1)}, u32[]{:S(2)}, u32[]{:S(2)}) collective-permute-start(bf16[1024,768]{1,0:T(8,128)(2,1)S(1)} %copy-done.1), channel_id=1, source_target_pairs={{0,1},{1,0},{2,3},{3,2},{4,5},{5,4},{6,7},{7,6},{8,9},{9,8},{10,11... | collective-permute-start | bytes 4718600 | tf_op jit(solution)/shard_map/ppermute | solution.py:1430
  53.9 43.2 %collective-permute-start.3 = (bf16[1024,768]{1,0:T(8,128)(2,1)}, bf16[1024,768]{1,0:T(8,128)(2,1)}, u32[]{:S(2)}, u32[]{:S(2)}) collective-permute-start(bf16[1024,768]{1,0:T(8,128)(2,1)} %get-tuple-element.124.refs_3_.refs_1_.refs_8_), channel_id=1, source_target_pairs={{0,1},{1,0},{2,3},{3,2},{4,5},{5,4},{6,7},{7,6},{8,9},{9,8},{10,11... | collective-permute-start | bytes 4718600 | tf_op jit(solution)/shard_map/ppermute | solution.py:1430
  136.8 104.9 %collective-permute-start.10 = (bf16[4,2,768,384]{3,2,1,0:T(8,128)(2,1)}, bf16[4,2,768,384]{3,2,1,0:T(8,128)(2,1)S(1)}, u32[]{:S(2)}, u32[]{:S(2)}) collective-permute-start(bf16[4,2,768,384]{3,2,1,0:T(8,128)(2,1)} %get-tuple-element.148), channel_id=1, source_target_pairs={{0,4},{2,6},{4,0},{6,2},{8,12},{10,14},{12,8},{14,10},{16,20},{18,... | collective-permute-start | bytes 14155784 | tf_op jit(solution)/shard_map/ppermute | solution.py:1430
  222.8 34.9 %collective-permute-start.9 = (bf16[1024,768]{1,0:T(8,128)(2,1)}, bf16[1024,768]{1,0:T(8,128)(2,1)}, u32[]{:S(2)}, u32[]{:S(2)}) collective-permute-start(bf16[1024,768]{1,0:T(8,128)(2,1)} %get-tuple-element.146), channel_id=1, source_target_pairs={{0,2},{2,0},{4,6},{6,4},{8,10},{10,8},{12,14},{14,12},{16,18},{18,... | collective-permute-start | bytes 4718600 | tf_op jit(solution)/shard_map/ppermute | solution.py:1430
  228.6 76.9 %collective-permute-start.25 = (bf16[4,1,768,384]{3,2,1,0:T(8,128)(2,1)}, bf16[4,1,768,384]{3,2,1,0:T(8,128)(2,1)}, u32[]{:S(2)}, u32[]{:S(2)}) collective-permute-start(bf16[4,1,768,384]{3,2,1,0:T(8,128)(2,1)} %get-tuple-element.174), channel_id=1, source_target_pairs={{0,4},{2,6},{4,0},{6,2},{8,12},{10,14},{12,8},{14,10},{16,20},{18,... | collective-permute-start | bytes 7077896 | tf_op jit(solution)/shard_map/ppermute | solution.py:1430
  231.6 28.6 %collective-permute-start.14 = (bf16[512,768]{1,0:T(8,128)(2,1)}, bf16[512,768]{1,0:T(8,128)(2,1)S(1)}, u32[]{:S(2)}, u32[]{:S(2)}) collective-permute-start(bf16[512,768]{1,0:T(8,128)(2,1)} %get-tuple-element.156), channel_id=1, source_target_pairs={{0,2},{2,0},{4,6},{6,4},{8,10},{10,8},{12,14},{14,12},{16,18},{18,... | collective-permute-start | bytes 2359304 | tf_op jit(solution)/shard_map/ppermute | solution.py:1430
  232.0 28.2 %collective-permute-start.15 = (bf16[512,768]{1,0:T(8,128)(2,1)}, bf16[512,768]{1,0:T(8,128)(2,1)}, u32[]{:S(2)}, u32[]{:S(2)}) collective-permute-start(bf16[512,768]{1,0:T(8,128)(2,1)} %get-tuple-element.157), channel_id=1, source_target_pairs={{0,2},{2,0},{4,6},{6,4},{8,10},{10,8},{12,14},{14,12},{16,18},{18,... | collective-permute-start | bytes 2359304 | tf_op jit(solution)/shard_map/ppermute | solution.py:1430
  255.9 51.7 %collective-permute-start.26 = (bf16[2,4,384,384]{3,2,1,0:T(8,128)(2,1)}, bf16[2,4,384,384]{3,2,1,0:T(8,128)(2,1)S(1)}, u32[]{:S(2)}, u32[]{:S(2)}) collective-permute-start(bf16[2,4,384,384]{3,2,1,0:T(8,128)(2,1)} %get-tuple-element.155.refs_1_), channel_id=1, source_target_pairs={{0,8},{2,10},{4,12},{6,14},{8,0},{10,2},{12,4},{14,6},{16,24},{18,... | collective-permute-start | bytes 7077896 | tf_op jit(solution)/shard_map/ppermute | solution.py:1430
  257.7 48.0 %collective-permute-start.20 = (bf16[1024,768]{1,0:T(8,128)(2,1)}, bf16[1024,768]{1,0:T(8,128)(2,1)}, u32[]{:S(2)}, u32[]{:S(2)}) collective-permute-start(bf16[1024,768]{1,0:T(8,128)(2,1)} %get-tuple-element.164), channel_id=1, source_target_pairs={{0,1},{1,0},{2,3},{3,2},{4,5},{5,4},{6,7},{7,6},{8,9},{9,8},{10,11... | collective-permute-start | bytes 4718600 | tf_op jit(solution)/shard_map/ppermute | solution.py:1430
  303.9 56.7 %collective-permute-start.29 = (bf16[4,1,768,384]{3,2,1,0:T(8,128)(2,1)}, bf16[4,1,768,384]{3,2,1,0:T(8,128)(2,1)}, u32[]{:S(2)}, u32[]{:S(2)}) collective-permute-start(bf16[4,1,768,384]{3,2,1,0:T(8,128)(2,1)} %touch.23.refs_5_), channel_id=1, source_target_pairs={{0,4},{2,6},{4,0},{6,2},{8,12},{10,14},{12,8},{14,10},{16,20},{18,... | collective-permute-start | bytes 7077896 | tf_op jit(solution)/shard_map/ppermute | solution.py:1430
  305.5 26.4 %collective-permute-start.22 = (bf16[768,768]{1,0:T(8,128)(2,1)}, bf16[768,768]{1,0:T(8,128)(2,1)S(1)}, u32[]{:S(2)}, u32[]{:S(2)}) collective-permute-start(bf16[768,768]{1,0:T(8,128)(2,1)} %get-tuple-element.170), channel_id=1, source_target_pairs={{0,2},{2,0},{4,6},{6,4},{8,10},{10,8},{12,14},{14,12},{16,18},{18,... | collective-permute-start | bytes 3538952 | tf_op jit(solution)/shard_map/ppermute | solution.py:1430
  305.7 28.9 %collective-permute-start.23 = (bf16[2,4,192,384]{3,2,1,0:T(8,128)(2,1)}, bf16[2,4,192,384]{3,2,1,0:T(8,128)(2,1)}, u32[]{:S(2)}, u32[]{:S(2)}) collective-permute-start(bf16[2,4,192,384]{3,2,1,0:T(8,128)(2,1)} %get-tuple-element.171), channel_id=1, source_target_pairs={{0,2},{2,0},{4,6},{6,4},{8,10},{10,8},{12,14},{14,12},{16,18},{18,... | collective-permute-start | bytes 3538952 | tf_op jit(solution)/shard_map/ppermute | solution.py:1430
  307.0 29.1 %collective-permute-start.24 = (bf16[2,4,192,384]{3,2,1,0:T(8,128)(2,1)}, bf16[2,4,192,384]{3,2,1,0:T(8,128)(2,1)}, u32[]{:S(2)}, u32[]{:S(2)}) collective-permute-start(bf16[2,4,192,384]{3,2,1,0:T(8,128)(2,1)} %get-tuple-element.172), channel_id=1, source_target_pairs={{0,2},{2,0},{4,6},{6,4},{8,10},{10,8},{12,14},{14,12},{16,18},{18,... | collective-permute-start | bytes 3538952 | tf_op jit(solution)/shard_map/ppermute | solution.py:1430
  307.6 53.0 %collective-permute-start.19 = (bf16[1024,768]{1,0:T(8,128)(2,1)S(1)}, bf16[1024,768]{1,0:T(8,128)(2,1)}, u32[]{:S(2)}, u32[]{:S(2)}) collective-permute-start(bf16[1024,768]{1,0:T(8,128)(2,1)S(1)} %copy-done.26), channel_id=1, source_target_pairs={{0,1},{1,0},{2,3},{3,2},{4,5},{5,4},{6,7},{7,6},{8,9},{9,8},{10,11... | collective-permute-start | bytes 4718600 | tf_op jit(solution)/shard_map/ppermute | solution.py:1430
  331.9 59.7 %collective-permute-start.27 = (bf16[2,4,192,384]{3,2,1,0:T(8,128)(2,1)S(1)}, bf16[2,4,192,384]{3,2,1,0:T(8,128)(2,1)S(1)}, u32[]{:S(2)}, u32[]{:S(2)}) collective-permute-start(bf16[2,4,192,384]{3,2,1,0:T(8,128)(2,1)S(1)} %copy-done.31), channel_id=1, source_target_pairs={{0,16},{2,18},{4,20},{6,22},{8,24},{10,26},{12,28},{14,30},{16,0},... | collective-permute-start | bytes 3538952 | tf_op jit(solution)/shard_map/ppermute | solution.py:1430
  334.6 52.0 %collective-permute-start.28 = (bf16[1,4,384,384]{3,2,1,0:T(8,128)(2,1)}, bf16[1,4,384,384]{3,2,1,0:T(8,128)(2,1)S(1)}, u32[]{:S(2)}, u32[]{:S(2)}) collective-permute-start(bf16[1,4,384,384]{3,2,1,0:T(8,128)(2,1)} %get-tuple-element.177.refs_6_), channel_id=1, source_target_pairs={{0,8},{2,10},{4,12},{6,14},{8,0},{10,2},{12,4},{14,6},{16,24},{18,... | collective-permute-start | bytes 3538952 | tf_op jit(solution)/shard_map/ppermute | solution.py:1430
  345.1 65.8 %collective-permute-start.32 = (bf16[2,1536,384]{2,1,0:T(8,128)(2,1)}, bf16[2,1536,384]{2,1,0:T(8,128)(2,1)}, u32[]{:S(2)}, u32[]{:S(2)}) collective-permute-start(bf16[2,1536,384]{2,1,0:T(8,128)(2,1)} %get-tuple-element.178.refs_7_), channel_id=1, source_target_pairs={{0,1},{1,0},{2,3},{3,2},{4,5},{5,4},{6,7},{7,6},{8,9},{9,8},{10,11... | collective-permute-start | bytes 7077896 | tf_op jit(solution)/shard_map/ppermute | solution.py:1430
  409.4 41.0 %collective-permute-start.35 = (bf16[1,4,384,384]{3,2,1,0:T(8,128)(2,1)}, bf16[1,4,384,384]{3,2,1,0:T(8,128)(2,1)S(1)}, u32[]{:S(2)}, u32[]{:S(2)}) collective-permute-start(bf16[1,4,384,384]{3,2,1,0:T(8,128)(2,1)} %get-tuple-element.184.refs_2_), channel_id=1, source_target_pairs={{0,8},{2,10},{4,12},{6,14},{8,0},{10,2},{12,4},{14,6},{16,24},{18,... | collective-permute-start | bytes 3538952 | tf_op jit(solution)/shard_map/ppermute | solution.py:1430
  410.5 38.9 %collective-permute-start.36 = (bf16[1,4,192,384]{3,2,1,0:T(8,128)(2,1)S(1)}, bf16[1,4,192,384]{3,2,1,0:T(8,128)(2,1)S(1)}, u32[]{:S(2)}, u32[]{:S(2)}) collective-permute-start(bf16[1,4,192,384]{3,2,1,0:T(8,128)(2,1)S(1)} %copy-done.41), channel_id=1, source_target_pairs={{0,16},{2,18},{4,20},{6,22},{8,24},{10,26},{12,28},{14,30},{16,0},... | collective-permute-start | bytes 1769480 | tf_op jit(solution)/shard_map/ppermute | solution.py:1430
  415.4 49.8 %collective-permute-start.33 = (bf16[2,768,384]{2,1,0:T(8,128)(2,1)}, bf16[2,768,384]{2,1,0:T(8,128)(2,1)}, u32[]{:S(2)}, u32[]{:S(2)}) collective-permute-start(bf16[2,768,384]{2,1,0:T(8,128)(2,1)} %get-tuple-element.190.refs_3_), channel_id=1, source_target_pairs={{0,4},{2,6},{4,0},{6,2},{8,12},{10,14},{12,8},{14,10},{16,20},{18,... | collective-permute-start | bytes 3538952 | tf_op jit(solution)/shard_map/ppermute | solution.py:1430
  420.7 38.0 %collective-permute-start.34 = (bf16[1,768,768]{2,1,0:T(8,128)(2,1)}, bf16[1,768,768]{2,1,0:T(8,128)(2,1)}, u32[]{:S(2)}, u32[]{:S(2)}) collective-permute-start(bf16[1,768,768]{2,1,0:T(8,128)(2,1)} %get-tuple-element.191.refs_8_), channel_id=1, source_target_pairs={{0,1},{1,0},{2,3},{3,2},{4,5},{5,4},{6,7},{7,6},{8,9},{9,8},{10,11... | collective-permute-start | bytes 3538952 | tf_op jit(solution)/shard_map/ppermute | solution.py:1430
  455.3 28.3 %collective-permute-start.40 = (bf16[1,4,192,384]{3,2,1,0:T(8,128)(2,1)}, bf16[1,4,192,384]{3,2,1,0:T(8,128)(2,1)S(1)}, u32[]{:S(2)}, u32[]{:S(2)}) collective-permute-start(bf16[1,4,192,384]{3,2,1,0:T(8,128)(2,1)} %get-tuple-element.201.refs_2_), channel_id=1, source_target_pairs={{0,16},{2,18},{4,20},{6,22},{8,24},{10,26},{12,28},{14,30},{16,0},... | collective-permute-start | bytes 1769480 | tf_op jit(solution)/shard_map/ppermute | solution.py:1430
  512.2 26.1 %collective-permute-start.46 = (bf16[1,96,768]{2,1,0:T(8,128)(2,1)S(1)}, bf16[1,96,768]{2,1,0:T(8,128)(2,1)}, u32[]{:S(2)}, u32[]{:S(2)}) collective-permute-start(bf16[1,96,768]{2,1,0:T(8,128)(2,1)S(1)} %copy-done.43), channel_id=1, source_target_pairs={{0,16},{2,18},{4,20},{6,22},{8,24},{10,26},{12,28},{14,30},{16,0},... | collective-permute-start | bytes 442376 | tf_op jit(solution)/shard_map/ppermute | solution.py:1430
  522.6 26.8 %collective-permute-start.60 = (bf16[192,768]{1,0:T(8,128)(2,1)}, bf16[192,768]{1,0:T(8,128)(2,1)S(1)}, u32[]{:S(2)}, u32[]{:S(2)}) collective-permute-start(bf16[192,768]{1,0:T(8,128)(2,1)} %get-tuple-element.217.refs_1_), channel_id=1, source_target_pairs={{0,2},{2,0},{4,6},{6,4},{8,10},{10,8},{12,14},{14,12},{16,18},{18,... | collective-permute-start | bytes 884744 | tf_op jit(solution)/shard_map/ppermute | solution.py:1430
  (100 other events, 791.2 us)

commit v4 on v3

--- a/solution.py
+++ b/solution.py
@@ -414,6 +414,15 @@
     return first, second, third
 
 
+def stacked(values):
+    return jnp.concatenate(three_parts(values), 0)
+
+
+def unstacked(product):
+    rows = product.shape[0] // 3
+    return product[:rows] + product[rows : 2 * rows] + product[2 * rows :]
+
+
 def sigmoid(values):
     return 1.0 / (1.0 + jnp.exp(-values))
 
@@ -475,15 +484,12 @@
     return total
 
 
-def modulate_kernel(blocks, pos_ref, emb_ref, ada_ref, cot_ref, mod_ref, act_ref, branch_ref):
+def modulate_kernel(blocks, pos_ref, emb_ref, ada_ref, cot_ref, mod_ref, act_ref, branch_ref, sent_ref):
     emb = emb_ref[...]
     used = jnp.where(pos_ref[LONG] > 0, jnp.broadcast_to(emb[0:1], emb.shape), emb)
     act = used * sigmoid(used)
     act_ref[...] = act
-    weight = ada_ref[...]
-    total = 0.0
-    for part in three_parts(act):
-        total = total + nn(part, weight)
+    total = unstacked(nn(stacked(act), ada_ref[...]))
     mod_ref[0] = total
 
     @pl.when(pl.program_id(0) == pl.num_programs(0) - 1)
@@ -491,17 +497,21 @@
         short = cot_ref.shape[0] // blocks
         for block in range(blocks):
             span = slice(block * short, (block + 1) * short)
-            branch_ref[span, :] = (cot_ref[span, :].astype(F32) * total[block : block + 1]).astype(BF16)
+            branch = (cot_ref[span, :].astype(F32) * total[block : block + 1]).astype(BF16)
+            branch_ref[span, :] = branch
+            sent_ref[span, :] = branch
+        sent_ref[cot_ref.shape[0] :, :] = jnp.zeros((sent_ref.shape[0] - cot_ref.shape[0], cot_ref.shape[1]), BF16)
 
 
 def modulate(pos, emb_pad, ada_weight, cot, blocks):
     rows, width = emb_pad.shape
     pieces = ada_weight.shape[1] // width
+    sent = (cot.shape[0] + 32, width)
     return run(
         functools.partial(modulate_kernel, blocks), (emb_pad, ada_weight, cot), (pieces,),
         [like(emb_pad), pl.BlockSpec((width, width), lambda i, *_: (0, i)), like(cot)],
-        [pl.BlockSpec((1, rows, width), lambda i, *_: (i, 0, 0)), like(emb_pad), like(cot)],
-        [shape((pieces, rows, width), F32), shape((rows, width), F32), shape(cot.shape, BF16)],
+        [pl.BlockSpec((1, rows, width), lambda i, *_: (i, 0, 0)), like(emb_pad), like(cot), full(sent)],
+        [shape((pieces, rows, width), F32), shape((rows, width), F32), shape(cot.shape, BF16), shape(sent, BF16)],
         "modulate", scalars=(pos,),
     )
 
@@ -795,7 +805,7 @@
             expert = pos_ref[FIRST_ALL] + slot
             gate = gate_rows(h_ref[...], routes_ref[...], router_ref[...], expert)
             gate_col = jnp.sum(pick * gate[0:1], -1, keepdims=True)
-            branch = nn(pick_low, b_ref[...])
+            branch = nn(pick_low, b_ref[:rows, :])
             x_s[span, :] = nn(pick_low, h_ref[...]).astype(BF16)
             b_s[span, :] = branch.astype(BF16)
             g_s[span, :] = (branch * gate_col).astype(BF16)
@@ -1212,25 +1222,24 @@
     )
 
 
-def finish_slices_kernel(merged, pos_ref, keep_ref, arrived_ref, *outs):
-    total = total_of(keep_ref[...], arrived_ref[...])
-    up = total[0]
-    if merged:
-        half = up.shape[0] // 2
-        up = jnp.concatenate([up[:half], up[half:]], 1)
-        mine, outs[3][...] = core_halves(pos_ref, jnp.transpose(total[1]))
-        outs[2][...] = mine.astype(BF16)
-    mine, outs[1][...] = core_halves(pos_ref, up)
-    outs[0][...] = mine.astype(BF16)
-
-
-def finish_slices(pos, keep, arrived, merged, after):
-    _, rows, cols = keep.shape
-    dims = [(rows // 4, 2 * cols), (cols // 2, rows)] if merged else [(rows // 2, cols)]
-    outs = [shape(d, BF16) for d in dims for _ in range(2)]
-    return run(
-        functools.partial(finish_slices_kernel, merged), (keep, arrived), (1,), [like(keep), like(arrived)],
-        [like(a) for a in outs], outs, "finish_slices", scalars=(pos,), after=after,
+def finish_slices_kernel(pos_ref, sk_ref, sa_ref, qk_ref, qa_ref, mine_ref, sent_ref, mine_down_ref, sent_down_ref):
+    total = total_of(sk_ref[...], sa_ref[...])
+    half = total.shape[1] // 2
+    up = jnp.concatenate([total[0, :half], total[0, half:]], 1)
+    for at, values in enumerate((total_of(qk_ref[0], qa_ref[0]), up)):
+        mine, sent_ref[at] = core_halves(pos_ref, values)
+        mine_ref[at] = mine.astype(BF16)
+    mine, sent_down_ref[...] = core_halves(pos_ref, jnp.transpose(total[1]))
+    mine_down_ref[...] = mine.astype(BF16)
+
+
+def finish_slices(pos, shared, shared_arrived, queries, queries_arrived, after):
+    _, rows, cols = shared.shape
+    args = (shared, shared_arrived, queries, queries_arrived)
+    outs = [shape((2, rows // 4, 2 * cols), BF16)] * 2 + [shape((cols // 2, rows), BF16)] * 2
+    return run(
+        finish_slices_kernel, args, (1,), [like(a) for a in args], [like(a) for a in outs], outs,
+        "finish_slices", scalars=(pos,), after=after,
     )
 
 
@@ -1248,10 +1257,10 @@
     grad_logits = gates * (grad_gates - inner)
     core = jnp.where(block < pl.num_programs(0) // 2, low_ref[...], high_ref[...])
     grad = gs_ref[...] + ga_ref[...].astype(F32) + core.astype(F32) + gc_ref[...].astype(F32)
-    drouter = 0.0
-    for piece in three_parts(grad_logits):
-        grad = grad + tn(piece, router_ref[...])
-        drouter = drouter + nn(piece, hidden)
+    pieces = stacked(grad_logits)
+    router = router_ref[...]
+    grad = grad + tn(pieces, jnp.concatenate([router] * 3, 0))
+    drouter = unstacked(nn(pieces, hidden))
     branch = branch_ref[...]
     gate_one = mod_ref[2, pl.ds(block, 1), :]
     middle = x_ref[...].astype(F32) + gate_one * branch
@@ -1395,8 +1404,7 @@
     def _():
         out_ref[...] = jnp.zeros_like(out_ref)
 
-    for part in three_parts(gm_ref[0]):
-        out_ref[...] += nt(part, ada_ref[...])
+    out_ref[...] += unstacked(nt(stacked(gm_ref[0]), ada_ref[...]))
 
     @pl.when(piece == pl.num_programs(0) - 1)
     def _():
@@ -1470,12 +1478,13 @@
     routes_t = routes.T
     routes_x = swap(routes_t, "stream", 1)
     routes_near = (routes_t, swap(routes_t, "dp", 1))
-    routes_far = (routes_x, swap(routes_x, "dp", 1))
     emb_pad = jnp.pad(embedding, ((0, 8 - blocks), (0, 0)))
     router_t = jnp.pad(router_weight.T, ((0, 16 - router_weight.shape[1]), (0, 0)))
-    mod, act, branch_grad = modulate(pos, emb_pad, ada_weight, cotangent, blocks)
-    branch_grad = touch(branch_grad, (routes_far[1], routes_near[1]))
-    branch_x = swap(branch_grad, "stream", 1)
+    mod, act, branch_grad, branch_sent = modulate(pos, emb_pad, ada_weight, cotangent, blocks)
+    routes_x = touch(routes_x, (mod,))
+    branch_grad = touch(branch_grad, (routes_x, routes_near[1]))
+    routes_far = (routes_x, swap(routes_x, "dp", 1))
+    branch_x = swap(touch(branch_sent, (branch_grad,)), "stream", 1)
     branches_near = (branch_grad, swap(branch_grad, "dp", 1))
 
     packed = qkv_forward(patches, mod, qkv_weight, blocks, (branch_grad,))
@@ -1486,8 +1495,7 @@
     hidden_x = swap(hidden, "stream", 1)
     hiddens_near = (hidden, swap(hidden, "dp", 1))
     rank_near, cols_near = ranks(pos, routes_near, (hidden,))
-    rank_far, cols_far = ranks(pos, routes_far, (rank_near,))
-    branch_x = touch(branch_x, (rank_far,))
+    branch_x = touch(branch_x, (rank_near,))
     branches_far = (branch_x, swap(branch_x, "dp", 1))
 
     def expert(slot, is_far, sends, prior, after):
@@ -1502,6 +1510,7 @@
     first, first_near = expert(0, False, 1, None, (branch_x,))
     hidden_x = touch(hidden_x, (first_near[2],))
     hiddens_far = (hidden_x, swap(hidden_x, "dp", 1))
+    rank_far, cols_far = ranks(pos, routes_far, (hidden_x,))
     first, first_far = expert(0, True, 1, first, ())
     first_arrived = swap(first[1], "dp", 2)
 
@@ -1513,25 +1522,25 @@
     out_near, out_core, gx_near, gx_core = combine(
         cols_near, [r[:2] for r in (first_near, second_near)], (0, 0), (gx_x,)
     )
-    gx_core = swap_all(gx_core, "dp", 1)
-    out_core = swap(out_core, "dp", 1)
-    gx_sum, out_sum = add_rows(gx_x, gx_xc, out_x, out_xc, (gx_near,))
+    gx_core = [touch(a, (gx_near,)) for a in swap_all(gx_core, "dp", 1)]
+    out_core = touch(swap(out_core, "dp", 1), (gx_near,))
+    near, far = (first_near, second_near), (first_far, second_far)
+    gg_near = [jnp.concatenate([r[2][source] for r in near], 0) for source in range(2)]
+    gg_far = [jnp.concatenate([r[2][source] for r in far], 0) for source in range(2)]
+    gg_back = swap(jnp.concatenate([gg_far[0], swap(gg_far[1], "dp", 1)], 0), "stream", 1)
+    gg_back = touch(gg_back, (gx_near,))
+    gg_rel = jnp.concatenate([gg_near[0], swap(gg_near[1], "dp", 1), gg_back], 0)
+    gx_sum, out_sum = add_rows(gx_x, gx_xc, out_x, out_xc, (gg_back, *gx_core, out_core))
     gx_back = swap(gx_sum, "stream", 1)
     out_back = swap(out_sum, "stream", 1)
     both, up, down = (0, 1), (0,), (1,)
     ea_keep, ea_send = halve_y(first[0], first_arrived, both, (out_sum,))
     ea_arrived = swap(ea_send, "dp", 4)
-    near, far = (first_near, second_near), (first_far, second_far)
-    gg_near = [jnp.concatenate([r[2][source] for r in near], 0) for source in range(2)]
-    gg_far = [jnp.concatenate([r[2][source] for r in far], 0) for source in range(2)]
-    gg_back = swap(jnp.concatenate([gg_far[0], swap(gg_far[1], "dp", 1)], 0), "stream", 1)
-    gg_rel = jnp.concatenate([gg_near[0], swap(gg_near[1], "dp", 1), gg_back], 0)
     order = jnp.arange(4, dtype=jnp.int32) ^ (stream * 2 + core)
     gg = gg_rel.reshape(4, here, rows)[order].reshape(EXPERTS, rows)
     gg = jnp.pad(gg, ((0, 16 - EXPERTS), (0, 0)))
 
-    out_core = touch(out_core, (ea_send,))
-    down_half = touch(second[2], (out_core,))
+    down_half = touch(second[2], (ea_send,))
     down_half_arrived = swap(down_half, "dp", 2)
     up_keep, up_send, down_keep, down_send, shared_out, shared_gx = shared_call(
         pos, hidden, branch_grad, shared_up, shared_down, (down_half, *gx_core, gg)
@@ -1572,61 +1581,69 @@
         return jnp.concatenate([factors, touch(swap(factors, axis, bit), (after,))], 0)
 
     grad_mod = jnp.concatenate([mods_one, mods_two, gate_two[None]], 0)
-    bu_arrived = touch(bu_arrived, (mods_one,))
-    bd_keep, bd_send = halve_z(bd_keep, bd_arrived, down, (bu_arrived,))
+    sh_keep, sh_send = halve(sh_keep, sh_arrived, (mods_one,))
+    sh_arrived = swap(sh_send, "dp", 4)
+    qk_keep, qk_send = halve(qk_keep, qk_arrived, (sh_send,))
+    qk_arrived = swap(qk_send, "dp", 2)
+    bd_keep, bd_send = halve_z(bd_keep, bd_arrived, down, (qk_send,))
     bd_arrived = swap(bd_send, "dp", 8)
-    qk_keep, qk_send = halve(qk_keep, qk_arrived, (bd_send,))
-    qk_arrived = swap(qk_send, "dp", 2)
-    factors = doubled("dp", 8, qk_send)
-    sh_keep, sh_send = halve(sh_keep, sh_arrived, (qk_send,))
-    sh_arrived = swap(sh_send, "dp", 4)
-    grad_embedding = used_backward(pos, grad_mod, ada_weight, emb_pad, blocks, (sh_send,))
+    bu_arrived = touch(bu_arrived, (bd_send,))
+    factors = doubled("dp", 8, bu_arrived)
+    grad_embedding = used_backward(pos, grad_mod, ada_weight, emb_pad, blocks, (bu_arrived,))
     factors = doubled("dp", 4, grad_embedding)
     qk_keep, qk_send = halve(qk_keep, qk_arrived, (grad_embedding,))
     qk_arrived = swap(qk_send, "dp", 4)
-    bd_arrived = touch(bd_arrived, (qk_send,))
-    factors = doubled("dp", 2, bd_arrived)
-    ea_done = finish_kinds(pos, ea_keep, ea_arrived, both, (bd_arrived,))
+    sh_keep, sh_send = halve(sh_keep, sh_arrived, (qk_send,))
+    sh_arrived = swap(sh_send, "dp", 8)
+    factors = doubled("dp", 2, sh_send)
+    ea_done = finish_kinds(pos, ea_keep, ea_arrived, both, (sh_send,))
     qk_keep, qk_send = halve(qk_keep, qk_arrived, (ea_done[1],))
     qk_arrived = swap(qk_send, "dp", 8)
-    factors = doubled("stream", 1, qk_send)
-    sh_keep, sh_send = halve(sh_keep, sh_arrived, (qk_send,))
-    sh_arrived = swap(sh_send, "dp", 8)
-    bu_done = finish_kinds(pos, bu_keep, bu_arrived, up, (sh_send,))
-    bd_done = finish_kinds(pos, bd_keep, bd_arrived, down, (bu_done[1],))
-    factors = doubled("dp", 1, bd_done[1])
+    bd_arrived = touch(bd_arrived, (qk_send,))
+    bu_done = finish_kinds(pos, bu_keep, bu_arrived, up, (bd_arrived,))
+    factors_x = touch(swap(factors, "stream", 1), (bu_done[1],))
+    bd_done = finish_kinds(pos, bd_keep, bd_arrived, down, (factors_x,))
+    bu_others = touch(swap(bu_done[1], "dp", 1), (bd_done[1],))
     ea_others = [touch(swap(a, "dp", 1), (bd_done[1],)) for a in (ea_done[1], ea_done[3])]
-    sh_arrived = touch(sh_arrived, (bd_done[1],))
+    bd_others = touch(swap(bd_done[1], "dp", 1), (bu_others,))
+    done = finish_slices(
+        pos, sh_keep, sh_arrived, qk_keep, qk_arrived, (bu_others, bd_others, *ea_others)
+    )
+    pieces = [factors, factors_x, swap(factors, "dp", 1), swap(factors_x, "dp", 1)]
+
+    pieces[:2] = [touch(a, (done[0],)) for a in pieces[:2]]
+    ea_others = [touch(a, (done[0],)) for a in ea_others]
+
+    def slices_out(mine, send):
+        near = in_order(core, mine, swap(send, "dp", 1), mine.ndim - 1)
+        far = in_order(core, swap(mine, "stream", 1), swap_across(send), mine.ndim - 1)
+        return in_order(stream, near, far, mine.ndim - 1).astype(F32)
+
+    rows_out = slices_out(*done[:2])
+    grad_qkv_out, grad_shared_up = rows_out[0], rows_out[1]
+    grad_shared_down = slices_out(*done[2:])
 
     share = width // dp_size
 
     def own_share(values):
         return lax.dynamic_slice_in_dim(values, dp * share, share, 1)
 
-    wide = 7 * width
-    acts = own_share(factors[:, :width])
-    grad_ada = lax.dot_general(acts, factors[:, width:wide], (((0,), (0,)), ((), ())), preferred_element_type=F32)
-    drouter_sum = jnp.sum(factors[:, wide:].astype(F32).reshape(-1, blocks, 2 * width), 0)
+    grad_ada, drouter_sum = 0.0, 0.0
+    for piece in pieces:
+        acts = own_share(piece[:, :width])
+        grad_ada = grad_ada + lax.dot_general(
+            acts, piece[:, width : 7 * width], (((0,), (0,)), ((), ())), preferred_element_type=F32
+        )
+        drouter_sum = drouter_sum + jnp.sum(piece[:, 7 * width :].astype(F32).reshape(-1, blocks, 2 * width), 0)
     grad_router = own_share(drouter_sum.reshape(EXPERTS, width)).T
-
-    qk_done = finish_slices(pos, qk_keep, qk_arrived, False, (grad_ada, sh_arrived, *ea_others))
-    bu_others = touch(swap(bu_done[1], "dp", 1), (qk_done[1],))
-    bd_others = touch(swap(bd_done[1], "dp", 1), (qk_done[1],))
-    sh_done = finish_slices(pos, sh_keep, sh_arrived, True, (qk_done[1],))
 
     def experts_out(one, two, one_other, two_other):
         mine, others = jnp.stack([one, two]), jnp.stack([one_other, two_other]).astype(F32)
         return in_order(core, mine, others, 0)
 
-    def slices_out(mine, send):
-        near = in_order(core, mine, swap(send, "dp", 1), 1)
-        far = in_order(core, swap(mine, "stream", 1), swap_across(send), 1)
-        return in_order(stream, near, far, 1).astype(F32)
-
-    grad_qkv_out = slices_out(*qk_done)
     return (
         mixed, grad_patches, grad_embedding[:blocks], grad_ada, grad_qkv_out[:, : 3 * width],
-        grad_qkv_out[:, 3 * width :], slices_out(*sh_done[:2]), slices_out(*sh_done[2:]), grad_router,
+        grad_qkv_out[:, 3 * width :], grad_shared_up, grad_shared_down, grad_router,
         experts_out(ea_done[0], bu_done[0], ea_others[0], bu_others),
         experts_out(ea_done[2], bd_done[0], ea_others[1], bd_others),
     )

time: 573 us -> 553 us (0.965)
  waiting for transfers between devices: 71.5 us -> 45 us
  Pallas kernels: 383 us -> 409 us
  starting transfers between devices: 56.2 us -> 42.4 us
    ppermute x58 -> x57, waiting for transfers between devices: 71.5 us -> 45 us  [swap(): return lax.ppermute(values, axis, [(i, i ^ bit) for i in range(size)])]
    pallas_call x39 -> x38, Pallas kernels: 383 us -> 409 us  [run(): pl.pallas_call(body, grid_spec=pltpu.PrefetchScalarGridSpec(num_scalar_pr...]
    ppermute x58 -> x57, starting transfers between devices: 55.1 us -> 41.8 us  [swap(): return lax.ppermute(values, axis, [(i, i ^ bit) for i in range(size)])]
    concatenate x2 -> x0, local copies, waits for them, and re-layouts: 9.22 us -> none  [doubled(): jnp.concatenate([factors, touch(swap(factors, axis, bit), (after,))], 0)]
    unnamed x133 -> x143, local copies, waits for them, and re-layouts: 20.3 us -> 21.3 us
  transfers between devices with their start and end apart: 61 -> 59, of which waited for: 20 -> 17; matrix products, arithmetic and copies ran while one was open for 5% -> 4% of each run, Pallas kernels for 61% -> 69%
where the time goes in v4:
time: 553 us; the launch traced here: 545 us
  Pallas kernels  409 us (74%)
  waiting for transfers between devices  45 us (8%)
  starting transfers between devices  42.4 us (8%)
  local copies, waits for them, and re-layouts  31.4 us (6%)
  other arithmetic  12.1 us (2%)
    pallas_call x38, Pallas kernels, run(): pl.pallas_call(body, grid_spec=pltpu.PrefetchScalarGridSpec(num_scalar_pr...  409 us
    ppermute x57, waiting for transfers between devices, swap(): return lax.ppermute(values, axis, [(i, i ^ bit) for i in range(size)])  45 us
    ppermute x57, starting transfers between devices, swap(): return lax.ppermute(values, axis, [(i, i ^ bit) for i in range(size)])  41.8 us
    unnamed x143, local copies, waits for them, and re-layouts  21.3 us
  transfers between devices with their start and end apart: 59, of which 17 were waited for; matrix products, arithmetic and copies ran while one was open for 4% of the time, Pallas kernels for 69%

profile of v4, /device:TPU:0, one launch (start us, length us, event | category | flops | bytes accessed | tf_op | source)
XLA Modules:
  0.0 544.5 jit_solution(17640243090108659521)
XLA Ops:
  6.2 8.7 %modulate.1 = (f32[6,8,768]{2,1,0:T(8,128)}, f32[8,768]{1,0:T(8,128)}, bf16[1024,768]{1,0:T(8,128)(2,1)}, bf16[1056,768]{1,0:T(8,128)(2,1)}) custom-call(s32[8]{0:T(128)} %stack.63.refs_0_, f32[8,768]{1,0:T(8,128)} %pad.12.refs_1_.refs_3_, bf16[768,4608]{1,0:T(8,128)(2,1)} %refs_2_.5, bf16[1024,768]{1,0:T(8,128)(2,1)} %refs_4_.2), custom_call_target="tpu_custom_call" | custom-call | flops 1000 | bytes 1000 | tf_op jit(solution)/shard_map/modulate/pallas_call | solution.py:445
  16.3 8.5 %qkv.1.refs_1_.refs_2_.refs_3_ = bf16[1024,2304]{1,0:T(8,128)(2,1)} custom-call(bf16[1024,768]{1,0:T(8,128)(2,1)} %refs_4_.3, f32[6,8,768]{2,1,0:T(8,128)} %get-tuple-element.120.refs_1_.refs_2_.refs_12_.refs_7_.refs_6_, bf16[768,2304]{1,0:T(8,128)(2,1)} %refs_3_.5, bf16[1024,768]{1,0:T(8,128)(2,1)} %touch.27.refs_3_.refs_1_.refs_2_), custom_call_target="tpu_custom_call" | custom-call | flops 1000 | bytes 1000 | tf_op jit(solution)/shard_map/qkv/pallas_call | solution.py:445
  24.8 19.4 %attend.1 = (bf16[1024,768]{1,0:T(8,128)(2,1)}, f32[1024,768]{1,0:T(8,128)}) custom-call(s32[8]{0:T(128)} %stack.63.refs_0_, bf16[1024,2304]{1,0:T(8,128)(2,1)} %qkv.1.refs_1_.refs_2_.refs_3_, bf16[1024,2304]{1,0:T(8,128)(2,1)} %qkv.1.refs_1_.refs_2_.refs_3_, bf16[1024,2304]{1,0:T(8,128)(2,1)} %qkv.1.refs_1_.refs_2_.refs_3_), custom_call_target="tpu_custom_call" | custom-call | flops 1000 | bytes 1000 | tf_op jit(solution)/shard_map/attend/pallas_call | solution.py:445
  44.2 6.0 %middle.1 = (f32[1024,768]{1,0:T(8,128)}, bf16[1024,768]{1,0:T(8,128)(2,1)}) custom-call(bf16[1024,768]{1,0:T(8,128)(2,1)} %get-tuple-element.122.refs_0_.refs_4_.refs_6_, bf16[1024,768]{1,0:T(8,128)(2,1)} %refs_4_.3, f32[6,8,768]{2,1,0:T(8,128)} %get-tuple-element.120.refs_1_.refs_2_.refs_12_.refs_7_.refs_6_, bf16[768,768]{1,0:T(8,128)(2,1)} %refs_13_.1), custom_call_target="tpu_custom_call" | custom-call | flops 1000 | bytes 1000 | tf_op jit(solution)/shard_map/middle/pallas_call | solution.py:445
  57.0 31.2 %expert.4 = (bf16[4,2,768,384]{3,2,1,0:T(8,128)(2,1)}, bf16[4,2,768,384]{3,2,1,0:T(8,128)(2,1)}, bf16[2,288,768]{2,1,0:T(8,128)(2,1)}, bf16[2,288,768]{2,1,0:T(8,128)(2,1)}, f32[2,1,1024]{2,1,0:T(1,128)}) custom-call(s32[8]{0:T(128)} %stack.63.refs_0_, bf16[1024,768]{1,0:T(8,128)(2,1)} %get-tuple-element.123.refs_3_.refs_1_.refs_8_, ...), custom_call_target="tpu_custom_call" | custom-call | flops 1000 | bytes 1000 | tf_op jit(solution)/shard_map/expert/pallas_call | solution.py:445
  97.0 32.8 %expert.5 = (bf16[4,2,768,384]{3,2,1,0:T(8,128)(2,1)}, bf16[4,2,768,384]{3,2,1,0:T(8,128)(2,1)}, bf16[2,288,768]{2,1,0:T(8,128)(2,1)}, bf16[2,288,768]{2,1,0:T(8,128)(2,1)}, f32[2,1,1024]{2,1,0:T(1,128)}) custom-call(s32[8]{0:T(128)} %stack.63.refs_0_, bf16[1024,768]{1,0:T(8,128)(2,1)} %touch.30.refs_3_.refs_1_, bf16[1024,768]{1,0:T(8,128)(2,1)} %copy-done.12, ...), custom_call_target="tpu_custom_call" | custom-call | flops 1000 | bytes 1000 | tf_op jit(solution)/shard_map/expert/pallas_call | solution.py:445
  132.3 31.1 %expert.6 = (bf16[4,2,768,384]{3,2,1,0:T(8,128)(2,1)}, bf16[4,1,768,384]{3,2,1,0:T(8,128)(2,1)}, bf16[4,1,768,384]{3,2,1,0:T(8,128)(2,1)}, bf16[2,288,768]{2,1,0...) custom-call(s32[8]{0:T(128)} %stack.63.refs_0_, ...), custom_call_target="tpu_custom_call" | custom-call | flops 1000 | bytes 1000 | tf_op jit(solution)/shard_map/expert/pallas_call | solution.py:445
  163.4 32.8 %expert.7 = (bf16[4,2,768,384]{3,2,1,0:T(8,128)(2,1)}, bf16[4,1,768,384]{3,2,1,0:T(8,128)(2,1)}, bf16[4,1,768,384]{3,2,1,0:T(8,128)(2,1)}, bf16[2,288,768]{2,1,0...) custom-call(s32[8]{0:T(128)} %stack.63.refs_0_, bf16[1024,768]{1,0:T(8,128)(2,1)} %touch.30.refs_3_.refs_1_, ...), custom_call_target="tpu_custom_call" | custom-call | flops 1000 | bytes 1000 | tf_op jit(solution)/shard_map/expert/pallas_call | solution.py:445
  196.2 10.1 %combine.2 = (bf16[1024,768]{1,0:T(8,128)(2,1)}, bf16[1024,768]{1,0:T(8,128)(2,1)}, bf16[1024,768]{1,0:T(8,128)(2,1)}, bf16[512,768]{1,0:T(8,128)(2,1)}, bf16[512,768]{1,0:T(8,128)(2,1)}) custom-call(s32[2,1024,128]{2,1,0:T(8,128)} %get-tuple-element.137.refs_0_, bf16[2,288,768]{2,1,0:T(8,128)(2,1)} %get-tuple-element.138.refs_1_, ...), custom_call_target="tpu_custom_call" | custom-call | flops 1000 | bytes 1000 | tf_op jit(solution)/shard_map/combine/pallas_call | solution.py:445
  206.3 10.1 %combine.3 = (bf16[1024,768]{1,0:T(8,128)(2,1)}, bf16[1024,768]{1,0:T(8,128)(2,1)}, bf16[1024,768]{1,0:T(8,128)(2,1)}, bf16[512,768]{1,0:T(8,128)(2,1)}, bf16[512,768]{1,0:T(8,128)(2,1)}) custom-call(s32[2,1024,128]{2,1,0:T(8,128)} %get-tuple-element.148.refs_0_, bf16[2,288,768]{2,1,0:T(8,128)(2,1)} %get-tuple-element.149.refs_1_, ...), custom_call_target="tpu_custom_call" | custom-call | flops 1000 | bytes 1000 | tf_op jit(solution)/shard_map/combine/pallas_call | solution.py:445
  229.3 5.4 add_rows.1
  235.5 7.0 %halve_y.3 = (f32[2,4,384,384]{3,2,1,0:T(8,128)}, bf16[2,4,384,384]{3,2,1,0:T(8,128)(2,1)}) custom-call(bf16[4,2,768,384]{3,2,1,0:T(8,128)(2,1)} %get-tuple-element.135.refs_0_, bf16[4,2,768,384]{3,2,1,0:T(8,128)(2,1)} %collective-permute-done.9.refs_1_, bf16[4,4,384,384]{3,2,1,0:T(8,128)(2,1)} %bitcast.86, ...), custom_call_target="tpu_custom_call" | custom-call | flops 1000 | bytes 1000 | tf_op jit(solution)/shard_map/halve_y/pallas_call | solution.py:445
  247.1 42.8 %shared.1 = (bf16[2,768,768]{2,1,0:T(8,128)(2,1)}, bf16[768,768]{1,0:T(8,128)(2,1)}, bf16[768,768]{1,0:T(8,128)(2,1)}, bf16[2,2,4,192,384]{4,3,2,1,0:T(8,128)(2,...) custom-call(s32[8]{0:T(128)} %stack.63.refs_0_, ...), custom_call_target="tpu_custom_call" | custom-call | flops 1000 | bytes 1000 | tf_op jit(solution)/shard_map/shared/pallas_call | solution.py:445
  297.1 12.0 %middle_back.1 = (f32[1024,768]{1,0:T(8,128)}, bf16[1024,768]{1,0:T(8,128)(2,1)}, bf16[1024,768]{1,0:T(8,128)(2,1)}, f32[3,8,768]{2,1,0:T(8,128)}, f32[16,768]{1,0:T(8,128)}) custom-call(f32[1024,768]{1,0:T(8,128)} %get-tuple-element.163.refs_0_, bf16[1024,768]{1,0:T(8,128)(2,1)} %get-tuple-element.153.refs_1_, bf16[512,768]{1,0:T(8,128)(2,1)} %touch.32.refs_6_.refs_2_, ...), custom_call_target="tpu_custom_call" | custom-call | flops 1000 | bytes 1000 | tf_op jit(solution)/shard_map/middle_back/pallas_call | solution.py:445
  309.2 5.3 halve_z.3
  322.6 9.0 %halve_slices.1 = (f32[2,1536,384]{2,1,0:T(8,128)}, bf16[2,1536,384]{2,1,0:T(8,128)(2,1)}) custom-call(bf16[2,768,768]{2,1,0:T(8,128)(2,1)} %get-tuple-element.167.refs_0_, bf16[2,1536,384]{2,1,0:T(8,128)(2,1)} %bitcast.107, bf16[768,768]{1,0:T(8,128)(2,1)} %copy-done.28, bf16[768,768]{1,0:T(8,128)(2,1)} %copy-done.29, bf16[1536,384]{1,0:T(8,128)(2,1)} %bitcast.112, ...), custom_call_target="tpu_custom_call" | custom-call | flops 1000 | bytes 1000 | tf_op jit(solution)/shard_map/halve_slices/pallas_call | solution.py:445
  333.0 36.6 %attend_back.1 = (bf16[1024,768]{1,0:T(8,128)(2,1)}, bf16[1024,768]{1,0:T(8,128)(2,1)}, bf16[1024,768]{1,0:T(8,128)(2,1)}) custom-call(s32[8]{0:T(128)} %stack.63.refs_0_, bf16[1024,2304]{1,0:T(8,128)(2,1)} %qkv.1.refs_1_.refs_2_.refs_3_, bf16[1024,2304]{1,0:T(8,128)(2,1)} %qkv.1.refs_1_.refs_2_.refs_3_, bf16[1024,2304]{1,0:T(8,128)(2,1)} %qkv.1.refs_1_.refs_2_.refs_3_, ...), custom_call_target="tpu_custom_call" | custom-call | flops 1000 | bytes 1000 | tf_op jit(solution)/shard_map/attend_back/pallas_call | solution.py:445
  379.2 14.7 %weight_grads.1 = (bf16[2,768,768]{2,1,0:T(8,128)(2,1)}, bf16[768,768]{1,0:T(8,128)(2,1)}, bf16[768,768]{1,0:T(8,128)(2,1)}) custom-call(s32[8]{0:T(128)} %stack.63.refs_0_, bf16[1024,768]{1,0:T(8,128)(2,1)} %refs_4_.3, f32[6,8,768]{2,1,0:T(8,128)} %get-tuple-element.120.refs_1_.refs_2_.refs_12_.refs_7_.refs_6_, ...), custom_call_target="tpu_custom_call" | custom-call | flops 1000 | bytes 1000 | tf_op jit(solution)/shard_map/weight_grads/pallas_call | solution.py:445
  407.9 7.6 %mixed.1 = (bf16[1024,768]{1,0:T(8,128)(2,1)}, f32[8,768]{1,0:T(8,128)}) custom-call(f32[1024,768]{1,0:T(8,128)} %get-tuple-element.160.refs_0_, bf16[1024,768]{1,0:T(8,128)(2,1)} %get-tuple-element.161.refs_1_, bf16[1024,768]{1,0:T(8,128)(2,1)} %touch.34.refs_8_.refs_2_, bf16[1024,768]{1,0:T(8,128)(2,1)} %touch.36.refs_4_.refs_3_, ...), custom_call_target="tpu_custom_call" | custom-call | flops 1000 | bytes 1000 | tf_op jit(solution)/shard_map/mixed/pallas_call | solution.py:445
  415.5 10.1 %inputs_back.1 = (f32[1024,768]{1,0:T(8,128)}, f32[2,8,768]{2,1,0:T(8,128)}) custom-call(bf16[1024,768]{1,0:T(8,128)(2,1)} %get-tuple-element.179.refs_1_.refs_3_.refs_0_, bf16[1024,768]{1,0:T(8,128)(2,1)} %get-tuple-element.180.refs_4_.refs_1_, bf16[1024,768]{1,0:T(8,128)(2,1)} %get-tuple-element.181.refs_5_.refs_2_, bf16[768,2304]{1,0:T(8,128)(2,1)} %refs_3_.5, ...), custom_call_target="tpu_custom_call" | custom-call | flops 1000 | bytes 1000 | tf_op jit(solution)/shard_map/inputs_back/pallas_call | solution.py:445
  450.6 7.3 %used_back.1.refs_1_.refs_2_ = f32[8,768]{1,0:T(8,128)} custom-call(s32[8]{0:T(128)} %stack.63.refs_0_, f32[6,8,768]{2,1,0:T(8,128)} %pad_maximum_fusion.10.refs_1_, bf16[768,4608]{1,0:T(8,128)(2,1)} %refs_2_.5, f32[8,768]{1,0:T(8,128)} %pad.12.refs_1_.refs_3_, bf16[1,4,192,384]{3,2,1,0:T(8,128)(2,1)} %touch.38.refs_4_.refs_1_.refs_2_), custom_call_target="tpu_custom_call" | custom-call | flops 1000 | bytes 1000 | tf_op jit(solution)/shard_map/used_back/pallas_call | solution.py:445
  474.5 5.6 %finish_kinds.3 = (f32[48,3072]{1,0:T(8,128)}, bf16[48,3072]{1,0:T(8,128)(2,1)}, f32[192,768]{1,0:T(8,128)}, bf16[192,768]{1,0:T(8,128)(2,1)}) custom-call(s32[8]{0:T(128)} %stack.63.refs_0_, f32[2,4,192,384]{3,2,1,0:T(8,128)} %get-tuple-element.212.refs_1_.refs_3_, bf16[2,4,192,384]{3,2,1,0:T(8,128)(2,1)} %touch.37.refs_8_.refs_2_.refs_4_, ...), custom_call_target="tpu_custom_call" | custom-call | flops 1000 | bytes 1000 | tf_op jit(solution)/shard_map/finish_kinds/pallas_call | solution.py:445
  481.0 11.1 %collective-permute-done.43 = bf16[1,192,768]{2,1,0:T(8,128)(2,1)} collective-permute-done((bf16[1,192,768]{2,1,0:T(8,128)(2,1)}, bf16[1,192,768]{2,1,0:T(8,128)(2,1)}, u32[]{:S(2)}, u32[]{:S(2)}) %collective-permute-start.43) | collective-permute-done | bytes 294944 | tf_op jit(solution)/shard_map/ppermute | solution.py:1438
  528.4 6.4 %collective-permute-done.57 = bf16[192,192]{1,0:T(8,128)(2,1)S(1)} collective-permute-done((bf16[192,192]{1,0:T(8,128)(2,1)S(1)}, bf16[192,192]{1,0:T(8,128)(2,1)S(1)}, u32[]{:S(2)}, u32[]{:S(2)}) %collective-permute-start.57) | collective-permute-done | bytes 73760 | tf_op jit(solution)/shard_map/ppermute | solution.py:1438
  (367 shorter events, 170.3 us)
Async XLA Ops:
  16.2 38.3 %collective-permute-start.5 = (bf16[1056,768]{1,0:T(8,128)(2,1)}, bf16[1056,768]{1,0:T(8,128)(2,1)S(1)}, u32[]{:S(2)}, u32[]{:S(2)}) collective-permute-start(bf16[1056,768]{1,0:T(8,128)(2,1)} %touch.28), channel_id=1, source_target_pairs={{0,1},{1,0},{2,3},{3,2},{4,5},{5,4},{6,7},{7,6},{8,9},{9,8},{10,11... | collective-permute-start | bytes 4866056 | tf_op jit(solution)/shard_map/ppermute | solution.py:1438
  50.7 37.5 %collective-permute-start.2 = (bf16[1024,768]{1,0:T(8,128)(2,1)}, bf16[1024,768]{1,0:T(8,128)(2,1)}, u32[]{:S(2)}, u32[]{:S(2)}) collective-permute-start(bf16[1024,768]{1,0:T(8,128)(2,1)} %get-tuple-element.123.refs_3_.refs_1_.refs_8_), channel_id=1, source_target_pairs={{0,1},{1,0},{2,3},{3,2},{4,5},{5,4},{6,7},{7,6},{8,9},{9,8},{10,11... | collective-permute-start | bytes 4718600 | tf_op jit(solution)/shard_map/ppermute | solution.py:1438
  55.6 39.7 %collective-permute-start.7 = (bf16[1056,768]{1,0:T(8,128)(2,1)}, bf16[1056,768]{1,0:T(8,128)(2,1)S(1)}, u32[]{:S(2)}, u32[]{:S(2)}) collective-permute-start(bf16[1056,768]{1,0:T(8,128)(2,1)} %touch.29.refs_11_.refs_3_), channel_id=1, source_target_pairs={{0,2},{2,0},{4,6},{6,4},{8,10},{10,8},{12,14},{14,12},{16,18},{18,... | collective-permute-start | bytes 4866056 | tf_op jit(solution)/shard_map/ppermute | solution.py:1438
  129.8 105.7 %collective-permute-start.9 = (bf16[4,2,768,384]{3,2,1,0:T(8,128)(2,1)}, bf16[4,2,768,384]{3,2,1,0:T(8,128)(2,1)}, u32[]{:S(2)}, u32[]{:S(2)}) collective-permute-start(bf16[4,2,768,384]{3,2,1,0:T(8,128)(2,1)} %get-tuple-element.136), channel_id=1, source_target_pairs={{0,4},{2,6},{4,0},{6,2},{8,12},{10,14},{12,8},{14,10},{16,20},{18,... | collective-permute-start | bytes 14155784 | tf_op jit(solution)/shard_map/ppermute | solution.py:1438
  224.1 67.6 %collective-permute-start.25 = (bf16[4,1,768,384]{3,2,1,0:T(8,128)(2,1)}, bf16[4,1,768,384]{3,2,1,0:T(8,128)(2,1)}, u32[]{:S(2)}, u32[]{:S(2)}) collective-permute-start(bf16[4,1,768,384]{3,2,1,0:T(8,128)(2,1)} %get-tuple-element.174), channel_id=1, source_target_pairs={{0,4},{2,6},{4,0},{6,2},{8,12},{10,14},{12,8},{14,10},{16,20},{18,... | collective-permute-start | bytes 7077896 | tf_op jit(solution)/shard_map/ppermute | solution.py:1438
  234.7 57.1 %collective-permute-start.20 = (bf16[1024,768]{1,0:T(8,128)(2,1)}, bf16[1024,768]{1,0:T(8,128)(2,1)}, u32[]{:S(2)}, u32[]{:S(2)}) collective-permute-start(bf16[1024,768]{1,0:T(8,128)(2,1)} %get-tuple-element.164), channel_id=1, source_target_pairs={{0,1},{1,0},{2,3},{3,2},{4,5},{5,4},{6,7},{7,6},{8,9},{9,8},{10,11... | collective-permute-start | bytes 4718600 | tf_op jit(solution)/shard_map/ppermute | solution.py:1438
  242.5 53.2 %collective-permute-start.26 = (bf16[2,4,384,384]{3,2,1,0:T(8,128)(2,1)}, bf16[2,4,384,384]{3,2,1,0:T(8,128)(2,1)S(1)}, u32[]{:S(2)}, u32[]{:S(2)}) collective-permute-start(bf16[2,4,384,384]{3,2,1,0:T(8,128)(2,1)} %get-tuple-element.158.refs_1_), channel_id=1, source_target_pairs={{0,8},{2,10},{4,12},{6,14},{8,0},{10,2},{12,4},{14,6},{16,24},{18,... | collective-permute-start | bytes 7077896 | tf_op jit(solution)/shard_map/ppermute | solution.py:1438
  290.2 79.4 %collective-permute-start.29 = (bf16[4,1,768,384]{3,2,1,0:T(8,128)(2,1)}, bf16[4,1,768,384]{3,2,1,0:T(8,128)(2,1)}, u32[]{:S(2)}, u32[]{:S(2)}) collective-permute-start(bf16[4,1,768,384]{3,2,1,0:T(8,128)(2,1)} %touch.35.refs_5_), channel_id=1, source_target_pairs={{0,4},{2,6},{4,0},{6,2},{8,12},{10,14},{12,8},{14,10},{16,20},{18,... | collective-permute-start | bytes 7077896 | tf_op jit(solution)/shard_map/ppermute | solution.py:1438
  291.7 27.3 %collective-permute-start.22 = (bf16[768,768]{1,0:T(8,128)(2,1)}, bf16[768,768]{1,0:T(8,128)(2,1)S(1)}, u32[]{:S(2)}, u32[]{:S(2)}) collective-permute-start(bf16[768,768]{1,0:T(8,128)(2,1)} %get-tuple-element.170), channel_id=1, source_target_pairs={{0,2},{2,0},{4,6},{6,4},{8,10},{10,8},{12,14},{14,12},{16,18},{18,... | collective-permute-start | bytes 3538952 | tf_op jit(solution)/shard_map/ppermute | solution.py:1438
  291.8 29.6 %collective-permute-start.23 = (bf16[2,4,192,384]{3,2,1,0:T(8,128)(2,1)}, bf16[2,4,192,384]{3,2,1,0:T(8,128)(2,1)S(1)}, u32[]{:S(2)}, u32[]{:S(2)}) collective-permute-start(bf16[2,4,192,384]{3,2,1,0:T(8,128)(2,1)} %get-tuple-element.171), channel_id=1, source_target_pairs={{0,2},{2,0},{4,6},{6,4},{8,10},{10,8},{12,14},{14,12},{16,18},{18,... | collective-permute-start | bytes 3538952 | tf_op jit(solution)/shard_map/ppermute | solution.py:1438
  293.1 29.6 %collective-permute-start.24 = (bf16[2,4,192,384]{3,2,1,0:T(8,128)(2,1)}, bf16[2,4,192,384]{3,2,1,0:T(8,128)(2,1)}, u32[]{:S(2)}, u32[]{:S(2)}) collective-permute-start(bf16[2,4,192,384]{3,2,1,0:T(8,128)(2,1)} %get-tuple-element.172), channel_id=1, source_target_pairs={{0,2},{2,0},{4,6},{6,4},{8,10},{10,8},{12,14},{14,12},{16,18},{18,... | collective-permute-start | bytes 3538952 | tf_op jit(solution)/shard_map/ppermute | solution.py:1438
  295.7 73.9 %collective-permute-start.19 = (bf16[1024,768]{1,0:T(8,128)(2,1)S(1)}, bf16[1024,768]{1,0:T(8,128)(2,1)}, u32[]{:S(2)}, u32[]{:S(2)}) collective-permute-start(bf16[1024,768]{1,0:T(8,128)(2,1)S(1)} %copy-done.26), channel_id=1, source_target_pairs={{0,1},{1,0},{2,3},{3,2},{4,5},{5,4},{6,7},{7,6},{8,9},{9,8},{10,11... | collective-permute-start | bytes 4718600 | tf_op jit(solution)/shard_map/ppermute | solution.py:1438
  319.0 59.2 %collective-permute-start.27 = (bf16[2,4,192,384]{3,2,1,0:T(8,128)(2,1)}, bf16[2,4,192,384]{3,2,1,0:T(8,128)(2,1)S(1)}, u32[]{:S(2)}, u32[]{:S(2)}) collective-permute-start(bf16[2,4,192,384]{3,2,1,0:T(8,128)(2,1)} %get-tuple-element.176.refs_2_), channel_id=1, source_target_pairs={{0,16},{2,18},{4,20},{6,22},{8,24},{10,26},{12,28},{14,30},{16,0},... | collective-permute-start | bytes 3538952 | tf_op jit(solution)/shard_map/ppermute | solution.py:1438
  321.4 52.8 %collective-permute-start.28 = (bf16[1,4,384,384]{3,2,1,0:T(8,128)(2,1)}, bf16[1,4,384,384]{3,2,1,0:T(8,128)(2,1)}, u32[]{:S(2)}, u32[]{:S(2)}) collective-permute-start(bf16[1,4,384,384]{3,2,1,0:T(8,128)(2,1)} %get-tuple-element.177.refs_6_), channel_id=1, source_target_pairs={{0,8},{2,10},{4,12},{6,14},{8,0},{10,2},{12,4},{14,6},{16,24},{18,... | collective-permute-start | bytes 3538952 | tf_op jit(solution)/shard_map/ppermute | solution.py:1438
  331.6 66.0 %collective-permute-start.32 = (bf16[2,1536,384]{2,1,0:T(8,128)(2,1)}, bf16[2,1536,384]{2,1,0:T(8,128)(2,1)S(1)}, u32[]{:S(2)}, u32[]{:S(2)}) collective-permute-start(bf16[2,1536,384]{2,1,0:T(8,128)(2,1)} %get-tuple-element.178.refs_7_), channel_id=1, source_target_pairs={{0,1},{1,0},{2,3},{3,2},{4,5},{5,4},{6,7},{7,6},{8,9},{9,8},{10,11... | collective-permute-start | bytes 7077896 | tf_op jit(solution)/shard_map/ppermute | solution.py:1438
  396.0 43.0 %collective-permute-start.34 = (bf16[1,4,384,384]{3,2,1,0:T(8,128)(2,1)}, bf16[1,4,384,384]{3,2,1,0:T(8,128)(2,1)S(1)}, u32[]{:S(2)}, u32[]{:S(2)}) collective-permute-start(bf16[1,4,384,384]{3,2,1,0:T(8,128)(2,1)} %get-tuple-element.184.refs_2_), channel_id=1, source_target_pairs={{0,8},{2,10},{4,12},{6,14},{8,0},{10,2},{12,4},{14,6},{16,24},{18,... | collective-permute-start | bytes 3538952 | tf_op jit(solution)/shard_map/ppermute | solution.py:1438
  396.1 47.9 %collective-permute-start.33 = (bf16[1,4,192,384]{3,2,1,0:T(8,128)(2,1)}, bf16[1,4,192,384]{3,2,1,0:T(8,128)(2,1)S(1)}, u32[]{:S(2)}, u32[]{:S(2)}) collective-permute-start(bf16[1,4,192,384]{3,2,1,0:T(8,128)(2,1)} %get-tuple-element.185.refs_1_), channel_id=1, source_target_pairs={{0,16},{2,18},{4,20},{6,22},{8,24},{10,26},{12,28},{14,30},{16,0},... | collective-permute-start | bytes 1769480 | tf_op jit(solution)/shard_map/ppermute | solution.py:1438
  403.5 27.6 %collective-permute-start.36 = (bf16[2,768,384]{2,1,0:T(8,128)(2,1)}, bf16[2,768,384]{2,1,0:T(8,128)(2,1)S(1)}, u32[]{:S(2)}, u32[]{:S(2)}) collective-permute-start(bf16[2,768,384]{2,1,0:T(8,128)(2,1)} %get-tuple-element.190.refs_3_), channel_id=1, source_target_pairs={{0,4},{2,6},{4,0},{6,2},{8,12},{10,14},{12,8},{14,10},{16,20},{18,... | collective-permute-start | bytes 3538952 | tf_op jit(solution)/shard_map/ppermute | solution.py:1438
  407.7 27.3 %collective-permute-start.35 = (bf16[1,768,768]{2,1,0:T(8,128)(2,1)}, bf16[1,768,768]{2,1,0:T(8,128)(2,1)S(1)}, u32[]{:S(2)}, u32[]{:S(2)}) collective-permute-start(bf16[1,768,768]{2,1,0:T(8,128)(2,1)} %get-tuple-element.191.refs_8_), channel_id=1, source_target_pairs={{0,1},{1,0},{2,3},{3,2},{4,5},{5,4},{6,7},{7,6},{8,9},{9,8},{10,11... | collective-permute-start | bytes 3538952 | tf_op jit(solution)/shard_map/ppermute | solution.py:1438
  459.5 35.4 %collective-permute-start.45 = (bf16[1,4,192,384]{3,2,1,0:T(8,128)(2,1)S(1)}, bf16[1,4,192,384]{3,2,1,0:T(8,128)(2,1)S(1)}, u32[]{:S(2)}, u32[]{:S(2)}) collective-permute-start(bf16[1,4,192,384]{3,2,1,0:T(8,128)(2,1)S(1)} %copy-done.40), channel_id=1, source_target_pairs={{0,16},{2,18},{4,20},{6,22},{8,24},{10,26},{12,28},{14,30},{16,0},... | collective-permute-start | bytes 1769480 | tf_op jit(solution)/shard_map/ppermute | solution.py:1438
  473.1 27.0 %collective-permute-start.47 = (bf16[32,6912]{1,0:T(8,128)(2,1)S(1)}, bf16[32,6912]{1,0:T(8,128)(2,1)S(1)}, u32[]{:S(2)}, u32[]{:S(2)}) collective-permute-start(bf16[32,6912]{1,0:T(8,128)(2,1)S(1)} %pad_maximum_fusion.6.refs_0_), channel_id=1, source_target_pairs={{0,1},{1,0},{2,3},{3,2},{4,5},{5,4},{6,7},{7,6},{8,9},{9,8},{10,11... | collective-permute-start | bytes 1327112 | tf_op jit(solution)/shard_map/ppermute | solution.py:1438
  473.9 31.8 %collective-permute-start.51 = (bf16[32,6912]{1,0:T(8,128)(2,1)S(1)}, bf16[32,6912]{1,0:T(8,128)(2,1)S(1)}, u32[]{:S(2)}, u32[]{:S(2)}) collective-permute-start(bf16[32,6912]{1,0:T(8,128)(2,1)S(1)} %pad_maximum_fusion.6.refs_0_), channel_id=1, source_target_pairs={{0,2},{2,0},{4,6},{6,4},{8,10},{10,8},{12,14},{14,12},{16,18},{18,... | collective-permute-start | bytes 1327112 | tf_op jit(solution)/shard_map/ppermute | solution.py:1438
  480.1 25.6 %collective-permute-start.49 = (bf16[48,3072]{1,0:T(8,128)(2,1)}, bf16[48,3072]{1,0:T(8,128)(2,1)S(1)}, u32[]{:S(2)}, u32[]{:S(2)}) collective-permute-start(bf16[48,3072]{1,0:T(8,128)(2,1)} %get-tuple-element.213.refs_2_), channel_id=1, source_target_pairs={{0,2},{2,0},{4,6},{6,4},{8,10},{10,8},{12,14},{14,12},{16,18},{18,... | collective-permute-start | bytes 884744 | tf_op jit(solution)/shard_map/ppermute | solution.py:1438
  507.0 31.8 %collective-permute-start.52 = (bf16[32,6912]{1,0:T(8,128)(2,1)S(1)}, bf16[32,6912]{1,0:T(8,128)(2,1)S(1)}, u32[]{:S(2)}, u32[]{:S(2)}) collective-permute-start(bf16[32,6912]{1,0:T(8,128)(2,1)S(1)} %copy-done.9), channel_id=1, source_target_pairs={{0,2},{2,0},{4,6},{6,4},{8,10},{10,8},{12,14},{14,12},{16,18},{18,... | collective-permute-start | bytes 1327112 | tf_op jit(solution)/shard_map/ppermute | solution.py:1438
  (104 other events, 664.8 us)

commit v5 on v4

--- a/solution.py
+++ b/solution.py
@@ -531,19 +531,22 @@
 
 
 def qkv_kernel(x_ref, mod_ref, w_ref, packed_ref):
-    block = pl.program_id(0)
-    normed, _ = norm_parts(x_ref[...].astype(F32))
-    shift, scale = mod_ref[0, pl.ds(block, 1), :], mod_ref[1, pl.ds(block, 1), :]
-    hidden = (normed * (1.0 + scale) + shift).astype(BF16)
-    packed_ref[...] = nn(hidden, w_ref[...]).astype(BF16)
+    short = x_ref.shape[0] // 2
+    halves = []
+    for at in range(2):
+        block = pl.program_id(0) * 2 + at
+        normed, _ = norm_parts(x_ref[at * short : (at + 1) * short, :].astype(F32))
+        shift, scale = mod_ref[0, pl.ds(block, 1), :], mod_ref[1, pl.ds(block, 1), :]
+        halves.append((normed * (1.0 + scale) + shift).astype(BF16))
+    packed_ref[...] = nn(jnp.concatenate(halves, 0), w_ref[...]).astype(BF16)
 
 
 def qkv_forward(patches, mod, weight, blocks, after):
     rows, width = patches.shape
-    short = rows // blocks
+    short = 2 * rows // blocks
     wide = weight.shape[1]
     return run(
-        qkv_kernel, (patches, mod, weight), (blocks,),
+        qkv_kernel, (patches, mod, weight), (blocks // 2,),
         [rows_spec(short, width), like(mod), like(weight)], rows_spec(short, wide),
         shape((rows, wide), BF16), "qkv", after=after,
     )
@@ -675,20 +678,22 @@
 
 
 def middle_kernel(att_ref, x_ref, mod_ref, w_ref, branch_ref, hidden_ref):
-    block = pl.program_id(0)
+    short = x_ref.shape[0] // 2
     branch = nn(att_ref[...], w_ref[...])
     branch_ref[...] = branch
-    middle = x_ref[...].astype(F32) + mod_ref[2, pl.ds(block, 1), :] * branch
-    normed, _ = norm_parts(middle)
-    shift, scale = mod_ref[3, pl.ds(block, 1), :], mod_ref[4, pl.ds(block, 1), :]
-    hidden_ref[...] = (normed * (1.0 + scale) + shift).astype(BF16)
+    for at in range(2):
+        block, span = pl.program_id(0) * 2 + at, slice(at * short, (at + 1) * short)
+        middle = x_ref[span, :].astype(F32) + mod_ref[2, pl.ds(block, 1), :] * branch[span]
+        normed, _ = norm_parts(middle)
+        shift, scale = mod_ref[3, pl.ds(block, 1), :], mod_ref[4, pl.ds(block, 1), :]
+        hidden_ref[span, :] = (normed * (1.0 + scale) + shift).astype(BF16)
 
 
 def middle_forward(attended, patches, mod, out_weight, blocks, after):
     rows, width = patches.shape
-    tile = rows_spec(rows // blocks, width)
-    return run(
-        middle_kernel, (attended, patches, mod, out_weight), (blocks,),
+    tile = rows_spec(2 * rows // blocks, width)
+    return run(
+        middle_kernel, (attended, patches, mod, out_weight), (blocks // 2,),
         [tile, tile, like(mod), like(out_weight)], [tile, tile],
         [shape((rows, width), F32), shape((rows, width), BF16)], "middle", after=after,
     )
@@ -748,7 +753,7 @@
     return jnp.where(ids == first, gate_one, 0.0) + jnp.where(ids == second, gate_two, 0.0)
 
 
-def ffn_phase_one(x, g, up_ref, down_ref, act_ref, pre_ref, step=256):
+def ffn_phase_one(x, g, up_ref, down_ref, act_ref, pre_ref, step=768):
     wide = act_ref.shape[1]
     for at in range(0, wide, step):
         cols = slice(at, at + step)
@@ -1015,12 +1020,9 @@
 def combine(rank_cols, pairs, places, after):
     count, rows, _ = rank_cols.shape
     width = pairs[0][0].shape[2]
-    block = rows // 4
+    block = rows // 2
     flat = [a for pair in pairs for a in pair]
-    halves = [
-        pl.BlockSpec((block, width), lambda i: (jnp.minimum(i, 1), 0)),
-        pl.BlockSpec((block, width), lambda i: (jnp.maximum(i - 2, 0), 0)),
-    ]
+    halves = [pl.BlockSpec((block, width), lambda i: (0, 0))] * 2
     *outs, low, high = run(
         functools.partial(combine_kernel, places), (rank_cols, *flat), (rows // block,),
         [pl.BlockSpec((count, block, 128), lambda i: (0, i, 0))] + [like(a) for a in flat],
@@ -1375,23 +1377,26 @@
 
 
 def inputs_back_kernel(dq_ref, dk_ref, dv_ref, w_ref, x_ref, gm_ref, mod_ref, gp_ref, mods_ref):
-    block = pl.program_id(0)
     width = x_ref.shape[1]
-    grad = nt(dq_ref[...], w_ref[:, :width])
-    grad = grad + nt(dk_ref[...], w_ref[:, width : 2 * width])
-    grad = grad + nt(dv_ref[...], w_ref[:, 2 * width :])
-    normed, spread = norm_parts(x_ref[...].astype(F32))
-    mods_ref[0, pl.ds(block, 1), :] = jnp.sum(grad, 0, keepdims=True)
-    mods_ref[1, pl.ds(block, 1), :] = jnp.sum(grad * normed, 0, keepdims=True)
-    scale = mod_ref[1, pl.ds(block, 1), :]
-    gp_ref[...] = gm_ref[...] + norm_back(grad * (1.0 + scale), normed, spread)
+    short = x_ref.shape[0] // 2
+    both = nt(dq_ref[...], w_ref[:, :width])
+    both = both + nt(dk_ref[...], w_ref[:, width : 2 * width])
+    both = both + nt(dv_ref[...], w_ref[:, 2 * width :])
+    for at in range(2):
+        block, span = pl.program_id(0) * 2 + at, slice(at * short, (at + 1) * short)
+        grad = both[span]
+        normed, spread = norm_parts(x_ref[span, :].astype(F32))
+        mods_ref[0, pl.ds(block, 1), :] = jnp.sum(grad, 0, keepdims=True)
+        mods_ref[1, pl.ds(block, 1), :] = jnp.sum(grad * normed, 0, keepdims=True)
+        scale = mod_ref[1, pl.ds(block, 1), :]
+        gp_ref[span, :] = gm_ref[span, :] + norm_back(grad * (1.0 + scale), normed, spread)
 
 
 def inputs_backward(grads, weight, patches, grad_middle, mod, blocks, after):
     rows, width = patches.shape
-    tile = rows_spec(rows // blocks, width)
-    return run(
-        inputs_back_kernel, (*grads, weight, patches, grad_middle, mod), (blocks,),
+    tile = rows_spec(2 * rows // blocks, width)
+    return run(
+        inputs_back_kernel, (*grads, weight, patches, grad_middle, mod), (blocks // 2,),
         [tile] * 3 + [like(weight), tile, tile, like(mod)], [tile, full((2, 8, width))],
         [shape((rows, width), F32), shape((2, 8, width), F32)], "inputs_back", after=after,
     )

time: 553 us -> 551 us (level)
  no operation moved by 1% of the time
where the time goes in v5:
time: 551 us; the launch traced here: 542 us
  Pallas kernels  406 us (74%)
  starting transfers between devices  45 us (8%)
  waiting for transfers between devices  43.5 us (8%)
  local copies, waits for them, and re-layouts  30.9 us (6%)
  other arithmetic  12.1 us (2%)
    pallas_call x38, Pallas kernels, run(): pl.pallas_call(body, grid_spec=pltpu.PrefetchScalarGridSpec(num_scalar_pr...  406 us
    ppermute x57, starting transfers between devices, swap(): return lax.ppermute(values, axis, [(i, i ^ bit) for i in range(size)])  43.8 us
    ppermute x57, waiting for transfers between devices, swap(): return lax.ppermute(values, axis, [(i, i ^ bit) for i in range(size)])  43.5 us
    unnamed x143, local copies, waits for them, and re-layouts  20.8 us
  transfers between devices with their start and end apart: 59, of which 17 were waited for; matrix products, arithmetic and copies ran while one was open for 4% of the time, Pallas kernels for 69%

profile of v5, /device:TPU:0, one launch (start us, length us, event | category | flops | bytes accessed | tf_op | source)
XLA Modules:
  0.0 542.0 jit_solution(1871554875596598365)
XLA Ops:
  6.2 8.7 %modulate.1 = (f32[6,8,768]{2,1,0:T(8,128)}, f32[8,768]{1,0:T(8,128)}, bf16[1024,768]{1,0:T(8,128)(2,1)}, bf16[1056,768]{1,0:T(8,128)(2,1)}) custom-call(s32[8]{0:T(128)} %stack.63.refs_0_, f32[8,768]{1,0:T(8,128)} %pad.12.refs_1_.refs_3_, bf16[768,4608]{1,0:T(8,128)(2,1)} %refs_2_.5, bf16[1024,768]{1,0:T(8,128)(2,1)} %refs_4_.2), custom_call_target="tpu_custom_call" | custom-call | flops 1000 | bytes 1000 | tf_op jit(solution)/shard_map/modulate/pallas_call | solution.py:445
  16.3 8.5 %qkv.1.refs_1_.refs_2_.refs_3_ = bf16[1024,2304]{1,0:T(8,128)(2,1)} custom-call(bf16[1024,768]{1,0:T(8,128)(2,1)} %refs_4_.3, f32[6,8,768]{2,1,0:T(8,128)} %get-tuple-element.120.refs_1_.refs_2_.refs_12_.refs_7_.refs_6_, bf16[768,2304]{1,0:T(8,128)(2,1)} %refs_3_.5, bf16[1024,768]{1,0:T(8,128)(2,1)} %touch.27.refs_3_.refs_1_.refs_2_), custom_call_target="tpu_custom_call" | custom-call | flops 1000 | bytes 1000 | tf_op jit(solution)/shard_map/qkv/pallas_call | solution.py:445
  24.8 19.4 %attend.1 = (bf16[1024,768]{1,0:T(8,128)(2,1)}, f32[1024,768]{1,0:T(8,128)}) custom-call(s32[8]{0:T(128)} %stack.63.refs_0_, bf16[1024,2304]{1,0:T(8,128)(2,1)} %qkv.1.refs_1_.refs_2_.refs_3_, bf16[1024,2304]{1,0:T(8,128)(2,1)} %qkv.1.refs_1_.refs_2_.refs_3_, bf16[1024,2304]{1,0:T(8,128)(2,1)} %qkv.1.refs_1_.refs_2_.refs_3_), custom_call_target="tpu_custom_call" | custom-call | flops 1000 | bytes 1000 | tf_op jit(solution)/shard_map/attend/pallas_call | solution.py:445
  44.2 5.4 %middle.1 = (f32[1024,768]{1,0:T(8,128)}, bf16[1024,768]{1,0:T(8,128)(2,1)}) custom-call(bf16[1024,768]{1,0:T(8,128)(2,1)} %get-tuple-element.122.refs_0_.refs_4_.refs_6_, bf16[1024,768]{1,0:T(8,128)(2,1)} %refs_4_.3, f32[6,8,768]{2,1,0:T(8,128)} %get-tuple-element.120.refs_1_.refs_2_.refs_12_.refs_7_.refs_6_, bf16[768,768]{1,0:T(8,128)(2,1)} %refs_13_.1), custom_call_target="tpu_custom_call" | custom-call | flops 1000 | bytes 1000 | tf_op jit(solution)/shard_map/middle/pallas_call | solution.py:445
  57.3 30.5 %expert.4 = (bf16[4,2,768,384]{3,2,1,0:T(8,128)(2,1)}, bf16[4,2,768,384]{3,2,1,0:T(8,128)(2,1)}, bf16[2,288,768]{2,1,0:T(8,128)(2,1)}, bf16[2,288,768]{2,1,0:T(8,128)(2,1)}, f32[2,1,1024]{2,1,0:T(1,128)}) custom-call(s32[8]{0:T(128)} %stack.63.refs_0_, bf16[1024,768]{1,0:T(8,128)(2,1)} %get-tuple-element.123.refs_3_.refs_1_.refs_8_, ...), custom_call_target="tpu_custom_call" | custom-call | flops 1000 | bytes 1000 | tf_op jit(solution)/shard_map/expert/pallas_call | solution.py:445
  96.7 32.1 %expert.5 = (bf16[4,2,768,384]{3,2,1,0:T(8,128)(2,1)}, bf16[4,2,768,384]{3,2,1,0:T(8,128)(2,1)}, bf16[2,288,768]{2,1,0:T(8,128)(2,1)}, bf16[2,288,768]{2,1,0:T(8,128)(2,1)}, f32[2,1,1024]{2,1,0:T(1,128)}) custom-call(s32[8]{0:T(128)} %stack.63.refs_0_, bf16[1024,768]{1,0:T(8,128)(2,1)} %touch.30.refs_3_.refs_1_, bf16[1024,768]{1,0:T(8,128)(2,1)} %copy-done.12, ...), custom_call_target="tpu_custom_call" | custom-call | flops 1000 | bytes 1000 | tf_op jit(solution)/shard_map/expert/pallas_call | solution.py:445
  130.4 30.3 %expert.6 = (bf16[4,2,768,384]{3,2,1,0:T(8,128)(2,1)}, bf16[4,1,768,384]{3,2,1,0:T(8,128)(2,1)}, bf16[4,1,768,384]{3,2,1,0:T(8,128)(2,1)}, bf16[2,288,768]{2,1,0...) custom-call(s32[8]{0:T(128)} %stack.63.refs_0_, ...), custom_call_target="tpu_custom_call" | custom-call | flops 1000 | bytes 1000 | tf_op jit(solution)/shard_map/expert/pallas_call | solution.py:445
  160.8 32.1 %expert.7 = (bf16[4,2,768,384]{3,2,1,0:T(8,128)(2,1)}, bf16[4,1,768,384]{3,2,1,0:T(8,128)(2,1)}, bf16[4,1,768,384]{3,2,1,0:T(8,128)(2,1)}, bf16[2,288,768]{2,1,0...) custom-call(s32[8]{0:T(128)} %stack.63.refs_0_, bf16[1024,768]{1,0:T(8,128)(2,1)} %touch.30.refs_3_.refs_1_, ...), custom_call_target="tpu_custom_call" | custom-call | flops 1000 | bytes 1000 | tf_op jit(solution)/shard_map/expert/pallas_call | solution.py:445
  192.9 10.2 %combine.2 = (bf16[1024,768]{1,0:T(8,128)(2,1)}, bf16[1024,768]{1,0:T(8,128)(2,1)}, bf16[1024,768]{1,0:T(8,128)(2,1)}, bf16[512,768]{1,0:T(8,128)(2,1)}, bf16[512,768]{1,0:T(8,128)(2,1)}) custom-call(s32[2,1024,128]{2,1,0:T(8,128)} %get-tuple-element.137.refs_0_, bf16[2,288,768]{2,1,0:T(8,128)(2,1)} %get-tuple-element.138.refs_1_, ...), custom_call_target="tpu_custom_call" | custom-call | flops 1000 | bytes 1000 | tf_op jit(solution)/shard_map/combine/pallas_call | solution.py:445
  203.1 10.1 %combine.3 = (bf16[1024,768]{1,0:T(8,128)(2,1)}, bf16[1024,768]{1,0:T(8,128)(2,1)}, bf16[1024,768]{1,0:T(8,128)(2,1)}, bf16[512,768]{1,0:T(8,128)(2,1)}, bf16[512,768]{1,0:T(8,128)(2,1)}) custom-call(s32[2,1024,128]{2,1,0:T(8,128)} %get-tuple-element.148.refs_0_, bf16[2,288,768]{2,1,0:T(8,128)(2,1)} %get-tuple-element.149.refs_1_, ...), custom_call_target="tpu_custom_call" | custom-call | flops 1000 | bytes 1000 | tf_op jit(solution)/shard_map/combine/pallas_call | solution.py:445
  226.2 5.0 add_rows.1
  233.8 7.0 %halve_y.3 = (f32[2,4,384,384]{3,2,1,0:T(8,128)}, bf16[2,4,384,384]{3,2,1,0:T(8,128)(2,1)}) custom-call(bf16[4,2,768,384]{3,2,1,0:T(8,128)(2,1)} %get-tuple-element.135.refs_0_, bf16[4,2,768,384]{3,2,1,0:T(8,128)(2,1)} %collective-permute-done.9.refs_1_, bf16[4,4,384,384]{3,2,1,0:T(8,128)(2,1)} %bitcast.86, ...), custom_call_target="tpu_custom_call" | custom-call | flops 1000 | bytes 1000 | tf_op jit(solution)/shard_map/halve_y/pallas_call | solution.py:445
  245.0 43.3 %shared.1 = (bf16[2,768,768]{2,1,0:T(8,128)(2,1)}, bf16[768,768]{1,0:T(8,128)(2,1)}, bf16[768,768]{1,0:T(8,128)(2,1)}, bf16[2,2,4,192,384]{4,3,2,1,0:T(8,128)(2,...) custom-call(s32[8]{0:T(128)} %stack.63.refs_0_, ...), custom_call_target="tpu_custom_call" | custom-call | flops 1000 | bytes 1000 | tf_op jit(solution)/shard_map/shared/pallas_call | solution.py:445
  293.5 12.0 %middle_back.1 = (f32[1024,768]{1,0:T(8,128)}, bf16[1024,768]{1,0:T(8,128)(2,1)}, bf16[1024,768]{1,0:T(8,128)(2,1)}, f32[3,8,768]{2,1,0:T(8,128)}, f32[16,768]{1,0:T(8,128)}) custom-call(f32[1024,768]{1,0:T(8,128)} %get-tuple-element.163.refs_0_, bf16[1024,768]{1,0:T(8,128)(2,1)} %get-tuple-element.153.refs_1_, bf16[512,768]{1,0:T(8,128)(2,1)} %touch.32.refs_6_.refs_2_, ...), custom_call_target="tpu_custom_call" | custom-call | flops 1000 | bytes 1000 | tf_op jit(solution)/shard_map/middle_back/pallas_call | solution.py:445
  305.5 5.3 halve_z.3
  319.8 8.8 %halve_slices.1 = (f32[2,1536,384]{2,1,0:T(8,128)}, bf16[2,1536,384]{2,1,0:T(8,128)(2,1)}) custom-call(bf16[2,768,768]{2,1,0:T(8,128)(2,1)} %get-tuple-element.167.refs_0_, bf16[2,1536,384]{2,1,0:T(8,128)(2,1)} %bitcast.107, bf16[768,768]{1,0:T(8,128)(2,1)} %copy-done.28, bf16[768,768]{1,0:T(8,128)(2,1)} %copy-done.29, bf16[1536,384]{1,0:T(8,128)(2,1)} %bitcast.112, ...), custom_call_target="tpu_custom_call" | custom-call | flops 1000 | bytes 1000 | tf_op jit(solution)/shard_map/halve_slices/pallas_call | solution.py:445
  329.8 36.8 %attend_back.1 = (bf16[1024,768]{1,0:T(8,128)(2,1)}, bf16[1024,768]{1,0:T(8,128)(2,1)}, bf16[1024,768]{1,0:T(8,128)(2,1)}) custom-call(s32[8]{0:T(128)} %stack.63.refs_0_, bf16[1024,2304]{1,0:T(8,128)(2,1)} %qkv.1.refs_1_.refs_2_.refs_3_, bf16[1024,2304]{1,0:T(8,128)(2,1)} %qkv.1.refs_1_.refs_2_.refs_3_, bf16[1024,2304]{1,0:T(8,128)(2,1)} %qkv.1.refs_1_.refs_2_.refs_3_, ...), custom_call_target="tpu_custom_call" | custom-call | flops 1000 | bytes 1000 | tf_op jit(solution)/shard_map/attend_back/pallas_call | solution.py:445
  376.3 14.7 %weight_grads.1 = (bf16[2,768,768]{2,1,0:T(8,128)(2,1)}, bf16[768,768]{1,0:T(8,128)(2,1)}, bf16[768,768]{1,0:T(8,128)(2,1)}) custom-call(s32[8]{0:T(128)} %stack.63.refs_0_, bf16[1024,768]{1,0:T(8,128)(2,1)} %refs_4_.3, f32[6,8,768]{2,1,0:T(8,128)} %get-tuple-element.120.refs_1_.refs_2_.refs_12_.refs_7_.refs_6_, ...), custom_call_target="tpu_custom_call" | custom-call | flops 1000 | bytes 1000 | tf_op jit(solution)/shard_map/weight_grads/pallas_call | solution.py:445
  405.9 7.6 %mixed.1 = (bf16[1024,768]{1,0:T(8,128)(2,1)}, f32[8,768]{1,0:T(8,128)}) custom-call(f32[1024,768]{1,0:T(8,128)} %get-tuple-element.160.refs_0_, bf16[1024,768]{1,0:T(8,128)(2,1)} %get-tuple-element.161.refs_1_, bf16[1024,768]{1,0:T(8,128)(2,1)} %touch.34.refs_8_.refs_2_, bf16[1024,768]{1,0:T(8,128)(2,1)} %touch.36.refs_4_.refs_3_, ...), custom_call_target="tpu_custom_call" | custom-call | flops 1000 | bytes 1000 | tf_op jit(solution)/shard_map/mixed/pallas_call | solution.py:445
  413.5 10.4 %inputs_back.1 = (f32[1024,768]{1,0:T(8,128)}, f32[2,8,768]{2,1,0:T(8,128)}) custom-call(bf16[1024,768]{1,0:T(8,128)(2,1)} %get-tuple-element.179.refs_1_.refs_3_.refs_0_, bf16[1024,768]{1,0:T(8,128)(2,1)} %get-tuple-element.180.refs_4_.refs_1_, bf16[1024,768]{1,0:T(8,128)(2,1)} %get-tuple-element.181.refs_5_.refs_2_, bf16[768,2304]{1,0:T(8,128)(2,1)} %refs_3_.5, ...), custom_call_target="tpu_custom_call" | custom-call | flops 1000 | bytes 1000 | tf_op jit(solution)/shard_map/inputs_back/pallas_call | solution.py:445
  447.6 7.3 %used_back.1.refs_1_.refs_2_ = f32[8,768]{1,0:T(8,128)} custom-call(s32[8]{0:T(128)} %stack.63.refs_0_, f32[6,8,768]{2,1,0:T(8,128)} %pad_maximum_fusion.10.refs_1_, bf16[768,4608]{1,0:T(8,128)(2,1)} %refs_2_.5, f32[8,768]{1,0:T(8,128)} %pad.12.refs_1_.refs_3_, bf16[1,4,192,384]{3,2,1,0:T(8,128)(2,1)} %touch.38.refs_4_.refs_1_.refs_2_), custom_call_target="tpu_custom_call" | custom-call | flops 1000 | bytes 1000 | tf_op jit(solution)/shard_map/used_back/pallas_call | solution.py:445
  472.6 5.6 %finish_kinds.3 = (f32[48,3072]{1,0:T(8,128)}, bf16[48,3072]{1,0:T(8,128)(2,1)}, f32[192,768]{1,0:T(8,128)}, bf16[192,768]{1,0:T(8,128)(2,1)}) custom-call(s32[8]{0:T(128)} %stack.63.refs_0_, f32[2,4,192,384]{3,2,1,0:T(8,128)} %get-tuple-element.212.refs_1_.refs_3_, bf16[2,4,192,384]{3,2,1,0:T(8,128)(2,1)} %touch.37.refs_8_.refs_2_.refs_4_, ...), custom_call_target="tpu_custom_call" | custom-call | flops 1000 | bytes 1000 | tf_op jit(solution)/shard_map/finish_kinds/pallas_call | solution.py:445
  479.1 10.6 %collective-permute-done.43 = bf16[1,192,768]{2,1,0:T(8,128)(2,1)} collective-permute-done((bf16[1,192,768]{2,1,0:T(8,128)(2,1)}, bf16[1,192,768]{2,1,0:T(8,128)(2,1)}, u32[]{:S(2)}, u32[]{:S(2)}) %collective-permute-start.43) | collective-permute-done | bytes 294944 | tf_op jit(solution)/shard_map/ppermute | solution.py:1443
  525.8 6.4 %collective-permute-done.57 = bf16[192,192]{1,0:T(8,128)(2,1)S(1)} collective-permute-done((bf16[192,192]{1,0:T(8,128)(2,1)S(1)}, bf16[192,192]{1,0:T(8,128)(2,1)S(1)}, u32[]{:S(2)}, u32[]{:S(2)}) %collective-permute-start.57) | collective-permute-done | bytes 73760 | tf_op jit(solution)/shard_map/ppermute | solution.py:1443
  (367 shorter events, 171.3 us)
Async XLA Ops:
  16.2 38.7 %collective-permute-start.5 = (bf16[1056,768]{1,0:T(8,128)(2,1)}, bf16[1056,768]{1,0:T(8,128)(2,1)S(1)}, u32[]{:S(2)}, u32[]{:S(2)}) collective-permute-start(bf16[1056,768]{1,0:T(8,128)(2,1)} %touch.28), channel_id=1, source_target_pairs={{0,1},{1,0},{2,3},{3,2},{4,5},{5,4},{6,7},{7,6},{8,9},{9,8},{10,11... | collective-permute-start | bytes 4866056 | tf_op jit(solution)/shard_map/ppermute | solution.py:1443
  50.1 37.9 %collective-permute-start.2 = (bf16[1024,768]{1,0:T(8,128)(2,1)}, bf16[1024,768]{1,0:T(8,128)(2,1)}, u32[]{:S(2)}, u32[]{:S(2)}) collective-permute-start(bf16[1024,768]{1,0:T(8,128)(2,1)} %get-tuple-element.123.refs_3_.refs_1_.refs_8_), channel_id=1, source_target_pairs={{0,1},{1,0},{2,3},{3,2},{4,5},{5,4},{6,7},{7,6},{8,9},{9,8},{10,11... | collective-permute-start | bytes 4718600 | tf_op jit(solution)/shard_map/ppermute | solution.py:1443
  56.0 39.1 %collective-permute-start.7 = (bf16[1056,768]{1,0:T(8,128)(2,1)}, bf16[1056,768]{1,0:T(8,128)(2,1)S(1)}, u32[]{:S(2)}, u32[]{:S(2)}) collective-permute-start(bf16[1056,768]{1,0:T(8,128)(2,1)} %touch.29.refs_11_.refs_3_), channel_id=1, source_target_pairs={{0,2},{2,0},{4,6},{6,4},{8,10},{10,8},{12,14},{14,12},{16,18},{18,... | collective-permute-start | bytes 4866056 | tf_op jit(solution)/shard_map/ppermute | solution.py:1443
  128.8 105.0 %collective-permute-start.9 = (bf16[4,2,768,384]{3,2,1,0:T(8,128)(2,1)}, bf16[4,2,768,384]{3,2,1,0:T(8,128)(2,1)}, u32[]{:S(2)}, u32[]{:S(2)}) collective-permute-start(bf16[4,2,768,384]{3,2,1,0:T(8,128)(2,1)} %get-tuple-element.136), channel_id=1, source_target_pairs={{0,4},{2,6},{4,0},{6,2},{8,12},{10,14},{12,8},{14,10},{16,20},{18,... | collective-permute-start | bytes 14155784 | tf_op jit(solution)/shard_map/ppermute | solution.py:1443
  220.9 69.2 %collective-permute-start.25 = (bf16[4,1,768,384]{3,2,1,0:T(8,128)(2,1)}, bf16[4,1,768,384]{3,2,1,0:T(8,128)(2,1)}, u32[]{:S(2)}, u32[]{:S(2)}) collective-permute-start(bf16[4,1,768,384]{3,2,1,0:T(8,128)(2,1)} %get-tuple-element.174), channel_id=1, source_target_pairs={{0,4},{2,6},{4,0},{6,2},{8,12},{10,14},{12,8},{14,10},{16,20},{18,... | collective-permute-start | bytes 7077896 | tf_op jit(solution)/shard_map/ppermute | solution.py:1443
  231.2 58.9 %collective-permute-start.20 = (bf16[1024,768]{1,0:T(8,128)(2,1)}, bf16[1024,768]{1,0:T(8,128)(2,1)}, u32[]{:S(2)}, u32[]{:S(2)}) collective-permute-start(bf16[1024,768]{1,0:T(8,128)(2,1)} %get-tuple-element.164), channel_id=1, source_target_pairs={{0,1},{1,0},{2,3},{3,2},{4,5},{5,4},{6,7},{7,6},{8,9},{9,8},{10,11... | collective-permute-start | bytes 4718600 | tf_op jit(solution)/shard_map/ppermute | solution.py:1443
  240.8 51.9 %collective-permute-start.26 = (bf16[2,4,384,384]{3,2,1,0:T(8,128)(2,1)}, bf16[2,4,384,384]{3,2,1,0:T(8,128)(2,1)S(1)}, u32[]{:S(2)}, u32[]{:S(2)}) collective-permute-start(bf16[2,4,384,384]{3,2,1,0:T(8,128)(2,1)} %get-tuple-element.158.refs_1_), channel_id=1, source_target_pairs={{0,8},{2,10},{4,12},{6,14},{8,0},{10,2},{12,4},{14,6},{16,24},{18,... | collective-permute-start | bytes 7077896 | tf_op jit(solution)/shard_map/ppermute | solution.py:1443
  288.6 78.1 %collective-permute-start.29 = (bf16[4,1,768,384]{3,2,1,0:T(8,128)(2,1)}, bf16[4,1,768,384]{3,2,1,0:T(8,128)(2,1)}, u32[]{:S(2)}, u32[]{:S(2)}) collective-permute-start(bf16[4,1,768,384]{3,2,1,0:T(8,128)(2,1)} %touch.35.refs_5_), channel_id=1, source_target_pairs={{0,4},{2,6},{4,0},{6,2},{8,12},{10,14},{12,8},{14,10},{16,20},{18,... | collective-permute-start | bytes 7077896 | tf_op jit(solution)/shard_map/ppermute | solution.py:1443
  290.1 25.3 %collective-permute-start.22 = (bf16[768,768]{1,0:T(8,128)(2,1)}, bf16[768,768]{1,0:T(8,128)(2,1)S(1)}, u32[]{:S(2)}, u32[]{:S(2)}) collective-permute-start(bf16[768,768]{1,0:T(8,128)(2,1)} %get-tuple-element.170), channel_id=1, source_target_pairs={{0,2},{2,0},{4,6},{6,4},{8,10},{10,8},{12,14},{14,12},{16,18},{18,... | collective-permute-start | bytes 3538952 | tf_op jit(solution)/shard_map/ppermute | solution.py:1443
  290.2 27.9 %collective-permute-start.23 = (bf16[2,4,192,384]{3,2,1,0:T(8,128)(2,1)}, bf16[2,4,192,384]{3,2,1,0:T(8,128)(2,1)S(1)}, u32[]{:S(2)}, u32[]{:S(2)}) collective-permute-start(bf16[2,4,192,384]{3,2,1,0:T(8,128)(2,1)} %get-tuple-element.171), channel_id=1, source_target_pairs={{0,2},{2,0},{4,6},{6,4},{8,10},{10,8},{12,14},{14,12},{16,18},{18,... | collective-permute-start | bytes 3538952 | tf_op jit(solution)/shard_map/ppermute | solution.py:1443
  291.5 28.3 %collective-permute-start.24 = (bf16[2,4,192,384]{3,2,1,0:T(8,128)(2,1)}, bf16[2,4,192,384]{3,2,1,0:T(8,128)(2,1)}, u32[]{:S(2)}, u32[]{:S(2)}) collective-permute-start(bf16[2,4,192,384]{3,2,1,0:T(8,128)(2,1)} %get-tuple-element.172), channel_id=1, source_target_pairs={{0,2},{2,0},{4,6},{6,4},{8,10},{10,8},{12,14},{14,12},{16,18},{18,... | collective-permute-start | bytes 3538952 | tf_op jit(solution)/shard_map/ppermute | solution.py:1443
  292.7 74.0 %collective-permute-start.19 = (bf16[1024,768]{1,0:T(8,128)(2,1)S(1)}, bf16[1024,768]{1,0:T(8,128)(2,1)}, u32[]{:S(2)}, u32[]{:S(2)}) collective-permute-start(bf16[1024,768]{1,0:T(8,128)(2,1)S(1)} %copy-done.26), channel_id=1, source_target_pairs={{0,1},{1,0},{2,3},{3,2},{4,5},{5,4},{6,7},{7,6},{8,9},{9,8},{10,11... | collective-permute-start | bytes 4718600 | tf_op jit(solution)/shard_map/ppermute | solution.py:1443
  315.4 59.8 %collective-permute-start.27 = (bf16[2,4,192,384]{3,2,1,0:T(8,128)(2,1)}, bf16[2,4,192,384]{3,2,1,0:T(8,128)(2,1)S(1)}, u32[]{:S(2)}, u32[]{:S(2)}) collective-permute-start(bf16[2,4,192,384]{3,2,1,0:T(8,128)(2,1)} %get-tuple-element.176.refs_2_), channel_id=1, source_target_pairs={{0,16},{2,18},{4,20},{6,22},{8,24},{10,26},{12,28},{14,30},{16,0},... | collective-permute-start | bytes 3538952 | tf_op jit(solution)/shard_map/ppermute | solution.py:1443
  318.0 53.2 %collective-permute-start.28 = (bf16[1,4,384,384]{3,2,1,0:T(8,128)(2,1)}, bf16[1,4,384,384]{3,2,1,0:T(8,128)(2,1)}, u32[]{:S(2)}, u32[]{:S(2)}) collective-permute-start(bf16[1,4,384,384]{3,2,1,0:T(8,128)(2,1)} %get-tuple-element.177.refs_6_), channel_id=1, source_target_pairs={{0,8},{2,10},{4,12},{6,14},{8,0},{10,2},{12,4},{14,6},{16,24},{18,... | collective-permute-start | bytes 3538952 | tf_op jit(solution)/shard_map/ppermute | solution.py:1443
  328.6 65.7 %collective-permute-start.32 = (bf16[2,1536,384]{2,1,0:T(8,128)(2,1)}, bf16[2,1536,384]{2,1,0:T(8,128)(2,1)S(1)}, u32[]{:S(2)}, u32[]{:S(2)}) collective-permute-start(bf16[2,1536,384]{2,1,0:T(8,128)(2,1)} %get-tuple-element.178.refs_7_), channel_id=1, source_target_pairs={{0,1},{1,0},{2,3},{3,2},{4,5},{5,4},{6,7},{7,6},{8,9},{9,8},{10,11... | collective-permute-start | bytes 7077896 | tf_op jit(solution)/shard_map/ppermute | solution.py:1443
  393.0 43.7 %collective-permute-start.34 = (bf16[1,4,384,384]{3,2,1,0:T(8,128)(2,1)}, bf16[1,4,384,384]{3,2,1,0:T(8,128)(2,1)S(1)}, u32[]{:S(2)}, u32[]{:S(2)}) collective-permute-start(bf16[1,4,384,384]{3,2,1,0:T(8,128)(2,1)} %get-tuple-element.184.refs_2_), channel_id=1, source_target_pairs={{0,8},{2,10},{4,12},{6,14},{8,0},{10,2},{12,4},{14,6},{16,24},{18,... | collective-permute-start | bytes 3538952 | tf_op jit(solution)/shard_map/ppermute | solution.py:1443
  394.1 47.9 %collective-permute-start.33 = (bf16[1,4,192,384]{3,2,1,0:T(8,128)(2,1)}, bf16[1,4,192,384]{3,2,1,0:T(8,128)(2,1)S(1)}, u32[]{:S(2)}, u32[]{:S(2)}) collective-permute-start(bf16[1,4,192,384]{3,2,1,0:T(8,128)(2,1)} %get-tuple-element.185.refs_1_), channel_id=1, source_target_pairs={{0,16},{2,18},{4,20},{6,22},{8,24},{10,26},{12,28},{14,30},{16,0},... | collective-permute-start | bytes 1769480 | tf_op jit(solution)/shard_map/ppermute | solution.py:1443
  400.2 27.6 %collective-permute-start.36 = (bf16[2,768,384]{2,1,0:T(8,128)(2,1)}, bf16[2,768,384]{2,1,0:T(8,128)(2,1)S(1)}, u32[]{:S(2)}, u32[]{:S(2)}) collective-permute-start(bf16[2,768,384]{2,1,0:T(8,128)(2,1)} %get-tuple-element.190.refs_3_), channel_id=1, source_target_pairs={{0,4},{2,6},{4,0},{6,2},{8,12},{10,14},{12,8},{14,10},{16,20},{18,... | collective-permute-start | bytes 3538952 | tf_op jit(solution)/shard_map/ppermute | solution.py:1443
  405.1 27.6 %collective-permute-start.35 = (bf16[1,768,768]{2,1,0:T(8,128)(2,1)}, bf16[1,768,768]{2,1,0:T(8,128)(2,1)S(1)}, u32[]{:S(2)}, u32[]{:S(2)}) collective-permute-start(bf16[1,768,768]{2,1,0:T(8,128)(2,1)} %get-tuple-element.191.refs_8_), channel_id=1, source_target_pairs={{0,1},{1,0},{2,3},{3,2},{4,5},{5,4},{6,7},{7,6},{8,9},{9,8},{10,11... | collective-permute-start | bytes 3538952 | tf_op jit(solution)/shard_map/ppermute | solution.py:1443
  457.5 35.5 %collective-permute-start.45 = (bf16[1,4,192,384]{3,2,1,0:T(8,128)(2,1)S(1)}, bf16[1,4,192,384]{3,2,1,0:T(8,128)(2,1)S(1)}, u32[]{:S(2)}, u32[]{:S(2)}) collective-permute-start(bf16[1,4,192,384]{3,2,1,0:T(8,128)(2,1)S(1)} %copy-done.40), channel_id=1, source_target_pairs={{0,16},{2,18},{4,20},{6,22},{8,24},{10,26},{12,28},{14,30},{16,0},... | collective-permute-start | bytes 1769480 | tf_op jit(solution)/shard_map/ppermute | solution.py:1443
  470.8 27.3 %collective-permute-start.47 = (bf16[32,6912]{1,0:T(8,128)(2,1)S(1)}, bf16[32,6912]{1,0:T(8,128)(2,1)S(1)}, u32[]{:S(2)}, u32[]{:S(2)}) collective-permute-start(bf16[32,6912]{1,0:T(8,128)(2,1)S(1)} %pad_maximum_fusion.6.refs_0_), channel_id=1, source_target_pairs={{0,1},{1,0},{2,3},{3,2},{4,5},{5,4},{6,7},{7,6},{8,9},{9,8},{10,11... | collective-permute-start | bytes 1327112 | tf_op jit(solution)/shard_map/ppermute | solution.py:1443
  471.6 31.8 %collective-permute-start.51 = (bf16[32,6912]{1,0:T(8,128)(2,1)S(1)}, bf16[32,6912]{1,0:T(8,128)(2,1)S(1)}, u32[]{:S(2)}, u32[]{:S(2)}) collective-permute-start(bf16[32,6912]{1,0:T(8,128)(2,1)S(1)} %pad_maximum_fusion.6.refs_0_), channel_id=1, source_target_pairs={{0,2},{2,0},{4,6},{6,4},{8,10},{10,8},{12,14},{14,12},{16,18},{18,... | collective-permute-start | bytes 1327112 | tf_op jit(solution)/shard_map/ppermute | solution.py:1443
  478.2 25.1 %collective-permute-start.49 = (bf16[48,3072]{1,0:T(8,128)(2,1)}, bf16[48,3072]{1,0:T(8,128)(2,1)S(1)}, u32[]{:S(2)}, u32[]{:S(2)}) collective-permute-start(bf16[48,3072]{1,0:T(8,128)(2,1)} %get-tuple-element.213.refs_2_), channel_id=1, source_target_pairs={{0,2},{2,0},{4,6},{6,4},{8,10},{10,8},{12,14},{14,12},{16,18},{18,... | collective-permute-start | bytes 884744 | tf_op jit(solution)/shard_map/ppermute | solution.py:1443
  504.6 31.7 %collective-permute-start.52 = (bf16[32,6912]{1,0:T(8,128)(2,1)S(1)}, bf16[32,6912]{1,0:T(8,128)(2,1)S(1)}, u32[]{:S(2)}, u32[]{:S(2)}) collective-permute-start(bf16[32,6912]{1,0:T(8,128)(2,1)S(1)} %copy-done.9), channel_id=1, source_target_pairs={{0,2},{2,0},{4,6},{6,4},{8,10},{10,8},{12,14},{14,12},{16,18},{18,... | collective-permute-start | bytes 1327112 | tf_op jit(solution)/shard_map/ppermute | solution.py:1443
  (104 other events, 661.1 us)

commit v6 on v5

--- a/solution.py
+++ b/solution.py
@@ -901,7 +901,7 @@
 
 def shared_kernel(
     pos_ref, h_ref, b_ref, up_ref, down_ref, ku_ref, su0_ref, su1_ref, kd_ref, sd0_ref, sd1_ref,
-    out_ref, gx_ref, xt_s, gt_s, act_s, pre_s,
+    out_ref, gx_ref, xt_s, gt_s, act_s, pre_s, out_acc, gx_acc,
 ):
     step = pl.program_id(0)
     nz, block = 4, kd_ref.shape[3]
@@ -914,13 +914,19 @@
             place = ((slice_at % 2) ^ pos_ref[CORE]) * 2 + ((slice_at // 2) ^ pos_ref[STREAM])
             at = pl.multiple_of(place * block, block)
             gt_s[pl.ds(at, block), :] = turned[slice_at * block : (slice_at + 1) * block]
-        out_ref[...] = jnp.zeros_like(out_ref)
-        gx_ref[...] = jnp.zeros_like(gx_ref)
+        out_acc[...] = jnp.zeros_like(out_acc)
+        gx_acc[...] = jnp.zeros_like(gx_acc)
 
     ffn_phase_one(h_ref[...], b_ref[...], up_ref, down_ref, act_s, pre_s)
     act, pre = act_s[...], pre_s[...]
-    out_ref[...] += nn(act, down_ref[0])
-    gx_ref[...] += nt(pre, up_ref[0])
+    out_acc[...] += nn(act, down_ref[0])
+    gx_acc[...] += nt(pre, up_ref[0])
+
+    @pl.when(step == nz - 1)
+    def _():
+        out_ref[...] = out_acc[...].astype(BF16)
+        gx_ref[...] = gx_acc[...].astype(BF16)
+
     dup = nn(xt_s[...], pre).astype(BF16)
 
     @pl.when(step < 2)
@@ -967,13 +973,15 @@
         [keep] + [full((width, tile))] * 2 + [downs, sent, sent, like(hidden), like(hidden)],
         [shape((2, width, tile), BF16)] + [shape((width, tile), BF16)] * 2
         + [shape((2, 2, nz, block, tile // 2), BF16)] + [shape((2, nz, block, tile // 2), BF16)] * 2
-        + [shape((rows, width), F32)] * 2,
+        + [shape((rows, width), BF16)] * 2,
         "shared", scalars=(pos,), after=after,
         scratch=[
             pltpu.VMEM((width, rows), BF16),
             pltpu.VMEM((width, rows), BF16),
             pltpu.VMEM((rows, tile), BF16),
             pltpu.VMEM((rows, tile), BF16),
+            pltpu.VMEM((rows, width), F32),
+            pltpu.VMEM((rows, width), F32),
         ],
     )
     return outs[0], outs[1:3], outs[3], outs[4:6], *outs[6:]
@@ -1258,7 +1266,7 @@
     inner = jnp.sum(gates * grad_gates, 0, keepdims=True)
     grad_logits = gates * (grad_gates - inner)
     core = jnp.where(block < pl.num_programs(0) // 2, low_ref[...], high_ref[...])
-    grad = gs_ref[...] + ga_ref[...].astype(F32) + core.astype(F32) + gc_ref[...].astype(F32)
+    grad = gs_ref[...].astype(F32) + ga_ref[...].astype(F32) + core.astype(F32) + gc_ref[...].astype(F32)
     pieces = stacked(grad_logits)
     router = router_ref[...]
     grad = grad + tn(pieces, jnp.concatenate([router] * 3, 0))
@@ -1311,7 +1319,7 @@
 
 def mixed_kernel(so_ref, ra_ref, rb_ref, rc_ref, cot_ref, branch_ref, x_ref, mod_ref, mixed_ref, gate_ref):
     block = pl.program_id(0)
-    second = so_ref[...] + ra_ref[...].astype(F32) + rb_ref[...].astype(F32) + rc_ref[...].astype(F32)
+    second = so_ref[...].astype(F32) + ra_ref[...].astype(F32) + rb_ref[...].astype(F32) + rc_ref[...].astype(F32)
     middle = x_ref[...].astype(F32) + mod_ref[2, pl.ds(block, 1), :] * branch_ref[...]
     mixed_ref[...] = (middle + mod_ref[5, pl.ds(block, 1), :] * second).astype(BF16)
     gate_ref[pl.ds(block, 1), :] = jnp.sum(cot_ref[...].astype(F32) * second, 0, keepdims=True)

time: 551 us -> 550 us (level)
  transfers between devices with their start and end apart: 59 -> 59, of which waited for: 17 -> 20; matrix products, arithmetic and copies ran while one was open for 4% -> 4% of each run, Pallas kernels for 69% -> 69%
where the time goes in v6:
time: 550 us; the launch traced here: 541 us
  Pallas kernels  406 us (74%)
  waiting for transfers between devices  44.9 us (8%)
  starting transfers between devices  42 us (8%)
  local copies, waits for them, and re-layouts  31.4 us (6%)
  other arithmetic  12.1 us (2%)
    pallas_call x38, Pallas kernels, run(): pl.pallas_call(body, grid_spec=pltpu.PrefetchScalarGridSpec(num_scalar_pr...  406 us
    ppermute x57, waiting for transfers between devices, swap(): return lax.ppermute(values, axis, [(i, i ^ bit) for i in range(size)])  44.9 us
    ppermute x57, starting transfers between devices, swap(): return lax.ppermute(values, axis, [(i, i ^ bit) for i in range(size)])  41 us
    unnamed x143, local copies, waits for them, and re-layouts  21.2 us
  transfers between devices with their start and end apart: 59, of which 20 were waited for; matrix products, arithmetic and copies ran while one was open for 4% of the time, Pallas kernels for 69%

profile of v6, /device:TPU:0, one launch (start us, length us, event | category | flops | bytes accessed | tf_op | source)
XLA Modules:
  0.0 541.0 jit_solution(5861289856769711904)
XLA Ops:
  6.3 8.7 %modulate.1 = (f32[6,8,768]{2,1,0:T(8,128)}, f32[8,768]{1,0:T(8,128)}, bf16[1024,768]{1,0:T(8,128)(2,1)}, bf16[1056,768]{1,0:T(8,128)(2,1)}) custom-call(s32[8]{0:T(128)} %stack.63.refs_0_, f32[8,768]{1,0:T(8,128)} %pad.12.refs_1_.refs_3_, bf16[768,4608]{1,0:T(8,128)(2,1)} %refs_2_.5, bf16[1024,768]{1,0:T(8,128)(2,1)} %refs_4_.2), custom_call_target="tpu_custom_call" | custom-call | flops 1000 | bytes 1000 | tf_op jit(solution)/shard_map/modulate/pallas_call | solution.py:445
  16.4 8.5 %qkv.1.refs_1_.refs_2_.refs_3_ = bf16[1024,2304]{1,0:T(8,128)(2,1)} custom-call(bf16[1024,768]{1,0:T(8,128)(2,1)} %refs_4_.3, f32[6,8,768]{2,1,0:T(8,128)} %get-tuple-element.120.refs_1_.refs_2_.refs_12_.refs_7_.refs_6_, bf16[768,2304]{1,0:T(8,128)(2,1)} %refs_3_.5, bf16[1024,768]{1,0:T(8,128)(2,1)} %touch.27.refs_3_.refs_1_.refs_2_), custom_call_target="tpu_custom_call" | custom-call | flops 1000 | bytes 1000 | tf_op jit(solution)/shard_map/qkv/pallas_call | solution.py:445
  24.8 19.4 %attend.1 = (bf16[1024,768]{1,0:T(8,128)(2,1)}, f32[1024,768]{1,0:T(8,128)}) custom-call(s32[8]{0:T(128)} %stack.63.refs_0_, bf16[1024,2304]{1,0:T(8,128)(2,1)} %qkv.1.refs_1_.refs_2_.refs_3_, bf16[1024,2304]{1,0:T(8,128)(2,1)} %qkv.1.refs_1_.refs_2_.refs_3_, bf16[1024,2304]{1,0:T(8,128)(2,1)} %qkv.1.refs_1_.refs_2_.refs_3_), custom_call_target="tpu_custom_call" | custom-call | flops 1000 | bytes 1000 | tf_op jit(solution)/shard_map/attend/pallas_call | solution.py:445
  44.3 5.5 %middle.1 = (f32[1024,768]{1,0:T(8,128)}, bf16[1024,768]{1,0:T(8,128)(2,1)}) custom-call(bf16[1024,768]{1,0:T(8,128)(2,1)} %get-tuple-element.122.refs_0_.refs_4_.refs_6_, bf16[1024,768]{1,0:T(8,128)(2,1)} %refs_4_.3, f32[6,8,768]{2,1,0:T(8,128)} %get-tuple-element.120.refs_1_.refs_2_.refs_12_.refs_7_.refs_6_, bf16[768,768]{1,0:T(8,128)(2,1)} %refs_13_.1), custom_call_target="tpu_custom_call" | custom-call | flops 1000 | bytes 1000 | tf_op jit(solution)/shard_map/middle/pallas_call | solution.py:445
  57.2 30.5 %expert.4 = (bf16[4,2,768,384]{3,2,1,0:T(8,128)(2,1)}, bf16[4,2,768,384]{3,2,1,0:T(8,128)(2,1)}, bf16[2,288,768]{2,1,0:T(8,128)(2,1)}, bf16[2,288,768]{2,1,0:T(8,128)(2,1)}, f32[2,1,1024]{2,1,0:T(1,128)}) custom-call(s32[8]{0:T(128)} %stack.63.refs_0_, bf16[1024,768]{1,0:T(8,128)(2,1)} %get-tuple-element.123.refs_3_.refs_1_.refs_8_, ...), custom_call_target="tpu_custom_call" | custom-call | flops 1000 | bytes 1000 | tf_op jit(solution)/shard_map/expert/pallas_call | solution.py:445
  96.8 32.2 %expert.5 = (bf16[4,2,768,384]{3,2,1,0:T(8,128)(2,1)}, bf16[4,2,768,384]{3,2,1,0:T(8,128)(2,1)}, bf16[2,288,768]{2,1,0:T(8,128)(2,1)}, bf16[2,288,768]{2,1,0:T(8,128)(2,1)}, f32[2,1,1024]{2,1,0:T(1,128)}) custom-call(s32[8]{0:T(128)} %stack.63.refs_0_, bf16[1024,768]{1,0:T(8,128)(2,1)} %touch.30.refs_3_.refs_1_, bf16[1024,768]{1,0:T(8,128)(2,1)} %copy-done.12, ...), custom_call_target="tpu_custom_call" | custom-call | flops 1000 | bytes 1000 | tf_op jit(solution)/shard_map/expert/pallas_call | solution.py:445
  130.7 30.3 %expert.6 = (bf16[4,2,768,384]{3,2,1,0:T(8,128)(2,1)}, bf16[4,1,768,384]{3,2,1,0:T(8,128)(2,1)}, bf16[4,1,768,384]{3,2,1,0:T(8,128)(2,1)}, bf16[2,288,768]{2,1,0...) custom-call(s32[8]{0:T(128)} %stack.63.refs_0_, ...), custom_call_target="tpu_custom_call" | custom-call | flops 1000 | bytes 1000 | tf_op jit(solution)/shard_map/expert/pallas_call | solution.py:445
  161.0 32.1 %expert.7 = (bf16[4,2,768,384]{3,2,1,0:T(8,128)(2,1)}, bf16[4,1,768,384]{3,2,1,0:T(8,128)(2,1)}, bf16[4,1,768,384]{3,2,1,0:T(8,128)(2,1)}, bf16[2,288,768]{2,1,0...) custom-call(s32[8]{0:T(128)} %stack.63.refs_0_, bf16[1024,768]{1,0:T(8,128)(2,1)} %touch.30.refs_3_.refs_1_, ...), custom_call_target="tpu_custom_call" | custom-call | flops 1000 | bytes 1000 | tf_op jit(solution)/shard_map/expert/pallas_call | solution.py:445
  193.1 10.2 %combine.2 = (bf16[1024,768]{1,0:T(8,128)(2,1)}, bf16[1024,768]{1,0:T(8,128)(2,1)}, bf16[1024,768]{1,0:T(8,128)(2,1)}, bf16[512,768]{1,0:T(8,128)(2,1)}, bf16[512,768]{1,0:T(8,128)(2,1)}) custom-call(s32[2,1024,128]{2,1,0:T(8,128)} %get-tuple-element.137.refs_0_, bf16[2,288,768]{2,1,0:T(8,128)(2,1)} %get-tuple-element.138.refs_1_, ...), custom_call_target="tpu_custom_call" | custom-call | flops 1000 | bytes 1000 | tf_op jit(solution)/shard_map/combine/pallas_call | solution.py:445
  203.4 10.2 %combine.3 = (bf16[1024,768]{1,0:T(8,128)(2,1)}, bf16[1024,768]{1,0:T(8,128)(2,1)}, bf16[1024,768]{1,0:T(8,128)(2,1)}, bf16[512,768]{1,0:T(8,128)(2,1)}, bf16[512,768]{1,0:T(8,128)(2,1)}) custom-call(s32[2,1024,128]{2,1,0:T(8,128)} %get-tuple-element.148.refs_0_, bf16[2,288,768]{2,1,0:T(8,128)(2,1)} %get-tuple-element.149.refs_1_, ...), custom_call_target="tpu_custom_call" | custom-call | flops 1000 | bytes 1000 | tf_op jit(solution)/shard_map/combine/pallas_call | solution.py:445
  226.5 5.0 add_rows.1
  234.1 7.0 %halve_y.3 = (f32[2,4,384,384]{3,2,1,0:T(8,128)}, bf16[2,4,384,384]{3,2,1,0:T(8,128)(2,1)}) custom-call(bf16[4,2,768,384]{3,2,1,0:T(8,128)(2,1)} %get-tuple-element.135.refs_0_, bf16[4,2,768,384]{3,2,1,0:T(8,128)(2,1)} %collective-permute-done.9.refs_1_, bf16[4,4,384,384]{3,2,1,0:T(8,128)(2,1)} %bitcast.86, ...), custom_call_target="tpu_custom_call" | custom-call | flops 1000 | bytes 1000 | tf_op jit(solution)/shard_map/halve_y/pallas_call | solution.py:445
  245.1 43.6 %shared.1 = (bf16[2,768,768]{2,1,0:T(8,128)(2,1)}, bf16[768,768]{1,0:T(8,128)(2,1)}, bf16[768,768]{1,0:T(8,128)(2,1)}, bf16[2,2,4,192,384]{4,3,2,1,0:T(8,128)(2,...) custom-call(s32[8]{0:T(128)} %stack.63.refs_0_, ...), custom_call_target="tpu_custom_call" | custom-call | flops 1000 | bytes 1000 | tf_op jit(solution)/shard_map/shared/pallas_call | solution.py:445
  293.9 11.8 %middle_back.1 = (f32[1024,768]{1,0:T(8,128)}, bf16[1024,768]{1,0:T(8,128)(2,1)}, bf16[1024,768]{1,0:T(8,128)(2,1)}, f32[3,8,768]{2,1,0:T(8,128)}, f32[16,768]{1,0:T(8,128)}) custom-call(bf16[1024,768]{1,0:T(8,128)(2,1)} %get-tuple-element.163.refs_0_, bf16[1024,768]{1,0:T(8,128)(2,1)} %get-tuple-element.153.refs_1_, ...), custom_call_target="tpu_custom_call" | custom-call | flops 1000 | bytes 1000 | tf_op jit(solution)/shard_map/middle_back/pallas_call | solution.py:445
  305.7 5.2 halve_z.3
  319.5 8.8 %halve_slices.1 = (f32[2,1536,384]{2,1,0:T(8,128)}, bf16[2,1536,384]{2,1,0:T(8,128)(2,1)}) custom-call(bf16[2,768,768]{2,1,0:T(8,128)(2,1)} %get-tuple-element.167.refs_0_, bf16[2,1536,384]{2,1,0:T(8,128)(2,1)} %bitcast.107, bf16[768,768]{1,0:T(8,128)(2,1)} %copy-done.28, bf16[768,768]{1,0:T(8,128)(2,1)} %copy-done.29, bf16[1536,384]{1,0:T(8,128)(2,1)} %bitcast.112, ...), custom_call_target="tpu_custom_call" | custom-call | flops 1000 | bytes 1000 | tf_op jit(solution)/shard_map/halve_slices/pallas_call | solution.py:445
  329.6 36.8 %attend_back.1 = (bf16[1024,768]{1,0:T(8,128)(2,1)}, bf16[1024,768]{1,0:T(8,128)(2,1)}, bf16[1024,768]{1,0:T(8,128)(2,1)}) custom-call(s32[8]{0:T(128)} %stack.63.refs_0_, bf16[1024,2304]{1,0:T(8,128)(2,1)} %qkv.1.refs_1_.refs_2_.refs_3_, bf16[1024,2304]{1,0:T(8,128)(2,1)} %qkv.1.refs_1_.refs_2_.refs_3_, bf16[1024,2304]{1,0:T(8,128)(2,1)} %qkv.1.refs_1_.refs_2_.refs_3_, ...), custom_call_target="tpu_custom_call" | custom-call | flops 1000 | bytes 1000 | tf_op jit(solution)/shard_map/attend_back/pallas_call | solution.py:445
  376.0 14.7 %weight_grads.1 = (bf16[2,768,768]{2,1,0:T(8,128)(2,1)}, bf16[768,768]{1,0:T(8,128)(2,1)}, bf16[768,768]{1,0:T(8,128)(2,1)}) custom-call(s32[8]{0:T(128)} %stack.63.refs_0_, bf16[1024,768]{1,0:T(8,128)(2,1)} %refs_4_.3, f32[6,8,768]{2,1,0:T(8,128)} %get-tuple-element.120.refs_1_.refs_2_.refs_12_.refs_7_.refs_6_, ...), custom_call_target="tpu_custom_call" | custom-call | flops 1000 | bytes 1000 | tf_op jit(solution)/shard_map/weight_grads/pallas_call | solution.py:445
  405.1 7.2 %mixed.1 = (bf16[1024,768]{1,0:T(8,128)(2,1)}, f32[8,768]{1,0:T(8,128)}) custom-call(bf16[1024,768]{1,0:T(8,128)(2,1)} %get-tuple-element.160.refs_0_, bf16[1024,768]{1,0:T(8,128)(2,1)} %get-tuple-element.161.refs_1_, bf16[1024,768]{1,0:T(8,128)(2,1)} %touch.34.refs_8_.refs_2_, bf16[1024,768]{1,0:T(8,128)(2,1)} %touch.36.refs_4_.refs_3_, ...), custom_call_target="tpu_custom_call" | custom-call | flops 1000 | bytes 1000 | tf_op jit(solution)/shard_map/mixed/pallas_call | solution.py:445
  412.3 10.4 %inputs_back.1 = (f32[1024,768]{1,0:T(8,128)}, f32[2,8,768]{2,1,0:T(8,128)}) custom-call(bf16[1024,768]{1,0:T(8,128)(2,1)} %get-tuple-element.179.refs_1_.refs_3_.refs_0_, bf16[1024,768]{1,0:T(8,128)(2,1)} %get-tuple-element.180.refs_4_.refs_1_, bf16[1024,768]{1,0:T(8,128)(2,1)} %get-tuple-element.181.refs_5_.refs_2_, bf16[768,2304]{1,0:T(8,128)(2,1)} %refs_3_.5, ...), custom_call_target="tpu_custom_call" | custom-call | flops 1000 | bytes 1000 | tf_op jit(solution)/shard_map/inputs_back/pallas_call | solution.py:445
  447.4 7.3 %used_back.1.refs_1_.refs_2_ = f32[8,768]{1,0:T(8,128)} custom-call(s32[8]{0:T(128)} %stack.63.refs_0_, f32[6,8,768]{2,1,0:T(8,128)} %pad_maximum_fusion.10.refs_1_, bf16[768,4608]{1,0:T(8,128)(2,1)} %refs_2_.5, f32[8,768]{1,0:T(8,128)} %pad.12.refs_1_.refs_3_, bf16[1,4,192,384]{3,2,1,0:T(8,128)(2,1)} %touch.38.refs_4_.refs_1_.refs_2_), custom_call_target="tpu_custom_call" | custom-call | flops 1000 | bytes 1000 | tf_op jit(solution)/shard_map/used_back/pallas_call | solution.py:445
  472.3 5.6 %finish_kinds.3 = (f32[48,3072]{1,0:T(8,128)}, bf16[48,3072]{1,0:T(8,128)(2,1)}, f32[192,768]{1,0:T(8,128)}, bf16[192,768]{1,0:T(8,128)(2,1)}) custom-call(s32[8]{0:T(128)} %stack.63.refs_0_, f32[2,4,192,384]{3,2,1,0:T(8,128)} %get-tuple-element.212.refs_1_.refs_3_, bf16[2,4,192,384]{3,2,1,0:T(8,128)(2,1)} %touch.37.refs_8_.refs_2_.refs_4_, ...), custom_call_target="tpu_custom_call" | custom-call | flops 1000 | bytes 1000 | tf_op jit(solution)/shard_map/finish_kinds/pallas_call | solution.py:445
  478.8 10.0 %collective-permute-done.43 = bf16[1,192,768]{2,1,0:T(8,128)(2,1)} collective-permute-done((bf16[1,192,768]{2,1,0:T(8,128)(2,1)}, bf16[1,192,768]{2,1,0:T(8,128)(2,1)}, u32[]{:S(2)}, u32[]{:S(2)}) %collective-permute-start.43) | collective-permute-done | bytes 294944 | tf_op jit(solution)/shard_map/ppermute | solution.py:1451
  524.8 6.4 %collective-permute-done.57 = bf16[192,192]{1,0:T(8,128)(2,1)S(1)} collective-permute-done((bf16[192,192]{1,0:T(8,128)(2,1)S(1)}, bf16[192,192]{1,0:T(8,128)(2,1)S(1)}, u32[]{:S(2)}, u32[]{:S(2)}) %collective-permute-start.57) | collective-permute-done | bytes 73760 | tf_op jit(solution)/shard_map/ppermute | solution.py:1451
  (367 shorter events, 171.1 us)
Async XLA Ops:
  16.3 38.5 %collective-permute-start.5 = (bf16[1056,768]{1,0:T(8,128)(2,1)}, bf16[1056,768]{1,0:T(8,128)(2,1)S(1)}, u32[]{:S(2)}, u32[]{:S(2)}) collective-permute-start(bf16[1056,768]{1,0:T(8,128)(2,1)} %touch.28), channel_id=1, source_target_pairs={{0,1},{1,0},{2,3},{3,2},{4,5},{5,4},{6,7},{7,6},{8,9},{9,8},{10,11... | collective-permute-start | bytes 4866056 | tf_op jit(solution)/shard_map/ppermute | solution.py:1451
  50.3 37.9 %collective-permute-start.2 = (bf16[1024,768]{1,0:T(8,128)(2,1)}, bf16[1024,768]{1,0:T(8,128)(2,1)}, u32[]{:S(2)}, u32[]{:S(2)}) collective-permute-start(bf16[1024,768]{1,0:T(8,128)(2,1)} %get-tuple-element.123.refs_3_.refs_1_.refs_8_), channel_id=1, source_target_pairs={{0,1},{1,0},{2,3},{3,2},{4,5},{5,4},{6,7},{7,6},{8,9},{9,8},{10,11... | collective-permute-start | bytes 4718600 | tf_op jit(solution)/shard_map/ppermute | solution.py:1451
  55.9 39.2 %collective-permute-start.7 = (bf16[1056,768]{1,0:T(8,128)(2,1)}, bf16[1056,768]{1,0:T(8,128)(2,1)S(1)}, u32[]{:S(2)}, u32[]{:S(2)}) collective-permute-start(bf16[1056,768]{1,0:T(8,128)(2,1)} %touch.29.refs_11_.refs_3_), channel_id=1, source_target_pairs={{0,2},{2,0},{4,6},{6,4},{8,10},{10,8},{12,14},{14,12},{16,18},{18,... | collective-permute-start | bytes 4866056 | tf_op jit(solution)/shard_map/ppermute | solution.py:1451
  129.0 105.0 %collective-permute-start.9 = (bf16[4,2,768,384]{3,2,1,0:T(8,128)(2,1)}, bf16[4,2,768,384]{3,2,1,0:T(8,128)(2,1)}, u32[]{:S(2)}, u32[]{:S(2)}) collective-permute-start(bf16[4,2,768,384]{3,2,1,0:T(8,128)(2,1)} %get-tuple-element.136), channel_id=1, source_target_pairs={{0,4},{2,6},{4,0},{6,2},{8,12},{10,14},{12,8},{14,10},{16,20},{18,... | collective-permute-start | bytes 14155784 | tf_op jit(solution)/shard_map/ppermute | solution.py:1451
  221.3 69.1 %collective-permute-start.25 = (bf16[4,1,768,384]{3,2,1,0:T(8,128)(2,1)}, bf16[4,1,768,384]{3,2,1,0:T(8,128)(2,1)}, u32[]{:S(2)}, u32[]{:S(2)}) collective-permute-start(bf16[4,1,768,384]{3,2,1,0:T(8,128)(2,1)} %get-tuple-element.174), channel_id=1, source_target_pairs={{0,4},{2,6},{4,0},{6,2},{8,12},{10,14},{12,8},{14,10},{16,20},{18,... | collective-permute-start | bytes 7077896 | tf_op jit(solution)/shard_map/ppermute | solution.py:1451
  231.5 59.0 %collective-permute-start.20 = (bf16[1024,768]{1,0:T(8,128)(2,1)}, bf16[1024,768]{1,0:T(8,128)(2,1)}, u32[]{:S(2)}, u32[]{:S(2)}) collective-permute-start(bf16[1024,768]{1,0:T(8,128)(2,1)} %get-tuple-element.164), channel_id=1, source_target_pairs={{0,1},{1,0},{2,3},{3,2},{4,5},{5,4},{6,7},{7,6},{8,9},{9,8},{10,11... | collective-permute-start | bytes 4718600 | tf_op jit(solution)/shard_map/ppermute | solution.py:1451
  241.0 51.9 %collective-permute-start.26 = (bf16[2,4,384,384]{3,2,1,0:T(8,128)(2,1)}, bf16[2,4,384,384]{3,2,1,0:T(8,128)(2,1)S(1)}, u32[]{:S(2)}, u32[]{:S(2)}) collective-permute-start(bf16[2,4,384,384]{3,2,1,0:T(8,128)(2,1)} %get-tuple-element.158.refs_1_), channel_id=1, source_target_pairs={{0,8},{2,10},{4,12},{6,14},{8,0},{10,2},{12,4},{14,6},{16,24},{18,... | collective-permute-start | bytes 7077896 | tf_op jit(solution)/shard_map/ppermute | solution.py:1451
  288.9 77.4 %collective-permute-start.29 = (bf16[4,1,768,384]{3,2,1,0:T(8,128)(2,1)}, bf16[4,1,768,384]{3,2,1,0:T(8,128)(2,1)}, u32[]{:S(2)}, u32[]{:S(2)}) collective-permute-start(bf16[4,1,768,384]{3,2,1,0:T(8,128)(2,1)} %touch.35.refs_5_), channel_id=1, source_target_pairs={{0,4},{2,6},{4,0},{6,2},{8,12},{10,14},{12,8},{14,10},{16,20},{18,... | collective-permute-start | bytes 7077896 | tf_op jit(solution)/shard_map/ppermute | solution.py:1451
  290.5 25.1 %collective-permute-start.22 = (bf16[768,768]{1,0:T(8,128)(2,1)}, bf16[768,768]{1,0:T(8,128)(2,1)S(1)}, u32[]{:S(2)}, u32[]{:S(2)}) collective-permute-start(bf16[768,768]{1,0:T(8,128)(2,1)} %get-tuple-element.170), channel_id=1, source_target_pairs={{0,2},{2,0},{4,6},{6,4},{8,10},{10,8},{12,14},{14,12},{16,18},{18,... | collective-permute-start | bytes 3538952 | tf_op jit(solution)/shard_map/ppermute | solution.py:1451
  290.5 27.3 %collective-permute-start.23 = (bf16[2,4,192,384]{3,2,1,0:T(8,128)(2,1)}, bf16[2,4,192,384]{3,2,1,0:T(8,128)(2,1)S(1)}, u32[]{:S(2)}, u32[]{:S(2)}) collective-permute-start(bf16[2,4,192,384]{3,2,1,0:T(8,128)(2,1)} %get-tuple-element.171), channel_id=1, source_target_pairs={{0,2},{2,0},{4,6},{6,4},{8,10},{10,8},{12,14},{14,12},{16,18},{18,... | collective-permute-start | bytes 3538952 | tf_op jit(solution)/shard_map/ppermute | solution.py:1451
  291.8 27.6 %collective-permute-start.24 = (bf16[2,4,192,384]{3,2,1,0:T(8,128)(2,1)}, bf16[2,4,192,384]{3,2,1,0:T(8,128)(2,1)}, u32[]{:S(2)}, u32[]{:S(2)}) collective-permute-start(bf16[2,4,192,384]{3,2,1,0:T(8,128)(2,1)} %get-tuple-element.172), channel_id=1, source_target_pairs={{0,2},{2,0},{4,6},{6,4},{8,10},{10,8},{12,14},{14,12},{16,18},{18,... | collective-permute-start | bytes 3538952 | tf_op jit(solution)/shard_map/ppermute | solution.py:1451
  292.9 73.5 %collective-permute-start.19 = (bf16[1024,768]{1,0:T(8,128)(2,1)S(1)}, bf16[1024,768]{1,0:T(8,128)(2,1)}, u32[]{:S(2)}, u32[]{:S(2)}) collective-permute-start(bf16[1024,768]{1,0:T(8,128)(2,1)S(1)} %copy-done.26), channel_id=1, source_target_pairs={{0,1},{1,0},{2,3},{3,2},{4,5},{5,4},{6,7},{7,6},{8,9},{9,8},{10,11... | collective-permute-start | bytes 4718600 | tf_op jit(solution)/shard_map/ppermute | solution.py:1451
  315.5 59.4 %collective-permute-start.27 = (bf16[2,4,192,384]{3,2,1,0:T(8,128)(2,1)}, bf16[2,4,192,384]{3,2,1,0:T(8,128)(2,1)S(1)}, u32[]{:S(2)}, u32[]{:S(2)}) collective-permute-start(bf16[2,4,192,384]{3,2,1,0:T(8,128)(2,1)} %get-tuple-element.176.refs_2_), channel_id=1, source_target_pairs={{0,16},{2,18},{4,20},{6,22},{8,24},{10,26},{12,28},{14,30},{16,0},... | collective-permute-start | bytes 3538952 | tf_op jit(solution)/shard_map/ppermute | solution.py:1451
  317.8 53.1 %collective-permute-start.28 = (bf16[1,4,384,384]{3,2,1,0:T(8,128)(2,1)}, bf16[1,4,384,384]{3,2,1,0:T(8,128)(2,1)}, u32[]{:S(2)}, u32[]{:S(2)}) collective-permute-start(bf16[1,4,384,384]{3,2,1,0:T(8,128)(2,1)} %get-tuple-element.177.refs_6_), channel_id=1, source_target_pairs={{0,8},{2,10},{4,12},{6,14},{8,0},{10,2},{12,4},{14,6},{16,24},{18,... | collective-permute-start | bytes 3538952 | tf_op jit(solution)/shard_map/ppermute | solution.py:1451
  328.3 65.7 %collective-permute-start.32 = (bf16[2,1536,384]{2,1,0:T(8,128)(2,1)}, bf16[2,1536,384]{2,1,0:T(8,128)(2,1)S(1)}, u32[]{:S(2)}, u32[]{:S(2)}) collective-permute-start(bf16[2,1536,384]{2,1,0:T(8,128)(2,1)} %get-tuple-element.178.refs_7_), channel_id=1, source_target_pairs={{0,1},{1,0},{2,3},{3,2},{4,5},{5,4},{6,7},{7,6},{8,9},{9,8},{10,11... | collective-permute-start | bytes 7077896 | tf_op jit(solution)/shard_map/ppermute | solution.py:1451
  392.7 43.2 %collective-permute-start.34 = (bf16[1,4,384,384]{3,2,1,0:T(8,128)(2,1)}, bf16[1,4,384,384]{3,2,1,0:T(8,128)(2,1)S(1)}, u32[]{:S(2)}, u32[]{:S(2)}) collective-permute-start(bf16[1,4,384,384]{3,2,1,0:T(8,128)(2,1)} %get-tuple-element.184.refs_2_), channel_id=1, source_target_pairs={{0,8},{2,10},{4,12},{6,14},{8,0},{10,2},{12,4},{14,6},{16,24},{18,... | collective-permute-start | bytes 3538952 | tf_op jit(solution)/shard_map/ppermute | solution.py:1451
  393.7 47.5 %collective-permute-start.33 = (bf16[1,4,192,384]{3,2,1,0:T(8,128)(2,1)}, bf16[1,4,192,384]{3,2,1,0:T(8,128)(2,1)S(1)}, u32[]{:S(2)}, u32[]{:S(2)}) collective-permute-start(bf16[1,4,192,384]{3,2,1,0:T(8,128)(2,1)} %get-tuple-element.185.refs_1_), channel_id=1, source_target_pairs={{0,16},{2,18},{4,20},{6,22},{8,24},{10,26},{12,28},{14,30},{16,0},... | collective-permute-start | bytes 1769480 | tf_op jit(solution)/shard_map/ppermute | solution.py:1451
  400.0 27.6 %collective-permute-start.36 = (bf16[2,768,384]{2,1,0:T(8,128)(2,1)}, bf16[2,768,384]{2,1,0:T(8,128)(2,1)S(1)}, u32[]{:S(2)}, u32[]{:S(2)}) collective-permute-start(bf16[2,768,384]{2,1,0:T(8,128)(2,1)} %get-tuple-element.190.refs_3_), channel_id=1, source_target_pairs={{0,4},{2,6},{4,0},{6,2},{8,12},{10,14},{12,8},{14,10},{16,20},{18,... | collective-permute-start | bytes 3538952 | tf_op jit(solution)/shard_map/ppermute | solution.py:1451
  404.1 27.9 %collective-permute-start.35 = (bf16[1,768,768]{2,1,0:T(8,128)(2,1)}, bf16[1,768,768]{2,1,0:T(8,128)(2,1)S(1)}, u32[]{:S(2)}, u32[]{:S(2)}) collective-permute-start(bf16[1,768,768]{2,1,0:T(8,128)(2,1)} %get-tuple-element.191.refs_8_), channel_id=1, source_target_pairs={{0,1},{1,0},{2,3},{3,2},{4,5},{5,4},{6,7},{7,6},{8,9},{9,8},{10,11... | collective-permute-start | bytes 3538952 | tf_op jit(solution)/shard_map/ppermute | solution.py:1451
  456.8 36.1 %collective-permute-start.45 = (bf16[1,4,192,384]{3,2,1,0:T(8,128)(2,1)S(1)}, bf16[1,4,192,384]{3,2,1,0:T(8,128)(2,1)S(1)}, u32[]{:S(2)}, u32[]{:S(2)}) collective-permute-start(bf16[1,4,192,384]{3,2,1,0:T(8,128)(2,1)S(1)} %copy-done.40), channel_id=1, source_target_pairs={{0,16},{2,18},{4,20},{6,22},{8,24},{10,26},{12,28},{14,30},{16,0},... | collective-permute-start | bytes 1769480 | tf_op jit(solution)/shard_map/ppermute | solution.py:1451
  470.4 27.6 %collective-permute-start.47 = (bf16[32,6912]{1,0:T(8,128)(2,1)S(1)}, bf16[32,6912]{1,0:T(8,128)(2,1)S(1)}, u32[]{:S(2)}, u32[]{:S(2)}) collective-permute-start(bf16[32,6912]{1,0:T(8,128)(2,1)S(1)} %pad_maximum_fusion.6.refs_0_), channel_id=1, source_target_pairs={{0,1},{1,0},{2,3},{3,2},{4,5},{5,4},{6,7},{7,6},{8,9},{9,8},{10,11... | collective-permute-start | bytes 1327112 | tf_op jit(solution)/shard_map/ppermute | solution.py:1451
  470.9 31.5 %collective-permute-start.51 = (bf16[32,6912]{1,0:T(8,128)(2,1)S(1)}, bf16[32,6912]{1,0:T(8,128)(2,1)S(1)}, u32[]{:S(2)}, u32[]{:S(2)}) collective-permute-start(bf16[32,6912]{1,0:T(8,128)(2,1)S(1)} %pad_maximum_fusion.6.refs_0_), channel_id=1, source_target_pairs={{0,2},{2,0},{4,6},{6,4},{8,10},{10,8},{12,14},{14,12},{16,18},{18,... | collective-permute-start | bytes 1327112 | tf_op jit(solution)/shard_map/ppermute | solution.py:1451
  477.9 24.5 %collective-permute-start.49 = (bf16[48,3072]{1,0:T(8,128)(2,1)}, bf16[48,3072]{1,0:T(8,128)(2,1)S(1)}, u32[]{:S(2)}, u32[]{:S(2)}) collective-permute-start(bf16[48,3072]{1,0:T(8,128)(2,1)} %get-tuple-element.213.refs_2_), channel_id=1, source_target_pairs={{0,2},{2,0},{4,6},{6,4},{8,10},{10,8},{12,14},{14,12},{16,18},{18,... | collective-permute-start | bytes 884744 | tf_op jit(solution)/shard_map/ppermute | solution.py:1451
  503.6 31.7 %collective-permute-start.52 = (bf16[32,6912]{1,0:T(8,128)(2,1)S(1)}, bf16[32,6912]{1,0:T(8,128)(2,1)S(1)}, u32[]{:S(2)}, u32[]{:S(2)}) collective-permute-start(bf16[32,6912]{1,0:T(8,128)(2,1)S(1)} %copy-done.9), channel_id=1, source_target_pairs={{0,2},{2,0},{4,6},{6,4},{8,10},{10,8},{12,14},{14,12},{16,18},{18,... | collective-permute-start | bytes 1327112 | tf_op jit(solution)/shard_map/ppermute | solution.py:1451
  (104 other events, 656.9 us)
